TPU v7x, 32 devices: a whole 2x2x4 slice. The times are simulated.
32 devices in a mesh: sp: 4 (over y, x), fsdp: 8 (over z, core).
Axes of the slice: x: 2, y: 2, z: 4, core: 2. Of those that a mesh axis runs over, the one named last changes fastest.
Arguments:
- tokens: bfloat16 [8, 1536, 2560], P('fsdp', 'sp'), may hold values from -6 to 6
- cotangent: bfloat16 [8, 1536, 2560], P('fsdp', 'sp'), may hold values from -6 to 6
- attn_gain: bfloat16 [2560], P('fsdp'), may hold values from 0.099609375 to 1.8984375
- w_query: bfloat16 [2560, 2560], P('fsdp'), may hold values from -0.25 to 0.25
- key_weight: bfloat16 [2560, 640], P('fsdp'), may hold values from -0.125 to 0.125
- value_weight: bfloat16 [2560, 640], P('fsdp'), may hold values from -0.125 to 0.125
- w_out: bfloat16 [2560, 2560], P('fsdp'), may hold values from -0.5 to 0.5
- mlp_gain: bfloat16 [2560], P('fsdp'), may hold values from 0.099609375 to 1.8984375
- w_gate: bfloat16 [2560, 7168], P('fsdp'), may hold values from -0.125 to 0.125
- w_up: bfloat16 [2560, 7168], P('fsdp'), may hold values from -0.125 to 0.125
- w_down: bfloat16 [7168, 2560], P('fsdp'), may hold values from -0.09375 to 0.09375
- positions: int32 [8, 1536], P('fsdp', 'sp'), may hold values from 0 to 32767
- lengths: int32 [8, 3], P('fsdp'), may hold values from 1 to 1344, 1536 in all within a row
- deal_slots: int32 [8, 4, 8], replicated, may hold values from 0 to 63, as said below
Outputs:
- layer_out: bfloat16 [8, 1536, 2560], P('fsdp', 'sp')
- input_grad: bfloat16 [8, 1536, 2560], P('fsdp', 'sp')
- grad_attn_gain: float32 [2560], P('fsdp')
- grad_query: float32 [2560, 2560], P('fsdp')
- grad_key: float32 [2560, 640], P('fsdp')
- grad_value: float32 [2560, 640], P('fsdp')
- grad_out: float32 [2560, 2560], P('fsdp')
- grad_mlp_gain: float32 [2560], P('fsdp')
- grad_gate: float32 [2560, 7168], P('fsdp')
- grad_up: float32 [2560, 7168], P('fsdp')
- grad_down: float32 [7168, 2560], P('fsdp')
Inputs may be any that keep to these rules, and one draw needn't show every extreme that they name: In each group the 3 lengths sum to 1536, and the largest is 1344. For each f and s, deal_slots[f, s, j] // 8 names every group once over j; for each s all 64 entries are different.
All inputs are finite; a program needn't handle non-finite values.
Results may differ from a plain program's by a relative error of at most 0.024.
Values may be sent and summed in bfloat16 or wider, within the bound.
No kernel may reach another device: no remote copies, remote signals or barrier semaphores. Data moves between devices by JAX's collectives and lax.ppermute only.
A program may use at most 768 MiB of HBM per device.

v0:
```python
import jax
import jax.numpy as jnp
from jax import lax
from jax.sharding import PartitionSpec as P

QUERY_HEADS = 32
KEY_VALUE_HEADS = 8
HEAD_SIZE = 80


eps = 1e-05
theta = 1000000.0
masked_score = -1e30
block_rows = 512


def rms_scale(value_matrix, gains):
    return (
        value_matrix
        * lax.rsqrt(jnp.mean(value_matrix * value_matrix, axis=-1, keepdims=True) + eps)
        * gains
    )


def rotary_tables(positions, head):
    halves = head // 2
    frequency = theta ** (-(2.0 * jnp.arange(halves, dtype=jnp.float32)) / head)
    angles = positions.astype(jnp.float32)[:, None] * frequency[None, :]
    cosine = jnp.concatenate([jnp.cos(angles), jnp.cos(angles)], axis=1)
    sine = jnp.concatenate([jnp.sin(angles), jnp.sin(angles)], axis=1)
    return (cosine, sine)


def rotate(value_matrix, cosine, sine):
    halves = value_matrix.shape[-1] // 2
    turned = jnp.concatenate([-value_matrix[..., halves:], value_matrix[..., :halves]], axis=-1)
    return value_matrix * cosine[:, None, :] + turned * sine[:, None, :]


def rotate_back(grads, cosine, sine):
    halves = grads.shape[-1] // 2
    scaled = grads * sine[:, None, :]
    turned = jnp.concatenate([scaled[..., halves:], -scaled[..., :halves]], axis=-1)
    return grads * cosine[:, None, :] + turned


def gated(gate, upward):
    return jax.nn.silu(gate) * upward


def allowed_mask(segment, row_first, token_count, row_stop):
    query_segment = segment[row_first : row_first + token_count]
    places = jnp.arange(row_stop, dtype=jnp.int32)
    own_places = places[row_first : row_first + token_count]
    return (query_segment[:, None] == segment[None, :row_stop]) & (
        places[None, :] <= own_places[:, None]
    )


def block_scores(query_rows, key_rows, allowed):
    scores = jnp.einsum(
        "qkgd,skd->kgqs", query_rows, key_rows, preferred_element_type=jnp.float32
    ) * HEAD_SIZE ** (-0.5)
    return jnp.where(allowed[None, None], scores, masked_score)


def local(
    tokens,
    cotangent,
    attn_gain,
    w_query,
    key_weight,
    value_weight,
    w_out,
    mlp_gain,
    w_gate,
    w_up,
    w_down,
    positions,
    lengths,
    deal_slots,
):
    groups = lax.axis_size("fsdp")
    width = tokens.shape[-1]
    fsdp_place = lax.axis_index("fsdp")
    sp_place = lax.axis_index("sp")
    lanes = jnp.arange(groups, dtype=jnp.int32)
    own_row = deal_slots[fsdp_place, sp_place]
    target = own_row // groups
    pick_send = jnp.sum(jnp.where(target[None, :] == lanes[:, None], lanes[None, :], 0), axis=1)
    column = deal_slots[:, sp_place, :]
    arrived_slot = jnp.sum(jnp.where(column // groups == fsdp_place, column % groups, 0), axis=1)
    pick_place = jnp.sum(
        jnp.where(arrived_slot[None, :] == lanes[:, None], lanes[None, :], 0), axis=1
    )
    token_blocks = tokens.reshape(groups, -1, width)
    incoming_blocks = cotangent.reshape(groups, -1, width)
    came_tokens, came_incoming = (
        lax.all_to_all(
            jnp.take(token_blocks, pick_send, axis=0),
            "fsdp",
            split_axis=0,
            concat_axis=0,
            tiled=True,
        ),
        lax.all_to_all(
            jnp.take(incoming_blocks, pick_send, axis=0),
            "fsdp",
            split_axis=0,
            concat_axis=0,
            tiled=True,
        ),
    )
    owner_tokens = jnp.take(came_tokens, pick_place, axis=0).reshape(-1, width)
    owner_incoming = jnp.take(came_incoming, pick_place, axis=0).reshape(-1, width)
    rows = owner_tokens.shape[0]
    inputs = owner_tokens.astype(jnp.float32)
    gain_one_all, query_all, key_all, value_all, out_all = (
        lax.all_gather(attn_gain, "fsdp", axis=0, tiled=True),
        lax.all_gather(w_query, "fsdp", axis=0, tiled=True),
        lax.all_gather(key_weight, "fsdp", axis=0, tiled=True),
        lax.all_gather(value_weight, "fsdp", axis=0, tiled=True),
        lax.all_gather(w_out, "fsdp", axis=0, tiled=True),
    )
    normed_input, norm_one_back = jax.vjp(rms_scale, inputs, gain_one_all.astype(jnp.float32))
    normed_low = normed_input.astype(jnp.bfloat16)
    cosine, sine = rotary_tables(positions.reshape(-1), HEAD_SIZE)
    query_rows = jnp.dot(normed_low, query_all, preferred_element_type=jnp.float32)
    key_rows = jnp.dot(normed_low, key_all, preferred_element_type=jnp.float32)
    value_low = jnp.dot(normed_low, value_all, preferred_element_type=jnp.float32).astype(
        jnp.bfloat16
    )
    query_low = (
        rotate(query_rows.reshape(rows, -1, HEAD_SIZE), cosine, sine)
        .reshape(rows, -1)
        .astype(jnp.bfloat16)
    )
    key_low = (
        rotate(key_rows.reshape(rows, -1, HEAD_SIZE), cosine, sine)
        .reshape(rows, -1)
        .astype(jnp.bfloat16)
    )
    head_query, head_key, head_value = (
        lax.all_to_all(query_low, "sp", split_axis=1, concat_axis=0, tiled=True),
        lax.all_to_all(key_low, "sp", split_axis=1, concat_axis=0, tiled=True),
        lax.all_to_all(value_low, "sp", split_axis=1, concat_axis=0, tiled=True),
    )
    total_tokens = head_query.shape[0]
    kv_heads = head_key.shape[1] // HEAD_SIZE
    query_per_key = QUERY_HEADS // KEY_VALUE_HEADS
    grouped_query = head_query.reshape(total_tokens, kv_heads, query_per_key, HEAD_SIZE)
    grouped_key = head_key.reshape(total_tokens, kv_heads, HEAD_SIZE)
    grouped_value = head_value.reshape(total_tokens, kv_heads, HEAD_SIZE)
    ends = jnp.cumsum(lengths.reshape(-1))
    places = jnp.arange(total_tokens, dtype=jnp.int32)
    segment = jnp.sum((places[:, None] >= ends[None, :]).astype(jnp.int32), axis=1)
    span = min(block_rows, total_tokens)
    pieces = []
    totals = []
    for block_index in range(total_tokens // span):
        row_first = block_index * span
        row_stop = row_first + span
        allowed = allowed_mask(segment, row_first, span, row_stop)
        scores = block_scores(grouped_query[row_first:row_stop], grouped_key[:row_stop], allowed)
        top = jnp.max(scores, axis=-1, keepdims=True)
        weights = jnp.exp(scores - top)
        summed = jnp.sum(weights, axis=-1, keepdims=True)
        probs = (weights / summed).astype(jnp.bfloat16)
        mixed_heads = jnp.einsum(
            "kgqs,skd->qkgd", probs, grouped_value[:row_stop], preferred_element_type=jnp.float32
        )
        pieces.append(mixed_heads.reshape(span, -1))
        totals.append(top + jnp.log(summed))
    head_mixed = jnp.concatenate(pieces, axis=0).astype(jnp.bfloat16)
    mixed_low = lax.all_to_all(head_mixed, "sp", split_axis=0, concat_axis=1, tiled=True)
    hidden_one = inputs + jnp.dot(mixed_low, out_all, preferred_element_type=jnp.float32)
    gain_two_all, gate_all, up_all, down_all = (
        lax.all_gather(mlp_gain, "fsdp", axis=0, tiled=True),
        lax.all_gather(w_gate, "fsdp", axis=0, tiled=True),
        lax.all_gather(w_up, "fsdp", axis=0, tiled=True),
        lax.all_gather(w_down, "fsdp", axis=0, tiled=True),
    )
    normed_two, norm_two_back = jax.vjp(rms_scale, hidden_one, gain_two_all.astype(jnp.float32))
    normed_two_low = normed_two.astype(jnp.bfloat16)
    gate_rows = jnp.dot(normed_two_low, gate_all, preferred_element_type=jnp.float32)
    up_rows = jnp.dot(normed_two_low, up_all, preferred_element_type=jnp.float32)
    active, active_back = jax.vjp(gated, gate_rows, up_rows)
    active_low = active.astype(jnp.bfloat16)
    result = hidden_one + jnp.dot(active_low, down_all, preferred_element_type=jnp.float32)
    result_low = result.astype(jnp.bfloat16)
    gate_back, up_back, down_back = (gate_all, up_all, down_all)
    incoming = owner_incoming.astype(jnp.float32)
    d_active = jnp.einsum(
        "td,fd->tf", owner_incoming, down_back, preferred_element_type=jnp.float32
    )
    d_gate, d_up = active_back(d_active)
    d_gate_low = d_gate.astype(jnp.bfloat16)
    d_up_low = d_up.astype(jnp.bfloat16)
    d_normed_two = jnp.einsum(
        "tf,df->td", d_gate_low, gate_back, preferred_element_type=jnp.float32
    ) + jnp.einsum("tf,df->td", d_up_low, up_back, preferred_element_type=jnp.float32)
    d_hidden_part, d_mlp_gain = norm_two_back(d_normed_two)
    d_hidden = incoming + d_hidden_part
    d_branch = d_hidden.astype(jnp.bfloat16)
    d_mixed = jnp.einsum("td,cd->tc", d_branch, out_all, preferred_element_type=jnp.float32).astype(
        jnp.bfloat16
    )
    head_grad = lax.all_to_all(d_mixed, "sp", split_axis=1, concat_axis=0, tiled=True)
    grouped_grad = head_grad.reshape(total_tokens, kv_heads, query_per_key, HEAD_SIZE)
    query_grads = []
    key_grad = jnp.zeros((total_tokens, kv_heads, HEAD_SIZE), jnp.float32)
    value_grad = jnp.zeros((total_tokens, kv_heads, HEAD_SIZE), jnp.float32)
    for block_index in range(total_tokens // span):
        row_first = block_index * span
        row_stop = row_first + span
        allowed = allowed_mask(segment, row_first, span, row_stop)
        scores = block_scores(grouped_query[row_first:row_stop], grouped_key[:row_stop], allowed)
        probs = jnp.exp(scores - totals[block_index])
        grad_rows = grouped_grad[row_first:row_stop]
        value_grad = value_grad.at[:row_stop].add(
            jnp.einsum(
                "kgqs,qkgd->skd",
                probs.astype(jnp.bfloat16),
                grad_rows,
                preferred_element_type=jnp.float32,
            )
        )
        d_probs = jnp.einsum(
            "qkgd,skd->kgqs",
            grad_rows,
            grouped_value[:row_stop],
            preferred_element_type=jnp.float32,
        )
        delta = jnp.sum(probs * d_probs, axis=-1, keepdims=True)
        d_scores = (probs * (d_probs - delta)).astype(jnp.bfloat16)
        query_part = jnp.einsum(
            "kgqs,skd->qkgd", d_scores, grouped_key[:row_stop], preferred_element_type=jnp.float32
        )
        query_grads.append((query_part * HEAD_SIZE ** (-0.5)).reshape(span, -1))
        key_part = jnp.einsum(
            "kgqs,qkgd->skd",
            d_scores,
            grouped_query[row_first:row_stop],
            preferred_element_type=jnp.float32,
        )
        key_grad = key_grad.at[:row_stop].add(key_part * HEAD_SIZE ** (-0.5))
    query_head_grad = jnp.concatenate(query_grads, axis=0).astype(jnp.bfloat16)
    tok_query_grad, tok_key_grad, tok_value_grad = (
        lax.all_to_all(query_head_grad, "sp", split_axis=0, concat_axis=1, tiled=True),
        lax.all_to_all(
            key_grad.reshape(total_tokens, -1).astype(jnp.bfloat16),
            "sp",
            split_axis=0,
            concat_axis=1,
            tiled=True,
        ),
        lax.all_to_all(
            value_grad.reshape(total_tokens, -1).astype(jnp.bfloat16),
            "sp",
            split_axis=0,
            concat_axis=1,
            tiled=True,
        ),
    )
    query_pre = (
        rotate_back(tok_query_grad.astype(jnp.float32).reshape(rows, -1, HEAD_SIZE), cosine, sine)
        .reshape(rows, -1)
        .astype(jnp.bfloat16)
    )
    key_pre = (
        rotate_back(tok_key_grad.astype(jnp.float32).reshape(rows, -1, HEAD_SIZE), cosine, sine)
        .reshape(rows, -1)
        .astype(jnp.bfloat16)
    )
    d_normed = (
        jnp.einsum("tc,dc->td", query_pre, query_all, preferred_element_type=jnp.float32)
        + jnp.einsum("tc,dc->td", key_pre, key_all, preferred_element_type=jnp.float32)
        + jnp.einsum("tc,dc->td", tok_value_grad, value_all, preferred_element_type=jnp.float32)
    )
    d_inputs_part, d_attn_gain = norm_one_back(d_normed)
    d_inputs = d_hidden + d_inputs_part
    ff_width = w_gate.shape[1]
    grad_query = jnp.einsum("td,tc->dc", normed_low, query_pre, preferred_element_type=jnp.float32)
    grad_key = jnp.einsum("td,tc->dc", normed_low, key_pre, preferred_element_type=jnp.float32)
    grad_value = jnp.einsum(
        "td,tc->dc", normed_low, tok_value_grad, preferred_element_type=jnp.float32
    )
    grad_out = jnp.einsum("tc,td->cd", mixed_low, d_branch, preferred_element_type=jnp.float32)
    shard_attn_gain, shard_mlp_gain, shard_query, shard_key, shard_value, shard_out = (
        lax.psum_scatter(
            d_attn_gain.astype(jnp.bfloat16), "fsdp", scatter_dimension=0, tiled=True
        ).astype(jnp.float32),
        lax.psum_scatter(
            d_mlp_gain.astype(jnp.bfloat16), "fsdp", scatter_dimension=0, tiled=True
        ).astype(jnp.float32),
        lax.psum_scatter(
            grad_query.astype(jnp.bfloat16), "fsdp", scatter_dimension=0, tiled=True
        ).astype(jnp.float32),
        lax.psum_scatter(
            grad_key.astype(jnp.bfloat16), "fsdp", scatter_dimension=0, tiled=True
        ).astype(jnp.float32),
        lax.psum_scatter(
            grad_value.astype(jnp.bfloat16), "fsdp", scatter_dimension=0, tiled=True
        ).astype(jnp.float32),
        lax.psum_scatter(
            grad_out.astype(jnp.bfloat16), "fsdp", scatter_dimension=0, tiled=True
        ).astype(jnp.float32),
    )
    columns = normed_two_low
    gate_up_shard = lax.psum_scatter(
        jnp.concatenate(
            [
                jnp.einsum("tc,tf->cf", columns, d_gate_low, preferred_element_type=jnp.float32),
                jnp.einsum("tc,tf->cf", columns, d_up_low, preferred_element_type=jnp.float32),
            ],
            axis=1,
        ).astype(jnp.bfloat16),
        "fsdp",
        scatter_dimension=0,
        tiled=True,
    ).astype(jnp.float32)
    columns = active_low
    down_shard = lax.psum_scatter(
        jnp.einsum("tf,td->fd", columns, owner_incoming, preferred_element_type=jnp.float32).astype(
            jnp.bfloat16
        ),
        "fsdp",
        scatter_dimension=0,
        tiled=True,
    )
    shard_gate = gate_up_shard[:, :ff_width]
    shard_up = gate_up_shard[:, ff_width:]
    summed_grads = (
        lax.psum(shard_attn_gain.astype(jnp.bfloat16), "sp").astype(jnp.float32),
        lax.psum(shard_query.astype(jnp.bfloat16), "sp").astype(jnp.float32),
        lax.psum(shard_key.astype(jnp.bfloat16), "sp").astype(jnp.float32),
        lax.psum(shard_value.astype(jnp.bfloat16), "sp").astype(jnp.float32),
        lax.psum(shard_out.astype(jnp.bfloat16), "sp").astype(jnp.float32),
        lax.psum(shard_mlp_gain.astype(jnp.bfloat16), "sp").astype(jnp.float32),
        lax.psum(shard_gate.astype(jnp.bfloat16), "sp").astype(jnp.float32),
        lax.psum(shard_up.astype(jnp.bfloat16), "sp").astype(jnp.float32),
        lax.psum(down_shard, "sp").astype(jnp.float32),
    )
    back_result = jnp.take(result_low.reshape(groups, -1, width), arrived_slot, axis=0)
    back_grad = jnp.take(
        d_inputs.astype(jnp.bfloat16).reshape(groups, -1, width), arrived_slot, axis=0
    )
    gone_result, gone_grad = (
        lax.all_to_all(back_result, "fsdp", split_axis=0, concat_axis=0, tiled=True),
        lax.all_to_all(back_grad, "fsdp", split_axis=0, concat_axis=0, tiled=True),
    )
    layer_out = jnp.take(gone_result, target, axis=0).reshape(tokens.shape)
    input_grad = jnp.take(gone_grad, target, axis=0).reshape(tokens.shape)
    return (
        layer_out,
        input_grad,
        summed_grads[0],
        summed_grads[1],
        summed_grads[2],
        summed_grads[3],
        summed_grads[4],
        summed_grads[5],
        summed_grads[6],
        summed_grads[7],
        summed_grads[8],
    )


def solution(mesh):
    placed = (
        P("fsdp", "sp", None),
        P("fsdp", "sp", None),
        P("fsdp"),
        P("fsdp", None),
        P("fsdp", None),
        P("fsdp", None),
        P("fsdp", None),
        P("fsdp"),
        P("fsdp", None),
        P("fsdp", None),
        P("fsdp", None),
        P("fsdp", "sp"),
        P("fsdp", None),
        P(),
    )
    return jax.shard_map(
        local,
        mesh=mesh,
        in_specs=placed,
        out_specs=(
            P("fsdp", "sp", None),
            P("fsdp", "sp", None),
            P("fsdp"),
            P("fsdp", None),
            P("fsdp", None),
            P("fsdp", None),
            P("fsdp", None),
            P("fsdp"),
            P("fsdp", None),
            P("fsdp", None),
            P("fsdp", None),
        ),
        check_vma=False,
    )
```

profile of v0, /device:TPU:9, one launch (start us, length us, event | category | flops | bytes accessed | tf_op | source)
XLA Modules:
  0.0 3253.5 jit_solution(3868572177429956507)
XLA Ops:
  31.8 93.0 %all-reduce.7 = (bf16[2560]{0:T(1024)(128)(2,1)S(1)}, bf16[2560]{0:T(1024)(128)(2,1)}) all-reduce(bf16[2560]{0:T(1024)(128)(2,1)S(1)} %dynamic-update-slice.16, bf16[2560]{0:T(1024)(128)(2,1)S(1)} %dynamic-update-slice.17), channel_id=1, replica_groups=mesh['sp'=4,'fsdp'=8] {'fsdp'}, use_global_device_ids=true, to_apply=%add.2 | all-reduce | flops 5120 | bytes 20480
  152.9 85.3 %all-gather.12.cloned.1.call-done = bf16[2560,2560]{1,0:T(8,128)(2,1)} async-done(((bf16[320,2560]{1,0:T(8,128)(2,1)}), bf16[2560,2560]{1,0:T(8,128)(2,1)}) %all-gather.12.cloned.1.call-update) | async-done | bytes 13107216 | tf_op jit(solution)/shard_map/all_gather | solution.py:120
  451.1 266.1 %all-gather.18.cloned.1.call-done = bf16[2560,7168]{1,0:T(8,128)(2,1)} async-done(((bf16[320,7168]{1,0:T(8,128)(2,1)}), bf16[2560,7168]{1,0:T(8,128)(2,1)}) %all-gather.18.cloned.1.call-update) | async-done | bytes 36700176 | tf_op jit(solution)/shard_map/all_gather | solution.py:180
  717.2 23.3 fusion.131
  740.5 293.1 %all-gather.16.cloned.1.call-done = bf16[2560,7168]{1,0:T(8,128)(2,1)} async-done(((bf16[320,7168]{1,0:T(8,128)(2,1)}), bf16[2560,7168]{1,0:T(8,128)(2,1)}) %all-gather.16.cloned.1.call-update) | async-done | bytes 36700176 | tf_op jit(solution)/shard_map/all_gather | solution.py:179
  1033.6 23.8 fusion.130
  1057.4 292.8 %all-gather.20.cloned.1.call-done = bf16[7168,2560]{1,0:T(8,128)(2,1)} async-done(((bf16[896,2560]{1,0:T(8,128)(2,1)}), bf16[7168,2560]{1,0:T(8,128)(2,1)}) %all-gather.20.cloned.1.call-update) | async-done | bytes 36700176 | tf_op jit(solution)/shard_map/all_gather | solution.py:181
  1350.1 29.0 multiply_convert_fusion
  1379.2 25.7 convolution_convert_fusion.1
  1404.9 24.0 convolution_convert_fusion.2
  1428.8 48.2 %pad_maximum_fusion = bf16[2560,14336]{1,0:T(8,128)(2,1)} fusion(bf16[2560,7168]{1,0:T(8,128)(2,1)} %convolution_convert_fusion.1, bf16[2560,7168]{1,0:T(8,128)(2,1)} %convolution_convert_fusion.2), kind=kLoop, calls=%fused_computation.8 | loop fusion | flops 146800640 | bytes 146800640 | tf_op jit(solution)/shard_map/concatenate | solution.py:311
  1500.1 26.6 multiply_reduce_fusion
  1545.8 23.0 all-to-all-done.7
  1797.8 25.9 convolution_convert_fusion
  1824.1 351.6 %reduce-scatter.15.cloned.1.call-done = bf16[320,14336]{1,0:T(8,128)(2,1)} async-done(((bf16[2560,14336]{1,0:T(8,128)(2,1)}), bf16[320,14336]{1,0:T(8,128)(2,1)}) %reduce-scatter.15.cloned.1.call-update) | async-done | bytes 9175056 | tf_op jit(solution)/shard_map/reduce_scatter | solution.py:310
  2183.6 34.7 %reduce-scatter.11.cloned.1.call-done = bf16[320,640]{1,0:T(8,128)(2,1)} async-done(((bf16[2560,640]{1,0:T(8,128)(2,1)}), bf16[320,640]{1,0:T(8,128)(2,1)}) %reduce-scatter.11.cloned.1.call-update) | async-done | bytes 409616 | tf_op jit(solution)/shard_map/reduce_scatter | solution.py:302
  2218.3 43.0 %reduce-scatter.9.cloned.1.call-done = bf16[320,640]{1,0:T(8,128)(2,1)} async-done(((bf16[2560,640]{1,0:T(8,128)(2,1)}), bf16[320,640]{1,0:T(8,128)(2,1)}) %reduce-scatter.9.cloned.1.call-update) | async-done | bytes 409616 | tf_op jit(solution)/shard_map/reduce_scatter | solution.py:299
  2261.3 135.3 %reduce-scatter.13.cloned.1.call-done = bf16[320,2560]{1,0:T(8,128)(2,1)} async-done(((bf16[2560,2560]{1,0:T(8,128)(2,1)}), bf16[320,2560]{1,0:T(8,128)(2,1)}) %reduce-scatter.13.cloned.1.call-update) | async-done | bytes 1638416 | tf_op jit(solution)/shard_map/reduce_scatter | solution.py:305
  2396.6 134.7 %reduce-scatter.7.cloned.1.call-done = bf16[320,2560]{1,0:T(8,128)(2,1)} async-done(((bf16[2560,2560]{1,0:T(8,128)(2,1)}), bf16[320,2560]{1,0:T(8,128)(2,1)}) %reduce-scatter.7.cloned.1.call-update) | async-done | bytes 1638416 | tf_op jit(solution)/shard_map/reduce_scatter | solution.py:296
  2531.3 355.9 %reduce-scatter.17.cloned.1.call-done = bf16[896,2560]{1,0:T(8,128)(2,1)} async-done(((bf16[7168,2560]{1,0:T(8,128)(2,1)}), bf16[896,2560]{1,0:T(8,128)(2,1)}) %reduce-scatter.17.cloned.1.call-update) | async-done | bytes 4587536 | tf_op jit(solution)/shard_map/reduce_scatter | solution.py:323
  2887.9 23.9 fusion.27
  2944.6 49.3 %all_to_all.132 = bf16[8,48,2560]{2,1,0:T(8,128)(2,1)} all-to-all(bf16[8,48,2560]{2,1,0:T(8,128)(2,1)S(1)} %get-tuple-element.147), channel_id=1, replica_groups=mesh['sp'=4,'fsdp'=8] {'fsdp'}, dimensions={0} | all-to-all | bytes 3932160 | tf_op jit(solution)/shard_map/all_to_all | solution.py:350
  3000.2 59.0 %all-reduce.6 = (bf16[2560]{0:T(1024)(128)(2,1)S(1)}, bf16[2560]{0:T(1024)(128)(2,1)S(1)}) all-reduce(bf16[2560]{0:T(1024)(128)(2,1)S(1)} %get-tuple-element.102, bf16[2560]{0:T(1024)(128)(2,1)S(1)} %copy-done.74), channel_id=2, replica_groups=mesh['sp'=4,'fsdp'=8] {'fsdp'}, use_global_device_ids=true, to_apply=%region_19.21.clone | all-reduce | flops 5120 | bytes 20480
  3078.2 144.0 %all-reduce.12.cloned.1.call-done = (bf16[320,2560]{1,0:T(8,128)(2,1)}, bf16[320,640]{1,0:T(8,128)(2,1)}, bf16[320,640]{1,0:T(8,128)(2,1)}, bf16[320,2560]{1,0:T...) async-done(((bf16[320,2560]{1,0:T(8,128)(2,1)}, bf16[320,640]{1,0:T(8,128)(2,1)}, bf16[320,640]{1,0:T(8,128)(2,1)}, ...) | async-done | bytes 17858576 | tf_op jit(solution)/shard_map/psum | solution.py:335
  (413 shorter events, 625.4 us)
Async XLA Ops:
  7.2 125.7 %all-gather.8.cloned.1.call-start = ((), (), s32[]{:S(2)}) async-start(), calls=%async_computation.18 | async-start | bytes 3686400 | tf_op jit(solution)/shard_map/all_gather | solution.py:122
  7.9 133.8 %all-gather.10.cloned.1.call-start = ((), (), s32[]{:S(2)}) async-start(), calls=%async_computation.19 | async-start | bytes 3686400 | tf_op jit(solution)/shard_map/all_gather | solution.py:121
  8.7 229.5 %all-gather.12.cloned.1.call-start = ((), (), s32[]{:S(2)}) async-start(), calls=%async_computation.20 | async-start | bytes 14745600 | tf_op jit(solution)/shard_map/all_gather | solution.py:120
  9.4 429.4 %all-gather.14.cloned.1.call-start = ((), (), s32[]{:S(2)}) async-start(), calls=%async_computation.21 | async-start | bytes 14745600 | tf_op jit(solution)/shard_map/all_gather | solution.py:123
  10.0 707.2 %all-gather.18.cloned.1.call-start = ((), (), s32[]{:S(2)}) async-start(), calls=%async_computation.23 | async-start | bytes 41287680 | tf_op jit(solution)/shard_map/all_gather | solution.py:180
  10.6 1023.0 %all-gather.16.cloned.1.call-start = ((), (), s32[]{:S(2)}) async-start(), calls=%async_computation.22 | async-start | bytes 41287680 | tf_op jit(solution)/shard_map/all_gather | solution.py:179
  11.2 1339.0 %all-gather.20.cloned.1.call-start = ((), (), s32[]{:S(2)}) async-start(), calls=%async_computation.24 | async-start | bytes 41287680 | tf_op jit(solution)/shard_map/all_gather | solution.py:181
  24.1 101.2 %all-to-all-start = ((bf16[8,48,2560]{2,1,0:T(8,128)(2,1)}), bf16[8,48,2560]{2,1,0:T(8,128)(2,1)}, u32[]{:S(2)}, u32[]{:S(2)}) async-start(bf16[8,48,2560]{2,1,0:T(8,128)(2,1)} %get-tuple-element.152), calls=%async_computation | async-start | bytes 3932160 | tf_op jit(solution)/shard_map/all_to_all | solution.py:99
  138.1 133.1 %all-to-all-start.1 = ((bf16[384,4,160]{0,2,1:T(8,128)(2,1)}), bf16[384,4,160]{0,2,1:T(8,128)(2,1)S(1)}, u32[]{:S(2)}, u32[]{:S(2)}) async-start(bf16[384,4,160]{0,2,1:T(8,128)(2,1)} %bitcast.5), calls=%async_computation.1 | async-start | bytes 983040 | tf_op jit(solution)/shard_map/all_to_all | solution.py:146
  271.2 11.4 all-to-all-start.2
  282.6 27.5 all-to-all-start.3
  310.1 97.9 %all-to-all-start.6 = ((bf16[8,48,2560]{2,1,0:T(8,128)(2,1)}), bf16[8,48,2560]{2,1,0:T(8,128)(2,1)}, u32[]{:S(2)}, u32[]{:S(2)}) async-start(bf16[8,48,2560]{2,1,0:T(8,128)(2,1)} %get-tuple-element.151), calls=%async_computation.6 | async-start | bytes 3932160 | tf_op jit(solution)/shard_map/all_to_all | solution.py:106
  408.0 27.9 all-to-all-start.4
  412.6 1763.0 %reduce-scatter.15.cloned.1.call-start = ((), (), s32[]{:S(2)}) async-start(), calls=%async_computation.29 | async-start | bytes 82575360 | tf_op jit(solution)/shard_map/reduce_scatter | solution.py:310
  740.5 609.7 %copy-start.17 = (bf16[8,48,2560]{2,1,0:T(8,128)(2,1)S(1)}, bf16[8,48,2560]{2,1,0:T(8,128)(2,1)}, u32[]{:S(2)}) copy-start(bf16[8,48,2560]{2,1,0:T(8,128)(2,1)} %get-tuple-element.149) | copy-start | bytes 5898244
  1541.8 27.1 all-to-all-start.7
  1600.9 46.9 %all-to-all-start.10 = ((bf16[4,384,160]{1,2,0:T(8,128)(2,1)}), bf16[4,384,160]{1,2,0:T(8,128)(2,1)S(1)}, u32[]{:S(2)}, u32[]{:S(2)}) async-start(bf16[4,384,160]{1,2,0:T(8,128)(2,1)} %copy.165), calls=%async_computation.10 | async-start | bytes 983040 | tf_op jit(solution)/shard_map/all_to_all | solution.py:257
  1604.4 613.8 %reduce-scatter.11.cloned.1.call-start = ((), (), s32[]{:S(2)}) async-start(), calls=%async_computation.27 | async-start | bytes 3686400 | tf_op jit(solution)/shard_map/reduce_scatter | solution.py:302
  1653.4 607.9 %reduce-scatter.9.cloned.1.call-start = ((), (), s32[]{:S(2)}) async-start(), calls=%async_computation.26 | async-start | bytes 3686400 | tf_op jit(solution)/shard_map/reduce_scatter | solution.py:299
  1716.4 680.2 %reduce-scatter.13.cloned.1.call-start = ((), (), s32[]{:S(2)}) async-start(), calls=%async_computation.28 | async-start | bytes 14745600 | tf_op jit(solution)/shard_map/reduce_scatter | solution.py:305
  1728.5 802.8 %reduce-scatter.7.cloned.1.call-start = ((), (), s32[]{:S(2)}) async-start(), calls=%async_computation.25 | async-start | bytes 14745600 | tf_op jit(solution)/shard_map/reduce_scatter | solution.py:296
  1796.3 1090.8 %reduce-scatter.17.cloned.1.call-start = ((), (), s32[]{:S(2)}) async-start(), calls=%async_computation.30 | async-start | bytes 41287680 | tf_op jit(solution)/shard_map/reduce_scatter | solution.py:323
  1823.8 1398.4 %all-reduce.12.cloned.1.call-start = ((), (), s32[]{:S(2)}) async-start(), calls=%async_computation.31 | async-start | bytes 35717120 | tf_op jit(solution)/shard_map/psum | solution.py:335
  2994.0 77.6 %all-to-all-start.5 = ((bf16[8,48,2560]{2,1,0:T(8,128)(2,1)}), bf16[8,48,2560]{2,1,0:T(8,128)(2,1)S(1)}, u32[]{:S(2)}, u32[]{:S(2)}) async-start(bf16[8,48,2560]{2,1,0:T(8,128)(2,1)} %get-tuple-element.148), calls=%async_computation.5 | async-start | bytes 3932160 | tf_op jit(solution)/shard_map/all_to_all | solution.py:349
  (99 other events, 2106.6 us)
Sparse Core Ops, SparseCore 0:
  9.7 55.9 all-gather.7
  67.3 49.6 all-gather.9
  118.6 119.4 all-gather.11
  239.7 156.4 all-gather.13
  397.6 319.5 all-gather.17
  718.7 314.8 all-gather.15
  1035.2 314.8 all-gather.19
  1477.2 698.3 reduce-scatter.14
  2178.5 39.6 reduce-scatter.10
  2221.1 40.1 reduce-scatter.8
  2263.6 132.9 reduce-scatter.12
  2398.8 132.4 reduce-scatter.6
  2533.7 353.4 reduce-scatter.16
  2892.4 329.7 all-reduce.11
where the time goes:
time: 3270 us; the launch traced here: 3250 us
  waiting for transfers between devices  2190 us (67%)
  matrix products  446 us (14%)
  blocking collectives  241 us (7%)
  other arithmetic  189 us (6%)
  local copies, waits for them, and re-layouts  127 us (4%)
  starting transfers between devices  44.9 us (1%)
    reduce_scatter x1, waiting for transfers between devices, local(): lax.psum_scatter(jnp.einsum('tf,td->fd', columns, owner_incoming, preferr...  356 us
    reduce_scatter x1, waiting for transfers between devices, local(): lax.psum_scatter(jnp.concatenate([jnp.einsum('tc,tf->cf', columns, d_gate...  352 us
    all_gather x1, waiting for transfers between devices, local(): lax.all_gather(w_gate, 'fsdp', axis=0, tiled=True)  293 us
    all_gather x1, waiting for transfers between devices, local(): lax.all_gather(w_down, 'fsdp', axis=0, tiled=True)  293 us
    all_gather x1, waiting for transfers between devices, local(): lax.all_gather(w_up, 'fsdp', axis=0, tiled=True)  266 us
    unnamed x2, blocking collectives  152 us
    psum x1, waiting for transfers between devices, local(): lax.psum(shard_query.astype(jnp.bfloat16), 'sp').astype(jnp.float32)  144 us
    reduce_scatter x1, waiting for transfers between devices, local(): lax.psum_scatter(grad_out.astype(jnp.bfloat16), 'fsdp', scatter_dimension...  135 us
  transfers between devices with their start and end apart: 23, of which 15 were waited for; matrix products, arithmetic and copies ran while one was open for 18% of the time, Pallas kernels for 0%

commit v1 on v0

v1 whole, which is shorter than its diff:
```python
import jax
import jax.numpy as jnp
from jax import lax
from jax.experimental.layout import Layout, with_layout_constraint
from jax.sharding import PartitionSpec as P

QUERY_HEADS = 32
KEY_VALUE_HEADS = 8
HEAD_SIZE = 80


eps = 1e-05
theta = 1000000.0
masked_score = -1e30
block_rows = 512


def swap(value, bit):
    size = lax.axis_size("sp")
    return lax.ppermute(value, "sp", [(i, i ^ bit) for i in range(size)])


def row_major(value):
    return with_layout_constraint(value, Layout(major_to_minor=tuple(range(value.ndim))))


def gather_sp(value):
    size = lax.axis_size("sp")
    if size != 4:
        return lax.all_gather(value, "sp", axis=0, tiled=False)
    place = lax.axis_index("sp")
    half = value.shape[0] // 2
    first, second = value[:half], value[half:]
    x_first, y_second = swap(first, 1), swap(second, 2)
    x_second, y_first = swap(second, 1), swap(first, 2)
    far_first, far_second = swap(x_first, 2), swap(y_second, 1)
    out = jnp.zeros((size,) + value.shape, value.dtype)
    zeros = (0,) * (value.ndim - 1)
    for turn, low, high in (
        (0, first, second),
        (1, x_first, x_second),
        (2, y_first, y_second),
        (3, far_first, far_second),
    ):
        out = lax.dynamic_update_slice(out, low[None], (place ^ turn, 0) + zeros)
        out = lax.dynamic_update_slice(out, high[None], (place ^ turn, half) + zeros)
    return row_major(out)


def scatter_sp(parts):
    size = lax.axis_size("sp")
    if size != 4:
        return lax.psum_scatter(
            parts, "sp", scatter_dimension=0, tiled=False
        ).astype(jnp.float32)
    place = lax.axis_index("sp")
    half = parts.shape[1] // 2
    parts = row_major(parts)

    def block(turn, lower):
        start = (place ^ turn, 0 if lower else half) + (0,) * (parts.ndim - 2)
        return lax.dynamic_slice(parts, start, (1, half) + parts.shape[2:])[0]

    wide = jnp.float32
    low = parts.dtype
    from_x, from_y = swap(block(3, True), 1), swap(block(3, False), 2)
    x_first, y_second = swap(block(1, True), 1), swap(block(2, False), 2)
    y_first = swap((block(2, True).astype(wide) + from_x.astype(wide)).astype(low), 2)
    x_second = swap((block(1, False).astype(wide) + from_y.astype(wide)).astype(low), 1)
    first = block(0, True).astype(wide) + x_first.astype(wide) + y_first.astype(wide)
    second = block(0, False).astype(wide) + x_second.astype(wide) + y_second.astype(wide)
    return jnp.concatenate([first, second], axis=0)


def rotary_tables(positions, head):
    halves = head // 2
    frequency = theta ** (-(2.0 * jnp.arange(halves, dtype=jnp.float32)) / head)
    angles = positions.astype(jnp.float32)[:, None] * frequency[None, :]
    cosine = jnp.concatenate([jnp.cos(angles), jnp.cos(angles)], axis=1)
    sine = jnp.concatenate([jnp.sin(angles), jnp.sin(angles)], axis=1)
    return (cosine, sine)


def rotate(value_matrix, cosine, sine):
    halves = value_matrix.shape[-1] // 2
    turned = jnp.concatenate([-value_matrix[..., halves:], value_matrix[..., :halves]], axis=-1)
    return value_matrix * cosine[:, None, :] + turned * sine[:, None, :]


def rotate_back(grads, cosine, sine):
    halves = grads.shape[-1] // 2
    scaled = grads * sine[:, None, :]
    turned = jnp.concatenate([scaled[..., halves:], -scaled[..., :halves]], axis=-1)
    return grads * cosine[:, None, :] + turned


def gated(gate, upward):
    return jax.nn.silu(gate) * upward


def allowed_mask(segment, row_first, token_count, row_stop):
    query_segment = segment[row_first : row_first + token_count]
    places = jnp.arange(row_stop, dtype=jnp.int32)
    own_places = places[row_first : row_first + token_count]
    return (query_segment[:, None] == segment[None, :row_stop]) & (
        places[None, :] <= own_places[:, None]
    )


def block_scores(query_rows, key_rows, allowed):
    scores = jnp.einsum(
        "qkgd,skd->kgqs", query_rows, key_rows, preferred_element_type=jnp.float32
    ) * HEAD_SIZE ** (-0.5)
    return jnp.where(allowed[None, None], scores, masked_score)


def attention(query_low, key_low, value_low, segment):
    total_tokens = query_low.shape[0]
    kv_heads = key_low.shape[1] // HEAD_SIZE
    grouped_query = query_low.reshape(total_tokens, kv_heads, -1, HEAD_SIZE)
    grouped_key = key_low.reshape(total_tokens, kv_heads, HEAD_SIZE)
    grouped_value = value_low.reshape(total_tokens, kv_heads, HEAD_SIZE)
    span = min(block_rows, total_tokens)
    pieces = []
    totals = []
    for block_index in range(total_tokens // span):
        row_first = block_index * span
        row_stop = row_first + span
        allowed = allowed_mask(segment, row_first, span, row_stop)
        scores = block_scores(grouped_query[row_first:row_stop], grouped_key[:row_stop], allowed)
        top = jnp.max(scores, axis=-1, keepdims=True)
        weights = jnp.exp(scores - top)
        summed = jnp.sum(weights, axis=-1, keepdims=True)
        probs = (weights / summed).astype(jnp.bfloat16)
        mixed_heads = jnp.einsum(
            "kgqs,skd->qkgd", probs, grouped_value[:row_stop], preferred_element_type=jnp.float32
        )
        pieces.append(mixed_heads.reshape(span, -1))
        totals.append(top + jnp.log(summed))
    return jnp.concatenate(pieces, axis=0).astype(jnp.bfloat16), totals


def attention_back(query_low, key_low, value_low, segment, totals, d_mixed):
    total_tokens = query_low.shape[0]
    kv_heads = key_low.shape[1] // HEAD_SIZE
    grouped_query = query_low.reshape(total_tokens, kv_heads, -1, HEAD_SIZE)
    grouped_key = key_low.reshape(total_tokens, kv_heads, HEAD_SIZE)
    grouped_value = value_low.reshape(total_tokens, kv_heads, HEAD_SIZE)
    grouped_grad = d_mixed.reshape(total_tokens, kv_heads, -1, HEAD_SIZE)
    span = min(block_rows, total_tokens)
    query_grads = []
    key_grad = jnp.zeros((total_tokens, kv_heads, HEAD_SIZE), jnp.float32)
    value_grad = jnp.zeros((total_tokens, kv_heads, HEAD_SIZE), jnp.float32)
    for block_index in range(total_tokens // span):
        row_first = block_index * span
        row_stop = row_first + span
        allowed = allowed_mask(segment, row_first, span, row_stop)
        scores = block_scores(grouped_query[row_first:row_stop], grouped_key[:row_stop], allowed)
        probs = jnp.exp(scores - totals[block_index])
        grad_rows = grouped_grad[row_first:row_stop]
        value_grad = value_grad.at[:row_stop].add(
            jnp.einsum(
                "kgqs,qkgd->skd",
                probs.astype(jnp.bfloat16),
                grad_rows,
                preferred_element_type=jnp.float32,
            )
        )
        d_probs = jnp.einsum(
            "qkgd,skd->kgqs",
            grad_rows,
            grouped_value[:row_stop],
            preferred_element_type=jnp.float32,
        )
        delta = jnp.sum(probs * d_probs, axis=-1, keepdims=True)
        d_scores = (probs * (d_probs - delta)).astype(jnp.bfloat16)
        query_part = jnp.einsum(
            "kgqs,skd->qkgd", d_scores, grouped_key[:row_stop], preferred_element_type=jnp.float32
        )
        query_grads.append((query_part * HEAD_SIZE ** (-0.5)).reshape(span, -1))
        key_part = jnp.einsum(
            "kgqs,qkgd->skd",
            d_scores,
            grouped_query[row_first:row_stop],
            preferred_element_type=jnp.float32,
        )
        key_grad = key_grad.at[:row_stop].add(key_part * HEAD_SIZE ** (-0.5))
    return (
        jnp.concatenate(query_grads, axis=0).astype(jnp.bfloat16),
        key_grad.reshape(total_tokens, -1).astype(jnp.bfloat16),
        value_grad.reshape(total_tokens, -1).astype(jnp.bfloat16),
    )


def dot(left, right):
    return jnp.dot(left, right, preferred_element_type=jnp.float32)


def dot_rows(left, right):
    return lax.dot_general(left, right, (((0,), (0,)), ((), ())), preferred_element_type=jnp.float32)


def dot_cols(left, right):
    return lax.dot_general(left, right, (((1,), (1,)), ((), ())), preferred_element_type=jnp.float32)


def local(
    tokens,
    cotangent,
    attn_gain,
    w_query,
    key_weight,
    value_weight,
    w_out,
    mlp_gain,
    w_gate,
    w_up,
    w_down,
    positions,
    lengths,
    deal_slots,
):
    groups = lax.axis_size("fsdp")
    parts = lax.axis_size("sp")
    width = tokens.shape[-1]
    rows = tokens.shape[1]
    fsdp_place = lax.axis_index("fsdp")
    sp_place = lax.axis_index("sp")
    low = jnp.bfloat16
    wide = jnp.float32

    lanes = jnp.arange(groups, dtype=jnp.int32)
    own_row = deal_slots[fsdp_place, sp_place]
    target = own_row // groups
    pick_send = jnp.sum(jnp.where(target[None, :] == lanes[:, None], lanes[None, :], 0), axis=1)
    column = deal_slots[:, sp_place, :]
    arrived_slot = jnp.sum(jnp.where(column // groups == fsdp_place, column % groups, 0), axis=1)
    pick_place = jnp.sum(
        jnp.where(arrived_slot[None, :] == lanes[:, None], lanes[None, :], 0), axis=1
    )

    def to_owner(given):
        blocks = jnp.take(given.reshape(groups, -1, width), pick_send, axis=0)
        came = lax.all_to_all(blocks, "fsdp", split_axis=0, concat_axis=0, tiled=True)
        return jnp.take(came, pick_place, axis=0).reshape(rows, width)

    def to_given(owned):
        blocks = jnp.take(owned.reshape(groups, -1, width), arrived_slot, axis=0)
        gone = lax.all_to_all(blocks, "fsdp", split_axis=0, concat_axis=0, tiled=True)
        return jnp.take(gone, target, axis=0).reshape(tokens.shape)

    def column_share(weight):
        share = weight.shape[1] // parts
        return lax.dynamic_slice_in_dim(weight, sp_place * share, share, axis=1)

    def gather_fsdp(shard):
        return lax.all_gather(shard, "fsdp", axis=0, tiled=True)

    ff_rows = w_down.shape[0]
    ff_share = ff_rows // parts

    def hidden_share(weight):
        def pick(place):
            starts = [i * ff_rows + place * ff_share for i in range(groups)]
            return lambda: jnp.concatenate([weight[:, i : i + ff_share] for i in starts], axis=1)

        return lax.switch(sp_place, [pick(place) for place in range(parts)])

    query_cols = w_query.shape[1] // parts
    key_cols = key_weight.shape[1] // parts
    qkv_cols = query_cols + 2 * key_cols
    extra = -qkv_cols % 128
    extra = extra if extra else 128
    gains = jnp.pad(jnp.stack([attn_gain, mlp_gain], axis=1), ((0, 0), (0, extra - 2)))
    qkv_shard = jnp.concatenate(
        [column_share(w_query), column_share(key_weight), column_share(value_weight), gains], axis=1
    )
    qkv_all = gather_fsdp(qkv_shard)
    out_all = gather_fsdp(column_share(w_out))
    gate_all = gather_fsdp(hidden_share(w_gate))
    up_all = gather_fsdp(hidden_share(w_up))
    down_all = gather_fsdp(lax.dynamic_slice_in_dim(w_down, sp_place * ff_share, ff_share, axis=0))
    qkv_weight = qkv_all[:, :qkv_cols]
    gain_one = qkv_all[:, qkv_cols].astype(wide)[None, :]
    gain_two = qkv_all[:, qkv_cols + 1].astype(wide)[None, :]

    group_inputs = gather_sp(to_owner(tokens)).reshape(-1, width)
    group_incoming = gather_sp(to_owner(cotangent)).reshape(-1, width)
    group_positions = gather_sp(positions.reshape(-1, 1)).reshape(-1)
    total = group_inputs.shape[0]

    inputs = group_inputs.astype(wide)
    rms_one = lax.rsqrt(jnp.mean(inputs * inputs, axis=-1, keepdims=True) + eps)
    normed = (inputs * rms_one * gain_one).astype(low)
    cosine, sine = rotary_tables(group_positions, HEAD_SIZE)
    qkv_rows = dot(normed, qkv_weight)

    def turn(matrix):
        return rotate(matrix.reshape(total, -1, HEAD_SIZE), cosine, sine).reshape(total, -1).astype(low)

    query_low = turn(qkv_rows[:, :query_cols])
    key_low = turn(qkv_rows[:, query_cols : query_cols + key_cols])
    value_low = qkv_rows[:, query_cols + key_cols :].astype(low)
    ends = jnp.cumsum(lengths.reshape(-1))
    places = jnp.arange(total, dtype=jnp.int32)
    segment = jnp.sum((places[:, None] >= ends[None, :]).astype(jnp.int32), axis=1)
    own_mixed, totals = attention(query_low, key_low, value_low, segment)

    def side_by_side(stacked):
        return jnp.concatenate([stacked[i] for i in range(parts)], axis=1)

    def by_columns(matrix):
        share = matrix.shape[1] // parts
        return jnp.stack([matrix[:, i * share : (i + 1) * share] for i in range(parts)], axis=0)

    share = width // parts

    def own_columns(matrix):
        return lax.dynamic_slice_in_dim(matrix, sp_place * share, share, axis=1)

    mixed = side_by_side(gather_sp(own_mixed))
    own_hidden = own_columns(group_inputs).astype(wide) + dot(mixed, out_all)
    hidden_low = side_by_side(gather_sp(own_hidden.astype(low)))

    hidden = hidden_low.astype(wide)
    rms_two = lax.rsqrt(jnp.mean(hidden * hidden, axis=-1, keepdims=True) + eps)
    normed_two = (hidden * rms_two * gain_two).astype(low)
    gate = dot(normed_two, gate_all)
    upward = dot(normed_two, up_all)
    active, active_back = jax.vjp(gated, gate, upward)
    active_low = active.astype(low)
    grad_down = dot_rows(active_low, group_incoming)
    d_active = dot_cols(group_incoming, down_all)
    d_gate, d_up = active_back(d_active)
    d_gate, d_up = d_gate.astype(low), d_up.astype(low)
    grad_gate = dot_rows(normed_two, d_gate).astype(low)
    grad_up = dot_rows(normed_two, d_up).astype(low)
    grad_down = grad_down.astype(low)
    d_gate, d_up, grad_gate, grad_up, grad_down = lax.optimization_barrier(
        (d_gate, d_up, grad_gate, grad_up, grad_down)
    )
    d_normed_two = dot_cols(d_gate, gate_all) + dot_cols(d_up, up_all)
    result_part = dot(active_low, down_all).astype(low)
    own_hidden_rows = lax.dynamic_slice_in_dim(hidden_low, sp_place * rows, rows, axis=0)
    result = own_hidden_rows.astype(wide) + scatter_sp(result_part.reshape(parts, rows, width))
    layer_out = to_given(result.astype(low))

    grad_gain_two = jnp.sum(d_normed_two * hidden * rms_two, axis=0)
    scaled = gain_two * d_normed_two
    back_two = rms_two * scaled - hidden * rms_two**3 * jnp.mean(scaled * hidden, axis=-1, keepdims=True)
    own_d_hidden = own_columns(group_incoming).astype(wide) + scatter_sp(by_columns(back_two.astype(low)))
    d_branch = own_d_hidden.astype(low)
    grad_out = dot_rows(mixed, d_branch)
    d_mixed = scatter_sp(by_columns(dot_cols(d_branch, out_all).astype(low))).astype(low)
    d_query, d_key, d_value = attention_back(query_low, key_low, value_low, segment, totals, d_mixed)

    def turn_back(matrix):
        return (
            rotate_back(matrix.astype(wide).reshape(total, -1, HEAD_SIZE), cosine, sine)
            .reshape(total, -1)
            .astype(low)
        )

    d_qkv = jnp.concatenate([turn_back(d_query), turn_back(d_key), d_value], axis=1)
    grad_qkv = dot_rows(normed, d_qkv)
    d_normed = dot_cols(d_qkv, qkv_weight)
    grad_gain_one = jnp.sum(d_normed * inputs * rms_one, axis=0)
    scaled_one = gain_one * d_normed
    back_one = rms_one * scaled_one - inputs * rms_one**3 * jnp.mean(
        scaled_one * inputs, axis=-1, keepdims=True
    )
    own_place = (jnp.arange(width, dtype=jnp.int32) // share == sp_place)[None, :]
    spread = jnp.concatenate([own_d_hidden] * parts, axis=1)
    back_one = back_one + jnp.where(own_place, spread, 0.0)
    d_inputs = scatter_sp(back_one.astype(low).reshape(parts, rows, width))
    input_grad = to_given(d_inputs.astype(low))

    def scatter_fsdp(matrix):
        return lax.psum_scatter(matrix.astype(low), "fsdp", scatter_dimension=0, tiled=True)

    def all_sp(shard, axis):
        return lax.all_gather(shard, "sp", axis=axis, tiled=True)

    down_shard = all_sp(scatter_fsdp(grad_down), 0).astype(wide)

    def hidden_whole(shard):
        gathered = lax.all_gather(shard, "sp", axis=0, tiled=False)
        return jnp.concatenate(
            [
                gathered[i, :, j * ff_share : (j + 1) * ff_share]
                for j in range(groups)
                for i in range(parts)
            ],
            axis=1,
        ).astype(wide)

    gate_shard = hidden_whole(scatter_fsdp(grad_gate))
    up_shard = hidden_whole(scatter_fsdp(grad_up))
    out_shard = all_sp(scatter_fsdp(grad_out), 1).astype(wide)
    gain_grads = jnp.pad(
        jnp.stack([grad_gain_one, grad_gain_two], axis=1), ((0, 0), (0, extra - 2))
    )
    qkv_shards = lax.all_gather(
        scatter_fsdp(jnp.concatenate([grad_qkv, gain_grads], axis=1)), "sp", axis=0, tiled=False
    ).astype(wide)
    edges = (0, query_cols, query_cols + key_cols, qkv_cols)
    query_shard, key_shard, value_shard = (
        side_by_side(qkv_shards[:, :, edges[i] : edges[i + 1]]) for i in range(3)
    )
    gain_shards = jnp.sum(qkv_shards[:, :, qkv_cols : qkv_cols + 2], axis=0)
    return (
        layer_out,
        input_grad,
        gain_shards[:, 0],
        query_shard,
        key_shard,
        value_shard,
        out_shard,
        gain_shards[:, 1],
        gate_shard,
        up_shard,
        down_shard,
    )


def solution(mesh):
    placed = (
        P("fsdp", "sp", None),
        P("fsdp", "sp", None),
        P("fsdp"),
        P("fsdp", None),
        P("fsdp", None),
        P("fsdp", None),
        P("fsdp", None),
        P("fsdp"),
        P("fsdp", None),
        P("fsdp", None),
        P("fsdp", None),
        P("fsdp", "sp"),
        P("fsdp", None),
        P(),
    )
    return jax.shard_map(
        local,
        mesh=mesh,
        in_specs=placed,
        out_specs=(
            P("fsdp", "sp", None),
            P("fsdp", "sp", None),
            P("fsdp"),
            P("fsdp", None),
            P("fsdp", None),
            P("fsdp", None),
            P("fsdp", None),
            P("fsdp"),
            P("fsdp", None),
            P("fsdp", None),
            P("fsdp", None),
        ),
        check_vma=False,
    )
```

time: 3270 us -> 1760 us (0.54)
  waiting for transfers between devices: 2190 us -> 868 us
  blocking collectives: 241 us -> 71.7 us
  matrix products: 446 us -> 396 us
    reduce_scatter x6 -> x5, waiting for transfers between devices: 1060 us -> 147 us  [scatter_fsdp(): lax.psum_scatter(matrix.astype(low), 'fsdp', scatter_dimension=0, tiled=T...]
    all_gather x7 -> x10, waiting for transfers between devices: 937 us -> 171 us  [the longest x2 84.4 us: hidden_whole(): gathered = lax.all_gather(shard, 'sp', axis=0, tiled=False)]
    ppermute x0 -> x54, waiting for transfers between devices: none -> 438 us  [swap(): return lax.ppermute(value, 'sp', [(i, i ^ bit) for i in range(size)])]
    unnamed x2 -> x0, blocking collectives: 152 us -> none
    psum x1 -> x0, waiting for transfers between devices: 144 us -> none  [local(): lax.psum(shard_query.astype(jnp.bfloat16), 'sp').astype(jnp.float32)]
    all_to_all x9 -> x3, waiting for transfers between devices: 47.4 us -> 108 us  [the longest x2 102 us: to_owner(): lax.all_to_all(blocks, 'fsdp', split_axis=0, concat_axis=0, tiled=True)]
    dot_general x36 -> x30, matrix products: 424 us -> 375 us  [the longest x5 102 us: dot_cols(): lax.dot_general(left, right, (((1,), (1,)), ((), ())), preferred_element_...]
    concatenate x3 -> x7, other arithmetic: 52.2 us -> 8.92 us  [the longest x3 4.72 us: side_by_side(): return jnp.concatenate([stacked[i] for i in range(parts)], axis=1)]
  transfers between devices with their start and end apart: 23 -> 72, of which waited for: 15 -> 37; matrix products, arithmetic and copies ran while one was open for 18% -> 31% of each run, Pallas kernels for 0% -> 0%
where the time goes in v1:
time: 1760 us; the launch traced here: 1750 us
  waiting for transfers between devices  868 us (49%)
  matrix products  396 us (22%)
  other arithmetic  180 us (10%)
  local copies, waits for them, and re-layouts  158 us (9%)
  blocking collectives  71.7 us (4%)
  starting transfers between devices  62.3 us (4%)
    ppermute x54, waiting for transfers between devices, swap(): return lax.ppermute(value, 'sp', [(i, i ^ bit) for i in range(size)])  438 us
    reduce_scatter x5, waiting for transfers between devices, scatter_fsdp(): lax.psum_scatter(matrix.astype(low), 'fsdp', scatter_dimension=0, tiled=T...  147 us
    all_to_all x2, waiting for transfers between devices, to_owner(): lax.all_to_all(blocks, 'fsdp', split_axis=0, concat_axis=0, tiled=True)  102 us
    dot_general x5, matrix products, dot_cols(): lax.dot_general(left, right, (((1,), (1,)), ((), ())), preferred_element_...  102 us
    dot_general x5, matrix products, dot(): return jnp.dot(left, right, preferred_element_type=jnp.float32)  86.1 us
    all_gather x2, waiting for transfers between devices, hidden_whole(): gathered = lax.all_gather(shard, 'sp', axis=0, tiled=False)  84.4 us
    dot_general x5, matrix products, dot_rows(): lax.dot_general(left, right, (((0,), (0,)), ((), ())), preferred_element_...  83.4 us
    all_to_all x1, blocking collectives, to_given(): lax.all_to_all(blocks, 'fsdp', split_axis=0, concat_axis=0, tiled=True)  71.7 us
  transfers between devices with their start and end apart: 72, of which 37 were waited for; matrix products, arithmetic and copies ran while one was open for 31% of the time, Pallas kernels for 0%

profile of v1, /device:TPU:9, one launch (start us, length us, event | category | flops | bytes accessed | tf_op | source)
XLA Modules:
  0.0 1752.7 jit_solution(12902052097149239760)
XLA Ops:
  50.2 56.5 %all-to-all-done.2 = bf16[8,48,2560]{2,1,0:T(8,128)(2,1)S(1)} async-done(((bf16[8,48,2560]{2,1,0:T(8,128)(2,1)}), bf16[8,48,2560]{2,1,0:T(8,128)(2,1)S(1)}, u32[]{:S(2)}, u32[]{:S(2)}) %all-to-all-start.2) | async-done | bytes 1966112 | tf_op jit(solution)/shard_map/all_to_all | solution.py:244
  139.5 45.9 %all-to-all-done = bf16[8,48,2560]{2,1,0:T(8,128)(2,1)} async-done(((bf16[8,48,2560]{2,1,0:T(8,128)(2,1)}), bf16[8,48,2560]{2,1,0:T(8,128)(2,1)}, u32[]{:S(2)}, u32[]{:S(2)}) %all-to-all-start) | async-done | bytes 1966112 | tf_op jit(solution)/shard_map/all_to_all | solution.py:244
  197.7 39.0 %collective-permute-done = bf16[192,2560]{1,0:T(8,128)(2,1)S(1)} collective-permute-done((bf16[192,2560]{1,0:T(8,128)(2,1)S(1)}, bf16[192,2560]{1,0:T(8,128)(2,1)S(1)}, u32[]{:S(2)}, u32[]{:S(2)}) %collective-permute-start) | collective-permute-done | bytes 983072 | tf_op jit(solution)/shard_map/ppermute | solution.py:20
  278.8 20.6 %collective-permute-done.3 = bf16[192,2560]{1,0:T(8,128)(2,1)S(1)} collective-permute-done((bf16[192,2560]{1,0:T(8,128)(2,1)S(1)}, bf16[192,2560]{1,0:T(8,128)(2,1)S(1)}, u32[]{:S(2)}, u32[]{:S(2)}) %collective-permute-start.3) | collective-permute-done | bytes 983072 | tf_op jit(solution)/shard_map/ppermute | solution.py:20
  301.5 40.2 %collective-permute-done.4 = bf16[192,2560]{1,0:T(8,128)(2,1)S(1)} collective-permute-done((bf16[192,2560]{1,0:T(8,128)(2,1)S(1)}, bf16[192,2560]{1,0:T(8,128)(2,1)S(1)}, u32[]{:S(2)}, u32[]{:S(2)}) %collective-permute-start.4) | collective-permute-done | bytes 983072 | tf_op jit(solution)/shard_map/ppermute | solution.py:20
  541.5 19.9 %collective-permute-done.18 = bf16[768,640]{1,0:T(8,128)(2,1)S(1)} collective-permute-done((bf16[768,640]{1,0:T(8,128)(2,1)S(1)}, bf16[768,640]{1,0:T(8,128)(2,1)S(1)}, u32[]{:S(2)}, u32[]{:S(2)}) %collective-permute-start.18) | collective-permute-done | bytes 983072 | tf_op jit(solution)/shard_map/ppermute | solution.py:20
  588.0 21.3 %fusion.147 = f32[1536,1792]{1,0:T(8,128)} fusion(bf16[2560,1792]{1,0:T(8,128)(2,1)} %all-gather.20.cloned.1.call-done, bf16[1536,2560]{1,0:T(8,128)(2,1)} %get-tuple-element.139, f32[2560]{0:T(1024)S(1)} %copy-done.64, f32[1536]{0:T(1024)S(1)} %get-tuple-element.350), kind=kOutput, calls=%fused_computation.453 | convolution fusion | flops 14108590080 | bytes 28065792 | tf_op jit(solution)/shard_map/dot_general | solution.py:196
  609.3 21.8 %fusion.149 = f32[1536,1792]{1,0:T(8,128)} fusion(bf16[2560,1792]{1,0:T(8,128)(2,1)} %all-gather.18.cloned.1.call-done, bf16[1536,2560]{1,0:T(8,128)(2,1)} %get-tuple-element.139, f32[2560]{0:T(1024)S(1)} %copy-done.64, f32[1536]{0:T(1024)S(1)} %get-tuple-element.350), kind=kOutput, calls=%fused_computation.454 | convolution fusion | flops 14108590080 | bytes 28065792 | tf_op jit(solution)/shard_map/dot_general | solution.py:196
  631.1 28.0 %multiply_convert_fusion = (bf16[1536,1792]{1,0:T(8,128)(2,1)}, bf16[1536,1792]{1,0:T(8,128)(2,1)}, bf16[1536,1792]{1,0:T(8,128)(2,1)}) fusion(f32[1536,1792]{1,0:T(8,128)} %fusion.149, f32[1536,1792]{1,0:T(8,128)} %fusion.147, bf16[1536,2560]{1,0:T(8,128)(2,1)} %bitcast.636, bf16[1792,2560]{1,0:T(8,128)(2,1)} %all-gather.22.cloned.1.call-done), kind=kOutput, calls=%fused_computation.72 | convolution fusion | flops 14136901632 | bytes 55574528 | tf_op jit(solution)/shard_map/dot_general | solution.py:204
  659.1 21.3 %convolution_convert_fusion.1 = bf16[2560,1792]{1,0:T(8,128)(2,1)} fusion(bf16[1536,1792]{1,0:T(8,128)(2,1)} %get-tuple-element.124, bf16[1536,2560]{1,0:T(8,128)(2,1)} %get-tuple-element.139, f32[2560]{0:T(1024)S(1)} %copy-done.64, f32[1536]{0:T(1024)S(1)} %get-tuple-element.350), kind=kOutput, calls=%fused_computation.65 | convolution fusion | flops 14113177600 | bytes 22560768 | tf_op jit(solution)/shard_map/dot_general | solution.py:200
  680.4 21.3 %convolution_convert_fusion.2 = bf16[2560,1792]{1,0:T(8,128)(2,1)} fusion(bf16[1536,1792]{1,0:T(8,128)(2,1)} %get-tuple-element.123, bf16[1536,2560]{1,0:T(8,128)(2,1)} %get-tuple-element.139, f32[2560]{0:T(1024)S(1)} %copy-done.64, f32[1536]{0:T(1024)S(1)} %get-tuple-element.350), kind=kOutput, calls=%fused_computation.66 | convolution fusion | flops 14113177600 | bytes 22560768 | tf_op jit(solution)/shard_map/dot_general | solution.py:200
  701.7 20.9 %convolution_convert_fusion.4 = bf16[1792,2560]{1,0:T(8,128)(2,1)} fusion(bf16[1536,1792]{1,0:T(8,128)(2,1)} %get-tuple-element.210, bf16[1536,2560]{1,0:T(8,128)(2,1)} %bitcast.637), kind=kOutput, calls=%fused_computation.68 | convolution fusion | flops 14097448960 | bytes 22544384 | tf_op jit(solution)/shard_map/dot_general | solution.py:200
  722.6 22.3 %fusion.171 = f32[1536,2560]{1,0:T(8,128)} fusion(bf16[1536,1792]{1,0:T(8,128)(2,1)} %get-tuple-element.123, bf16[2560,1792]{1,0:T(8,128)(2,1)} %all-gather.18.cloned.1.call-done), kind=kOutput, calls=%fused_computation.475 | convolution fusion | flops 14092861440 | bytes 30408704 | tf_op jit(solution)/shard_map/dot_general | solution.py:204
  744.9 25.8 %fusion.25 = (bf16[2560]{0:T(1024)(128)(2,1)S(1)}, f32[1536]{0:T(1024)S(1)}, f32[1536,2560]{1,0:T(8,128)}) fusion(bf16[1536,2560]{1,0:T(8,128)(2,1)} %get-tuple-element.139, f32[1536]{0:T(1024)S(1)} %get-tuple-element.350, f32[2560]{0:T(1024)S(1)} %copy-done.64, f32[1536,2560]{1,0:T(8,128)} %fusion.171, bf16[1536,1792]{1,0:T(8,128)(2,1)} %get-tuple-element.124, ...), kind=kOutput, calls=%fused_computation.55 | convolution fusion | flops 14124314624 | bytes 54029312 | tf_op jit(solution)/shard_map/dot_general | solution.py:204
  1080.1 73.3 %reduce-scatter.16.cloned.1.call-done = bf16[320,1024]{1,0:T(8,128)(2,1)} async-done(((bf16[2560,1024]{1,0:T(8,128)(2,1)}), bf16[320,1024]{1,0:T(8,128)(2,1)}) %reduce-scatter.16.cloned.1.call-update) | async-done | bytes 655376 | tf_op jit(solution)/shard_map/reduce_scatter | solution.py:379
  1178.3 73.6 %reduce-scatter.10.cloned.1.call-done = bf16[320,1792]{1,0:T(8,128)(2,1)} async-done(((bf16[2560,1792]{1,0:T(8,128)(2,1)}), bf16[320,1792]{1,0:T(8,128)(2,1)}) %reduce-scatter.10.cloned.1.call-update) | async-done | bytes 1146896 | tf_op jit(solution)/shard_map/reduce_scatter | solution.py:379
  1338.1 21.3 %collective-permute-done.51 = bf16[192,2560]{1,0:T(8,128)(2,1)} collective-permute-done((bf16[192,2560]{1,0:T(8,128)(2,1)S(1)}, bf16[192,2560]{1,0:T(8,128)(2,1)}, u32[]{:S(2)}, u32[]{:S(2)}) %collective-permute-start.51) | collective-permute-done | bytes 983072 | tf_op jit(solution)/shard_map/ppermute | solution.py:20
  1359.4 21.1 %collective-permute-done.50 = bf16[192,2560]{1,0:T(8,128)(2,1)} collective-permute-done((bf16[192,2560]{1,0:T(8,128)(2,1)}, bf16[192,2560]{1,0:T(8,128)(2,1)}, u32[]{:S(2)}, u32[]{:S(2)}) %collective-permute-start.50) | collective-permute-done | bytes 983072 | tf_op jit(solution)/shard_map/ppermute | solution.py:20
  1415.4 71.7 %all_to_all.20 = bf16[8,48,2560]{2,1,0:T(8,128)(2,1)} all-to-all(bf16[8,48,2560]{2,1,0:T(8,128)(2,1)S(1)} %get-tuple-element.360), channel_id=1, replica_groups=mesh['sp'=4,'fsdp'=8] {'fsdp'}, dimensions={0} | all-to-all | bytes 3932160 | tf_op jit(solution)/shard_map/all_to_all | solution.py:249
  1493.9 29.3 %all-gather.24.cloned.1.call-done = bf16[320,2560]{1,0:T(8,128)(2,1)} async-done(((bf16[320,640]{1,0:T(8,128)(2,1)}), bf16[320,2560]{1,0:T(8,128)(2,1)}) %all-gather.24.cloned.1.call-update) | async-done | bytes 1638416 | tf_op jit(solution)/shard_map/all_gather | solution.py:382
  1542.4 22.3 %all-gather.28.cloned.1.call-done = bf16[1280,1024]{1,0:T(8,128)(2,1)} async-done(((bf16[320,1024]{1,0:T(8,128)(2,1)}), bf16[1280,1024]{1,0:T(8,128)(2,1)}) %all-gather.28.cloned.1.call-update) | async-done | bytes 2621456 | tf_op jit(solution)/shard_map/all_gather | solution.py:403
  1573.7 49.0 %all-gather.30.cloned.1.call-done = bf16[1280,1792]{1,0:T(8,128)(2,1)} async-done(((bf16[320,1792]{1,0:T(8,128)(2,1)}), bf16[1280,1792]{1,0:T(8,128)(2,1)}) %all-gather.30.cloned.1.call-update) | async-done | bytes 4587536 | tf_op jit(solution)/shard_map/all_gather | solution.py:387
  1645.2 35.4 %all-gather.32.cloned.1.call-done = bf16[1280,1792]{1,0:T(8,128)(2,1)} async-done(((bf16[320,1792]{1,0:T(8,128)(2,1)}), bf16[1280,1792]{1,0:T(8,128)(2,1)}) %all-gather.32.cloned.1.call-update) | async-done | bytes 4587536 | tf_op jit(solution)/shard_map/all_gather | solution.py:387
  1703.2 35.3 %all-gather.26.cloned.1.call-done = bf16[896,2560]{1,0:T(8,128)(2,1)} async-done(((bf16[224,2560]{1,0:T(8,128)(2,1)}), bf16[896,2560]{1,0:T(8,128)(2,1)}) %all-gather.26.cloned.1.call-update) | async-done | bytes 4587536 | tf_op jit(solution)/shard_map/all_gather | solution.py:382
  (545 shorter events, 909.1 us)
Async XLA Ops:
  7.2 339.4 %all-gather.14.cloned.1.call-start = ((), (), s32[]{:S(2)}) async-start(), calls=%async_computation.9 | async-start | bytes 5898240 | tf_op jit(solution)/shard_map/all_gather | solution.py:257
  12.2 500.1 %all-gather.16.cloned.1.call-start = ((), (), s32[]{:S(2)}) async-start(), calls=%async_computation.10 | async-start | bytes 3686400 | tf_op jit(solution)/shard_map/all_gather | solution.py:257
  14.1 573.9 %all-gather.20.cloned.1.call-start = ((), (), s32[]{:S(2)}) async-start(), calls=%async_computation.12 | async-start | bytes 10321920 | tf_op jit(solution)/shard_map/all_gather | solution.py:257
  20.1 589.3 %all-gather.18.cloned.1.call-start = ((), (), s32[]{:S(2)}) async-start(), calls=%async_computation.11 | async-start | bytes 10321920 | tf_op jit(solution)/shard_map/all_gather | solution.py:257
  42.2 588.9 %all-gather.22.cloned.1.call-start = ((), (), s32[]{:S(2)}) async-start(), calls=%async_computation.13 | async-start | bytes 10321920 | tf_op jit(solution)/shard_map/all_gather | solution.py:257
  42.8 80.7 %collective-permute-start.9 = (s32[192,1]{0,1:T(1,128)}, s32[192,1]{0,1:T(1,128)S(1)}, u32[]{:S(2)}, u32[]{:S(2)}) collective-permute-start(s32[192,1]{0,1:T(1,128)} %get-tuple-element.354), channel_id=1, source_target_pairs={{0,16},{8,24},{16,0},{24,8},{1,17},{9,25},{17,1},{25,9},{2,18},{10... | collective-permute-start | bytes 2312 | tf_op jit(solution)/shard_map/ppermute | solution.py:20
  45.7 75.0 %collective-permute-start.7 = (s32[192,1]{0,1:T(1,128)}, s32[192,1]{0,1:T(1,128)}, u32[]{:S(2)}, u32[]{:S(2)}) collective-permute-start(s32[192,1]{0,1:T(1,128)} %get-tuple-element.354), channel_id=1, source_target_pairs={{0,8},{8,0},{16,24},{24,16},{1,9},{9,1},{17,25},{25,17},{2,10},{10... | collective-permute-start | bytes 2312 | tf_op jit(solution)/shard_map/ppermute | solution.py:20
  106.7 78.8 %all-to-all-start = ((bf16[8,48,2560]{2,1,0:T(8,128)(2,1)}), bf16[8,48,2560]{2,1,0:T(8,128)(2,1)}, u32[]{:S(2)}, u32[]{:S(2)}) async-start(bf16[8,48,2560]{2,1,0:T(8,128)(2,1)} %get-tuple-element.365), calls=%async_computation | async-start | bytes 3932160 | tf_op jit(solution)/shard_map/all_to_all | solution.py:244
  114.9 964.5 %reduce-scatter.8.cloned.1.call-start = ((), (), s32[]{:S(2)}) async-start(), calls=%async_computation.14 | async-start | bytes 3686400 | tf_op jit(solution)/shard_map/reduce_scatter | solution.py:379
  191.6 109.7 %collective-permute-start.32 = (bf16[192,2560]{1,0:T(8,128)(2,1)S(1)}, bf16[192,2560]{1,0:T(8,128)(2,1)S(1)}, u32[]{:S(2)}, u32[]{:S(2)}) collective-permute-start(bf16[192,2560]{1,0:T(8,128)(2,1)S(1)} %bitcast.670), channel_id=1, source_target_pairs={{0,16},{8,24},{16,0},{24,8},{1,17},{9,25},{17,1},{25,9},{2,18},{10... | collective-permute-start | bytes 2949128 | tf_op jit(solution)/shard_map/ppermute | solution.py:20
  194.1 105.6 %collective-permute-start.33 = (bf16[192,2560]{1,0:T(8,128)(2,1)S(1)}, bf16[192,2560]{1,0:T(8,128)(2,1)}, u32[]{:S(2)}, u32[]{:S(2)}) collective-permute-start(bf16[192,2560]{1,0:T(8,128)(2,1)S(1)} %bitcast.673), channel_id=1, source_target_pairs={{0,16},{8,24},{16,0},{24,8},{1,17},{9,25},{17,1},{25,9},{2,18},{10... | collective-permute-start | bytes 2949128 | tf_op jit(solution)/shard_map/ppermute | solution.py:20
  278.4 169.2 %collective-permute-start.34 = (bf16[192,2560]{1,0:T(8,128)(2,1)}, bf16[192,2560]{1,0:T(8,128)(2,1)}, u32[]{:S(2)}, u32[]{:S(2)}) collective-permute-start(bf16[192,2560]{1,0:T(8,128)(2,1)} %collective-permute-done.30), channel_id=1, source_target_pairs={{0,16},{8,24},{16,0},{24,8},{1,17},{9,25},{17,1},{25,9},{2,18},{10... | collective-permute-start | bytes 2949128 | tf_op jit(solution)/shard_map/ppermute | solution.py:20
  301.0 223.0 %collective-permute-start.35 = (bf16[192,2560]{1,0:T(8,128)(2,1)}, bf16[192,2560]{1,0:T(8,128)(2,1)}, u32[]{:S(2)}, u32[]{:S(2)}) collective-permute-start(bf16[192,2560]{1,0:T(8,128)(2,1)} %collective-permute-done.33), channel_id=1, source_target_pairs={{0,8},{8,0},{16,24},{24,16},{1,9},{9,1},{17,25},{25,17},{2,10},{10... | collective-permute-start | bytes 2949128 | tf_op jit(solution)/shard_map/ppermute | solution.py:20
  898.0 255.5 %reduce-scatter.16.cloned.1.call-start = ((), (), s32[]{:S(2)}) async-start(), calls=%async_computation.23 | async-start | bytes 5898240 | tf_op jit(solution)/shard_map/reduce_scatter | solution.py:379
  1077.3 174.6 %reduce-scatter.10.cloned.1.call-start = ((), (), s32[]{:S(2)}) async-start(), calls=%async_computation.16 | async-start | bytes 10321920 | tf_op jit(solution)/shard_map/reduce_scatter | solution.py:379
  1078.0 307.6 %reduce-scatter.12.cloned.1.call-start = ((), (), s32[]{:S(2)}) async-start(), calls=%async_computation.17 | async-start | bytes 10321920 | tf_op jit(solution)/shard_map/reduce_scatter | solution.py:379
  1078.8 414.9 %reduce-scatter.14.cloned.1.call-start = ((), (), s32[]{:S(2)}) async-start(), calls=%async_computation.18 | async-start | bytes 10321920 | tf_op jit(solution)/shard_map/reduce_scatter | solution.py:379
  1079.4 443.8 %all-gather.24.cloned.1.call-start = ((), (), s32[]{:S(2)}) async-start(), calls=%async_computation.15 | async-start | bytes 2048000 | tf_op jit(solution)/shard_map/all_gather | solution.py:382
  1080.1 484.6 %all-gather.28.cloned.1.call-start = ((), (), s32[]{:S(2)}) async-start(), calls=%async_computation.20 | async-start | bytes 3276800 | tf_op jit(solution)/shard_map/all_gather | solution.py:403
  1153.5 469.3 %all-gather.30.cloned.1.call-start = ((), (), s32[]{:S(2)}) async-start(), calls=%async_computation.21 | async-start | bytes 5734400 | tf_op jit(solution)/shard_map/all_gather | solution.py:387
  1177.1 96.4 %collective-permute-start.25 = (bf16[192,2560]{1,0:T(8,128)(2,1)S(1)}, bf16[192,2560]{1,0:T(8,128)(2,1)}, u32[]{:S(2)}, u32[]{:S(2)}) collective-permute-start(bf16[192,2560]{1,0:T(8,128)(2,1)S(1)} %get-tuple-element.241), channel_id=1, source_target_pairs={{0,8},{8,0},{16,24},{24,16},{1,9},{9,1},{17,25},{25,17},{2,10},{10... | collective-permute-start | bytes 2949128 | tf_op jit(solution)/shard_map/ppermute | solution.py:20
  1251.9 428.7 %all-gather.32.cloned.1.call-start = ((), (), s32[]{:S(2)}) async-start(), calls=%async_computation.22 | async-start | bytes 5734400 | tf_op jit(solution)/shard_map/all_gather | solution.py:387
  1275.7 110.0 %collective-permute-start.29 = (bf16[192,2560]{1,0:T(8,128)(2,1)S(1)}, bf16[192,2560]{1,0:T(8,128)(2,1)S(1)}, u32[]{:S(2)}, u32[]{:S(2)}) collective-permute-start(bf16[192,2560]{1,0:T(8,128)(2,1)S(1)} %get-tuple-element.242), channel_id=1, source_target_pairs={{0,16},{8,24},{16,0},{24,8},{1,17},{9,25},{17,1},{25,9},{2,18},{10... | collective-permute-start | bytes 2949128 | tf_op jit(solution)/shard_map/ppermute | solution.py:20
  1493.3 245.1 %all-gather.26.cloned.1.call-start = ((), (), s32[]{:S(2)}) async-start(), calls=%async_computation.19 | async-start | bytes 5734400 | tf_op jit(solution)/shard_map/all_gather | solution.py:382
  (129 other events, 3584.3 us)
Sparse Core Ops, SparseCore 0:
  12.4 78.3 all-gather.13
  92.4 66.0 all-gather.15
  160.8 90.2 all-gather.19
  253.2 89.4 all-gather.17
  344.2 87.0 all-gather.21
  898.1 65.0 reduce-scatter.7
  1077.4 75.9 reduce-scatter.15
  1156.4 95.3 reduce-scatter.9
  1254.9 95.6 reduce-scatter.11
  1353.5 137.4 reduce-scatter.13
  1493.0 30.1 all-gather.23
  1525.1 39.6 all-gather.27
  1566.7 55.9 all-gather.29
  1624.6 55.9 all-gather.31
  1682.4 55.9 all-gather.25

commit v2 on v1

v2 whole, which is shorter than its diff:
```python
import functools
import jax
import jax.numpy as jnp
from jax import lax
from jax.experimental import pallas as pl
from jax.experimental.pallas import tpu as pltpu
from jax.experimental.layout import Layout, with_layout_constraint
from jax.sharding import PartitionSpec as P

QUERY_HEADS = 32
KEY_VALUE_HEADS = 8
HEAD_SIZE = 80
LANES = 128


eps = 1e-05
theta = 1000000.0
log2e = 1.4426950408889634


def swap(value, bit):
    size = lax.axis_size("sp")
    return lax.ppermute(value, "sp", [(i, i ^ bit) for i in range(size)])


def row_major(value):
    return with_layout_constraint(value, Layout(major_to_minor=tuple(range(value.ndim))))


def gather_sp(value):
    size = lax.axis_size("sp")
    if size != 4:
        return lax.all_gather(value, "sp", axis=0, tiled=False)
    place = lax.axis_index("sp")
    half = value.shape[0] // 2
    first, second = value[:half], value[half:]
    x_first, y_second = swap(first, 1), swap(second, 2)
    x_second, y_first = swap(second, 1), swap(first, 2)
    far_first, far_second = swap(x_first, 2), swap(y_second, 1)
    out = jnp.zeros((size,) + value.shape, value.dtype)
    zeros = (0,) * (value.ndim - 1)
    for turn, low, high in (
        (0, first, second),
        (1, x_first, x_second),
        (2, y_first, y_second),
        (3, far_first, far_second),
    ):
        out = lax.dynamic_update_slice(out, low[None], (place ^ turn, 0) + zeros)
        out = lax.dynamic_update_slice(out, high[None], (place ^ turn, half) + zeros)
    return row_major(out)


def scatter_sp(parts):
    size = lax.axis_size("sp")
    if size != 4:
        return lax.psum_scatter(
            parts, "sp", scatter_dimension=0, tiled=False
        ).astype(jnp.float32)
    place = lax.axis_index("sp")
    half = parts.shape[1] // 2
    parts = row_major(parts)

    def block(turn, lower):
        start = (place ^ turn, 0 if lower else half) + (0,) * (parts.ndim - 2)
        return lax.dynamic_slice(parts, start, (1, half) + parts.shape[2:])[0]

    wide = jnp.float32
    low = parts.dtype
    from_x, from_y = swap(block(3, True), 1), swap(block(3, False), 2)
    x_first, y_second = swap(block(1, True), 1), swap(block(2, False), 2)
    y_first = swap((block(2, True).astype(wide) + from_x.astype(wide)).astype(low), 2)
    x_second = swap((block(1, False).astype(wide) + from_y.astype(wide)).astype(low), 1)
    first = block(0, True).astype(wide) + x_first.astype(wide) + y_first.astype(wide)
    second = block(0, False).astype(wide) + x_second.astype(wide) + y_second.astype(wide)
    return jnp.concatenate([first, second], axis=0)


def rotary_tables(positions):
    halves = HEAD_SIZE // 2
    frequency = theta ** (-(2.0 * jnp.arange(halves, dtype=jnp.float32)) / HEAD_SIZE)
    angles = positions.astype(jnp.float32)[:, None] * frequency[None, :]
    cosine, sine = jnp.cos(angles), jnp.sin(angles)
    rest = jnp.zeros((positions.shape[0], LANES - HEAD_SIZE), jnp.float32)
    return (
        jnp.concatenate([cosine, cosine, rest], axis=1),
        jnp.concatenate([-sine, sine, rest], axis=1),
    )


def gated(gate, upward):
    return jax.nn.silu(gate) * upward


def dot(left, right):
    return jnp.dot(left, right, preferred_element_type=jnp.float32)


def dot_rows(left, right):
    return lax.dot_general(left, right, (((0,), (0,)), ((), ())), preferred_element_type=jnp.float32)


def dot_cols(left, right):
    return lax.dot_general(left, right, (((1,), (1,)), ((), ())), preferred_element_type=jnp.float32)


def head_of(matrix, head):
    first = head * HEAD_SIZE
    if first + LANES <= matrix.shape[1]:
        return matrix[:, first : first + LANES]
    kept = matrix[:, first : first + HEAD_SIZE]
    return jnp.concatenate([kept, jnp.zeros((kept.shape[0], LANES - HEAD_SIZE), kept.dtype)], axis=1)


def half_turn(padded):
    lane = lax.broadcasted_iota(jnp.int32, padded.shape, 1)
    half = HEAD_SIZE // 2
    return jnp.where(lane < half, pltpu.roll(padded, LANES - half, 1), pltpu.roll(padded, half, 1))


def qkv_kernel(heads, keys, x_ref, gain_ref, weight_ref, cos_ref, sin_ref, normed_ref, q_ref, k_ref, v_ref):
    x = x_ref[...].astype(jnp.float32)
    scale = lax.rsqrt(jnp.mean(x * x, axis=1, keepdims=True) + eps)
    normed = (x * scale * gain_ref[...]).astype(jnp.bfloat16)
    normed_ref[...] = normed
    rows = jnp.dot(normed, weight_ref[...], preferred_element_type=jnp.float32)
    cosine, sine = cos_ref[...], sin_ref[...]
    inside = lax.broadcasted_iota(jnp.int32, cosine.shape, 1) < HEAD_SIZE
    for i in range(heads + keys):
        v = head_of(rows, i)
        turned = (v * cosine + half_turn(v) * sine).astype(jnp.bfloat16)
        if i < heads:
            q_ref[:, i * LANES : (i + 1) * LANES] = turned
        else:
            k_ref[:, (i - heads) * LANES : (i - heads + 1) * LANES] = turned
    for i in range(keys):
        v = head_of(rows, heads + keys + i)
        v_ref[:, i * LANES : (i + 1) * LANES] = jnp.where(inside, v, 0.0).astype(jnp.bfloat16)


def qkv_call(x, gain, weight, cosine, sine, heads, keys):
    total, width = x.shape
    block = 256
    bf = jnp.bfloat16
    row = lambda n: pl.BlockSpec((block, n), lambda i: (i, 0))
    whole = lambda a: pl.BlockSpec(a.shape, lambda i: (0, 0))
    return pl.pallas_call(
        functools.partial(qkv_kernel, heads, keys),
        grid=(total // block,),
        in_specs=[row(width), whole(gain), whole(weight), row(LANES), row(LANES)],
        out_specs=[row(width), row(heads * LANES), row(keys * LANES), row(keys * LANES)],
        out_shape=[
            jax.ShapeDtypeStruct((total, width), bf),
            jax.ShapeDtypeStruct((total, heads * LANES), bf),
            jax.ShapeDtypeStruct((total, keys * LANES), bf),
            jax.ShapeDtypeStruct((total, keys * LANES), bf),
        ],
        compiler_params=pltpu.CompilerParams(vmem_limit_bytes=48 * 2**20),
        cost_estimate=pl.CostEstimate(
            flops=2 * total * width * weight.shape[1], bytes_accessed=20 * 2**20, transcendentals=0
        ),
    )(x, gain, weight, cosine, sine)


def attend_kernel(heads, keys, block, q_ref, k_ref, v_ref, start_ref, mixed_ref, lse_ref, bias_ref):
    total = q_ref.shape[0]
    group = heads // keys
    factor = HEAD_SIZE**-0.5 * log2e
    for i in range(total // block):
        first, stop = i * block, (i + 1) * block
        column = lax.broadcasted_iota(jnp.int32, (block, stop), 1)
        row = lax.broadcasted_iota(jnp.int32, (block, stop), 0) + first
        good = (column >= start_ref[first:stop, :]) & (column <= row)
        bias_ref[:, :stop] = jnp.where(good, 0.0, -1e30)
        for head in range(heads):
            lanes = slice(head * LANES, (head + 1) * LANES)
            key = slice(head // group * LANES, (head // group + 1) * LANES)
            scores = dot_cols(q_ref[first:stop, lanes], k_ref[:stop, key]) * factor + bias_ref[:, :stop]
            top = jnp.max(scores, axis=1, keepdims=True)
            weights = jnp.exp2(scores - top)
            summed = jnp.sum(weights, axis=1, keepdims=True)
            mixed = jnp.dot(
                weights.astype(jnp.bfloat16), v_ref[:stop, key], preferred_element_type=jnp.float32
            ) / summed
            mixed_ref[first:stop, head * HEAD_SIZE : (head + 1) * HEAD_SIZE] = mixed[:, :HEAD_SIZE].astype(
                jnp.bfloat16
            )
            lse_ref[first:stop, head : head + 1] = top + jnp.log2(summed)


def attend_call(q, k, v, start, block=256):
    total = q.shape[0]
    heads, keys = q.shape[1] // LANES, k.shape[1] // LANES
    return pl.pallas_call(
        functools.partial(attend_kernel, heads, keys, block),
        out_shape=[
            jax.ShapeDtypeStruct((total, heads * HEAD_SIZE), jnp.bfloat16),
            jax.ShapeDtypeStruct((total, heads), jnp.float32),
        ],
        scratch_shapes=[pltpu.VMEM((block, total), jnp.float32)],
        compiler_params=pltpu.CompilerParams(vmem_limit_bytes=56 * 2**20),
        cost_estimate=pl.CostEstimate(
            flops=heads * total * total * 512, bytes_accessed=8 * 2**20, transcendentals=heads * total * total // 2
        ),
    )(q, k, v, start)


def attend_back_kernel(
    heads, keys, block, q_ref, k_ref, v_ref, grad_ref, lse_ref, start_ref, cos_ref, sin_ref, out_ref, bias_ref, dk_ref, dv_ref
):
    total = q_ref.shape[0]
    group = heads // keys
    scale = HEAD_SIZE**-0.5
    factor = scale * log2e
    low = jnp.bfloat16
    dk_ref[...] = jnp.zeros_like(dk_ref)
    dv_ref[...] = jnp.zeros_like(dv_ref)
    inside = lax.broadcasted_iota(jnp.int32, (block, LANES), 1) < HEAD_SIZE
    half = HEAD_SIZE // 2

    def turned_back(w, rows):
        w = w.astype(low).astype(jnp.float32)
        scaled = w * sin_ref[rows, :]
        lane = lax.broadcasted_iota(jnp.int32, w.shape, 1)
        moved = jnp.where(lane < half, pltpu.roll(scaled, LANES - half, 1), pltpu.roll(scaled, half, 1))
        return (w * cos_ref[rows, :] + moved).astype(low)

    for i in range(total // block):
        first, stop = i * block, (i + 1) * block
        rows = slice(first, stop)
        key_place = lax.broadcasted_iota(jnp.int32, (stop, block), 0)
        place = lax.broadcasted_iota(jnp.int32, (stop, block), 1) + first
        good = (key_place >= start_ref[:, rows]) & (key_place <= place)
        bias_ref[:stop, :] = jnp.where(good, 0.0, -1e30)
        grads = grad_ref[rows, :].astype(jnp.float32)
        for head in range(heads):
            lanes = slice(head * LANES, (head + 1) * LANES)
            key = slice(head // group * LANES, (head // group + 1) * LANES)
            query = q_ref[rows, lanes]
            grad = jnp.where(inside, head_of(grads, head), 0.0).astype(low)
            scores = dot_cols(k_ref[:stop, key], query) * factor + bias_ref[:stop, :]
            probs = jnp.exp2(scores - lse_ref[head : head + 1, rows])
            dv_ref[:stop, key] += jnp.dot(probs.astype(low), grad, preferred_element_type=jnp.float32)
            d_probs = dot_cols(v_ref[:stop, key], grad)
            delta = jnp.sum(probs * d_probs, axis=0, keepdims=True)
            d_scores = (probs * (d_probs - delta)).astype(low)
            dk_ref[:stop, key] += jnp.dot(d_scores, query, preferred_element_type=jnp.float32)
            d_query = dot_rows(d_scores, k_ref[:stop, key]) * scale
            out_ref[rows, head * HEAD_SIZE : (head + 1) * HEAD_SIZE] = turned_back(d_query, rows)[:, :HEAD_SIZE]
    for i in range(total // block):
        rows = slice(i * block, (i + 1) * block)
        for j in range(keys):
            lanes = slice(j * LANES, (j + 1) * LANES)
            at = (heads + j) * HEAD_SIZE
            out_ref[rows, at : at + HEAD_SIZE] = turned_back(dk_ref[rows, lanes] * scale, rows)[:, :HEAD_SIZE]
            at = (heads + keys + j) * HEAD_SIZE
            out_ref[rows, at : at + HEAD_SIZE] = dv_ref[rows, lanes][:, :HEAD_SIZE].astype(low)


def attend_back_call(q, k, v, grad, lse_rows, start_row, cosine, sine_back, block=256):
    total = q.shape[0]
    heads, keys = q.shape[1] // LANES, k.shape[1] // LANES
    return pl.pallas_call(
        functools.partial(attend_back_kernel, heads, keys, block),
        out_shape=jax.ShapeDtypeStruct((total, (heads + 2 * keys) * HEAD_SIZE), jnp.bfloat16),
        scratch_shapes=[
            pltpu.VMEM((total, block), jnp.float32),
            pltpu.VMEM((total, keys * LANES), jnp.float32),
            pltpu.VMEM((total, keys * LANES), jnp.float32),
        ],
        compiler_params=pltpu.CompilerParams(vmem_limit_bytes=56 * 2**20),
        cost_estimate=pl.CostEstimate(
            flops=heads * total * total * 1280, bytes_accessed=12 * 2**20, transcendentals=heads * total * total // 2
        ),
    )(q, k, v, grad, lse_rows, start_row, cosine, sine_back)

def spread_kernel(groups, parts_ref, out_ref):
    parts, _, columns = parts_ref.shape
    share = columns // groups
    for i in range(parts):
        for j in range(groups):
            at = (j * parts + i) * share
            out_ref[:, at : at + share] = parts_ref[i, :, j * share : (j + 1) * share].astype(jnp.float32)


def spread_call(gathered, groups):
    parts, rows, columns = gathered.shape
    block = rows // 5 if rows % 80 == 0 else rows
    return pl.pallas_call(
        functools.partial(spread_kernel, groups),
        grid=(rows // block,),
        in_specs=[pl.BlockSpec((parts, block, columns), lambda i: (0, i, 0))],
        out_specs=pl.BlockSpec((block, parts * columns), lambda i: (i, 0)),
        out_shape=jax.ShapeDtypeStruct((rows, parts * columns), jnp.float32),
        compiler_params=pltpu.CompilerParams(vmem_limit_bytes=32 * 2**20),
        cost_estimate=pl.CostEstimate(
            flops=0, bytes_accessed=6 * parts * rows * columns, transcendentals=0
        ),
    )(gathered)


def after(value, *others):
    return lax.optimization_barrier((value,) + others)[0]


def local(
    tokens,
    cotangent,
    attn_gain,
    w_query,
    key_weight,
    value_weight,
    w_out,
    mlp_gain,
    w_gate,
    w_up,
    w_down,
    positions,
    lengths,
    deal_slots,
):
    groups = lax.axis_size("fsdp")
    parts = lax.axis_size("sp")
    width = tokens.shape[-1]
    rows = tokens.shape[1]
    fsdp_place = lax.axis_index("fsdp")
    sp_place = lax.axis_index("sp")
    low = jnp.bfloat16
    wide = jnp.float32

    lanes = jnp.arange(groups, dtype=jnp.int32)
    own_row = deal_slots[fsdp_place, sp_place]
    target = own_row // groups
    pick_send = jnp.sum(jnp.where(target[None, :] == lanes[:, None], lanes[None, :], 0), axis=1)
    column = deal_slots[:, sp_place, :]
    arrived_slot = jnp.sum(jnp.where(column // groups == fsdp_place, column % groups, 0), axis=1)
    pick_place = jnp.sum(
        jnp.where(arrived_slot[None, :] == lanes[:, None], lanes[None, :], 0), axis=1
    )

    def deal(given):
        blocks = jnp.take(given.reshape(groups, -1, width), pick_send, axis=0)
        return lax.all_to_all(blocks, "fsdp", split_axis=0, concat_axis=0, tiled=True)

    def in_place(came):
        return jnp.take(came, pick_place, axis=0).reshape(rows, width)

    def to_given(owned):
        blocks = jnp.take(owned.reshape(groups, -1, width), arrived_slot, axis=0)
        gone = lax.all_to_all(blocks, "fsdp", split_axis=0, concat_axis=0, tiled=True)
        return jnp.take(gone, target, axis=0).reshape(tokens.shape)

    def column_share(weight):
        share = weight.shape[1] // parts
        return lax.dynamic_slice_in_dim(weight, sp_place * share, share, axis=1)

    def gather_fsdp(shard):
        return lax.all_gather(shard, "fsdp", axis=0, tiled=True)

    ff_rows = w_down.shape[0]
    ff_share = ff_rows // parts

    def hidden_share(weight):
        def pick(place):
            starts = [i * ff_rows + place * ff_share for i in range(groups)]
            return lambda: jnp.concatenate([weight[:, i : i + ff_share] for i in starts], axis=1)

        return lax.switch(sp_place, [pick(place) for place in range(parts)])

    query_cols = w_query.shape[1] // parts
    key_cols = key_weight.shape[1] // parts
    qkv_cols = query_cols + 2 * key_cols
    extra = -qkv_cols % 128
    extra = extra if extra else 128
    gains = jnp.pad(jnp.stack([attn_gain, mlp_gain], axis=1), ((0, 0), (0, extra - 2)))
    came_tokens = deal(tokens)
    w_query, w_out, w_gate, w_up, w_down = (
        after(w, came_tokens) for w in (w_query, w_out, w_gate, w_up, w_down)
    )
    qkv_shard = jnp.concatenate(
        [column_share(w_query), column_share(key_weight), column_share(value_weight), gains], axis=1
    )
    qkv_all = gather_fsdp(qkv_shard)
    out_all = gather_fsdp(column_share(w_out))
    gate_all = gather_fsdp(hidden_share(w_gate))
    up_all = gather_fsdp(hidden_share(w_up))
    down_all = gather_fsdp(lax.dynamic_slice_in_dim(w_down, sp_place * ff_share, ff_share, axis=0))
    qkv_weight = qkv_all[:, :qkv_cols]
    gain_one = qkv_all[:, qkv_cols].astype(wide)[None, :]
    gain_two = qkv_all[:, qkv_cols + 1].astype(wide)[None, :]

    group_inputs = gather_sp(in_place(came_tokens)).reshape(-1, width)
    group_incoming = gather_sp(in_place(deal(after(cotangent, qkv_all)))).reshape(-1, width)
    group_positions = gather_sp(positions.reshape(-1, 1)).reshape(-1)
    total = group_inputs.shape[0]

    cosine, sine = rotary_tables(group_positions)
    heads, keys = query_cols // HEAD_SIZE, key_cols // HEAD_SIZE
    normed, query_low, key_low, value_low = qkv_call(
        group_inputs, gain_one, qkv_all, cosine, sine, heads, keys
    )
    sizes = lengths.reshape(-1)
    ends = jnp.cumsum(sizes)
    places = jnp.arange(total, dtype=jnp.int32)
    start = jnp.sum(jnp.where(places[:, None] >= ends[None, :], sizes[None, :], 0), axis=1)
    own_mixed, logs = attend_call(query_low, key_low, value_low, start[:, None])

    def side_by_side(stacked):
        return jnp.concatenate([stacked[i] for i in range(parts)], axis=1)

    def by_columns(matrix):
        share = matrix.shape[1] // parts
        return jnp.stack([matrix[:, i * share : (i + 1) * share] for i in range(parts)], axis=0)

    share = width // parts

    def own_columns(matrix):
        return lax.dynamic_slice_in_dim(matrix, sp_place * share, share, axis=1)

    mixed = side_by_side(gather_sp(own_mixed))
    own_hidden = own_columns(group_inputs).astype(wide) + dot(mixed, out_all)
    hidden_low = side_by_side(gather_sp(own_hidden.astype(low)))

    hidden = hidden_low.astype(wide)
    rms_two = lax.rsqrt(jnp.mean(hidden * hidden, axis=-1, keepdims=True) + eps)
    normed_two = (hidden * rms_two * gain_two).astype(low)
    gate = dot(normed_two, gate_all)
    upward = dot(normed_two, up_all)
    active, active_back = jax.vjp(gated, gate, upward)
    active_low = active.astype(low)
    grad_down = dot_rows(active_low, group_incoming).astype(low)
    d_active = dot_cols(after(group_incoming, grad_down), down_all)
    d_gate, d_up = active_back(d_active)
    d_gate, d_up = d_gate.astype(low), d_up.astype(low)
    d_normed_two = dot_cols(d_gate, gate_all) + dot_cols(d_up, up_all)
    grad_gate = dot_rows(normed_two, d_gate).astype(low)
    grad_up = dot_rows(normed_two, d_up).astype(low)
    grad_gain_two = jnp.sum(d_normed_two * hidden * rms_two, axis=0)
    scaled = gain_two * d_normed_two
    back_two = rms_two * scaled - hidden * rms_two**3 * jnp.mean(scaled * hidden, axis=-1, keepdims=True)
    own_d_hidden = own_columns(group_incoming).astype(wide) + scatter_sp(by_columns(back_two.astype(low)))
    d_branch = own_d_hidden.astype(low)
    grad_out = dot_rows(mixed, d_branch)
    d_mixed = scatter_sp(by_columns(dot_cols(d_branch, out_all).astype(low))).astype(low)
    result_part = dot(after(active_low, d_mixed), down_all).astype(low)
    own_hidden_rows = lax.dynamic_slice_in_dim(hidden_low, sp_place * rows, rows, axis=0)
    result = own_hidden_rows.astype(wide) + scatter_sp(result_part.reshape(parts, rows, width))
    layer_out = to_given(result.astype(low))

    d_qkv = attend_back_call(
        query_low, key_low, value_low, d_mixed, logs.T, start[None, :], cosine, sine
    )
    grad_qkv = dot_rows(normed, d_qkv)
    d_normed = dot_cols(d_qkv, qkv_weight)
    inputs = group_inputs.astype(wide)
    rms_one = lax.rsqrt(jnp.mean(inputs * inputs, axis=-1, keepdims=True) + eps)
    grad_gain_one = jnp.sum(d_normed * inputs * rms_one, axis=0)
    scaled_one = gain_one * d_normed
    back_one = rms_one * scaled_one - inputs * rms_one**3 * jnp.mean(
        scaled_one * inputs, axis=-1, keepdims=True
    )
    own_place = (jnp.arange(width, dtype=jnp.int32) // share == sp_place)[None, :]
    spread = jnp.concatenate([own_d_hidden] * parts, axis=1)
    back_one = back_one + jnp.where(own_place, spread, 0.0)
    d_inputs = scatter_sp(back_one.astype(low).reshape(parts, rows, width))
    input_grad = to_given(d_inputs.astype(low))

    def scatter_fsdp(matrix):
        return lax.psum_scatter(matrix.astype(low), "fsdp", scatter_dimension=0, tiled=True)

    def all_sp(shard, axis):
        return lax.all_gather(shard, "sp", axis=axis, tiled=True)

    gain_grads = jnp.pad(
        jnp.stack([grad_gain_one, grad_gain_two], axis=1), ((0, 0), (0, extra - 2))
    )
    down_sum = scatter_fsdp(grad_down)
    gate_sum = scatter_fsdp(after(grad_gate, down_sum))
    up_sum = scatter_fsdp(after(grad_up, gate_sum))
    out_sum = scatter_fsdp(after(grad_out.astype(low), up_sum))
    qkv_sum = scatter_fsdp(after(jnp.concatenate([grad_qkv, gain_grads], axis=1).astype(low), out_sum))

    down_shard = all_sp(down_sum, 0).astype(wide)

    def hidden_whole(shard):
        return spread_call(lax.all_gather(shard, "sp", axis=0, tiled=False), groups)

    gate_shard = hidden_whole(gate_sum)
    up_shard = hidden_whole(up_sum)
    out_shard = side_by_side(gather_sp(out_sum)).astype(wide)
    qkv_shards = gather_sp(qkv_sum).astype(wide)
    edges = (0, query_cols, query_cols + key_cols, qkv_cols)
    query_shard, key_shard, value_shard = (
        side_by_side(qkv_shards[:, :, edges[i] : edges[i + 1]]) for i in range(3)
    )
    gain_shards = jnp.sum(qkv_shards[:, :, qkv_cols : qkv_cols + 2], axis=0)
    return (
        layer_out,
        input_grad,
        gain_shards[:, 0],
        query_shard,
        key_shard,
        value_shard,
        out_shard,
        gain_shards[:, 1],
        gate_shard,
        up_shard,
        down_shard,
    )


def solution(mesh):
    placed = (
        P("fsdp", "sp", None),
        P("fsdp", "sp", None),
        P("fsdp"),
        P("fsdp", None),
        P("fsdp", None),
        P("fsdp", None),
        P("fsdp", None),
        P("fsdp"),
        P("fsdp", None),
        P("fsdp", None),
        P("fsdp", None),
        P("fsdp", "sp"),
        P("fsdp", None),
        P(),
    )
    return jax.shard_map(
        local,
        mesh=mesh,
        in_specs=placed,
        out_specs=(
            P("fsdp", "sp", None),
            P("fsdp", "sp", None),
            P("fsdp"),
            P("fsdp", None),
            P("fsdp", None),
            P("fsdp", None),
            P("fsdp", None),
            P("fsdp"),
            P("fsdp", None),
            P("fsdp", None),
            P("fsdp", None),
        ),
        check_vma=False,
    )
```

time: 1760 us -> 1550 us (0.88)
  matrix products: 396 us -> 260 us
  Pallas kernels: 0 us -> 111 us
  blocking collectives: 71.7 us -> 0 us
  other arithmetic: 180 us -> 112 us
  waiting for transfers between devices: 868 us -> 803 us
  starting transfers between devices: 62.3 us -> 117 us
  local copies, waits for them, and re-layouts: 158 us -> 109 us
    dot_general x18 -> x0, matrix products: 125 us -> none  [the longest x3 35.6 us: attention_back(): jnp.einsum('qkgd,skd->kgqs', grad_rows, grouped_value[:row_stop], preferr...]
    all_to_all x1 -> x2, waiting for transfers between devices: 5.79 us -> 119 us  [to_given(): lax.all_to_all(blocks, 'fsdp', split_axis=0, concat_axis=0, tiled=True)]
    pallas_call x0 -> x5, Pallas kernels: none -> 111 us  [the longest x1 49.9 us: attend_back_call(): pl.pallas_call(functools.partial(attend_back_kernel, heads, keys, block),...]
    all_gather x3 -> x2, waiting for transfers between devices: 107 us -> 0.02 us  [hidden_whole(): return spread_call(lax.all_gather(shard, 'sp', axis=0, tiled=False), groups)]
    all_to_all x1 -> x0, blocking collectives: 71.7 us -> none  [to_given(): lax.all_to_all(blocks, 'fsdp', split_axis=0, concat_axis=0, tiled=True)]
    all_gather x2 -> x1, waiting for transfers between devices: 64.5 us -> 0.01 us  [all_sp(): return lax.all_gather(shard, 'sp', axis=axis, tiled=True)]
    convert_element_type x13 -> x3, other arithmetic: 58.9 us -> 9.98 us  [the longest x1 7.22 us: local(): down_shard = all_sp(down_sum, 0).astype(wide)]
    all_gather x5, waiting for transfers between devices: 0.03 us -> 39.5 us  [gather_fsdp(): return lax.all_gather(shard, 'fsdp', axis=0, tiled=True)]
  transfers between devices with their start and end apart: 72 -> 83, of which waited for: 37 -> 35; matrix products, arithmetic and copies ran while one was open for 31% -> 29% of each run, Pallas kernels for 0% -> 7%
where the time goes in v2:
time: 1550 us; the launch traced here: 1530 us
  waiting for transfers between devices  803 us (52%)
  matrix products  260 us (17%)
  starting transfers between devices  117 us (8%)
  other arithmetic  112 us (7%)
  Pallas kernels  111 us (7%)
  local copies, waits for them, and re-layouts  109 us (7%)
  between operations  15.6 us (1%)
    ppermute x66, waiting for transfers between devices, swap(): return lax.ppermute(value, 'sp', [(i, i ^ bit) for i in range(size)])  425 us
    reduce_scatter x5, waiting for transfers between devices, scatter_fsdp(): lax.psum_scatter(matrix.astype(low), 'fsdp', scatter_dimension=0, tiled=T...  129 us
    all_to_all x2, waiting for transfers between devices, to_given(): lax.all_to_all(blocks, 'fsdp', split_axis=0, concat_axis=0, tiled=True)  119 us
    dot_general x5, matrix products, dot_cols(): lax.dot_general(left, right, (((1,), (1,)), ((), ())), preferred_element_...  103 us
    all_to_all x2, waiting for transfers between devices, deal(): lax.all_to_all(blocks, 'fsdp', split_axis=0, concat_axis=0, tiled=True)  90.2 us
    dot_general x5, matrix products, dot_rows(): lax.dot_general(left, right, (((0,), (0,)), ((), ())), preferred_element_...  84.4 us
    dot_general x4, matrix products, dot(): return jnp.dot(left, right, preferred_element_type=jnp.float32)  73.2 us
    ppermute x66, starting transfers between devices, swap(): return lax.ppermute(value, 'sp', [(i, i ^ bit) for i in range(size)])  62.2 us
  transfers between devices with their start and end apart: 83, of which 35 were waited for; matrix products, arithmetic and copies ran while one was open for 29% of the time, Pallas kernels for 7%

profile of v2, /device:TPU:9, one launch (start us, length us, event | category | flops | bytes accessed | tf_op | source)
XLA Modules:
  0.0 1526.8 jit_solution(15085417390419246932)
XLA Ops:
  22.0 41.2 %all-to-all-done = bf16[8,48,2560]{2,1,0:T(8,128)(2,1)S(1)} async-done(((bf16[8,48,2560]{2,1,0:T(8,128)(2,1)}), bf16[8,48,2560]{2,1,0:T(8,128)(2,1)S(1)}, u32[]{:S(2)}, u32[]{:S(2)}) %all-to-all-start) | async-done | bytes 1966112 | tf_op jit(solution)/shard_map/all_to_all | solution.py:342
  82.6 39.5 %all-gather.11.cloned.1.call-done.weight_ref = bf16[2560,1024]{1,0:T(8,128)(2,1)} async-done(((bf16[320,1024]{1,0:T(8,128)(2,1)}), bf16[2560,1024]{1,0:T(8,128)(2,1)}) %all-gather.11.cloned.1.call-update) | async-done | bytes 5242896 | tf_op jit(solution)/shard_map/all_gather | solution.py:357
  151.8 49.0 %all-to-all-done.1 = bf16[8,48,2560]{2,1,0:T(8,128)(2,1)} async-done(((bf16[8,48,2560]{2,1,0:T(8,128)(2,1)}), bf16[8,48,2560]{2,1,0:T(8,128)(2,1)}, u32[]{:S(2)}, u32[]{:S(2)}) %all-to-all-start.1) | async-done | bytes 1966112 | tf_op jit(solution)/shard_map/all_to_all | solution.py:342
  319.3 23.7 %shard_map.221 = (bf16[1536,2560]{1,0:T(8,128)(2,1)}, bf16[1536,1024]{1,0:T(8,128)(2,1)}, bf16[1536,256]{1,0:T(8,128)(2,1)S(1)}, bf16[1536,256]{1,0:T(8,128)(2,1)S(1)}) custom-call(bf16[1536,2560]{1,0:T(8,128)(2,1)} %bitcast.311, f32[1,2560]{1,0:T(1,128)S(1)} %reshape.266.gain_ref, bf16[2560,1024]{1,0:T(8,128)(2,1)} %all-gather.11.cloned.1.call-done.weight_ref, ...), custom_call_target="tpu_custom_call" | custom-call | flops 8053063680 | bytes 20971520 | tf_op jit(solution)/shard_map/pallas_call | solution.py:146
  344.7 27.4 %shard_map.222 = (bf16[1536,640]{1,0:T(8,128)(2,1)}, f32[1536,8]{1,0:T(8,128)}) custom-call(bf16[1536,1024]{1,0:T(8,128)(2,1)} %get-tuple-element.49.q_ref, bf16[1536,256]{1,0:T(8,128)(2,1)} %copy-done.6, bf16[1536,256]{1,0:T(8,128)(2,1)} %copy-done.7, s32[1536,1]{1,0:T(8,128)} %broadcast_in_dim.365.start_ref), custom_call_target="tpu_custom_call" | custom-call | flops 9663676416 | bytes 8388608 | tf_op jit(solution)/shard_map/pallas_call | solution.py:193
  395.5 20.3 %collective-permute-done.15 = bf16[768,640]{1,0:T(8,128)(2,1)S(1)} collective-permute-done((bf16[768,640]{1,0:T(8,128)(2,1)S(1)}, bf16[768,640]{1,0:T(8,128)(2,1)S(1)}, u32[]{:S(2)}, u32[]{:S(2)}) %collective-permute-start.15) | collective-permute-done | bytes 983072 | tf_op jit(solution)/shard_map/ppermute | solution.py:23
  456.8 34.6 %collective-permute-done.18 = bf16[768,640]{1,0:T(8,128)(2,1)S(1)} collective-permute-done((bf16[768,640]{1,0:T(8,128)(2,1)S(1)}, bf16[768,640]{1,0:T(8,128)(2,1)S(1)}, u32[]{:S(2)}, u32[]{:S(2)}) %collective-permute-start.18) | collective-permute-done | bytes 983072 | tf_op jit(solution)/shard_map/ppermute | solution.py:23
  520.1 21.4 %fusion.67 = f32[1536,1792]{1,0:T(8,128)} fusion(bf16[2560,1792]{1,0:T(8,128)(2,1)} %all-gather.15.cloned.1.call-done, bf16[1536,2560]{1,0:T(8,128)(2,1)} %get-tuple-element.77, f32[2560]{0:T(1024)S(1)} %get-tuple-element.70, f32[1536]{0:T(1024)S(1)} %get-tuple-element.216), kind=kOutput, calls=%fused_computation.299 | convolution fusion | flops 14108590080 | bytes 28065792 | tf_op jit(solution)/shard_map/dot_general | solution.py:95
  541.5 23.2 %multiply_convert_fusion.1 = (bf16[1536,1792]{1,0:T(8,128)(2,1)S(1)}, f32[1536,1792]{1,0:T(8,128)}) fusion(f32[1536,1792]{1,0:T(8,128)} %fusion.67, bf16[2560,1792]{1,0:T(8,128)(2,1)} %all-gather.17.cloned.1.call-done, bf16[1536,2560]{1,0:T(8,128)(2,1)} %get-tuple-element.77, f32[2560]{0:T(1024)S(1)} %get-tuple-element.70, f32[1536]{0:T(1024)S(1)} %get-tuple-element.216), kind=kOutput, calls=%fused_computation.45 | convolution fusion | flops 14125105152 | bytes 44580864 | tf_op jit(solution)/shard_map/dot_general | solution.py:95
  586.8 27.1 %multiply_convert_fusion = (bf16[1536,1792]{1,0:T(8,128)(2,1)}, bf16[1536,1792]{1,0:T(8,128)(2,1)}) fusion(f32[1536,1792]{1,0:T(8,128)} %fusion.67, f32[1536,1792]{1,0:T(8,128)} %get-tuple-element.230, bf16[1536,2560]{1,0:T(8,128)(2,1)} %bitcast.318, bf16[1792,2560]{1,0:T(8,128)(2,1)} %all-gather.19.cloned.1.call-done), kind=kOutput, calls=%fused_computation.44 | convolution fusion | flops 14131396608 | bytes 50069504 | tf_op jit(solution)/shard_map/dot_general | solution.py:103
  613.9 21.2 %convolution_convert_fusion.1 = bf16[2560,1792]{1,0:T(8,128)(2,1)} fusion(bf16[1536,1792]{1,0:T(8,128)(2,1)} %get-tuple-element.143, bf16[1536,2560]{1,0:T(8,128)(2,1)} %get-tuple-element.77, f32[2560]{0:T(1024)S(1)} %get-tuple-element.70, f32[1536]{0:T(1024)S(1)} %get-tuple-element.216), kind=kOutput, calls=%fused_computation.37 | convolution fusion | flops 14113177600 | bytes 22560768 | tf_op jit(solution)/shard_map/dot_general | solution.py:99
  635.1 51.6 %reduce-scatter.6.cloned.1.call-done = bf16[224,2560]{1,0:T(8,128)(2,1)} async-done(((bf16[1792,2560]{1,0:T(8,128)(2,1)}), bf16[224,2560]{1,0:T(8,128)(2,1)}) %reduce-scatter.6.cloned.1.call-update) | async-done | bytes 1146896 | tf_op jit(solution)/shard_map/reduce_scatter | solution.py:468
  686.8 21.3 %convolution_convert_fusion.2 = bf16[2560,1792]{1,0:T(8,128)(2,1)} fusion(bf16[1536,1792]{1,0:T(8,128)(2,1)} %get-tuple-element.142, bf16[1536,2560]{1,0:T(8,128)(2,1)} %get-tuple-element.77, f32[2560]{0:T(1024)S(1)} %get-tuple-element.70, f32[1536]{0:T(1024)S(1)} %get-tuple-element.216), kind=kOutput, calls=%fused_computation.38 | convolution fusion | flops 14113177600 | bytes 22560768 | tf_op jit(solution)/shard_map/dot_general | solution.py:99
  708.1 76.9 %reduce-scatter.8.cloned.1.call-done = bf16[320,1792]{1,0:T(8,128)(2,1)} async-done(((bf16[2560,1792]{1,0:T(8,128)(2,1)}), bf16[320,1792]{1,0:T(8,128)(2,1)}) %reduce-scatter.8.cloned.1.call-update) | async-done | bytes 1146896 | tf_op jit(solution)/shard_map/reduce_scatter | solution.py:468
  785.1 22.3 %fusion.83 = f32[1536,2560]{1,0:T(8,128)} fusion(bf16[1536,1792]{1,0:T(8,128)(2,1)} %get-tuple-element.143, bf16[2560,1792]{1,0:T(8,128)(2,1)} %all-gather.15.cloned.1.call-done), kind=kOutput, calls=%fused_computation.314 | convolution fusion | flops 14092861440 | bytes 30408704 | tf_op jit(solution)/shard_map/dot_general | solution.py:103
  807.4 26.0 %fusion.15 = (bf16[2560]{0:T(1024)(128)(2,1)S(1)}, f32[1536]{0:T(1024)S(1)}, f32[1536,2560]{1,0:T(8,128)}) fusion(bf16[1536,2560]{1,0:T(8,128)(2,1)} %get-tuple-element.77, f32[1536]{0:T(1024)S(1)} %get-tuple-element.216, f32[2560]{0:T(1024)S(1)} %get-tuple-element.70, f32[1536,2560]{1,0:T(8,128)} %fusion.83, bf16[1536,1792]{1,0:T(8,128)(2,1)} %get-tuple-element.142, ...), kind=kOutput, calls=%fused_computation.32 | convolution fusion | flops 14124314624 | bytes 54029312 | tf_op jit(solution)/shard_map/dot_general | solution.py:103
  848.3 21.2 %collective-permute-done.31 = bf16[768,640]{1,0:T(8,128)(2,1)S(1)} collective-permute-done((bf16[768,640]{1,0:T(8,128)(2,1)S(1)}, bf16[768,640]{1,0:T(8,128)(2,1)S(1)}, u32[]{:S(2)}, u32[]{:S(2)}) %collective-permute-start.31) | collective-permute-done | bytes 983072 | tf_op jit(solution)/shard_map/ppermute | solution.py:23
  1004.8 23.1 %collective-permute-done.41 = bf16[768,640]{1,0:T(8,128)(2,1)} collective-permute-done((bf16[768,640]{1,0:T(8,128)(2,1)S(1)}, bf16[768,640]{1,0:T(8,128)(2,1)}, u32[]{:S(2)}, u32[]{:S(2)}) %collective-permute-start.41) | collective-permute-done | bytes 983072 | tf_op jit(solution)/shard_map/ppermute | solution.py:23
  1059.1 49.9 %shard_map.223 = bf16[1536,960]{1,0:T(8,128)(2,1)} custom-call(bf16[1536,1024]{1,0:T(8,128)(2,1)} %get-tuple-element.49.q_ref, bf16[1536,256]{1,0:T(8,128)(2,1)} %copy-done.6, bf16[1536,256]{1,0:T(8,128)(2,1)} %copy-done.7, bf16[1536,640]{1,0:T(8,128)(2,1)} %pad_maximum_fusion.5.grad_ref, f32[8,1536]{1,0:T(8,128)} %bitcast.341, ...), custom_call_target="tpu_custom_call" | custom-call | flops 24159191040 | bytes 12582912 | tf_op jit(solution)/shard_map/pallas_call | solution.py:262
  1177.8 25.2 %collective-permute-done.51 = bf16[192,2560]{1,0:T(8,128)(2,1)} collective-permute-done((bf16[192,2560]{1,0:T(8,128)(2,1)}, bf16[192,2560]{1,0:T(8,128)(2,1)}, u32[]{:S(2)}, u32[]{:S(2)}) %collective-permute-start.51) | collective-permute-done | bytes 983072 | tf_op jit(solution)/shard_map/ppermute | solution.py:23
  1203.0 34.4 %collective-permute-done.50 = bf16[192,2560]{1,0:T(8,128)(2,1)} collective-permute-done((bf16[192,2560]{1,0:T(8,128)(2,1)}, bf16[192,2560]{1,0:T(8,128)(2,1)}, u32[]{:S(2)}, u32[]{:S(2)}) %collective-permute-start.50) | collective-permute-done | bytes 983072 | tf_op jit(solution)/shard_map/ppermute | solution.py:23
  1278.6 33.1 %all-to-all-start.2 = ((bf16[8,48,2560]{2,1,0:T(8,128)(2,1)}), bf16[8,48,2560]{2,1,0:T(8,128)(2,1)S(1)}, u32[]{:S(2)}, u32[]{:S(2)}) async-start(bf16[8,48,2560]{2,1,0:T(8,128)(2,1)} %get-tuple-element.224), calls=%async_computation.2 | async-start | bytes 3932160 | tf_op jit(solution)/shard_map/all_to_all | solution.py:349
  1317.4 64.0 %all-to-all-done.2 = bf16[8,48,2560]{2,1,0:T(8,128)(2,1)S(1)} async-done(((bf16[8,48,2560]{2,1,0:T(8,128)(2,1)}), bf16[8,48,2560]{2,1,0:T(8,128)(2,1)S(1)}, u32[]{:S(2)}, u32[]{:S(2)}) %all-to-all-start.2) | async-done | bytes 1966112 | tf_op jit(solution)/shard_map/all_to_all | solution.py:349
  1391.3 54.9 %all-to-all-done.3 = bf16[8,48,2560]{2,1,0:T(8,128)(2,1)} async-done(((bf16[8,48,2560]{2,1,0:T(8,128)(2,1)}), bf16[8,48,2560]{2,1,0:T(8,128)(2,1)}, u32[]{:S(2)}, u32[]{:S(2)}) %all-to-all-start.3) | async-done | bytes 1966112 | tf_op jit(solution)/shard_map/all_to_all | solution.py:349
  (449 shorter events, 687.0 us)
Async XLA Ops:
  20.6 101.5 %all-gather.11.cloned.1.call-start = ((), (), s32[]{:S(2)}) async-start(), calls=%async_computation.9 | async-start | bytes 5898240 | tf_op jit(solution)/shard_map/all_gather | solution.py:357
  65.6 374.8 %all-gather.13.cloned.1.call-start = ((), (), s32[]{:S(2)}) async-start(), calls=%async_computation.10 | async-start | bytes 3686400 | tf_op jit(solution)/shard_map/all_gather | solution.py:357
  67.5 452.6 %all-gather.15.cloned.1.call-start = ((), (), s32[]{:S(2)}) async-start(), calls=%async_computation.11 | async-start | bytes 10321920 | tf_op jit(solution)/shard_map/all_gather | solution.py:357
  73.5 468.0 %all-gather.17.cloned.1.call-start = ((), (), s32[]{:S(2)}) async-start(), calls=%async_computation.12 | async-start | bytes 10321920 | tf_op jit(solution)/shard_map/all_gather | solution.py:357
  125.8 75.0 %all-to-all-start.1 = ((bf16[8,48,2560]{2,1,0:T(8,128)(2,1)}), bf16[8,48,2560]{2,1,0:T(8,128)(2,1)}, u32[]{:S(2)}, u32[]{:S(2)}) async-start(bf16[8,48,2560]{2,1,0:T(8,128)(2,1)} %broadcast_select_fusion.6), calls=%async_computation.1 | async-start | bytes 3932160 | tf_op jit(solution)/shard_map/all_to_all | solution.py:342
  132.3 454.5 %all-gather.19.cloned.1.call-start = ((), (), s32[]{:S(2)}) async-start(), calls=%async_computation.13 | async-start | bytes 10321920 | tf_op jit(solution)/shard_map/all_gather | solution.py:357
  145.9 540.8 %reduce-scatter.6.cloned.1.call-start = ((), (), s32[]{:S(2)}) async-start(), calls=%async_computation.14 | async-start | bytes 10321920 | tf_op jit(solution)/shard_map/reduce_scatter | solution.py:468
  293.6 83.0 %collective-permute-start.28 = (bf16[192,2560]{1,0:T(8,128)(2,1)S(1)}, bf16[192,2560]{1,0:T(8,128)(2,1)S(1)}, u32[]{:S(2)}, u32[]{:S(2)}) collective-permute-start(bf16[192,2560]{1,0:T(8,128)(2,1)S(1)} %collective-permute-done.24), channel_id=1, source_target_pairs={{0,16},{8,24},{16,0},{24,8},{1,17},{9,25},{17,1},{25,9},{2,18},{10... | collective-permute-start | bytes 2949128 | tf_op jit(solution)/shard_map/ppermute | solution.py:23
  295.0 158.1 %collective-permute-start.29 = (bf16[192,2560]{1,0:T(8,128)(2,1)S(1)}, bf16[192,2560]{1,0:T(8,128)(2,1)}, u32[]{:S(2)}, u32[]{:S(2)}) collective-permute-start(bf16[192,2560]{1,0:T(8,128)(2,1)S(1)} %collective-permute-done.27), channel_id=1, source_target_pairs={{0,8},{8,0},{16,24},{24,16},{1,9},{9,1},{17,25},{25,17},{2,10},{10... | collective-permute-start | bytes 2949128 | tf_op jit(solution)/shard_map/ppermute | solution.py:23
  586.7 198.3 %reduce-scatter.8.cloned.1.call-start = ((), (), s32[]{:S(2)}) async-start(), calls=%async_computation.15 | async-start | bytes 10321920 | tf_op jit(solution)/shard_map/reduce_scatter | solution.py:468
  686.7 244.6 %reduce-scatter.10.cloned.1.call-start = ((), (), s32[]{:S(2)}) async-start(), calls=%async_computation.16 | async-start | bytes 10321920 | tf_op jit(solution)/shard_map/reduce_scatter | solution.py:468
  785.0 532.3 %reduce-scatter.12.cloned.1.call-start = ((), (), s32[]{:S(2)}) async-start(), calls=%async_computation.17 | async-start | bytes 3686400 | tf_op jit(solution)/shard_map/reduce_scatter | solution.py:468
  931.4 522.3 %all-gather.21.cloned.1.call-start = ((), (), s32[]{:S(2)}) async-start(), calls=%async_computation.19 | async-start | bytes 5734400 | tf_op jit(solution)/shard_map/all_gather | solution.py:471
  948.4 512.4 %all-gather.23.cloned.1.call-start = ((), (), s32[]{:S(2)}) async-start(), calls=%async_computation.20 | async-start | bytes 5734400 | tf_op jit(solution)/shard_map/all_gather | solution.py:485
  1055.0 86.3 %collective-permute-start.43 = (bf16[192,2560]{1,0:T(8,128)(2,1)S(1)}, bf16[192,2560]{1,0:T(8,128)(2,1)}, u32[]{:S(2)}, u32[]{:S(2)}) collective-permute-start(bf16[192,2560]{1,0:T(8,128)(2,1)S(1)} %get-tuple-element.154), channel_id=1, source_target_pairs={{0,8},{8,0},{16,24},{24,16},{1,9},{9,1},{17,25},{25,17},{2,10},{10... | collective-permute-start | bytes 2949128 | tf_op jit(solution)/shard_map/ppermute | solution.py:23
  1056.8 106.1 %collective-permute-start.42 = (bf16[192,2560]{1,0:T(8,128)(2,1)}, bf16[192,2560]{1,0:T(8,128)(2,1)S(1)}, u32[]{:S(2)}, u32[]{:S(2)}) collective-permute-start(bf16[192,2560]{1,0:T(8,128)(2,1)} %get-tuple-element.152), channel_id=1, source_target_pairs={{0,8},{8,0},{16,24},{24,16},{1,9},{9,1},{17,25},{25,17},{2,10},{10... | collective-permute-start | bytes 2949128 | tf_op jit(solution)/shard_map/ppermute | solution.py:23
  1056.8 106.1 %collective-permute-start.45 = (bf16[192,2560]{1,0:T(8,128)(2,1)}, bf16[192,2560]{1,0:T(8,128)(2,1)}, u32[]{:S(2)}, u32[]{:S(2)}) collective-permute-start(bf16[192,2560]{1,0:T(8,128)(2,1)} %get-tuple-element.153), channel_id=1, source_target_pairs={{0,16},{8,24},{16,0},{24,8},{1,17},{9,25},{17,1},{25,9},{2,18},{10... | collective-permute-start | bytes 2949128 | tf_op jit(solution)/shard_map/ppermute | solution.py:23
  1058.6 421.6 %all-gather.25.cloned.1.call-start = ((), (), s32[]{:S(2)}) async-start(), calls=%async_computation.21 | async-start | bytes 5734400 | tf_op jit(solution)/shard_map/all_gather | solution.py:485
  1157.3 85.6 %collective-permute-start.47 = (bf16[192,2560]{1,0:T(8,128)(2,1)S(1)}, bf16[192,2560]{1,0:T(8,128)(2,1)S(1)}, u32[]{:S(2)}, u32[]{:S(2)}) collective-permute-start(bf16[192,2560]{1,0:T(8,128)(2,1)S(1)} %get-tuple-element.155), channel_id=1, source_target_pairs={{0,16},{8,24},{16,0},{24,8},{1,17},{9,25},{17,1},{25,9},{2,18},{10... | collective-permute-start | bytes 2949128 | tf_op jit(solution)/shard_map/ppermute | solution.py:23
  1162.9 74.5 %collective-permute-start.50 = (bf16[192,2560]{1,0:T(8,128)(2,1)}, bf16[192,2560]{1,0:T(8,128)(2,1)}, u32[]{:S(2)}, u32[]{:S(2)}) collective-permute-start(bf16[192,2560]{1,0:T(8,128)(2,1)} %fusion.28), channel_id=1, source_target_pairs={{0,16},{8,24},{16,0},{24,8},{1,17},{9,25},{17,1},{25,9},{2,18},{10... | collective-permute-start | bytes 2949128 | tf_op jit(solution)/shard_map/ppermute | solution.py:23
  1168.5 75.3 %collective-permute-start.46 = (bf16[192,2560]{1,0:T(8,128)(2,1)}, bf16[192,2560]{1,0:T(8,128)(2,1)}, u32[]{:S(2)}, u32[]{:S(2)}) collective-permute-start(bf16[192,2560]{1,0:T(8,128)(2,1)} %get-tuple-element.151), channel_id=1, source_target_pairs={{0,8},{8,0},{16,24},{24,16},{1,9},{9,1},{17,25},{25,17},{2,10},{10... | collective-permute-start | bytes 2949128 | tf_op jit(solution)/shard_map/ppermute | solution.py:23
  1177.7 92.1 %collective-permute-start.53 = (bf16[192,2560]{1,0:T(8,128)(2,1)}, bf16[192,2560]{1,0:T(8,128)(2,1)}, u32[]{:S(2)}, u32[]{:S(2)}) collective-permute-start(bf16[192,2560]{1,0:T(8,128)(2,1)} %get-tuple-element.149), channel_id=1, source_target_pairs={{0,16},{8,24},{16,0},{24,8},{1,17},{9,25},{17,1},{25,9},{2,18},{10... | collective-permute-start | bytes 2949128 | tf_op jit(solution)/shard_map/ppermute | solution.py:23
  1278.6 102.8 %all-to-all-start.2 = ((bf16[8,48,2560]{2,1,0:T(8,128)(2,1)}), bf16[8,48,2560]{2,1,0:T(8,128)(2,1)S(1)}, u32[]{:S(2)}, u32[]{:S(2)}) async-start(bf16[8,48,2560]{2,1,0:T(8,128)(2,1)} %get-tuple-element.224), calls=%async_computation.2 | async-start | bytes 3932160 | tf_op jit(solution)/shard_map/all_to_all | solution.py:349
  1311.7 178.0 %reduce-scatter.14.cloned.1.call-start = ((), (), s32[]{:S(2)}) async-start(), calls=%async_computation.18 | async-start | bytes 5898240 | tf_op jit(solution)/shard_map/reduce_scatter | solution.py:468
  (102 other events, 2990.5 us)
Sparse Core Ops, SparseCore 0:
  65.7 56.3 all-gather.10
  123.7 69.1 all-gather.12
  195.1 89.5 all-gather.14
  286.8 87.0 all-gather.16
  375.4 87.0 all-gather.18
  586.8 99.8 reduce-scatter.5
  689.6 95.3 reduce-scatter.7
  787.9 95.5 reduce-scatter.9
  931.5 40.6 reduce-scatter.11
  974.0 79.5 all-gather.20
  1058.7 83.9 all-gather.22
  1144.5 117.6 all-gather.24
  1317.5 130.6 reduce-scatter.13

commit v3 on v2

--- a/solution.py
+++ b/solution.py
@@ -48,6 +48,18 @@
         out = lax.dynamic_update_slice(out, low[None], (place ^ turn, 0) + zeros)
         out = lax.dynamic_update_slice(out, high[None], (place ^ turn, half) + zeros)
     return row_major(out)
+
+
+def gather_small(value):
+    size = lax.axis_size("sp")
+    if size != 4:
+        return lax.all_gather(value, "sp", axis=0, tiled=False)
+    place = lax.axis_index("sp")
+    pieces = [value] + [swap(value, turn) for turn in range(1, size)]
+    here = [
+        sum(jnp.where(place ^ turn == i, pieces[turn], 0) for turn in range(size)) for i in range(size)
+    ]
+    return jnp.stack(here, axis=0)
 
 
 def scatter_sp(parts):
@@ -298,8 +310,54 @@
     )(gathered)
 
 
+def pass_kernel(*refs):
+    pass
+
+
 def after(value, *others):
-    return lax.optimization_barrier((value,) + others)[0]
+    here = pl.BlockSpec(memory_space=pl.ANY)
+    return pl.pallas_call(
+        pass_kernel,
+        in_specs=[here] * (1 + len(others)),
+        out_specs=here,
+        out_shape=jax.ShapeDtypeStruct(value.shape, value.dtype),
+        input_output_aliases={0: 0},
+        cost_estimate=pl.CostEstimate(flops=0, bytes_accessed=0, transcendentals=0),
+    )(value, *others)
+
+
+def pack_kernel(groups, parts, place_ref, gate_ref, up_ref, _, out_ref):
+    rows, columns = gate_ref.shape
+    share = columns // (groups * parts)
+    for place in range(parts):
+
+        @pl.when(place_ref[0] == place)
+        def _():
+            for i, ref in enumerate((gate_ref, up_ref)):
+                for j in range(groups):
+                    at = (i * groups + j) * share
+                    begin = (j * parts + place) * share
+                    out_ref[:, at : at + share] = ref[:, begin : begin + share]
+
+
+def pack_call(place, gate, up, when, groups, parts):
+    rows, columns = gate.shape
+    block = rows // 5 if rows % 80 == 0 else rows
+    spec = pl.BlockSpec((block, columns), lambda i: (i, 0))
+    return pl.pallas_call(
+        functools.partial(pack_kernel, groups, parts),
+        grid=(rows // block,),
+        in_specs=[
+            pl.BlockSpec(memory_space=pltpu.SMEM),
+            spec,
+            spec,
+            pl.BlockSpec(memory_space=pl.ANY),
+        ],
+        out_specs=pl.BlockSpec((block, 2 * columns // parts), lambda i: (i, 0)),
+        out_shape=jax.ShapeDtypeStruct((rows, 2 * columns // parts), gate.dtype),
+        compiler_params=pltpu.CompilerParams(vmem_limit_bytes=32 * 2**20),
+        cost_estimate=pl.CostEstimate(flops=0, bytes_accessed=5 * rows * columns, transcendentals=0),
+    )(place, gate, up, when)
 
 
 def local(
@@ -337,8 +395,10 @@
         jnp.where(arrived_slot[None, :] == lanes[:, None], lanes[None, :], 0), axis=1
     )
 
-    def deal(given):
-        blocks = jnp.take(given.reshape(groups, -1, width), pick_send, axis=0)
+    def picked(given):
+        return jnp.take(given.reshape(groups, -1, width), pick_send, axis=0)
+
+    def deal(blocks):
         return lax.all_to_all(blocks, "fsdp", split_axis=0, concat_axis=0, tiled=True)
 
     def in_place(came):
@@ -358,13 +418,6 @@
 
     ff_rows = w_down.shape[0]
     ff_share = ff_rows // parts
-
-    def hidden_share(weight):
-        def pick(place):
-            starts = [i * ff_rows + place * ff_share for i in range(groups)]
-            return lambda: jnp.concatenate([weight[:, i : i + ff_share] for i in starts], axis=1)
-
-        return lax.switch(sp_place, [pick(place) for place in range(parts)])
 
     query_cols = w_query.shape[1] // parts
     key_cols = key_weight.shape[1] // parts
@@ -372,25 +425,25 @@
     extra = -qkv_cols % 128
     extra = extra if extra else 128
     gains = jnp.pad(jnp.stack([attn_gain, mlp_gain], axis=1), ((0, 0), (0, extra - 2)))
-    came_tokens = deal(tokens)
-    w_query, w_out, w_gate, w_up, w_down = (
-        after(w, came_tokens) for w in (w_query, w_out, w_gate, w_up, w_down)
-    )
+    came_tokens = deal(picked(tokens))
+    came_incoming = deal(after(picked(cotangent), came_tokens))
+    gate_up_shard = pack_call(sp_place.reshape(1), w_gate, w_up, came_tokens, groups, parts)
     qkv_shard = jnp.concatenate(
         [column_share(w_query), column_share(key_weight), column_share(value_weight), gains], axis=1
     )
     qkv_all = gather_fsdp(qkv_shard)
     out_all = gather_fsdp(column_share(w_out))
-    gate_all = gather_fsdp(hidden_share(w_gate))
-    up_all = gather_fsdp(hidden_share(w_up))
+    gate_up_all = gather_fsdp(gate_up_shard)
+    hidden_units = gate_up_all.shape[1] // 2
+    gate_all, up_all = gate_up_all[:, :hidden_units], gate_up_all[:, hidden_units:]
     down_all = gather_fsdp(lax.dynamic_slice_in_dim(w_down, sp_place * ff_share, ff_share, axis=0))
     qkv_weight = qkv_all[:, :qkv_cols]
     gain_one = qkv_all[:, qkv_cols].astype(wide)[None, :]
     gain_two = qkv_all[:, qkv_cols + 1].astype(wide)[None, :]
 
     group_inputs = gather_sp(in_place(came_tokens)).reshape(-1, width)
-    group_incoming = gather_sp(in_place(deal(after(cotangent, qkv_all)))).reshape(-1, width)
-    group_positions = gather_sp(positions.reshape(-1, 1)).reshape(-1)
+    group_incoming = gather_sp(after(in_place(came_incoming), group_inputs)).reshape(-1, width)
+    group_positions = gather_small(positions.reshape(-1)).reshape(-1)
     total = group_inputs.shape[0]
 
     cosine, sine = rotary_tables(group_positions)
@@ -428,20 +481,24 @@
     active, active_back = jax.vjp(gated, gate, upward)
     active_low = active.astype(low)
     grad_down = dot_rows(active_low, group_incoming).astype(low)
-    d_active = dot_cols(after(group_incoming, grad_down), down_all)
+    down_all = after(down_all, grad_down)
+    d_active = dot_cols(group_incoming, down_all)
     d_gate, d_up = active_back(d_active)
     d_gate, d_up = d_gate.astype(low), d_up.astype(low)
-    d_normed_two = dot_cols(d_gate, gate_all) + dot_cols(d_up, up_all)
-    grad_gate = dot_rows(normed_two, d_gate).astype(low)
-    grad_up = dot_rows(normed_two, d_up).astype(low)
+    d_hidden_units = jnp.concatenate([d_gate, d_up], axis=1)
+    d_normed_two = dot_cols(d_hidden_units, gate_up_all)
     grad_gain_two = jnp.sum(d_normed_two * hidden * rms_two, axis=0)
     scaled = gain_two * d_normed_two
     back_two = rms_two * scaled - hidden * rms_two**3 * jnp.mean(scaled * hidden, axis=-1, keepdims=True)
-    own_d_hidden = own_columns(group_incoming).astype(wide) + scatter_sp(by_columns(back_two.astype(low)))
+    back_two = back_two.astype(low)
+    d_hidden_units = after(d_hidden_units, back_two)
+    grad_gate = dot_rows(normed_two, d_hidden_units[:, :hidden_units]).astype(low)
+    grad_up = dot_rows(normed_two, d_hidden_units[:, hidden_units:]).astype(low)
+    own_d_hidden = own_columns(group_incoming).astype(wide) + scatter_sp(by_columns(back_two))
     d_branch = own_d_hidden.astype(low)
     grad_out = dot_rows(mixed, d_branch)
     d_mixed = scatter_sp(by_columns(dot_cols(d_branch, out_all).astype(low))).astype(low)
-    result_part = dot(after(active_low, d_mixed), down_all).astype(low)
+    result_part = after(dot(after(active_low, d_branch, grad_down), down_all).astype(low), d_mixed)
     own_hidden_rows = lax.dynamic_slice_in_dim(hidden_low, sp_place * rows, rows, axis=0)
     result = own_hidden_rows.astype(wide) + scatter_sp(result_part.reshape(parts, rows, width))
     layer_out = to_given(result.astype(low))
@@ -467,25 +524,26 @@
     def scatter_fsdp(matrix):
         return lax.psum_scatter(matrix.astype(low), "fsdp", scatter_dimension=0, tiled=True)
 
-    def all_sp(shard, axis):
-        return lax.all_gather(shard, "sp", axis=axis, tiled=True)
+    def all_sp(shard):
+        return lax.all_gather(shard, "sp", axis=0, tiled=False)
 
     gain_grads = jnp.pad(
         jnp.stack([grad_gain_one, grad_gain_two], axis=1), ((0, 0), (0, extra - 2))
     )
     down_sum = scatter_fsdp(grad_down)
-    gate_sum = scatter_fsdp(after(grad_gate, down_sum))
-    up_sum = scatter_fsdp(after(grad_up, gate_sum))
-    out_sum = scatter_fsdp(after(grad_out.astype(low), up_sum))
-    qkv_sum = scatter_fsdp(after(jnp.concatenate([grad_qkv, gain_grads], axis=1).astype(low), out_sum))
-
-    down_shard = all_sp(down_sum, 0).astype(wide)
-
-    def hidden_whole(shard):
-        return spread_call(lax.all_gather(shard, "sp", axis=0, tiled=False), groups)
-
-    gate_shard = hidden_whole(gate_sum)
-    up_shard = hidden_whole(up_sum)
+    gate_sum = scatter_fsdp(grad_gate)
+    up_sum = scatter_fsdp(grad_up)
+    out_sum = scatter_fsdp(grad_out)
+    qkv_sum = scatter_fsdp(jnp.concatenate([grad_qkv, gain_grads], axis=1))
+
+    down_parts = all_sp(down_sum)
+    gate_parts = all_sp(after(gate_sum, down_parts))
+    up_parts = all_sp(after(up_sum, gate_parts))
+    out_sum = after(out_sum, up_parts)
+    qkv_sum = after(qkv_sum, out_sum)
+    down_shard = down_parts.reshape(-1, width).astype(wide)
+    gate_shard = spread_call(gate_parts, groups)
+    up_shard = spread_call(up_parts, groups)
     out_shard = side_by_side(gather_sp(out_sum)).astype(wide)
     qkv_shards = gather_sp(qkv_sum).astype(wide)
     edges = (0, query_cols, query_cols + key_cols, qkv_cols)

time: 1550 us -> 1390 us (0.90)
  waiting for transfers between devices: 803 us -> 531 us
  blocking collectives: 0 us -> 151 us
  starting transfers between devices: 117 us -> 63.8 us
  other arithmetic: 112 us -> 134 us
    all_to_all x0 -> x2, blocking collectives: none -> 151 us  [the longest x1 84.2 us: deal(): lax.all_to_all(blocks, 'fsdp', split_axis=0, concat_axis=0, tiled=True)]
    reduce_scatter x5, waiting for transfers between devices: 129 us -> 5.97 us  [scatter_fsdp(): lax.psum_scatter(matrix.astype(low), 'fsdp', scatter_dimension=0, tiled=T...]
    all_to_all x2 -> x1, waiting for transfers between devices: 119 us -> 39.1 us  [to_given(): lax.all_to_all(blocks, 'fsdp', split_axis=0, concat_axis=0, tiled=True)]
    all_gather x3, waiting for transfers between devices: 0.02 us -> 57.8 us  [all_sp(): return lax.all_gather(shard, 'sp', axis=0, tiled=False)]
    ppermute x66 -> x63, waiting for transfers between devices: 425 us -> 378 us  [swap(): return lax.ppermute(value, 'sp', [(i, i ^ bit) for i in range(size)])]
    all_to_all x2 -> x1, waiting for transfers between devices: 90.2 us -> 49.2 us  [deal(): lax.all_to_all(blocks, 'fsdp', split_axis=0, concat_axis=0, tiled=True)]
    all_gather x5 -> x4, waiting for transfers between devices: 39.5 us -> 0.02 us  [gather_fsdp(): return lax.all_gather(shard, 'fsdp', axis=0, tiled=True)]
    all_to_all x2 -> x1, starting transfers between devices: 41.1 us -> 6.28 us  [to_given(): lax.all_to_all(blocks, 'fsdp', split_axis=0, concat_axis=0, tiled=True)]
  transfers between devices with their start and end apart: 83 -> 77, of which waited for: 35 -> 32; matrix products, arithmetic and copies ran while one was open for 29% -> 34% of each run, Pallas kernels for 7% -> 8%
where the time goes in v3:
time: 1390 us; the launch traced here: 1380 us
  waiting for transfers between devices  531 us (38%)
  matrix products  253 us (18%)
  blocking collectives  151 us (11%)
  other arithmetic  134 us (10%)
  local copies, waits for them, and re-layouts  119 us (9%)
  Pallas kernels  112 us (8%)
  starting transfers between devices  63.8 us (5%)
  between operations  16 us (1%)
    ppermute x63, waiting for transfers between devices, swap(): return lax.ppermute(value, 'sp', [(i, i ^ bit) for i in range(size)])  378 us
    dot_general x4, matrix products, dot_cols(): lax.dot_general(left, right, (((1,), (1,)), ((), ())), preferred_element_...  92.1 us
    dot_general x5, matrix products, dot_rows(): lax.dot_general(left, right, (((0,), (0,)), ((), ())), preferred_element_...  86.9 us
    all_to_all x1, blocking collectives, deal(): lax.all_to_all(blocks, 'fsdp', split_axis=0, concat_axis=0, tiled=True)  84.2 us
    dot_general x4, matrix products, dot(): return jnp.dot(left, right, preferred_element_type=jnp.float32)  73.8 us
    all_to_all x1, blocking collectives, to_given(): lax.all_to_all(blocks, 'fsdp', split_axis=0, concat_axis=0, tiled=True)  67.2 us
    all_gather x3, waiting for transfers between devices, all_sp(): return lax.all_gather(shard, 'sp', axis=0, tiled=False)  57.8 us
    ppermute x63, starting transfers between devices, swap(): return lax.ppermute(value, 'sp', [(i, i ^ bit) for i in range(size)])  50.2 us
  transfers between devices with their start and end apart: 77, of which 32 were waited for; matrix products, arithmetic and copies ran while one was open for 34% of the time, Pallas kernels for 8%

profile of v3, /device:TPU:9, one launch (start us, length us, event | category | flops | bytes accessed | tf_op | source)
XLA Modules:
  0.0 1379.3 jit_solution(1460122029534110800)
XLA Ops:
  24.1 84.2 %all_to_all.20._.refs_1_ = bf16[8,48,2560]{2,1,0:T(8,128)(2,1)S(1)} all-to-all(bf16[8,48,2560]{2,1,0:T(8,128)(2,1)S(1)} %get-tuple-element.123), channel_id=1, replica_groups=mesh['sp'=4,'fsdp'=8] {'fsdp'}, dimensions={0} | all-to-all | bytes 3932160 | tf_op jit(solution)/shard_map/all_to_all | solution.py:402
  135.8 49.2 %all-to-all-done.1 = bf16[8,48,2560]{2,1,0:T(8,128)(2,1)} async-done(((bf16[8,48,2560]{2,1,0:T(8,128)(2,1)}), bf16[8,48,2560]{2,1,0:T(8,128)(2,1)}, u32[]{:S(2)}, u32[]{:S(2)}) %all-to-all-start.1) | async-done | bytes 1966112 | tf_op jit(solution)/shard_map/all_to_all | solution.py:402
  240.6 19.0 %collective-permute-done.4 = bf16[192,2560]{1,0:T(8,128)(2,1)S(1)} collective-permute-done((bf16[192,2560]{1,0:T(8,128)(2,1)S(1)}, bf16[192,2560]{1,0:T(8,128)(2,1)S(1)}, u32[]{:S(2)}, u32[]{:S(2)}) %collective-permute-start.4) | collective-permute-done | bytes 983072 | tf_op jit(solution)/shard_map/ppermute | solution.py:23
  276.1 23.7 %shard_map.221 = (bf16[1536,2560]{1,0:T(8,128)(2,1)}, bf16[1536,1024]{1,0:T(8,128)(2,1)}, bf16[1536,256]{1,0:T(8,128)(2,1)S(1)}, bf16[1536,256]{1,0:T(8,128)(2,1)S(1)}) custom-call(bf16[1536,2560]{1,0:T(8,128)(2,1)} %bitcast.13.x_ref.refs_1_, f32[1,2560]{1,0:T(1,128)S(1)} %reshape.271.gain_ref, bf16[2560,1024]{1,0:T(8,128)(2,1)} %all-gather.11.cloned.1.call-done.weight_ref, ...), custom_call_target="tpu_custom_call" | custom-call | flops 8053063680 | bytes 20971520 | tf_op jit(solution)/shard_map/pallas_call | solution.py:158
  301.6 27.4 %shard_map.222 = (bf16[1536,640]{1,0:T(8,128)(2,1)}, f32[1536,8]{1,0:T(8,128)}) custom-call(bf16[1536,1024]{1,0:T(8,128)(2,1)} %get-tuple-element.18.q_ref, bf16[1536,256]{1,0:T(8,128)(2,1)} %copy-done.9, bf16[1536,256]{1,0:T(8,128)(2,1)} %copy-done.10, s32[1536,1]{1,0:T(8,128)} %broadcast_in_dim.349.start_ref), custom_call_target="tpu_custom_call" | custom-call | flops 9663676416 | bytes 8388608 | tf_op jit(solution)/shard_map/pallas_call | solution.py:205
  352.1 20.5 %collective-permute-done.10 = bf16[768,640]{1,0:T(8,128)(2,1)S(1)} collective-permute-done((bf16[768,640]{1,0:T(8,128)(2,1)S(1)}, bf16[768,640]{1,0:T(8,128)(2,1)S(1)}, u32[]{:S(2)}, u32[]{:S(2)}) %collective-permute-start.10) | collective-permute-done | bytes 983072 | tf_op jit(solution)/shard_map/ppermute | solution.py:23
  375.4 19.3 %collective-permute-done.25 = bf16[192,2560]{1,0:T(8,128)(2,1)S(1)} collective-permute-done((bf16[192,2560]{1,0:T(8,128)(2,1)}, bf16[192,2560]{1,0:T(8,128)(2,1)S(1)}, u32[]{:S(2)}, u32[]{:S(2)}) %collective-permute-start.25) | collective-permute-done | bytes 983072 | tf_op jit(solution)/shard_map/ppermute | solution.py:23
  395.7 20.0 %collective-permute-done.13 = bf16[768,640]{1,0:T(8,128)(2,1)S(1)} collective-permute-done((bf16[768,640]{1,0:T(8,128)(2,1)S(1)}, bf16[768,640]{1,0:T(8,128)(2,1)S(1)}, u32[]{:S(2)}, u32[]{:S(2)}) %collective-permute-start.13) | collective-permute-done | bytes 983072 | tf_op jit(solution)/shard_map/ppermute | solution.py:23
  435.7 34.5 %collective-permute-done.15 = bf16[768,640]{1,0:T(8,128)(2,1)S(1)} collective-permute-done((bf16[768,640]{1,0:T(8,128)(2,1)S(1)}, bf16[768,640]{1,0:T(8,128)(2,1)S(1)}, u32[]{:S(2)}, u32[]{:S(2)}) %collective-permute-start.15) | collective-permute-done | bytes 983072 | tf_op jit(solution)/shard_map/ppermute | solution.py:23
  472.9 20.5 %collective-permute-done.19 = bf16[768,640]{1,0:T(8,128)(2,1)S(1)} collective-permute-done((bf16[768,640]{1,0:T(8,128)(2,1)S(1)}, bf16[768,640]{1,0:T(8,128)(2,1)S(1)}, u32[]{:S(2)}, u32[]{:S(2)}) %collective-permute-start.19) | collective-permute-done | bytes 983072 | tf_op jit(solution)/shard_map/ppermute | solution.py:23
  499.2 21.6 %fusion.23 = f32[1536,1792]{1,0:T(8,128)} fusion(bf16[2560,3584]{1,0:T(8,128)(2,1)} %all-gather.15.cloned.1.call-done, bf16[1536,2560]{1,0:T(8,128)(2,1)} %get-tuple-element.37, f32[2560]{0:T(1024)S(1)} %get-tuple-element.28, f32[1536]{0:T(1024)S(1)} %get-tuple-element.112), kind=kOutput, calls=%fused_computation.52 | convolution fusion | flops 14108590080 | bytes 28065792 | tf_op jit(solution)/shard_map/dot_general | solution.py:107
  520.8 22.5 %multiply_convert_fusion.1 = (bf16[1536,1792]{1,0:T(8,128)(2,1)}, f32[1536,1792]{1,0:T(8,128)}) fusion(f32[1536,1792]{1,0:T(8,128)} %fusion.23, bf16[2560,3584]{1,0:T(8,128)(2,1)} %all-gather.15.cloned.1.call-done, bf16[1536,2560]{1,0:T(8,128)(2,1)S(1)} %copy-done.11, f32[2560]{0:T(1024)S(1)} %get-tuple-element.28, f32[1536]{0:T(1024)S(1)} %get-tuple-element.112), kind=kOutput, calls=%fused_computation.45 | convolution fusion | flops 14125105152 | bytes 44580864 | tf_op jit(solution)/shard_map/dot_general | solution.py:107
  543.3 20.7 %convolution_convert_fusion.4.refs_1_.refs_2_ = bf16[1792,2560]{1,0:T(8,128)(2,1)} fusion(bf16[1536,1792]{1,0:T(8,128)(2,1)} %get-tuple-element.126.refs_0_, bf16[1536,2560]{1,0:T(8,128)(2,1)} %bitcast.52), kind=kOutput, calls=%fused_computation.39 | convolution fusion | flops 14097448960 | bytes 22544384 | tf_op jit(solution)/shard_map/dot_general | solution.py:111
  564.1 27.1 %fusion.18 = (bf16[1536,1792]{1,0:T(8,128)(2,1)}, bf16[1536,1792]{1,0:T(8,128)(2,1)}) fusion(f32[1536,1792]{1,0:T(8,128)} %fusion.23, f32[1536,1792]{1,0:T(8,128)} %get-tuple-element.127, bf16[1536,2560]{1,0:T(8,128)(2,1)} %bitcast.52, bf16[1792,2560]{1,0:T(8,128)(2,1)} %shard_map.226), kind=kOutput, calls=%fused_computation.42 | convolution fusion | flops 14131396608 | bytes 50069504 | tf_op jit(solution)/shard_map/dot_general | solution.py:115
  591.2 39.0 %fusion.15 = (bf16[2560]{0:T(1024)(128)(2,1)S(1)}, f32[1536]{0:T(1024)S(1)}, f32[1536,2560]{1,0:T(8,128)}) fusion(bf16[1536,2560]{1,0:T(8,128)(2,1)} %get-tuple-element.37, f32[1536]{0:T(1024)S(1)} %get-tuple-element.112, f32[2560]{0:T(1024)S(1)} %get-tuple-element.28, bf16[2560,3584]{1,0:T(8,128)(2,1)} %all-gather.15.cloned.1.call-done, ...), kind=kOutput, calls=%fused_computation.32 | convolution fusion | flops 28235264000 | bytes 52980736 | tf_op jit(solution)/shard_map/dot_general | solution.py:115
  652.0 21.4 %convolution_convert_fusion.1 = bf16[2560,1792]{1,0:T(8,128)(2,1)} fusion(bf16[1536,3584]{1,0:T(8,128)(2,1)} %shard_map.230, bf16[1536,2560]{1,0:T(8,128)(2,1)} %get-tuple-element.37, f32[2560]{0:T(1024)S(1)} %get-tuple-element.28, f32[1536]{0:T(1024)S(1)} %get-tuple-element.112), kind=kOutput, calls=%fused_computation.36 | convolution fusion | flops 14113177600 | bytes 22560768 | tf_op jit(solution)/shard_map/dot_general | solution.py:111
  674.2 21.5 %convolution_convert_fusion.2 = bf16[2560,1792]{1,0:T(8,128)(2,1)} fusion(bf16[1536,3584]{1,0:T(8,128)(2,1)} %shard_map.230, bf16[1536,2560]{1,0:T(8,128)(2,1)} %get-tuple-element.37, f32[2560]{0:T(1024)S(1)} %get-tuple-element.28, f32[1536]{0:T(1024)S(1)} %get-tuple-element.112), kind=kOutput, calls=%fused_computation.37 | convolution fusion | flops 14113177600 | bytes 22560768 | tf_op jit(solution)/shard_map/dot_general | solution.py:111
  722.3 19.3 %collective-permute-done.27 = bf16[768,640]{1,0:T(8,128)(2,1)S(1)} collective-permute-done((bf16[768,640]{1,0:T(8,128)(2,1)S(1)}, bf16[768,640]{1,0:T(8,128)(2,1)S(1)}, u32[]{:S(2)}, u32[]{:S(2)}) %collective-permute-start.27) | collective-permute-done | bytes 983072 | tf_op jit(solution)/shard_map/ppermute | solution.py:23
  774.1 57.7 %all-gather.19.cloned.1.call-done = bf16[896,2560]{1,0:T(8,128)(2,1)} async-done(((bf16[224,2560]{1,0:T(8,128)(2,1)}), bf16[896,2560]{1,0:T(8,128)(2,1)}) %all-gather.19.cloned.1.call-update) | async-done | bytes 4587536 | tf_op jit(solution)/shard_map/all_gather | solution.py:528
  903.9 19.8 %convolution_convert_fusion.3.refs_0_ = bf16[1536,2560]{1,0:T(8,128)(2,1)} fusion(bf16[1536,1792]{1,0:T(8,128)(2,1)S(1)} %copy-done.26, bf16[1792,2560]{1,0:T(8,128)(2,1)} %shard_map.226), kind=kOutput, calls=%fused_computation.38 | convolution fusion | flops 14096793600 | bytes 22544384 | tf_op jit(solution)/shard_map/dot_general | solution.py:107
  927.3 49.9 %shard_map.229 = bf16[1536,960]{1,0:T(8,128)(2,1)} custom-call(bf16[1536,1024]{1,0:T(8,128)(2,1)} %get-tuple-element.18.q_ref, bf16[1536,256]{1,0:T(8,128)(2,1)} %copy-done.9, bf16[1536,256]{1,0:T(8,128)(2,1)} %copy-done.10, bf16[1536,640]{1,0:T(8,128)(2,1)} %pad_maximum_fusion.6.refs_1_.grad_ref, f32[8,1536]{1,0:T(8,128)} %bitcast.325, ...), custom_call_target="tpu_custom_call" | custom-call | flops 24159191040 | bytes 12582912 | tf_op jit(solution)/shard_map/pallas_call | solution.py:274
  1048.3 56.3 %collective-permute-done.40 = bf16[192,2560]{1,0:T(8,128)(2,1)} collective-permute-done((bf16[192,2560]{1,0:T(8,128)(2,1)}, bf16[192,2560]{1,0:T(8,128)(2,1)}, u32[]{:S(2)}, u32[]{:S(2)}) %collective-permute-start.40) | collective-permute-done | bytes 983072 | tf_op jit(solution)/shard_map/ppermute | solution.py:23
  1185.3 67.2 %all_to_all.21 = bf16[8,48,2560]{2,1,0:T(8,128)(2,1)} all-to-all(bf16[8,48,2560]{2,1,0:T(8,128)(2,1)S(1)} %get-tuple-element.118), channel_id=1, replica_groups=mesh['sp'=4,'fsdp'=8] {'fsdp'}, dimensions={0} | all-to-all | bytes 3932160 | tf_op jit(solution)/shard_map/all_to_all | solution.py:409
  1262.4 39.1 %all-to-all-done.2 = bf16[8,48,2560]{2,1,0:T(8,128)(2,1)S(1)} async-done(((bf16[8,48,2560]{2,1,0:T(8,128)(2,1)}), bf16[8,48,2560]{2,1,0:T(8,128)(2,1)S(1)}, u32[]{:S(2)}, u32[]{:S(2)}) %all-to-all-start.2) | async-done | bytes 1966112 | tf_op jit(solution)/shard_map/all_to_all | solution.py:409
  (453 shorter events, 561.8 us)
Async XLA Ops:
  7.2 266.4 %all-gather.11.cloned.1.call-start = ((), (), s32[]{:S(2)}) async-start(), calls=%async_computation.9 | async-start | bytes 5898240 | tf_op jit(solution)/shard_map/all_gather | solution.py:417
  12.2 407.2 %all-gather.13.cloned.1.call-start = ((), (), s32[]{:S(2)}) async-start(), calls=%async_computation.10 | async-start | bytes 3686400 | tf_op jit(solution)/shard_map/all_gather | solution.py:417
  14.1 485.0 %all-gather.15.cloned.1.call-start = ((), (), s32[]{:S(2)}) async-start(), calls=%async_computation.11 | async-start | bytes 20643840 | tf_op jit(solution)/shard_map/all_gather | solution.py:417
  113.8 71.3 %all-to-all-start.1 = ((bf16[8,48,2560]{2,1,0:T(8,128)(2,1)}), bf16[8,48,2560]{2,1,0:T(8,128)(2,1)}, u32[]{:S(2)}, u32[]{:S(2)}) async-start(bf16[8,48,2560]{2,1,0:T(8,128)(2,1)} %shard_map.224), calls=%async_computation.1 | async-start | bytes 3932160 | tf_op jit(solution)/shard_map/all_to_all | solution.py:402
  120.4 443.6 %all-gather.17.cloned.1.call-start = ((), (), s32[]{:S(2)}) async-start(), calls=%async_computation.12 | async-start | bytes 10321920 | tf_op jit(solution)/shard_map/all_gather | solution.py:417
  125.9 547.6 %reduce-scatter.14.cloned.1.call-start = ((), (), s32[]{:S(2)}) async-start(), calls=%async_computation.17 | async-start | bytes 10321920 | tf_op jit(solution)/shard_map/reduce_scatter | solution.py:525
  264.7 67.2 %collective-permute-start.21 = (bf16[192,2560]{1,0:T(8,128)(2,1)}, bf16[192,2560]{1,0:T(8,128)(2,1)}, u32[]{:S(2)}, u32[]{:S(2)}) collective-permute-start(bf16[192,2560]{1,0:T(8,128)(2,1)} %get-tuple-element.93), channel_id=1, source_target_pairs={{0,8},{8,0},{16,24},{24,16},{1,9},{9,1},{17,25},{25,17},{2,10},{10... | collective-permute-start | bytes 2949128 | tf_op jit(solution)/shard_map/ppermute | solution.py:23
  264.8 74.3 %collective-permute-start.23 = (bf16[192,2560]{1,0:T(8,128)(2,1)}, bf16[192,2560]{1,0:T(8,128)(2,1)}, u32[]{:S(2)}, u32[]{:S(2)}) collective-permute-start(bf16[192,2560]{1,0:T(8,128)(2,1)} %get-tuple-element.93), channel_id=1, source_target_pairs={{0,16},{8,24},{16,0},{24,8},{1,17},{9,25},{17,1},{25,9},{2,18},{10... | collective-permute-start | bytes 2949128 | tf_op jit(solution)/shard_map/ppermute | solution.py:23
  266.2 69.4 %collective-permute-start.22 = (bf16[192,2560]{1,0:T(8,128)(2,1)}, bf16[192,2560]{1,0:T(8,128)(2,1)}, u32[]{:S(2)}, u32[]{:S(2)}) collective-permute-start(bf16[192,2560]{1,0:T(8,128)(2,1)} %get-tuple-element.92), channel_id=1, source_target_pairs={{0,8},{8,0},{16,24},{24,16},{1,9},{9,1},{17,25},{25,17},{2,10},{10... | collective-permute-start | bytes 2949128 | tf_op jit(solution)/shard_map/ppermute | solution.py:23
  267.4 74.2 %collective-permute-start.24 = (bf16[192,2560]{1,0:T(8,128)(2,1)}, bf16[192,2560]{1,0:T(8,128)(2,1)S(1)}, u32[]{:S(2)}, u32[]{:S(2)}) collective-permute-start(bf16[192,2560]{1,0:T(8,128)(2,1)} %get-tuple-element.92), channel_id=1, source_target_pairs={{0,16},{8,24},{16,0},{24,8},{1,17},{9,25},{17,1},{25,9},{2,18},{10... | collective-permute-start | bytes 2949128 | tf_op jit(solution)/shard_map/ppermute | solution.py:23
  341.6 53.1 %collective-permute-start.25 = (bf16[192,2560]{1,0:T(8,128)(2,1)}, bf16[192,2560]{1,0:T(8,128)(2,1)S(1)}, u32[]{:S(2)}, u32[]{:S(2)}) collective-permute-start(bf16[192,2560]{1,0:T(8,128)(2,1)} %collective-permute-done.21), channel_id=1, source_target_pairs={{0,16},{8,24},{16,0},{24,8},{1,17},{9,25},{17,1},{25,9},{2,18},{10... | collective-permute-start | bytes 2949128 | tf_op jit(solution)/shard_map/ppermute | solution.py:23
  351.4 81.0 %collective-permute-start.26 = (bf16[192,2560]{1,0:T(8,128)(2,1)S(1)}, bf16[192,2560]{1,0:T(8,128)(2,1)}, u32[]{:S(2)}, u32[]{:S(2)}) collective-permute-start(bf16[192,2560]{1,0:T(8,128)(2,1)S(1)} %collective-permute-done.24), channel_id=1, source_target_pairs={{0,8},{8,0},{16,24},{24,16},{1,9},{9,1},{17,25},{25,17},{2,10},{10... | collective-permute-start | bytes 2949128 | tf_op jit(solution)/shard_map/ppermute | solution.py:23
  564.0 210.1 %reduce-scatter.12.cloned.1.call-start = ((), (), s32[]{:S(2)}) async-start(), calls=%async_computation.16 | async-start | bytes 10321920 | tf_op jit(solution)/shard_map/reduce_scatter | solution.py:525
  673.4 158.4 %all-gather.19.cloned.1.call-start = ((), (), s32[]{:S(2)}) async-start(), calls=%async_computation.18 | async-start | bytes 5734400 | tf_op jit(solution)/shard_map/all_gather | solution.py:528
  674.2 320.2 %reduce-scatter.10.cloned.1.call-start = ((), (), s32[]{:S(2)}) async-start(), calls=%async_computation.15 | async-start | bytes 10321920 | tf_op jit(solution)/shard_map/reduce_scatter | solution.py:525
  695.8 298.6 %all-gather.21.cloned.1.call-start = ((), (), s32[]{:S(2)}) async-start(), calls=%async_computation.19 | async-start | bytes 5734400 | tf_op jit(solution)/shard_map/all_gather | solution.py:528
  831.8 486.0 %reduce-scatter.8.cloned.1.call-start = ((), (), s32[]{:S(2)}) async-start(), calls=%async_computation.14 | async-start | bytes 3686400 | tf_op jit(solution)/shard_map/reduce_scatter | solution.py:525
  886.1 431.8 %all-gather.23.cloned.1.call-start = ((), (), s32[]{:S(2)}) async-start(), calls=%async_computation.20 | async-start | bytes 5734400 | tf_op jit(solution)/shard_map/all_gather | solution.py:528
  994.4 323.5 %reduce-scatter.6.cloned.1.call-start = ((), (), s32[]{:S(2)}) async-start(), calls=%async_computation.13 | async-start | bytes 5898240 | tf_op jit(solution)/shard_map/reduce_scatter | solution.py:525
  1016.3 139.1 %collective-permute-start.50 = (bf16[192,2560]{1,0:T(8,128)(2,1)S(1)}, bf16[192,2560]{1,0:T(8,128)(2,1)}, u32[]{:S(2)}, u32[]{:S(2)}) collective-permute-start(bf16[192,2560]{1,0:T(8,128)(2,1)S(1)} %get-tuple-element.45), channel_id=1, source_target_pairs={{0,16},{8,24},{16,0},{24,8},{1,17},{9,25},{17,1},{25,9},{2,18},{10... | collective-permute-start | bytes 2949128 | tf_op jit(solution)/shard_map/ppermute | solution.py:23
  1017.7 90.4 %collective-permute-start.45 = (bf16[192,2560]{1,0:T(8,128)(2,1)}, bf16[192,2560]{1,0:T(8,128)(2,1)S(1)}, u32[]{:S(2)}, u32[]{:S(2)}) collective-permute-start(bf16[192,2560]{1,0:T(8,128)(2,1)} %get-tuple-element.42), channel_id=1, source_target_pairs={{0,8},{8,0},{16,24},{24,16},{1,9},{9,1},{17,25},{25,17},{2,10},{10... | collective-permute-start | bytes 2949128 | tf_op jit(solution)/shard_map/ppermute | solution.py:23
  1018.3 90.1 %collective-permute-start.48 = (bf16[192,2560]{1,0:T(8,128)(2,1)}, bf16[192,2560]{1,0:T(8,128)(2,1)}, u32[]{:S(2)}, u32[]{:S(2)}) collective-permute-start(bf16[192,2560]{1,0:T(8,128)(2,1)} %get-tuple-element.43), channel_id=1, source_target_pairs={{0,16},{8,24},{16,0},{24,8},{1,17},{9,25},{17,1},{25,9},{2,18},{10... | collective-permute-start | bytes 2949128 | tf_op jit(solution)/shard_map/ppermute | solution.py:23
  1023.5 81.0 %collective-permute-start.40 = (bf16[192,2560]{1,0:T(8,128)(2,1)}, bf16[192,2560]{1,0:T(8,128)(2,1)}, u32[]{:S(2)}, u32[]{:S(2)}) collective-permute-start(bf16[192,2560]{1,0:T(8,128)(2,1)} %get-tuple-element.50), channel_id=1, source_target_pairs={{0,8},{8,0},{16,24},{24,16},{1,9},{9,1},{17,25},{25,17},{2,10},{10... | collective-permute-start | bytes 2949128 | tf_op jit(solution)/shard_map/ppermute | solution.py:23
  1039.0 70.6 %collective-permute-start.47 = (bf16[192,2560]{1,0:T(8,128)(2,1)}, bf16[192,2560]{1,0:T(8,128)(2,1)}, u32[]{:S(2)}, u32[]{:S(2)}) collective-permute-start(bf16[192,2560]{1,0:T(8,128)(2,1)} %fusion.34), channel_id=1, source_target_pairs={{0,16},{8,24},{16,0},{24,8},{1,17},{9,25},{17,1},{25,9},{2,18},{10... | collective-permute-start | bytes 2949128 | tf_op jit(solution)/shard_map/ppermute | solution.py:23
  (105 other events, 2806.0 us)
Sparse Core Ops, SparseCore 0:
  12.4 90.6 all-gather.10
  104.7 64.2 all-gather.12
  171.2 170.7 all-gather.14
  344.1 86.9 all-gather.16
  564.1 99.4 reduce-scatter.13
  673.6 100.4 reduce-scatter.11
  775.9 55.8 all-gather.18
  834.7 95.5 reduce-scatter.9
  932.1 55.8 all-gather.20
  990.7 40.0 reduce-scatter.7
  1032.8 91.5 all-gather.22
  1127.3 67.6 reduce-scatter.5

commit v4 on v3

--- a/solution.py
+++ b/solution.py
@@ -65,9 +65,8 @@
 def scatter_sp(parts):
     size = lax.axis_size("sp")
     if size != 4:
-        return lax.psum_scatter(
-            parts, "sp", scatter_dimension=0, tiled=False
-        ).astype(jnp.float32)
+        summed = lax.psum_scatter(parts, "sp", scatter_dimension=0, tiled=False)
+        return summed.astype(jnp.float32), ((summed,), (summed,))
     place = lax.axis_index("sp")
     half = parts.shape[1] // 2
     parts = row_major(parts)
@@ -80,11 +79,12 @@
     low = parts.dtype
     from_x, from_y = swap(block(3, True), 1), swap(block(3, False), 2)
     x_first, y_second = swap(block(1, True), 1), swap(block(2, False), 2)
-    y_first = swap((block(2, True).astype(wide) + from_x.astype(wide)).astype(low), 2)
-    x_second = swap((block(1, False).astype(wide) + from_y.astype(wide)).astype(low), 1)
+    y_sent = (block(2, True).astype(wide) + from_x.astype(wide)).astype(low)
+    x_sent = (block(1, False).astype(wide) + from_y.astype(wide)).astype(low)
+    y_first, x_second = swap(y_sent, 2), swap(x_sent, 1)
     first = block(0, True).astype(wide) + x_first.astype(wide) + y_first.astype(wide)
     second = block(0, False).astype(wide) + x_second.astype(wide) + y_second.astype(wide)
-    return jnp.concatenate([first, second], axis=0)
+    return jnp.concatenate([first, second], axis=0), ((y_sent, x_sent), (x_first, y_second))
 
 
 def rotary_tables(positions):
@@ -97,10 +97,6 @@
         jnp.concatenate([cosine, cosine, rest], axis=1),
         jnp.concatenate([-sine, sine, rest], axis=1),
     )
-
-
-def gated(gate, upward):
-    return jax.nn.silu(gate) * upward
 
 
 def dot(left, right):
@@ -281,33 +277,333 @@
         ],
         compiler_params=pltpu.CompilerParams(vmem_limit_bytes=56 * 2**20),
         cost_estimate=pl.CostEstimate(
-            flops=heads * total * total * 1280, bytes_accessed=12 * 2**20, transcendentals=heads * total * total // 2
+            flops=8000 * heads * total * total * 128, bytes_accessed=12 * 2**20, transcendentals=heads * total * total // 2
         ),
     )(q, k, v, grad, lse_rows, start_row, cosine, sine_back)
 
-def spread_kernel(groups, parts_ref, out_ref):
-    parts, _, columns = parts_ref.shape
-    share = columns // groups
+def gate_up_kernel(x_ref, gate_weight_ref, up_weight_ref, active_ref, gate_ref, up_ref):
+    x = x_ref[...]
+    gate = jnp.dot(x, gate_weight_ref[...], preferred_element_type=jnp.float32)
+    upward = jnp.dot(x, up_weight_ref[...], preferred_element_type=jnp.float32)
+    active_ref[...] = (gate / (1.0 + jnp.exp(-gate)) * upward).astype(jnp.bfloat16)
+    gate_ref[...] = gate.astype(jnp.bfloat16)
+    up_ref[...] = upward.astype(jnp.bfloat16)
+
+
+def unit_block(units):
+    return 256 if units % 256 == 0 else 128
+
+
+def gate_up_call(x, weights):
+    total, width = x.shape
+    units = weights.shape[1] // 2
+    block = unit_block(units)
+    count = units // block
+    out = pl.BlockSpec((total, block), lambda j: (0, j))
+    return pl.pallas_call(
+        gate_up_kernel,
+        grid=(count,),
+        in_specs=[
+            pl.BlockSpec((total, width), lambda j: (0, 0)),
+            pl.BlockSpec((width, block), lambda j: (0, j)),
+            pl.BlockSpec((width, block), lambda j: (0, j + count)),
+        ],
+        out_specs=[out] * 3,
+        out_shape=[jax.ShapeDtypeStruct((total, units), jnp.bfloat16)] * 3,
+        compiler_params=pltpu.CompilerParams(vmem_limit_bytes=56 * 2**20),
+        cost_estimate=pl.CostEstimate(
+            flops=4 * total * width * units, bytes_accessed=45 * 2**20, transcendentals=0
+        ),
+    )(x, weights, weights)
+
+
+def unit_back_kernel(incoming_ref, down_ref, gate_ref, up_ref, d_gate_ref, d_up_ref):
+    d_active = dot_cols(incoming_ref[...], down_ref[...])
+    gate = gate_ref[...].astype(jnp.float32)
+    upward = up_ref[...].astype(jnp.float32)
+    logistic = 1.0 / (1.0 + jnp.exp(-gate))
+    d_gate_ref[...] = (d_active * upward * logistic * (1.0 + gate * (1.0 - logistic))).astype(jnp.bfloat16)
+    d_up_ref[...] = (d_active * gate * logistic).astype(jnp.bfloat16)
+
+
+def unit_back_call(incoming, down, gate, up):
+    total, width = incoming.shape
+    units = down.shape[0]
+    block = unit_block(units)
+    column = pl.BlockSpec((total, block), lambda j: (0, j))
+    return pl.pallas_call(
+        unit_back_kernel,
+        grid=(units // block,),
+        in_specs=[
+            pl.BlockSpec((total, width), lambda j: (0, 0)),
+            pl.BlockSpec((block, width), lambda j: (j, 0)),
+            column,
+            column,
+        ],
+        out_specs=[column] * 2,
+        out_shape=[jax.ShapeDtypeStruct((total, units), jnp.bfloat16)] * 2,
+        compiler_params=pltpu.CompilerParams(vmem_limit_bytes=56 * 2**20),
+        cost_estimate=pl.CostEstimate(
+            flops=2 * total * width * units, bytes_accessed=40 * 2**20, transcendentals=0
+        ),
+    )(incoming, down, gate, up)
+
+
+def norm_back(d_normed, x, gain):
+    scale = lax.rsqrt(jnp.mean(x * x, axis=1, keepdims=True) + eps)
+    grad_gain = jnp.sum(d_normed * (x * scale), axis=0, keepdims=True)
+    scaled = d_normed * gain
+    inner = jnp.mean(scaled * x, axis=1, keepdims=True)
+    return scale * scaled - x * (scale * scale * scale * inner), grad_gain
+
+
+def add_up(ref, value):
+    @pl.when(pl.program_id(0) == 0)
+    def _():
+        ref[...] = jnp.zeros_like(ref)
+
+    ref[...] += value
+
+
+def mlp_back_kernel(d_gate_ref, d_up_ref, weight_ref, x_ref, gain_ref, *refs):
+    out_ref, grad_ref = refs[-2:]
+    units = d_gate_ref.shape[1]
+    d_normed = dot_cols(d_gate_ref[...], weight_ref[:, :units]) + dot_cols(
+        d_up_ref[...], weight_ref[:, units:]
+    )
+    back, grad_gain = norm_back(d_normed, x_ref[...].astype(jnp.float32), gain_ref[...])
+    parts, _, share = out_ref.shape
     for i in range(parts):
-        for j in range(groups):
-            at = (j * parts + i) * share
-            out_ref[:, at : at + share] = parts_ref[i, :, j * share : (j + 1) * share].astype(jnp.float32)
-
-
-def spread_call(gathered, groups):
-    parts, rows, columns = gathered.shape
-    block = rows // 5 if rows % 80 == 0 else rows
-    return pl.pallas_call(
-        functools.partial(spread_kernel, groups),
-        grid=(rows // block,),
-        in_specs=[pl.BlockSpec((parts, block, columns), lambda i: (0, i, 0))],
-        out_specs=pl.BlockSpec((block, parts * columns), lambda i: (i, 0)),
-        out_shape=jax.ShapeDtypeStruct((rows, parts * columns), jnp.float32),
+        out_ref[i] = back[:, i * share : (i + 1) * share].astype(jnp.bfloat16)
+    add_up(grad_ref, grad_gain)
+
+
+def mlp_back_call(d_gate, d_up, weights, x, gain, parts, *when):
+    total, units = d_gate.shape
+    width = x.shape[1]
+    share = width // parts
+    block = 512
+    row = lambda n: pl.BlockSpec((block, n), lambda i: (i, 0))
+    whole = lambda a: pl.BlockSpec(a.shape, lambda i: (0, 0), pipeline_mode=pl.Buffered(1))
+    return pl.pallas_call(
+        mlp_back_kernel,
+        grid=(total // block,),
+        in_specs=[row(units), row(units), whole(weights), row(width), whole(gain)]
+        + [pl.BlockSpec(memory_space=pl.ANY)] * len(when),
+        out_specs=[
+            pl.BlockSpec((parts, block, share), lambda i: (0, i, 0)),
+            pl.BlockSpec((1, width), lambda i: (0, 0)),
+        ],
+        out_shape=[
+            jax.ShapeDtypeStruct((parts, total, share), jnp.bfloat16),
+            jax.ShapeDtypeStruct((1, width), jnp.float32),
+        ],
+        compiler_params=pltpu.CompilerParams(vmem_limit_bytes=60 * 2**20),
+        cost_estimate=pl.CostEstimate(
+            flops=4 * total * width * units, bytes_accessed=45 * 2**20, transcendentals=0
+        ),
+    )(d_gate, d_up, weights, x, gain, *when)
+
+
+def attend_norm_kernel(parts, place_ref, d_qkv_ref, weight_ref, x_ref, gain_ref, own_ref, *refs):
+    out_ref, grad_ref = refs[-2:]
+    d_normed = dot_cols(d_qkv_ref[...], weight_ref[:, : d_qkv_ref.shape[1]])
+    back, grad_gain = norm_back(d_normed, x_ref[...].astype(jnp.float32), gain_ref[...])
+    out_ref[...] = back.astype(jnp.bfloat16)
+    share = own_ref.shape[1]
+    for place in range(parts):
+
+        @pl.when(place_ref[0] == place)
+        def _():
+            lanes = slice(place * share, (place + 1) * share)
+            out_ref[:, lanes] = (back[:, lanes] + own_ref[...]).astype(jnp.bfloat16)
+
+    add_up(grad_ref, grad_gain)
+
+
+def attend_norm_call(place, d_qkv, weights, x, gain, own, parts, *when):
+    total, width = x.shape
+    block = 256
+    row = lambda n: pl.BlockSpec((block, n), lambda i: (i, 0))
+    whole = lambda a: pl.BlockSpec(a.shape, lambda i: (0, 0), pipeline_mode=pl.Buffered(1))
+    return pl.pallas_call(
+        functools.partial(attend_norm_kernel, parts),
+        grid=(total // block,),
+        in_specs=[
+            pl.BlockSpec(memory_space=pltpu.SMEM),
+            row(d_qkv.shape[1]),
+            whole(weights),
+            row(width),
+            whole(gain),
+            row(own.shape[1]),
+        ]
+        + [pl.BlockSpec(memory_space=pl.ANY)] * len(when),
+        out_specs=[row(width), pl.BlockSpec((1, width), lambda i: (0, 0))],
+        out_shape=[
+            jax.ShapeDtypeStruct((total, width), jnp.bfloat16),
+            jax.ShapeDtypeStruct((1, width), jnp.float32),
+        ],
+        compiler_params=pltpu.CompilerParams(vmem_limit_bytes=56 * 2**20),
+        cost_estimate=pl.CostEstimate(
+            flops=2 * total * width * d_qkv.shape[1], bytes_accessed=30 * 2**20, transcendentals=0
+        ),
+    )(place, d_qkv, weights, x, gain, own, *when)
+
+
+def out_back_kernel(d_ref, weight_ref, *refs):
+    refs[-1][0] = dot_cols(d_ref[...], weight_ref[...]).astype(jnp.bfloat16)
+
+
+def out_back_call(d_branch, weights, parts, *when):
+    total, share = d_branch.shape
+    rows = weights.shape[0] // parts
+    return pl.pallas_call(
+        out_back_kernel,
+        grid=(parts,),
+        in_specs=[
+            pl.BlockSpec((total, share), lambda i: (0, 0)),
+            pl.BlockSpec((rows, share), lambda i: (i, 0)),
+        ]
+        + [pl.BlockSpec(memory_space=pl.ANY)] * len(when),
+        out_specs=pl.BlockSpec((1, total, rows), lambda i: (i, 0, 0)),
+        out_shape=jax.ShapeDtypeStruct((parts, total, rows), jnp.bfloat16),
         compiler_params=pltpu.CompilerParams(vmem_limit_bytes=32 * 2**20),
         cost_estimate=pl.CostEstimate(
-            flops=0, bytes_accessed=6 * parts * rows * columns, transcendentals=0
-        ),
-    )(gathered)
+            flops=2 * total * share * weights.shape[0], bytes_accessed=14 * 2**20, transcendentals=0
+        ),
+    )(d_branch, weights, *when)
+
+
+def rows_kernel(left_ref, right_ref, *refs):
+    refs[-1][...] = dot_rows(left_ref[...], right_ref[...]).astype(jnp.bfloat16)
+
+
+def rows_call(left, right, *when):
+    total, rows = left.shape
+    columns = right.shape[1]
+    block = 256 if columns % 256 == 0 else 128
+    return pl.pallas_call(
+        rows_kernel,
+        grid=(columns // block,),
+        in_specs=[
+            pl.BlockSpec((total, rows), lambda j: (0, 0)),
+            pl.BlockSpec((total, block), lambda j: (0, j)),
+        ]
+        + [pl.BlockSpec(memory_space=pl.ANY)] * len(when),
+        out_specs=pl.BlockSpec((rows, block), lambda j: (0, j)),
+        out_shape=jax.ShapeDtypeStruct((rows, columns), jnp.bfloat16),
+        compiler_params=pltpu.CompilerParams(vmem_limit_bytes=56 * 2**20),
+        cost_estimate=pl.CostEstimate(flops=0, bytes_accessed=0, transcendentals=0),
+    )(left, right, *when)
+
+
+def product_kernel(left_ref, right_ref, *refs):
+    refs[-1][...] = jnp.dot(left_ref[...], right_ref[...], preferred_element_type=jnp.float32).astype(
+        jnp.bfloat16
+    )
+
+
+def product_call(left, right, *when):
+    total, depth = left.shape
+    columns = right.shape[1]
+    block = 256 if columns % 256 == 0 else 128
+    return pl.pallas_call(
+        product_kernel,
+        grid=(columns // block,),
+        in_specs=[
+            pl.BlockSpec((total, depth), lambda j: (0, 0)),
+            pl.BlockSpec((depth, block), lambda j: (0, j)),
+        ]
+        + [pl.BlockSpec(memory_space=pl.ANY)] * len(when),
+        out_specs=pl.BlockSpec((total, block), lambda j: (0, j)),
+        out_shape=jax.ShapeDtypeStruct((total, columns), jnp.bfloat16),
+        compiler_params=pltpu.CompilerParams(vmem_limit_bytes=56 * 2**20),
+        cost_estimate=pl.CostEstimate(flops=0, bytes_accessed=0, transcendentals=0),
+    )(left, right, *when)
+
+
+def qkv_grad_kernel(normed_ref, d_qkv_ref, gain_ref, out_ref):
+    columns = d_qkv_ref.shape[1]
+    out_ref[:, :columns] = dot_rows(normed_ref[...], d_qkv_ref[...]).astype(jnp.bfloat16)
+    rest = jnp.transpose(gain_ref[...])
+    fill = out_ref.shape[1] - columns - rest.shape[1]
+    if fill:
+        rest = jnp.concatenate([rest, jnp.zeros((rest.shape[0], fill), rest.dtype)], axis=1)
+    out_ref[:, columns:] = rest.astype(jnp.bfloat16)
+
+
+def qkv_grad_call(normed, d_qkv, gain_grads, columns):
+    total, width = normed.shape
+    block = 512
+    return pl.pallas_call(
+        qkv_grad_kernel,
+        grid=(width // block,),
+        in_specs=[
+            pl.BlockSpec((total, block), lambda i: (0, i)),
+            pl.BlockSpec(d_qkv.shape, lambda i: (0, 0)),
+            pl.BlockSpec((gain_grads.shape[0], block), lambda i: (0, i)),
+        ],
+        out_specs=pl.BlockSpec((block, columns), lambda i: (i, 0)),
+        out_shape=jax.ShapeDtypeStruct((width, columns), jnp.bfloat16),
+        compiler_params=pltpu.CompilerParams(vmem_limit_bytes=48 * 2**20),
+        cost_estimate=pl.CostEstimate(flops=0, bytes_accessed=0, transcendentals=0),
+    )(normed, d_qkv, gain_grads)
+
+
+def pieces_sp(value):
+    return [value] + [swap(value, turn) for turn in range(1, lax.axis_size("sp"))]
+
+
+def spread_kernel(layout, count, place_ref, *refs):
+    pieces, outs = refs[:count], refs[count:]
+    for place in range(count):
+
+        @pl.when(place_ref[0] == place)
+        def _():
+            for part in range(count):
+                for first, width, out, at, step in layout:
+                    goal = at + part * step
+                    outs[out][:, goal : goal + width] = pieces[place ^ part][:, first : first + width].astype(
+                        jnp.float32
+                    )
+
+
+def spread_call(place, pieces, layout, widths):
+    rows, columns = pieces[0].shape
+    block = rows // 5 if rows % 80 == 0 else rows
+    return pl.pallas_call(
+        functools.partial(spread_kernel, layout, len(pieces)),
+        grid=(rows // block,),
+        in_specs=[pl.BlockSpec(memory_space=pltpu.SMEM)]
+        + [pl.BlockSpec((block, columns), lambda i: (i, 0))] * len(pieces),
+        out_specs=[pl.BlockSpec((block, w), lambda i: (i, 0)) for w in widths],
+        out_shape=[jax.ShapeDtypeStruct((rows, w), jnp.float32) for w in widths],
+        compiler_params=pltpu.CompilerParams(vmem_limit_bytes=40 * 2**20),
+        cost_estimate=pl.CostEstimate(
+            flops=0, bytes_accessed=6 * len(pieces) * rows * columns, transcendentals=0
+        ),
+    )(place, *pieces)
+
+
+def stack_kernel(count, place_ref, *refs):
+    for turn in range(count):
+        refs[count][place_ref[0] ^ turn] = refs[turn][...].astype(jnp.float32)
+
+
+def stack_call(place, pieces):
+    rows, columns = pieces[0].shape
+    block = 32 if rows % 32 == 0 else rows
+    count = len(pieces)
+    return pl.pallas_call(
+        functools.partial(stack_kernel, count),
+        grid=(rows // block,),
+        in_specs=[pl.BlockSpec(memory_space=pltpu.SMEM)]
+        + [pl.BlockSpec((block, columns), lambda i: (i, 0))] * count,
+        out_specs=pl.BlockSpec((count, block, columns), lambda i: (0, i, 0)),
+        out_shape=jax.ShapeDtypeStruct((count, rows, columns), jnp.float32),
+        compiler_params=pltpu.CompilerParams(vmem_limit_bytes=40 * 2**20),
+        cost_estimate=pl.CostEstimate(flops=0, bytes_accessed=6 * count * rows * columns, transcendentals=0),
+    )(place, *pieces).reshape(count * rows, columns)
 
 
 def pass_kernel(*refs):
@@ -425,24 +721,22 @@
     extra = -qkv_cols % 128
     extra = extra if extra else 128
     gains = jnp.pad(jnp.stack([attn_gain, mlp_gain], axis=1), ((0, 0), (0, extra - 2)))
+    place = sp_place.reshape(1)
     came_tokens = deal(picked(tokens))
-    came_incoming = deal(after(picked(cotangent), came_tokens))
-    gate_up_shard = pack_call(sp_place.reshape(1), w_gate, w_up, came_tokens, groups, parts)
+    gate_up_shard = pack_call(place, w_gate, w_up, came_tokens, groups, parts)
     qkv_shard = jnp.concatenate(
         [column_share(w_query), column_share(key_weight), column_share(value_weight), gains], axis=1
     )
     qkv_all = gather_fsdp(qkv_shard)
     out_all = gather_fsdp(column_share(w_out))
     gate_up_all = gather_fsdp(gate_up_shard)
-    hidden_units = gate_up_all.shape[1] // 2
-    gate_all, up_all = gate_up_all[:, :hidden_units], gate_up_all[:, hidden_units:]
     down_all = gather_fsdp(lax.dynamic_slice_in_dim(w_down, sp_place * ff_share, ff_share, axis=0))
     qkv_weight = qkv_all[:, :qkv_cols]
     gain_one = qkv_all[:, qkv_cols].astype(wide)[None, :]
     gain_two = qkv_all[:, qkv_cols + 1].astype(wide)[None, :]
 
     group_inputs = gather_sp(in_place(came_tokens)).reshape(-1, width)
-    group_incoming = gather_sp(after(in_place(came_incoming), group_inputs)).reshape(-1, width)
+    came_incoming = deal(after(picked(cotangent), group_inputs))
     group_positions = gather_small(positions.reshape(-1)).reshape(-1)
     total = group_inputs.shape[0]
 
@@ -460,10 +754,6 @@
     def side_by_side(stacked):
         return jnp.concatenate([stacked[i] for i in range(parts)], axis=1)
 
-    def by_columns(matrix):
-        share = matrix.shape[1] // parts
-        return jnp.stack([matrix[:, i * share : (i + 1) * share] for i in range(parts)], axis=0)
-
     share = width // parts
 
     def own_columns(matrix):
@@ -473,84 +763,80 @@
     own_hidden = own_columns(group_inputs).astype(wide) + dot(mixed, out_all)
     hidden_low = side_by_side(gather_sp(own_hidden.astype(low)))
 
+    group_incoming = gather_sp(after(in_place(came_incoming), hidden_low)).reshape(-1, width)
+
     hidden = hidden_low.astype(wide)
     rms_two = lax.rsqrt(jnp.mean(hidden * hidden, axis=-1, keepdims=True) + eps)
     normed_two = (hidden * rms_two * gain_two).astype(low)
-    gate = dot(normed_two, gate_all)
-    upward = dot(normed_two, up_all)
-    active, active_back = jax.vjp(gated, gate, upward)
-    active_low = active.astype(low)
-    grad_down = dot_rows(active_low, group_incoming).astype(low)
+    active_low, gate, upward = gate_up_call(normed_two, gate_up_all)
+    grad_down = rows_call(active_low, group_incoming)
     down_all = after(down_all, grad_down)
-    d_active = dot_cols(group_incoming, down_all)
-    d_gate, d_up = active_back(d_active)
-    d_gate, d_up = d_gate.astype(low), d_up.astype(low)
-    d_hidden_units = jnp.concatenate([d_gate, d_up], axis=1)
-    d_normed_two = dot_cols(d_hidden_units, gate_up_all)
-    grad_gain_two = jnp.sum(d_normed_two * hidden * rms_two, axis=0)
-    scaled = gain_two * d_normed_two
-    back_two = rms_two * scaled - hidden * rms_two**3 * jnp.mean(scaled * hidden, axis=-1, keepdims=True)
-    back_two = back_two.astype(low)
-    d_hidden_units = after(d_hidden_units, back_two)
-    grad_gate = dot_rows(normed_two, d_hidden_units[:, :hidden_units]).astype(low)
-    grad_up = dot_rows(normed_two, d_hidden_units[:, hidden_units:]).astype(low)
-    own_d_hidden = own_columns(group_incoming).astype(wide) + scatter_sp(by_columns(back_two))
+    d_gate, d_up = unit_back_call(group_incoming, down_all, gate, upward)
+    grad_gate = rows_call(normed_two, d_gate)
+    back_two, grad_gain_two = mlp_back_call(
+        d_gate, d_up, gate_up_all, hidden_low, gain_two, parts, grad_gate
+    )
+    from_others, _ = scatter_sp(back_two)
+    grad_up = rows_call(normed_two, d_up, back_two)
+    own_d_hidden = own_columns(group_incoming).astype(wide) + from_others
     d_branch = own_d_hidden.astype(low)
-    grad_out = dot_rows(mixed, d_branch)
-    d_mixed = scatter_sp(by_columns(dot_cols(d_branch, out_all).astype(low))).astype(low)
-    result_part = after(dot(after(active_low, d_branch, grad_down), down_all).astype(low), d_mixed)
+    grad_up = after(grad_up, d_branch)
+    d_mixed, (sums_mixed, _) = scatter_sp(out_back_call(d_branch, out_all, parts, grad_up))
+    d_mixed = d_mixed.astype(low)
+    grad_out = rows_call(mixed, d_branch)
+    result_part = product_call(active_low, down_all, grad_out, *sums_mixed)
     own_hidden_rows = lax.dynamic_slice_in_dim(hidden_low, sp_place * rows, rows, axis=0)
-    result = own_hidden_rows.astype(wide) + scatter_sp(result_part.reshape(parts, rows, width))
-    layer_out = to_given(result.astype(low))
+    result_sum, (sums_result, _) = scatter_sp(after(result_part, d_mixed).reshape(parts, rows, width))
+    layer_out = to_given((own_hidden_rows.astype(wide) + result_sum).astype(low))
 
     d_qkv = attend_back_call(
         query_low, key_low, value_low, d_mixed, logs.T, start[None, :], cosine, sine
     )
-    grad_qkv = dot_rows(normed, d_qkv)
-    d_normed = dot_cols(d_qkv, qkv_weight)
-    inputs = group_inputs.astype(wide)
-    rms_one = lax.rsqrt(jnp.mean(inputs * inputs, axis=-1, keepdims=True) + eps)
-    grad_gain_one = jnp.sum(d_normed * inputs * rms_one, axis=0)
-    scaled_one = gain_one * d_normed
-    back_one = rms_one * scaled_one - inputs * rms_one**3 * jnp.mean(
-        scaled_one * inputs, axis=-1, keepdims=True
-    )
-    own_place = (jnp.arange(width, dtype=jnp.int32) // share == sp_place)[None, :]
-    spread = jnp.concatenate([own_d_hidden] * parts, axis=1)
-    back_one = back_one + jnp.where(own_place, spread, 0.0)
-    d_inputs = scatter_sp(back_one.astype(low).reshape(parts, rows, width))
+    back_one, grad_gain_one = attend_norm_call(
+        place, d_qkv, qkv_all, group_inputs, gain_one, own_d_hidden, parts, *sums_result
+    )
+    gain_grads = jnp.concatenate(
+        [grad_gain_one, grad_gain_two, jnp.zeros((6, width), wide)], axis=0
+    )
+    grad_qkv = qkv_grad_call(normed, d_qkv, gain_grads, qkv_all.shape[1])
+    d_inputs = scatter_sp(back_one.reshape(parts, rows, width))[0]
     input_grad = to_given(d_inputs.astype(low))
 
     def scatter_fsdp(matrix):
         return lax.psum_scatter(matrix.astype(low), "fsdp", scatter_dimension=0, tiled=True)
 
-    def all_sp(shard):
-        return lax.all_gather(shard, "sp", axis=0, tiled=False)
-
-    gain_grads = jnp.pad(
-        jnp.stack([grad_gain_one, grad_gain_two], axis=1), ((0, 0), (0, extra - 2))
-    )
     down_sum = scatter_fsdp(grad_down)
     gate_sum = scatter_fsdp(grad_gate)
     up_sum = scatter_fsdp(grad_up)
     out_sum = scatter_fsdp(grad_out)
-    qkv_sum = scatter_fsdp(jnp.concatenate([grad_qkv, gain_grads], axis=1))
-
-    down_parts = all_sp(down_sum)
-    gate_parts = all_sp(after(gate_sum, down_parts))
-    up_parts = all_sp(after(up_sum, gate_parts))
-    out_sum = after(out_sum, up_parts)
-    qkv_sum = after(qkv_sum, out_sum)
-    down_shard = down_parts.reshape(-1, width).astype(wide)
-    gate_shard = spread_call(gate_parts, groups)
-    up_shard = spread_call(up_parts, groups)
-    out_shard = side_by_side(gather_sp(out_sum)).astype(wide)
-    qkv_shards = gather_sp(qkv_sum).astype(wide)
-    edges = (0, query_cols, query_cols + key_cols, qkv_cols)
-    query_shard, key_shard, value_shard = (
-        side_by_side(qkv_shards[:, :, edges[i] : edges[i + 1]]) for i in range(3)
-    )
-    gain_shards = jnp.sum(qkv_shards[:, :, qkv_cols : qkv_cols + 2], axis=0)
+    qkv_sum = scatter_fsdp(grad_qkv)
+
+    down_pieces = pieces_sp(down_sum)
+    gate_pieces = pieces_sp(after(gate_sum, *down_pieces[1:]))
+    up_pieces = pieces_sp(after(up_sum, *gate_pieces[1:]))
+    out_pieces = pieces_sp(after(out_sum, *up_pieces[1:]))
+    qkv_pieces = pieces_sp(after(qkv_sum, *out_pieces[1:]))
+
+    down_shard = stack_call(place, down_pieces)
+    hidden_layout = [
+        (j * ff_share, ff_share, 0, j * parts * ff_share, ff_share) for j in range(groups)
+    ]
+    (gate_shard,) = spread_call(place, gate_pieces, hidden_layout, [w_gate.shape[1]])
+    (up_shard,) = spread_call(place, up_pieces, hidden_layout, [w_up.shape[1]])
+    (out_shard,) = spread_call(place, out_pieces, [(0, share, 0, 0, share)], [width])
+    qkv_layout = [
+        (0, query_cols, 0, 0, query_cols),
+        (query_cols, key_cols, 1, 0, key_cols),
+        (query_cols + key_cols, key_cols, 2, 0, key_cols),
+        (qkv_cols, 2, 3, 0, 2),
+    ]
+    query_shard, key_shard, value_shard, gain_parts = spread_call(
+        place,
+        qkv_pieces,
+        qkv_layout,
+        [w_query.shape[1], key_weight.shape[1], value_weight.shape[1], 2 * parts],
+    )
+    gain_shards = jnp.sum(gain_parts.reshape(-1, parts, 2), axis=1)
     return (
         layer_out,
         input_grad,

time: 1390 us -> 1240 us (0.89)
  Pallas kernels: 112 us -> 370 us
  matrix products: 253 us -> 9.9 us
  blocking collectives: 151 us -> 82.7 us
  waiting for transfers between devices: 531 us -> 463 us
  other arithmetic: 134 us -> 77 us
  starting transfers between devices: 63.8 us -> 109 us
  local copies, waits for them, and re-layouts: 119 us -> 104 us
    pallas_call x2 -> x16, Pallas kernels: 9.72 us -> 268 us  [the longest x4 77.2 us: rows_call(): pl.pallas_call(rows_kernel, grid=(columns // block,), in_specs=[pl.BlockS...]
    dot_general x9 -> x0, matrix products: 179 us -> none  [the longest x4 92.1 us: dot_cols(): lax.dot_general(left, right, (((1,), (1,)), ((), ())), preferred_element_...]
    all_to_all x1 -> x0, blocking collectives: 67.2 us -> none  [to_given(): lax.all_to_all(blocks, 'fsdp', split_axis=0, concat_axis=0, tiled=True)]
    dot_general x4 -> x1, matrix products: 73.8 us -> 9.9 us  [dot(): return jnp.dot(left, right, preferred_element_type=jnp.float32)]
    all_gather x3 -> x0, waiting for transfers between devices: 57.8 us -> none  [all_sp(): return lax.all_gather(shard, 'sp', axis=0, tiled=False)]
    all_to_all x1 -> x2, starting transfers between devices: 6.28 us -> 43.8 us  [to_given(): lax.all_to_all(blocks, 'fsdp', split_axis=0, concat_axis=0, tiled=True)]
    convert_element_type x10 -> x6, other arithmetic: 45.5 us -> 18.5 us  [the longest x1 8.29 us: local(): normed_two = (hidden * rms_two * gain_two).astype(low)]
    all_to_all x1, waiting for transfers between devices: 49.2 us -> 29.1 us  [deal(): lax.all_to_all(blocks, 'fsdp', split_axis=0, concat_axis=0, tiled=True)]
  transfers between devices with their start and end apart: 77 -> 78, of which waited for: 32 -> 33; matrix products, arithmetic and copies ran while one was open for 34% -> 14% of each run, Pallas kernels for 8% -> 30%
where the time goes in v4:
time: 1240 us; the launch traced here: 1230 us
  waiting for transfers between devices  463 us (37%)
  Pallas kernels  370 us (30%)
  starting transfers between devices  109 us (9%)
  local copies, waits for them, and re-layouts  104 us (8%)
  blocking collectives  82.7 us (7%)
  other arithmetic  77 us (6%)
  between operations  15.4 us (1%)
    ppermute x66, waiting for transfers between devices, swap(): return lax.ppermute(value, 'sp', [(i, i ^ bit) for i in range(size)])  378 us
    all_to_all x1, blocking collectives, deal(): lax.all_to_all(blocks, 'fsdp', split_axis=0, concat_axis=0, tiled=True)  82.7 us
    pallas_call x4, Pallas kernels, rows_call(): pl.pallas_call(rows_kernel, grid=(columns // block,), in_specs=[pl.BlockS...  77.2 us
    all_to_all x2, waiting for transfers between devices, to_given(): lax.all_to_all(blocks, 'fsdp', split_axis=0, concat_axis=0, tiled=True)  56 us
    ppermute x66, starting transfers between devices, swap(): return lax.ppermute(value, 'sp', [(i, i ^ bit) for i in range(size)])  55.2 us
    pallas_call x1, Pallas kernels, attend_back_call(): pl.pallas_call(functools.partial(attend_back_kernel, heads, keys, block),...  50.1 us
    pallas_call x1, Pallas kernels, mlp_back_call(): pl.pallas_call(mlp_back_kernel, grid=(total // block,), in_specs=[row(uni...  43.9 us
    all_to_all x2, starting transfers between devices, to_given(): lax.all_to_all(blocks, 'fsdp', split_axis=0, concat_axis=0, tiled=True)  43.8 us
  transfers between devices with their start and end apart: 78, of which 33 were waited for; matrix products, arithmetic and copies ran while one was open for 14% of the time, Pallas kernels for 30%

profile of v4, /device:TPU:9, one launch (start us, length us, event | category | flops | bytes accessed | tf_op | source)
XLA Modules:
  0.0 1231.2 jit_solution(3293735365923746085)
XLA Ops:
  25.7 82.7 %all_to_all.20._ = bf16[8,48,2560]{2,1,0:T(8,128)(2,1)S(1)} all-to-all(bf16[8,48,2560]{2,1,0:T(8,128)(2,1)S(1)} %get-tuple-element.113), channel_id=1, replica_groups=mesh['sp'=4,'fsdp'=8] {'fsdp'}, dimensions={0} | all-to-all | bytes 3932160 | tf_op jit(solution)/shard_map/all_to_all | solution.py:698
  148.0 18.8 %collective-permute-done.1 = bf16[192,2560]{1,0:T(8,128)(2,1)S(1)} collective-permute-done((bf16[192,2560]{1,0:T(8,128)(2,1)}, bf16[192,2560]{1,0:T(8,128)(2,1)S(1)}, u32[]{:S(2)}, u32[]{:S(2)}) %collective-permute-start.1) | collective-permute-done | bytes 983072 | tf_op jit(solution)/shard_map/ppermute | solution.py:23
  169.9 18.8 %collective-permute-done.4 = bf16[192,2560]{1,0:T(8,128)(2,1)S(1)} collective-permute-done((bf16[192,2560]{1,0:T(8,128)(2,1)S(1)}, bf16[192,2560]{1,0:T(8,128)(2,1)S(1)}, u32[]{:S(2)}, u32[]{:S(2)}) %collective-permute-start.4) | collective-permute-done | bytes 983072 | tf_op jit(solution)/shard_map/ppermute | solution.py:23
  205.8 23.5 %shard_map.221 = (bf16[1536,2560]{1,0:T(8,128)(2,1)}, bf16[1536,1024]{1,0:T(8,128)(2,1)}, bf16[1536,256]{1,0:T(8,128)(2,1)S(1)}, bf16[1536,256]{1,0:T(8,128)(2,1)S(1)}) custom-call(bf16[1536,2560]{1,0:T(8,128)(2,1)} %bitcast.13.x_ref.refs_1_, f32[1,2560]{1,0:T(1,128)S(1)} %reshape.228.gain_ref, bf16[2560,1024]{1,0:T(8,128)(2,1)} %all-gather.5.cloned.1.call-done.weight_ref, ...), custom_call_target="tpu_custom_call" | custom-call | flops 8053063680 | bytes 20971520 | tf_op jit(solution)/shard_map/pallas_call | solution.py:154
  231.2 27.8 %shard_map.222 = (bf16[1536,640]{1,0:T(8,128)(2,1)}, f32[1536,8]{1,0:T(8,128)}) custom-call(bf16[1536,1024]{1,0:T(8,128)(2,1)} %get-tuple-element.31.q_ref, bf16[1536,256]{1,0:T(8,128)(2,1)} %copy-done.35, bf16[1536,256]{1,0:T(8,128)(2,1)} %copy-done.36, s32[1536,1]{1,0:T(8,128)} %broadcast_in_dim.263.start_ref), custom_call_target="tpu_custom_call" | custom-call | flops 9663676416 | bytes 8388608 | tf_op jit(solution)/shard_map/pallas_call | solution.py:201
  266.9 29.1 %all-to-all-done.1 = bf16[8,48,2560]{2,1,0:T(8,128)(2,1)} async-done(((bf16[8,48,2560]{2,1,0:T(8,128)(2,1)}), bf16[8,48,2560]{2,1,0:T(8,128)(2,1)}, u32[]{:S(2)}, u32[]{:S(2)}) %all-to-all-start.1) | async-done | bytes 1966112 | tf_op jit(solution)/shard_map/all_to_all | solution.py:698
  321.9 20.6 %collective-permute-done.13 = bf16[768,640]{1,0:T(8,128)(2,1)S(1)} collective-permute-done((bf16[768,640]{1,0:T(8,128)(2,1)}, bf16[768,640]{1,0:T(8,128)(2,1)S(1)}, u32[]{:S(2)}, u32[]{:S(2)}) %collective-permute-start.13) | collective-permute-done | bytes 983072 | tf_op jit(solution)/shard_map/ppermute | solution.py:23
  362.7 37.8 %collective-permute-done.15 = bf16[768,640]{1,0:T(8,128)(2,1)S(1)} collective-permute-done((bf16[768,640]{1,0:T(8,128)(2,1)S(1)}, bf16[768,640]{1,0:T(8,128)(2,1)S(1)}, u32[]{:S(2)}, u32[]{:S(2)}) %collective-permute-start.15) | collective-permute-done | bytes 983072 | tf_op jit(solution)/shard_map/ppermute | solution.py:23
  451.6 20.0 %collective-permute-done.24 = bf16[192,2560]{1,0:T(8,128)(2,1)S(1)} collective-permute-done((bf16[192,2560]{1,0:T(8,128)(2,1)S(1)}, bf16[192,2560]{1,0:T(8,128)(2,1)S(1)}, u32[]{:S(2)}, u32[]{:S(2)}) %collective-permute-start.24) | collective-permute-done | bytes 983072 | tf_op jit(solution)/shard_map/ppermute | solution.py:23
  494.8 36.8 %shard_map.224 = (bf16[1536,1792]{1,0:T(8,128)(2,1)}, bf16[1536,1792]{1,0:T(8,128)(2,1)}, bf16[1536,1792]{1,0:T(8,128)(2,1)}) custom-call(bf16[1536,2560]{1,0:T(8,128)(2,1)} %fusion.2.x_ref.left_ref, bf16[2560,3584]{1,0:T(8,128)(2,1)} %all-gather.9.cloned.1.call-done.gate_weight_ref.up_weight_ref.weight_ref, ...), custom_call_target="tpu_custom_call" | custom-call | flops 28185722880 | bytes 47185920 | tf_op jit(solution)/shard_map/pallas_call | solution.py:303
  531.6 20.3 %shard_map.227.refs_1_ = bf16[1792,2560]{1,0:T(8,128)(2,1)} custom-call(bf16[1536,1792]{1,0:T(8,128)(2,1)} %get-tuple-element.35.left_ref, bf16[1536,2560]{1,0:T(8,128)(2,1)} %bitcast.52.right_ref.incoming_ref), custom_call_target="tpu_custom_call" | custom-call | tf_op jit(solution)/shard_map/pallas_call | solution.py:485
  552.0 25.6 %shard_map.229 = (bf16[1536,1792]{1,0:T(8,128)(2,1)}, bf16[1536,1792]{1,0:T(8,128)(2,1)}) custom-call(bf16[1536,2560]{1,0:T(8,128)(2,1)} %bitcast.52.right_ref.incoming_ref, bf16[1792,2560]{1,0:T(8,128)(2,1)} %shard_map.228.down_ref.right_ref, bf16[1536,1792]{1,0:T(8,128)(2,1)} %get-tuple-element.36.gate_ref, bf16[1536,1792]{1,0:T(8,128)(2,1)} %get-tuple-element.37.up_ref), custom_call_target="tpu_custom_call" | custom-call | flops 14092861440 | bytes 41943040 | tf_op jit(solution)/shard_map/pallas_call | solution.py:334
  577.6 20.5 %shard_map.230.refs_0_ = bf16[2560,1792]{1,0:T(8,128)(2,1)} custom-call(bf16[1536,2560]{1,0:T(8,128)(2,1)} %fusion.2.x_ref.left_ref, bf16[1536,1792]{1,0:T(8,128)(2,1)} %get-tuple-element.38.right_ref.d_gate_ref), custom_call_target="tpu_custom_call" | custom-call | tf_op jit(solution)/shard_map/pallas_call | solution.py:485
  598.8 43.9 %shard_map.231 = (bf16[4,1536,640]{2,1,0:T(8,128)(2,1)}, f32[1,2560]{1,0:T(1,128)}) custom-call(bf16[1536,1792]{1,0:T(8,128)(2,1)} %get-tuple-element.38.right_ref.d_gate_ref, bf16[1536,1792]{1,0:T(8,128)(2,1)} %get-tuple-element.39.d_up_ref.right_ref, bf16[2560,3584]{1,0:T(8,128)(2,1)} %all-gather.9.cloned.1.call-done.gate_weight_ref.up_weight_ref.weight_ref, ...), custom_call_target="tpu_custom_call" | custom-call | flops 28185722880 | bytes 47185920 | tf_op jit(solution)/shard_map/pallas_call | solution.py:388
  688.0 20.7 %shard_map.233.refs_0_ = bf16[2560,1792]{1,0:T(8,128)(2,1)} custom-call(bf16[1536,2560]{1,0:T(8,128)(2,1)} %fusion.2.x_ref.left_ref, bf16[1536,1792]{1,0:T(8,128)(2,1)} %get-tuple-element.39.d_up_ref.right_ref, bf16[4,1536,640]{2,1,0:T(8,128)(2,1)} %get-tuple-element.40.refs_0_), custom_call_target="tpu_custom_call" | custom-call | tf_op jit(solution)/shard_map/pallas_call | solution.py:485
  764.2 20.1 %shard_map.236.refs_0_ = bf16[1536,2560]{1,0:T(8,128)(2,1)} custom-call(bf16[1536,1792]{1,0:T(8,128)(2,1)} %get-tuple-element.35.left_ref, bf16[1792,2560]{1,0:T(8,128)(2,1)} %shard_map.228.down_ref.right_ref, bf16[2560,640]{1,0:T(8,128)(2,1)} %shard_map.232.refs_0_, bf16[768,640]{1,0:T(8,128)(2,1)} %copy-done.42, bf16[768,640]{1,0:T(8,128)(2,1)} %copy-done.41), custom_call_target="tpu_custom_call" | custom-call | tf_op jit(solution)/shard_map/pallas_call | solution.py:510
  812.2 50.1 %shard_map.238.d_qkv_ref = bf16[1536,960]{1,0:T(8,128)(2,1)} custom-call(bf16[1536,1024]{1,0:T(8,128)(2,1)} %get-tuple-element.31.q_ref, bf16[1536,256]{1,0:T(8,128)(2,1)} %copy-done.35, bf16[1536,256]{1,0:T(8,128)(2,1)} %copy-done.36, bf16[1536,640]{1,0:T(8,128)(2,1)} %pad_maximum_fusion.2.refs_1_.grad_ref, f32[8,1536]{1,0:T(8,128)} %bitcast.214, ...), custom_call_target="tpu_custom_call" | custom-call | flops 19327352832000 | bytes 12582912 | tf_op jit(solution)/shard_map/pallas_call | solution.py:270
  866.9 20.5 %shard_map.239 = (bf16[1536,2560]{1,0:T(8,128)(2,1)}, f32[1,2560]{1,0:T(1,128)}) custom-call(s32[1]{0:T(128)} %bitcast.41.place_ref, bf16[1536,960]{1,0:T(8,128)(2,1)} %shard_map.238.d_qkv_ref, bf16[2560,1024]{1,0:T(8,128)(2,1)} %all-gather.5.cloned.1.call-done.weight_ref, bf16[1536,2560]{1,0:T(8,128)(2,1)} %bitcast.13.x_ref.refs_1_, f32[1,2560]{1,0:T(1,128)} %copy-done.34, ...), custom_call_target="tpu_custom_call" | custom-call | flops 7549747200 | bytes 31457280 | tf_op jit(solution)/shard_map/pallas_call | solution.py:429
  965.5 35.3 %all-to-all-start.3 = ((bf16[8,48,2560]{2,1,0:T(8,128)(2,1)}), bf16[8,48,2560]{2,1,0:T(8,128)(2,1)}, u32[]{:S(2)}, u32[]{:S(2)}) async-start(bf16[8,48,2560]{2,1,0:T(8,128)(2,1)} %get-tuple-element.110), calls=%async_computation.3 | async-start | bytes 3932160 | tf_op jit(solution)/shard_map/all_to_all | solution.py:705
  1003.5 56.0 %all-to-all-done.3 = bf16[8,48,2560]{2,1,0:T(8,128)(2,1)} async-done(((bf16[8,48,2560]{2,1,0:T(8,128)(2,1)}), bf16[8,48,2560]{2,1,0:T(8,128)(2,1)}, u32[]{:S(2)}, u32[]{:S(2)}) %all-to-all-start.3) | async-done | bytes 1966112 | tf_op jit(solution)/shard_map/all_to_all | solution.py:705
  1072.0 24.2 %collective-permute-done.54.refs_1_ = bf16[320,1792]{1,0:T(8,128)(2,1)S(1)} collective-permute-done((bf16[320,1792]{1,0:T(8,128)(2,1)}, bf16[320,1792]{1,0:T(8,128)(2,1)S(1)}, u32[]{:S(2)}, u32[]{:S(2)}) %collective-permute-start.54) | collective-permute-done | bytes 1146912 | tf_op jit(solution)/shard_map/ppermute | solution.py:23
  1097.0 24.7 %collective-permute-done.56.refs_3_ = bf16[320,1792]{1,0:T(8,128)(2,1)} collective-permute-done((bf16[320,1792]{1,0:T(8,128)(2,1)}, bf16[320,1792]{1,0:T(8,128)(2,1)}, u32[]{:S(2)}, u32[]{:S(2)}) %collective-permute-start.56) | collective-permute-done | bytes 1146912 | tf_op jit(solution)/shard_map/ppermute | solution.py:23
  1124.4 22.2 %collective-permute-done.57.refs_1_ = bf16[320,1792]{1,0:T(8,128)(2,1)S(1)} collective-permute-done((bf16[320,1792]{1,0:T(8,128)(2,1)}, bf16[320,1792]{1,0:T(8,128)(2,1)S(1)}, u32[]{:S(2)}, u32[]{:S(2)}) %collective-permute-start.57) | collective-permute-done | bytes 1146912 | tf_op jit(solution)/shard_map/ppermute | solution.py:23
  1151.2 19.9 %collective-permute-done.59.refs_3_ = bf16[320,1792]{1,0:T(8,128)(2,1)} collective-permute-done((bf16[320,1792]{1,0:T(8,128)(2,1)}, bf16[320,1792]{1,0:T(8,128)(2,1)}, u32[]{:S(2)}, u32[]{:S(2)}) %collective-permute-start.59) | collective-permute-done | bytes 1146912 | tf_op jit(solution)/shard_map/ppermute | solution.py:23
  (420 shorter events, 496.0 us)
Async XLA Ops:
  7.2 195.9 %all-gather.5.cloned.1.call-start = ((), (), s32[]{:S(2)}) async-start(), calls=%async_computation.9 | async-start | bytes 5898240 | tf_op jit(solution)/shard_map/all_gather | solution.py:713
  12.2 334.9 %all-gather.7.cloned.1.call-start = ((), (), s32[]{:S(2)}) async-start(), calls=%async_computation.10 | async-start | bytes 3686400 | tf_op jit(solution)/shard_map/all_gather | solution.py:713
  14.1 480.6 %all-gather.9.cloned.1.call-start = ((), (), s32[]{:S(2)}) async-start(), calls=%async_computation.11 | async-start | bytes 20643840 | tf_op jit(solution)/shard_map/all_gather | solution.py:713
  146.5 43.3 %collective-permute-start.5 = (bf16[192,2560]{1,0:T(8,128)(2,1)S(1)}, bf16[192,2560]{1,0:T(8,128)(2,1)S(1)}, u32[]{:S(2)}, u32[]{:S(2)}) collective-permute-start(bf16[192,2560]{1,0:T(8,128)(2,1)S(1)} %collective-permute-done.3), channel_id=1, source_target_pairs={{0,8},{8,0},{16,24},{24,16},{1,9},{9,1},{17,25},{25,17},{2,10},{10... | collective-permute-start | bytes 2949128 | tf_op jit(solution)/shard_map/ppermute | solution.py:23
  190.8 105.2 %all-to-all-start.1 = ((bf16[8,48,2560]{2,1,0:T(8,128)(2,1)}), bf16[8,48,2560]{2,1,0:T(8,128)(2,1)}, u32[]{:S(2)}, u32[]{:S(2)}) async-start(bf16[8,48,2560]{2,1,0:T(8,128)(2,1)} %shard_map.225), calls=%async_computation.1 | async-start | bytes 3932160 | tf_op jit(solution)/shard_map/all_to_all | solution.py:698
  199.5 352.5 %all-gather.11.cloned.1.call-start = ((), (), s32[]{:S(2)}) async-start(), calls=%async_computation.12 | async-start | bytes 10321920 | tf_op jit(solution)/shard_map/all_gather | solution.py:713
  266.7 734.1 %reduce-scatter.14.cloned.1.call-start = ((), (), s32[]{:S(2)}) async-start(), calls=%async_computation.17 | async-start | bytes 10321920 | tf_op jit(solution)/shard_map/reduce_scatter | solution.py:806
  357.2 45.9 %collective-permute-start.16 = (bf16[768,640]{1,0:T(8,128)(2,1)S(1)}, bf16[768,640]{1,0:T(8,128)(2,1)S(1)}, u32[]{:S(2)}, u32[]{:S(2)}) collective-permute-start(bf16[768,640]{1,0:T(8,128)(2,1)S(1)} %get-tuple-element.96), channel_id=1, source_target_pairs={{0,8},{8,0},{16,24},{24,16},{1,9},{9,1},{17,25},{25,17},{2,10},{10... | collective-permute-start | bytes 2949128 | tf_op jit(solution)/shard_map/ppermute | solution.py:23
  551.9 516.0 %reduce-scatter.12.cloned.1.call-start = ((), (), s32[]{:S(2)}) async-start(), calls=%async_computation.16 | async-start | bytes 10321920 | tf_op jit(solution)/shard_map/reduce_scatter | solution.py:806
  598.2 523.5 %reduce-scatter.10.cloned.1.call-start = ((), (), s32[]{:S(2)}) async-start(), calls=%async_computation.15 | async-start | bytes 10321920 | tf_op jit(solution)/shard_map/reduce_scatter | solution.py:806
  714.9 409.5 %reduce-scatter.8.cloned.1.call-start = ((), (), s32[]{:S(2)}) async-start(), calls=%async_computation.14 | async-start | bytes 3686400 | tf_op jit(solution)/shard_map/reduce_scatter | solution.py:806
  733.3 51.0 %collective-permute-start.35 = (bf16[768,640]{1,0:T(8,128)(2,1)}, bf16[768,640]{1,0:T(8,128)(2,1)S(1)}, u32[]{:S(2)}, u32[]{:S(2)}) collective-permute-start(bf16[768,640]{1,0:T(8,128)(2,1)} %get-tuple-element.74), channel_id=1, source_target_pairs={{0,8},{8,0},{16,24},{24,16},{1,9},{9,1},{17,25},{25,17},{2,10},{10... | collective-permute-start | bytes 2949128 | tf_op jit(solution)/shard_map/ppermute | solution.py:23
  733.8 50.5 %collective-permute-start.38 = (bf16[768,640]{1,0:T(8,128)(2,1)}, bf16[768,640]{1,0:T(8,128)(2,1)}, u32[]{:S(2)}, u32[]{:S(2)}) collective-permute-start(bf16[768,640]{1,0:T(8,128)(2,1)} %get-tuple-element.77), channel_id=1, source_target_pairs={{0,16},{8,24},{16,0},{24,8},{1,17},{9,25},{17,1},{25,9},{2,18},{10... | collective-permute-start | bytes 2949128 | tf_op jit(solution)/shard_map/ppermute | solution.py:23
  794.3 387.3 %reduce-scatter.6.cloned.1.call-start = ((), (), s32[]{:S(2)}) async-start(), calls=%async_computation.13 | async-start | bytes 5898240 | tf_op jit(solution)/shard_map/reduce_scatter | solution.py:806
  794.5 67.7 %collective-permute-start.39 = (bf16[192,2560]{1,0:T(8,128)(2,1)}, bf16[192,2560]{1,0:T(8,128)(2,1)}, u32[]{:S(2)}, u32[]{:S(2)}) collective-permute-start(bf16[192,2560]{1,0:T(8,128)(2,1)} %get-tuple-element.68), channel_id=1, source_target_pairs={{0,8},{8,0},{16,24},{24,16},{1,9},{9,1},{17,25},{25,17},{2,10},{10... | collective-permute-start | bytes 2949128 | tf_op jit(solution)/shard_map/ppermute | solution.py:23
  796.1 66.2 %collective-permute-start.42 = (bf16[192,2560]{1,0:T(8,128)(2,1)}, bf16[192,2560]{1,0:T(8,128)(2,1)}, u32[]{:S(2)}, u32[]{:S(2)}) collective-permute-start(bf16[192,2560]{1,0:T(8,128)(2,1)} %get-tuple-element.69), channel_id=1, source_target_pairs={{0,16},{8,24},{16,0},{24,8},{1,17},{9,25},{17,1},{25,9},{2,18},{10... | collective-permute-start | bytes 2949128 | tf_op jit(solution)/shard_map/ppermute | solution.py:23
  811.2 51.0 %collective-permute-start.41 = (bf16[192,2560]{1,0:T(8,128)(2,1)}, bf16[192,2560]{1,0:T(8,128)(2,1)}, u32[]{:S(2)}, u32[]{:S(2)}) collective-permute-start(bf16[192,2560]{1,0:T(8,128)(2,1)} %fusion.12.refs_0_), channel_id=1, source_target_pairs={{0,16},{8,24},{16,0},{24,8},{1,17},{9,25},{17,1},{25,9},{2,18},{10... | collective-permute-start | bytes 2949128 | tf_op jit(solution)/shard_map/ppermute | solution.py:23
  965.5 94.0 %all-to-all-start.3 = ((bf16[8,48,2560]{2,1,0:T(8,128)(2,1)}), bf16[8,48,2560]{2,1,0:T(8,128)(2,1)}, u32[]{:S(2)}, u32[]{:S(2)}) async-start(bf16[8,48,2560]{2,1,0:T(8,128)(2,1)} %get-tuple-element.110), calls=%async_computation.3 | async-start | bytes 3932160 | tf_op jit(solution)/shard_map/all_to_all | solution.py:705
  1000.8 67.1 %collective-permute-start.51 = (bf16[224,2560]{1,0:T(8,128)(2,1)}, bf16[224,2560]{1,0:T(8,128)(2,1)S(1)}, u32[]{:S(2)}, u32[]{:S(2)}) collective-permute-start(bf16[224,2560]{1,0:T(8,128)(2,1)} %reduce-scatter.14.cloned.1.call-done.refs_0_), channel_id=1, source_target_pairs={{0,8},{8,0},{16,24},{24,16},{1,9},{9,1},{17,25},{25,17},{2,10},{10... | collective-permute-start | bytes 3440648 | tf_op jit(solution)/shard_map/ppermute | solution.py:23
  1001.3 66.7 %collective-permute-start.52 = (bf16[224,2560]{1,0:T(8,128)(2,1)}, bf16[224,2560]{1,0:T(8,128)(2,1)S(1)}, u32[]{:S(2)}, u32[]{:S(2)}) collective-permute-start(bf16[224,2560]{1,0:T(8,128)(2,1)} %reduce-scatter.14.cloned.1.call-done.refs_0_), channel_id=1, source_target_pairs={{0,16},{8,24},{16,0},{24,8},{1,17},{9,25},{17,1},{25,9},{2,18},{10... | collective-permute-start | bytes 3440648 | tf_op jit(solution)/shard_map/ppermute | solution.py:23
  1002.4 65.5 %collective-permute-start.53 = (bf16[224,2560]{1,0:T(8,128)(2,1)}, bf16[224,2560]{1,0:T(8,128)(2,1)}, u32[]{:S(2)}, u32[]{:S(2)}) collective-permute-start(bf16[224,2560]{1,0:T(8,128)(2,1)} %reduce-scatter.14.cloned.1.call-done.refs_0_), channel_id=1, source_target_pairs={{0,24},{8,16},{16,8},{24,0},{1,25},{9,17},{17,9},{25,1},{2,26},{10... | collective-permute-start | bytes 3440648 | tf_op jit(solution)/shard_map/ppermute | solution.py:23
  1059.5 118.6 %all-to-all-start.2 = ((bf16[8,48,2560]{2,1,0:T(8,128)(2,1)}), bf16[8,48,2560]{2,1,0:T(8,128)(2,1)}, u32[]{:S(2)}, u32[]{:S(2)}) async-start(bf16[8,48,2560]{2,1,0:T(8,128)(2,1)} %get-tuple-element.111), calls=%async_computation.2 | async-start | bytes 3932160 | tf_op jit(solution)/shard_map/all_to_all | solution.py:705
  1071.7 50.0 %collective-permute-start.56 = (bf16[320,1792]{1,0:T(8,128)(2,1)}, bf16[320,1792]{1,0:T(8,128)(2,1)}, u32[]{:S(2)}, u32[]{:S(2)}) collective-permute-start(bf16[320,1792]{1,0:T(8,128)(2,1)} %shard_map.241.refs_0_), channel_id=1, source_target_pairs={{0,24},{8,16},{16,8},{24,0},{1,25},{9,17},{17,9},{25,1},{2,26},{10... | collective-permute-start | bytes 3440648 | tf_op jit(solution)/shard_map/ppermute | solution.py:23
  1123.2 47.9 %collective-permute-start.59 = (bf16[320,1792]{1,0:T(8,128)(2,1)}, bf16[320,1792]{1,0:T(8,128)(2,1)}, u32[]{:S(2)}, u32[]{:S(2)}) collective-permute-start(bf16[320,1792]{1,0:T(8,128)(2,1)} %shard_map.242.refs_0_), channel_id=1, source_target_pairs={{0,24},{8,16},{16,8},{24,0},{1,25},{9,17},{17,9},{25,1},{2,26},{10... | collective-permute-start | bytes 3440648 | tf_op jit(solution)/shard_map/ppermute | solution.py:23
  (112 other events, 2317.6 us)
Sparse Core Ops, SparseCore 0:
  12.4 90.0 all-gather.4
  104.7 42.3 all-gather.6
  149.3 199.8 all-gather.8
  350.7 89.8 all-gather.10
  552.0 100.4 reduce-scatter.13
  655.2 95.3 reduce-scatter.11
  753.6 95.6 reduce-scatter.9
  852.2 39.3 reduce-scatter.7
  923.1 134.1 reduce-scatter.5

commit v5 on v4

--- a/solution.py
+++ b/solution.py
@@ -27,10 +27,11 @@
     return with_layout_constraint(value, Layout(major_to_minor=tuple(range(value.ndim))))
 
 
-def gather_sp(value):
+def gather_sp(value, *hold):
     size = lax.axis_size("sp")
     if size != 4:
-        return lax.all_gather(value, "sp", axis=0, tiled=False)
+        whole = lax.all_gather(value, "sp", axis=0, tiled=False)
+        return whole, (whole,)
     place = lax.axis_index("sp")
     half = value.shape[0] // 2
     first, second = value[:half], value[half:]
@@ -38,6 +39,8 @@
     x_second, y_first = swap(second, 1), swap(first, 2)
     far_first, far_second = swap(x_first, 2), swap(y_second, 1)
     out = jnp.zeros((size,) + value.shape, value.dtype)
+    if hold:
+        out = after(out, *hold)
     zeros = (0,) * (value.ndim - 1)
     for turn, low, high in (
         (0, first, second),
@@ -47,7 +50,11 @@
     ):
         out = lax.dynamic_update_slice(out, low[None], (place ^ turn, 0) + zeros)
         out = lax.dynamic_update_slice(out, high[None], (place ^ turn, half) + zeros)
-    return row_major(out)
+    return row_major(out), (x_first, y_second)
+
+
+def rows_of(blocks, picks):
+    return blocks.at[picks].get(mode="promise_in_bounds")
 
 
 def gather_small(value):
@@ -62,7 +69,7 @@
     return jnp.stack(here, axis=0)
 
 
-def scatter_sp(parts):
+def scatter_sp(parts, *hold):
     size = lax.axis_size("sp")
     if size != 4:
         summed = lax.psum_scatter(parts, "sp", scatter_dimension=0, tiled=False)
@@ -78,6 +85,8 @@
     wide = jnp.float32
     low = parts.dtype
     from_x, from_y = swap(block(3, True), 1), swap(block(3, False), 2)
+    if hold:
+        from_x = after(from_x, *hold)
     x_first, y_second = swap(block(1, True), 1), swap(block(2, False), 2)
     y_sent = (block(2, True).astype(wide) + from_x.astype(wide)).astype(low)
     x_sent = (block(1, False).astype(wide) + from_y.astype(wide)).astype(low)
@@ -164,12 +173,13 @@
         ],
         compiler_params=pltpu.CompilerParams(vmem_limit_bytes=48 * 2**20),
         cost_estimate=pl.CostEstimate(
-            flops=2 * total * width * weight.shape[1], bytes_accessed=20 * 2**20, transcendentals=0
+            flops=72 * 10**9, bytes_accessed=0, transcendentals=0
         ),
     )(x, gain, weight, cosine, sine)
 
 
-def attend_kernel(heads, keys, block, q_ref, k_ref, v_ref, start_ref, mixed_ref, lse_ref, bias_ref):
+def attend_kernel(heads, keys, block, q_ref, k_ref, v_ref, start_ref, *refs):
+    mixed_ref, lse_ref, bias_ref = refs[-3:]
     total = q_ref.shape[0]
     group = heads // keys
     factor = HEAD_SIZE**-0.5 * log2e
@@ -195,11 +205,14 @@
             lse_ref[first:stop, head : head + 1] = top + jnp.log2(summed)
 
 
-def attend_call(q, k, v, start, block=256):
+def attend_call(q, k, v, start, *when):
+    block = 256
     total = q.shape[0]
     heads, keys = q.shape[1] // LANES, k.shape[1] // LANES
     return pl.pallas_call(
         functools.partial(attend_kernel, heads, keys, block),
+        in_specs=[pl.BlockSpec(memory_space=pltpu.VMEM)] * 4
+        + [pl.BlockSpec(memory_space=pl.ANY)] * len(when),
         out_shape=[
             jax.ShapeDtypeStruct((total, heads * HEAD_SIZE), jnp.bfloat16),
             jax.ShapeDtypeStruct((total, heads), jnp.float32),
@@ -207,14 +220,15 @@
         scratch_shapes=[pltpu.VMEM((block, total), jnp.float32)],
         compiler_params=pltpu.CompilerParams(vmem_limit_bytes=56 * 2**20),
         cost_estimate=pl.CostEstimate(
-            flops=heads * total * total * 512, bytes_accessed=8 * 2**20, transcendentals=heads * total * total // 2
+            flops=84 * 10**9, bytes_accessed=0, transcendentals=0
         ),
-    )(q, k, v, start)
+    )(q, k, v, start, *when)
 
 
 def attend_back_kernel(
-    heads, keys, block, q_ref, k_ref, v_ref, grad_ref, lse_ref, start_ref, cos_ref, sin_ref, out_ref, bias_ref, dk_ref, dv_ref
+    heads, keys, block, q_ref, k_ref, v_ref, grad_ref, lse_ref, start_ref, cos_ref, sin_ref, *refs
 ):
+    out_ref, bias_ref, dk_ref, dv_ref = refs[-4:]
     total = q_ref.shape[0]
     group = heads // keys
     scale = HEAD_SIZE**-0.5
@@ -264,11 +278,14 @@
             out_ref[rows, at : at + HEAD_SIZE] = dv_ref[rows, lanes][:, :HEAD_SIZE].astype(low)
 
 
-def attend_back_call(q, k, v, grad, lse_rows, start_row, cosine, sine_back, block=256):
+def attend_back_call(q, k, v, grad, lse_rows, start_row, cosine, sine_back, *when):
+    block = 256
     total = q.shape[0]
     heads, keys = q.shape[1] // LANES, k.shape[1] // LANES
     return pl.pallas_call(
         functools.partial(attend_back_kernel, heads, keys, block),
+        in_specs=[pl.BlockSpec(memory_space=pltpu.VMEM)] * 8
+        + [pl.BlockSpec(memory_space=pl.ANY)] * len(when),
         out_shape=jax.ShapeDtypeStruct((total, (heads + 2 * keys) * HEAD_SIZE), jnp.bfloat16),
         scratch_shapes=[
             pltpu.VMEM((total, block), jnp.float32),
@@ -277,9 +294,9 @@
         ],
         compiler_params=pltpu.CompilerParams(vmem_limit_bytes=56 * 2**20),
         cost_estimate=pl.CostEstimate(
-            flops=8000 * heads * total * total * 128, bytes_accessed=12 * 2**20, transcendentals=heads * total * total // 2
+            flops=150 * 10**9, bytes_accessed=0, transcendentals=0
         ),
-    )(q, k, v, grad, lse_rows, start_row, cosine, sine_back)
+    )(q, k, v, grad, lse_rows, start_row, cosine, sine_back, *when)
 
 def gate_up_kernel(x_ref, gate_weight_ref, up_weight_ref, active_ref, gate_ref, up_ref):
     x = x_ref[...]
@@ -312,12 +329,13 @@
         out_shape=[jax.ShapeDtypeStruct((total, units), jnp.bfloat16)] * 3,
         compiler_params=pltpu.CompilerParams(vmem_limit_bytes=56 * 2**20),
         cost_estimate=pl.CostEstimate(
-            flops=4 * total * width * units, bytes_accessed=45 * 2**20, transcendentals=0
+            flops=111 * 10**9, bytes_accessed=0, transcendentals=0
         ),
     )(x, weights, weights)
 
 
-def unit_back_kernel(incoming_ref, down_ref, gate_ref, up_ref, d_gate_ref, d_up_ref):
+def unit_back_kernel(incoming_ref, down_ref, gate_ref, up_ref, *refs):
+    d_gate_ref, d_up_ref = refs[-2:]
     d_active = dot_cols(incoming_ref[...], down_ref[...])
     gate = gate_ref[...].astype(jnp.float32)
     upward = up_ref[...].astype(jnp.float32)
@@ -326,7 +344,7 @@
     d_up_ref[...] = (d_active * gate * logistic).astype(jnp.bfloat16)
 
 
-def unit_back_call(incoming, down, gate, up):
+def unit_back_call(incoming, down, gate, up, *when):
     total, width = incoming.shape
     units = down.shape[0]
     block = unit_block(units)
@@ -339,14 +357,15 @@
             pl.BlockSpec((block, width), lambda j: (j, 0)),
             column,
             column,
-        ],
+        ]
+        + [pl.BlockSpec(memory_space=pl.ANY)] * len(when),
         out_specs=[column] * 2,
         out_shape=[jax.ShapeDtypeStruct((total, units), jnp.bfloat16)] * 2,
         compiler_params=pltpu.CompilerParams(vmem_limit_bytes=56 * 2**20),
         cost_estimate=pl.CostEstimate(
-            flops=2 * total * width * units, bytes_accessed=40 * 2**20, transcendentals=0
+            flops=78 * 10**9, bytes_accessed=0, transcendentals=0
         ),
-    )(incoming, down, gate, up)
+    )(incoming, down, gate, up, *when)
 
 
 def norm_back(d_normed, x, gain):
@@ -400,7 +419,7 @@
         ],
         compiler_params=pltpu.CompilerParams(vmem_limit_bytes=60 * 2**20),
         cost_estimate=pl.CostEstimate(
-            flops=4 * total * width * units, bytes_accessed=45 * 2**20, transcendentals=0
+            flops=132 * 10**9, bytes_accessed=0, transcendentals=0
         ),
     )(d_gate, d_up, weights, x, gain, *when)
 
@@ -445,7 +464,7 @@
         ],
         compiler_params=pltpu.CompilerParams(vmem_limit_bytes=56 * 2**20),
         cost_estimate=pl.CostEstimate(
-            flops=2 * total * width * d_qkv.shape[1], bytes_accessed=30 * 2**20, transcendentals=0
+            flops=60 * 10**9, bytes_accessed=0, transcendentals=0
         ),
     )(place, d_qkv, weights, x, gain, own, *when)
 
@@ -469,9 +488,93 @@
         out_shape=jax.ShapeDtypeStruct((parts, total, rows), jnp.bfloat16),
         compiler_params=pltpu.CompilerParams(vmem_limit_bytes=32 * 2**20),
         cost_estimate=pl.CostEstimate(
-            flops=2 * total * share * weights.shape[0], bytes_accessed=14 * 2**20, transcendentals=0
+            flops=24 * 10**9, bytes_accessed=0, transcendentals=0
         ),
     )(d_branch, weights, *when)
+
+
+def norm_kernel(stack_ref, gain_ref, x_ref, normed_ref):
+    parts, _, share = stack_ref.shape
+    squares = 0.0
+    for i in range(parts):
+        piece = stack_ref[i].astype(jnp.float32)
+        squares = squares + jnp.sum(piece * piece, axis=1, keepdims=True)
+    scale = lax.rsqrt(squares / (parts * share) + eps)
+    for i in range(parts):
+        lanes = slice(i * share, (i + 1) * share)
+        x_ref[:, lanes] = stack_ref[i]
+        normed = stack_ref[i].astype(jnp.float32) * scale * gain_ref[:, lanes]
+        normed_ref[:, lanes] = normed.astype(jnp.bfloat16)
+
+
+def norm_call(stack, gain):
+    parts, total, share = stack.shape
+    block = 256
+    row = pl.BlockSpec((block, parts * share), lambda i: (i, 0))
+    return pl.pallas_call(
+        norm_kernel,
+        grid=(total // block,),
+        in_specs=[
+            pl.BlockSpec((parts, block, share), lambda i: (0, i, 0)),
+            pl.BlockSpec((1, parts * share), lambda i: (0, 0)),
+        ],
+        out_specs=[row, row],
+        out_shape=[jax.ShapeDtypeStruct((total, parts * share), jnp.bfloat16)] * 2,
+        compiler_params=pltpu.CompilerParams(vmem_limit_bytes=32 * 2**20),
+        cost_estimate=pl.CostEstimate(flops=24 * 10**9, bytes_accessed=0, transcendentals=0),
+    )(stack, gain)
+
+
+def out_kernel(stack_ref, weight_ref, x_ref, out_ref):
+    parts, _, depth = stack_ref.shape
+    total = x_ref[...].astype(jnp.float32)
+    for i in range(parts):
+        total = total + jnp.dot(
+            stack_ref[i], weight_ref[i * depth : (i + 1) * depth, :], preferred_element_type=jnp.float32
+        )
+    out_ref[...] = total.astype(jnp.bfloat16)
+
+
+def out_call(stack, weight, x):
+    parts, total, depth = stack.shape
+    columns = weight.shape[1]
+    block = 512
+    row = pl.BlockSpec((block, columns), lambda i: (i, 0))
+    return pl.pallas_call(
+        out_kernel,
+        grid=(total // block,),
+        in_specs=[
+            pl.BlockSpec((parts, block, depth), lambda i: (0, i, 0)),
+            pl.BlockSpec(weight.shape, lambda i: (0, 0)),
+            row,
+        ],
+        out_specs=row,
+        out_shape=jax.ShapeDtypeStruct((total, columns), jnp.bfloat16),
+        compiler_params=pltpu.CompilerParams(vmem_limit_bytes=40 * 2**20),
+        cost_estimate=pl.CostEstimate(flops=27 * 10**9, bytes_accessed=0, transcendentals=0),
+    )(stack, weight, x)
+
+
+def stack_rows_kernel(left_ref, right_ref, *refs):
+    refs[-1][...] = dot_rows(left_ref[0], right_ref[...]).astype(jnp.bfloat16)
+
+
+def stack_rows_call(stack, right, *when):
+    parts, total, rows = stack.shape
+    columns = right.shape[1]
+    return pl.pallas_call(
+        stack_rows_kernel,
+        grid=(parts,),
+        in_specs=[
+            pl.BlockSpec((1, total, rows), lambda i: (i, 0, 0)),
+            pl.BlockSpec((total, columns), lambda i: (0, 0)),
+        ]
+        + [pl.BlockSpec(memory_space=pl.ANY)] * len(when),
+        out_specs=pl.BlockSpec((rows, columns), lambda i: (i, 0)),
+        out_shape=jax.ShapeDtypeStruct((parts * rows, columns), jnp.bfloat16),
+        compiler_params=pltpu.CompilerParams(vmem_limit_bytes=40 * 2**20),
+        cost_estimate=pl.CostEstimate(flops=45 * 10**9, bytes_accessed=0, transcendentals=0),
+    )(stack, right, *when)
 
 
 def rows_kernel(left_ref, right_ref, *refs):
@@ -493,7 +596,7 @@
         out_specs=pl.BlockSpec((rows, block), lambda j: (0, j)),
         out_shape=jax.ShapeDtypeStruct((rows, columns), jnp.bfloat16),
         compiler_params=pltpu.CompilerParams(vmem_limit_bytes=56 * 2**20),
-        cost_estimate=pl.CostEstimate(flops=0, bytes_accessed=0, transcendentals=0),
+        cost_estimate=pl.CostEstimate(flops=60 * 10**9, bytes_accessed=0, transcendentals=0),
     )(left, right, *when)
 
 
@@ -518,11 +621,12 @@
         out_specs=pl.BlockSpec((total, block), lambda j: (0, j)),
         out_shape=jax.ShapeDtypeStruct((total, columns), jnp.bfloat16),
         compiler_params=pltpu.CompilerParams(vmem_limit_bytes=56 * 2**20),
-        cost_estimate=pl.CostEstimate(flops=0, bytes_accessed=0, transcendentals=0),
+        cost_estimate=pl.CostEstimate(flops=60 * 10**9, bytes_accessed=0, transcendentals=0),
     )(left, right, *when)
 
 
-def qkv_grad_kernel(normed_ref, d_qkv_ref, gain_ref, out_ref):
+def qkv_grad_kernel(normed_ref, d_qkv_ref, gain_ref, *refs):
+    out_ref = refs[-1]
     columns = d_qkv_ref.shape[1]
     out_ref[:, :columns] = dot_rows(normed_ref[...], d_qkv_ref[...]).astype(jnp.bfloat16)
     rest = jnp.transpose(gain_ref[...])
@@ -532,7 +636,7 @@
     out_ref[:, columns:] = rest.astype(jnp.bfloat16)
 
 
-def qkv_grad_call(normed, d_qkv, gain_grads, columns):
+def qkv_grad_call(normed, d_qkv, gain_grads, columns, *when):
     total, width = normed.shape
     block = 512
     return pl.pallas_call(
@@ -542,20 +646,36 @@
             pl.BlockSpec((total, block), lambda i: (0, i)),
             pl.BlockSpec(d_qkv.shape, lambda i: (0, 0)),
             pl.BlockSpec((gain_grads.shape[0], block), lambda i: (0, i)),
-        ],
+        ]
+        + [pl.BlockSpec(memory_space=pl.ANY)] * len(when),
         out_specs=pl.BlockSpec((block, columns), lambda i: (i, 0)),
         out_shape=jax.ShapeDtypeStruct((width, columns), jnp.bfloat16),
         compiler_params=pltpu.CompilerParams(vmem_limit_bytes=48 * 2**20),
-        cost_estimate=pl.CostEstimate(flops=0, bytes_accessed=0, transcendentals=0),
-    )(normed, d_qkv, gain_grads)
-
-
-def pieces_sp(value):
-    return [value] + [swap(value, turn) for turn in range(1, lax.axis_size("sp"))]
-
-
-def spread_kernel(layout, count, place_ref, *refs):
-    pieces, outs = refs[:count], refs[count:]
+        cost_estimate=pl.CostEstimate(flops=36 * 10**9, bytes_accessed=0, transcendentals=0),
+    )(normed, d_qkv, gain_grads, *when)
+
+
+def pieces_sp(value, split):
+    size = lax.axis_size("sp")
+    columns = value.shape[1]
+    if not split or size != 4 or columns % (2 * LANES):
+        others = [(swap(value, turn),) for turn in range(1, size)]
+        return [(value,)] + others, [piece for (piece,) in others], []
+    half = columns // 2
+    left, right = value[:, :half], value[:, half:]
+    x_left, y_right = swap(left, 1), swap(right, 2)
+    x_right, y_left = swap(right, 1), swap(left, 2)
+    far_left, far_right = swap(x_left, 2), swap(y_right, 1)
+    return (
+        [(left, right), (x_left, x_right), (y_left, y_right), (far_left, far_right)],
+        [x_left, y_right, x_right, y_left],
+        [far_left, far_right],
+    )
+
+
+def spread_kernel(layout, count, chunks, place_ref, *refs):
+    pieces, outs = refs[: count * chunks], refs[count * chunks :]
+    size = pieces[0].shape[1]
     for place in range(count):
 
         @pl.when(place_ref[0] == place)
@@ -563,47 +683,57 @@
             for part in range(count):
                 for first, width, out, at, step in layout:
                     goal = at + part * step
-                    outs[out][:, goal : goal + width] = pieces[place ^ part][:, first : first + width].astype(
-                        jnp.float32
-                    )
+                    while width:
+                        chunk, begin = divmod(first, size)
+                        some = min(width, size - begin)
+                        piece = pieces[(place ^ part) * chunks + chunk]
+                        outs[out][:, goal : goal + some] = piece[:, begin : begin + some].astype(jnp.float32)
+                        first, goal, width = first + some, goal + some, width - some
 
 
 def spread_call(place, pieces, layout, widths):
-    rows, columns = pieces[0].shape
+    count, chunks = len(pieces), len(pieces[0])
+    rows, columns = pieces[0][0].shape
     block = rows // 5 if rows % 80 == 0 else rows
     return pl.pallas_call(
-        functools.partial(spread_kernel, layout, len(pieces)),
+        functools.partial(spread_kernel, layout, count, chunks),
         grid=(rows // block,),
         in_specs=[pl.BlockSpec(memory_space=pltpu.SMEM)]
-        + [pl.BlockSpec((block, columns), lambda i: (i, 0))] * len(pieces),
+        + [pl.BlockSpec((block, columns), lambda i: (i, 0))] * (count * chunks),
         out_specs=[pl.BlockSpec((block, w), lambda i: (i, 0)) for w in widths],
         out_shape=[jax.ShapeDtypeStruct((rows, w), jnp.float32) for w in widths],
         compiler_params=pltpu.CompilerParams(vmem_limit_bytes=40 * 2**20),
         cost_estimate=pl.CostEstimate(
-            flops=0, bytes_accessed=6 * len(pieces) * rows * columns, transcendentals=0
+            flops=0, bytes_accessed=6 * count * chunks * rows * columns, transcendentals=0
         ),
-    )(place, *pieces)
-
-
-def stack_kernel(count, place_ref, *refs):
+    )(place, *[chunk for piece in pieces for chunk in piece])
+
+
+def stack_kernel(count, chunks, place_ref, *refs):
+    out_ref = refs[-1]
+    size = refs[0].shape[1]
     for turn in range(count):
-        refs[count][place_ref[0] ^ turn] = refs[turn][...].astype(jnp.float32)
+        for chunk in range(chunks):
+            value = refs[turn * chunks + chunk][...].astype(jnp.float32)
+            out_ref[place_ref[0] ^ turn, :, chunk * size : (chunk + 1) * size] = value
 
 
 def stack_call(place, pieces):
-    rows, columns = pieces[0].shape
+    count, chunks = len(pieces), len(pieces[0])
+    rows, columns = pieces[0][0].shape
     block = 32 if rows % 32 == 0 else rows
-    count = len(pieces)
-    return pl.pallas_call(
-        functools.partial(stack_kernel, count),
+    return pl.pallas_call(
+        functools.partial(stack_kernel, count, chunks),
         grid=(rows // block,),
         in_specs=[pl.BlockSpec(memory_space=pltpu.SMEM)]
-        + [pl.BlockSpec((block, columns), lambda i: (i, 0))] * count,
-        out_specs=pl.BlockSpec((count, block, columns), lambda i: (0, i, 0)),
-        out_shape=jax.ShapeDtypeStruct((count, rows, columns), jnp.float32),
+        + [pl.BlockSpec((block, columns), lambda i: (i, 0))] * (count * chunks),
+        out_specs=pl.BlockSpec((count, block, chunks * columns), lambda i: (0, i, 0)),
+        out_shape=jax.ShapeDtypeStruct((count, rows, chunks * columns), jnp.float32),
         compiler_params=pltpu.CompilerParams(vmem_limit_bytes=40 * 2**20),
-        cost_estimate=pl.CostEstimate(flops=0, bytes_accessed=6 * count * rows * columns, transcendentals=0),
-    )(place, *pieces).reshape(count * rows, columns)
+        cost_estimate=pl.CostEstimate(
+            flops=0, bytes_accessed=6 * count * chunks * rows * columns, transcendentals=0
+        ),
+    )(place, *[chunk for piece in pieces for chunk in piece]).reshape(count * rows, chunks * columns)
 
 
 def pass_kernel(*refs):
@@ -692,18 +822,19 @@
     )
 
     def picked(given):
-        return jnp.take(given.reshape(groups, -1, width), pick_send, axis=0)
+        return rows_of(given.reshape(groups, -1, width), pick_send)
 
     def deal(blocks):
         return lax.all_to_all(blocks, "fsdp", split_axis=0, concat_axis=0, tiled=True)
 
     def in_place(came):
-        return jnp.take(came, pick_place, axis=0).reshape(rows, width)
-
-    def to_given(owned):
-        blocks = jnp.take(owned.reshape(groups, -1, width), arrived_slot, axis=0)
-        gone = lax.all_to_all(blocks, "fsdp", split_axis=0, concat_axis=0, tiled=True)
-        return jnp.take(gone, target, axis=0).reshape(tokens.shape)
+        return rows_of(came, pick_place).reshape(rows, width)
+
+    def blocks_back(owned):
+        return rows_of(owned.reshape(groups, -1, width), arrived_slot)
+
+    def scatter_fsdp(matrix):
+        return lax.psum_scatter(matrix, "fsdp", scatter_dimension=0, tiled=True)
 
     def column_share(weight):
         share = weight.shape[1] // parts
@@ -727,16 +858,15 @@
     qkv_shard = jnp.concatenate(
         [column_share(w_query), column_share(key_weight), column_share(value_weight), gains], axis=1
     )
-    qkv_all = gather_fsdp(qkv_shard)
+    came_incoming = deal(after(picked(cotangent), came_tokens))
+    qkv_all = gather_fsdp(after(qkv_shard, came_tokens))
     out_all = gather_fsdp(column_share(w_out))
     gate_up_all = gather_fsdp(gate_up_shard)
     down_all = gather_fsdp(lax.dynamic_slice_in_dim(w_down, sp_place * ff_share, ff_share, axis=0))
-    qkv_weight = qkv_all[:, :qkv_cols]
     gain_one = qkv_all[:, qkv_cols].astype(wide)[None, :]
     gain_two = qkv_all[:, qkv_cols + 1].astype(wide)[None, :]
 
-    group_inputs = gather_sp(in_place(came_tokens)).reshape(-1, width)
-    came_incoming = deal(after(picked(cotangent), group_inputs))
+    group_inputs = gather_sp(in_place(came_tokens))[0].reshape(-1, width)
     group_positions = gather_small(positions.reshape(-1)).reshape(-1)
     total = group_inputs.shape[0]
 
@@ -751,71 +881,62 @@
     start = jnp.sum(jnp.where(places[:, None] >= ends[None, :], sizes[None, :], 0), axis=1)
     own_mixed, logs = attend_call(query_low, key_low, value_low, start[:, None])
 
-    def side_by_side(stacked):
-        return jnp.concatenate([stacked[i] for i in range(parts)], axis=1)
-
     share = width // parts
 
     def own_columns(matrix):
         return lax.dynamic_slice_in_dim(matrix, sp_place * share, share, axis=1)
 
-    mixed = side_by_side(gather_sp(own_mixed))
-    own_hidden = own_columns(group_inputs).astype(wide) + dot(mixed, out_all)
-    hidden_low = side_by_side(gather_sp(own_hidden.astype(low)))
-
-    group_incoming = gather_sp(after(in_place(came_incoming), hidden_low)).reshape(-1, width)
-
-    hidden = hidden_low.astype(wide)
-    rms_two = lax.rsqrt(jnp.mean(hidden * hidden, axis=-1, keepdims=True) + eps)
-    normed_two = (hidden * rms_two * gain_two).astype(low)
+    mixed, _ = gather_sp(own_mixed)
+    own_hidden = out_call(mixed, out_all, own_columns(group_inputs))
+    hidden_low, normed_two = norm_call(gather_sp(own_hidden)[0], gain_two)
+
     active_low, gate, upward = gate_up_call(normed_two, gate_up_all)
+    own_incoming = after(in_place(after(came_incoming, own_hidden)), normed_two)
+    group_incoming = gather_sp(own_incoming, active_low)[0].reshape(-1, width)
     grad_down = rows_call(active_low, group_incoming)
-    down_all = after(down_all, grad_down)
-    d_gate, d_up = unit_back_call(group_incoming, down_all, gate, upward)
+    result_part = product_call(active_low, down_all, grad_down)
+    d_gate, d_up = unit_back_call(group_incoming, down_all, gate, upward, result_part)
     grad_gate = rows_call(normed_two, d_gate)
+    result_sum, (sums_result, _) = scatter_sp(result_part.reshape(parts, rows, width), grad_gate)
+    own_hidden_rows = lax.dynamic_slice_in_dim(hidden_low, sp_place * rows, rows, axis=0)
+    blocks_result = blocks_back((own_hidden_rows.astype(wide) + result_sum).astype(low))
+
     back_two, grad_gain_two = mlp_back_call(
-        d_gate, d_up, gate_up_all, hidden_low, gain_two, parts, grad_gate
-    )
+        d_gate, d_up, gate_up_all, hidden_low, gain_two, parts, grad_gate, *sums_result
+    )
+    back_two = after(back_two, result_sum)
     from_others, _ = scatter_sp(back_two)
     grad_up = rows_call(normed_two, d_up, back_two)
+    gone_result = deal(blocks_result)
     own_d_hidden = own_columns(group_incoming).astype(wide) + from_others
     d_branch = own_d_hidden.astype(low)
     grad_up = after(grad_up, d_branch)
-    d_mixed, (sums_mixed, _) = scatter_sp(out_back_call(d_branch, out_all, parts, grad_up))
+    grad_out = stack_rows_call(mixed, d_branch)
+    d_mixed, _ = scatter_sp(out_back_call(d_branch, out_all, parts, grad_up), grad_out)
     d_mixed = d_mixed.astype(low)
-    grad_out = rows_call(mixed, d_branch)
-    result_part = product_call(active_low, down_all, grad_out, *sums_mixed)
-    own_hidden_rows = lax.dynamic_slice_in_dim(hidden_low, sp_place * rows, rows, axis=0)
-    result_sum, (sums_result, _) = scatter_sp(after(result_part, d_mixed).reshape(parts, rows, width))
-    layer_out = to_given((own_hidden_rows.astype(wide) + result_sum).astype(low))
-
+
+    down_sum = after(scatter_fsdp(grad_down), d_mixed)
+    gate_sum = after(scatter_fsdp(grad_gate), d_mixed, down_sum)
+    down_pieces, down_first, _ = pieces_sp(down_sum, False)
+    gate_pieces, gate_first, _ = pieces_sp(gate_sum, False)
     d_qkv = attend_back_call(
-        query_low, key_low, value_low, d_mixed, logs.T, start[None, :], cosine, sine
+        query_low, key_low, value_low, d_mixed, logs.T, start[None, :], cosine, sine, gone_result
     )
     back_one, grad_gain_one = attend_norm_call(
-        place, d_qkv, qkv_all, group_inputs, gain_one, own_d_hidden, parts, *sums_result
+        place, d_qkv, qkv_all, group_inputs, gain_one, own_d_hidden, parts, *down_first, *gate_first[:-1]
     )
     gain_grads = jnp.concatenate(
         [grad_gain_one, grad_gain_two, jnp.zeros((6, width), wide)], axis=0
     )
     grad_qkv = qkv_grad_call(normed, d_qkv, gain_grads, qkv_all.shape[1])
     d_inputs = scatter_sp(back_one.reshape(parts, rows, width))[0]
-    input_grad = to_given(d_inputs.astype(low))
-
-    def scatter_fsdp(matrix):
-        return lax.psum_scatter(matrix.astype(low), "fsdp", scatter_dimension=0, tiled=True)
-
-    down_sum = scatter_fsdp(grad_down)
-    gate_sum = scatter_fsdp(grad_gate)
-    up_sum = scatter_fsdp(grad_up)
-    out_sum = scatter_fsdp(grad_out)
-    qkv_sum = scatter_fsdp(grad_qkv)
-
-    down_pieces = pieces_sp(down_sum)
-    gate_pieces = pieces_sp(after(gate_sum, *down_pieces[1:]))
-    up_pieces = pieces_sp(after(up_sum, *gate_pieces[1:]))
-    out_pieces = pieces_sp(after(out_sum, *up_pieces[1:]))
-    qkv_pieces = pieces_sp(after(qkv_sum, *out_pieces[1:]))
+    gone_grad = deal(blocks_back(d_inputs.astype(low)))
+    layer_out = rows_of(gone_result, target).reshape(tokens.shape)
+    input_grad = rows_of(gone_grad, target).reshape(tokens.shape)
+
+    up_pieces = pieces_sp(scatter_fsdp(grad_up), True)[0]
+    out_pieces = pieces_sp(scatter_fsdp(grad_out), False)[0]
+    qkv_pieces = pieces_sp(scatter_fsdp(grad_qkv), True)[0]
 
     down_shard = stack_call(place, down_pieces)
     hidden_layout = [

time: 1240 us -> 1160 us (0.935)
  blocking collectives: 82.7 us -> 0 us
  local copies, waits for them, and re-layouts: 104 us -> 157 us
  waiting for transfers between devices: 463 us -> 425 us
  other arithmetic: 77 us -> 44.2 us
  Pallas kernels: 370 us -> 387 us
    all_to_all x1 -> x0, blocking collectives: 82.7 us -> none  [deal(): lax.all_to_all(blocks, 'fsdp', split_axis=0, concat_axis=0, tiled=True)]
    all_to_all x2 -> x0, waiting for transfers between devices: 56 us -> none  [to_given(): lax.all_to_all(blocks, 'fsdp', split_axis=0, concat_axis=0, tiled=True)]
    all_to_all x1 -> x4, starting transfers between devices: 8.69 us -> 57.8 us  [deal(): lax.all_to_all(blocks, 'fsdp', split_axis=0, concat_axis=0, tiled=True)]
    all_to_all x2 -> x0, starting transfers between devices: 43.8 us -> none  [to_given(): lax.all_to_all(blocks, 'fsdp', split_axis=0, concat_axis=0, tiled=True)]
    all_to_all x1 -> x4, waiting for transfers between devices: 29.1 us -> 63.8 us  [deal(): lax.all_to_all(blocks, 'fsdp', split_axis=0, concat_axis=0, tiled=True)]
    pallas_call x6 -> x9, Pallas kernels: 52.4 us -> 85.6 us  [the longest x1 27.7 us: attend_call(): pl.pallas_call(functools.partial(attend_kernel, heads, keys, block), in_s...]
    unnamed x116 -> x126, local copies, waits for them, and re-layouts: 18.4 us -> 39.8 us
    ppermute x66 -> x72, waiting for transfers between devices: 378 us -> 361 us  [swap(): return lax.ppermute(value, 'sp', [(i, i ^ bit) for i in range(size)])]
  transfers between devices with their start and end apart: 78 -> 85, of which waited for: 33 -> 33; matrix products, arithmetic and copies ran while one was open for 14% -> 14% of each run, Pallas kernels for 30% -> 33%
where the time goes in v5:
time: 1160 us; the launch traced here: 1150 us
  waiting for transfers between devices  425 us (37%)
  Pallas kernels  387 us (33%)
  local copies, waits for them, and re-layouts  157 us (14%)
  starting transfers between devices  117 us (10%)
  other arithmetic  44.2 us (4%)
  between operations  15.2 us (1%)
    ppermute x72, waiting for transfers between devices, swap(): return lax.ppermute(value, 'sp', [(i, i ^ bit) for i in range(size)])  361 us
    all_to_all x4, waiting for transfers between devices, deal(): lax.all_to_all(blocks, 'fsdp', split_axis=0, concat_axis=0, tiled=True)  63.8 us
    pallas_call x3, Pallas kernels, rows_call(): pl.pallas_call(rows_kernel, grid=(columns // block,), in_specs=[pl.BlockS...  61.2 us
    ppermute x72, starting transfers between devices, swap(): return lax.ppermute(value, 'sp', [(i, i ^ bit) for i in range(size)])  58 us
    all_to_all x4, starting transfers between devices, deal(): lax.all_to_all(blocks, 'fsdp', split_axis=0, concat_axis=0, tiled=True)  57.8 us
    pallas_call x1, Pallas kernels, attend_back_call(): pl.pallas_call(functools.partial(attend_back_kernel, heads, keys, block),...  49.9 us
    pallas_call x1, Pallas kernels, mlp_back_call(): pl.pallas_call(mlp_back_kernel, grid=(total // block,), in_specs=[row(uni...  43.4 us
    unnamed x126, local copies, waits for them, and re-layouts  39.8 us
  transfers between devices with their start and end apart: 85, of which 33 were waited for; matrix products, arithmetic and copies ran while one was open for 14% of the time, Pallas kernels for 33%

profile of v5, /device:TPU:9, one launch (start us, length us, event | category | flops | bytes accessed | tf_op | source)
XLA Modules:
  0.0 1145.7 jit_solution(2310519938005818197)
XLA Ops:
  20.0 39.2 %all-to-all-done.refs_1_._ = bf16[8,48,2560]{2,1,0:T(8,128)(2,1)S(1)} async-done(((bf16[8,48,2560]{2,1,0:T(8,128)(2,1)}), bf16[8,48,2560]{2,1,0:T(8,128)(2,1)S(1)}, u32[]{:S(2)}, u32[]{:S(2)}) %all-to-all-start) | async-done | bytes 1966112 | tf_op jit(solution)/shard_map/all_to_all | solution.py:828
  104.6 16.3 %collective-permute-done.1 = bf16[192,2560]{1,0:T(8,128)(2,1)} collective-permute-done((bf16[192,2560]{1,0:T(8,128)(2,1)}, bf16[192,2560]{1,0:T(8,128)(2,1)}, u32[]{:S(2)}, u32[]{:S(2)}) %collective-permute-start.1) | collective-permute-done | bytes 983072 | tf_op jit(solution)/shard_map/ppermute | solution.py:23
  148.0 23.5 %shard_map.222 = (bf16[1536,2560]{1,0:T(8,128)(2,1)}, bf16[1536,1024]{1,0:T(8,128)(2,1)}, bf16[1536,256]{1,0:T(8,128)(2,1)S(1)}, bf16[1536,256]{1,0:T(8,128)(2,1)S(1)}) custom-call(bf16[1536,2560]{1,0:T(8,128)(2,1)} %bitcast.17.x_ref, f32[1,2560]{1,0:T(1,128)S(1)} %reshape.330.gain_ref, bf16[2560,1024]{1,0:T(8,128)(2,1)} %all-gather.5.cloned.1.call-done.weight_ref, ...), custom_call_target="tpu_custom_call" | custom-call | flops 71999995904 | tf_op jit(solution)/shard_map/pallas_call | solution.py:163
  173.3 27.7 %shard_map.223 = (bf16[1536,640]{1,0:T(8,128)(2,1)}, f32[1536,8]{1,0:T(8,128)}) custom-call(bf16[1536,1024]{1,0:T(8,128)(2,1)} %get-tuple-element.32.q_ref, bf16[1536,256]{1,0:T(8,128)(2,1)} %copy-done.33, bf16[1536,256]{1,0:T(8,128)(2,1)} %copy-done.34, s32[1536,1]{1,0:T(8,128)} %broadcast_in_dim.224.start_ref), custom_call_target="tpu_custom_call" | custom-call | flops 83999997952 | tf_op jit(solution)/shard_map/pallas_call | solution.py:212
  250.4 17.2 %collective-permute-done.13 = bf16[768,640]{1,0:T(8,128)(2,1)S(1)} collective-permute-done((bf16[768,640]{1,0:T(8,128)(2,1)}, bf16[768,640]{1,0:T(8,128)(2,1)S(1)}, u32[]{:S(2)}, u32[]{:S(2)}) %collective-permute-start.13) | collective-permute-done | bytes 983072 | tf_op jit(solution)/shard_map/ppermute | solution.py:23
  287.3 24.6 %all-to-all-done.1.refs_0_ = bf16[8,48,2560]{2,1,0:T(8,128)(2,1)} async-done(((bf16[8,48,2560]{2,1,0:T(8,128)(2,1)}), bf16[8,48,2560]{2,1,0:T(8,128)(2,1)}, u32[]{:S(2)}, u32[]{:S(2)}) %all-to-all-start.1) | async-done | bytes 1966112 | tf_op jit(solution)/shard_map/all_to_all | solution.py:828
  329.6 17.2 %collective-permute-done.19 = bf16[768,640]{1,0:T(8,128)(2,1)S(1)} collective-permute-done((bf16[768,640]{1,0:T(8,128)(2,1)}, bf16[768,640]{1,0:T(8,128)(2,1)S(1)}, u32[]{:S(2)}, u32[]{:S(2)}) %collective-permute-start.19) | collective-permute-done | bytes 983072 | tf_op jit(solution)/shard_map/ppermute | solution.py:23
  388.2 36.6 %shard_map.227 = (bf16[1536,1792]{1,0:T(8,128)(2,1)}, bf16[1536,1792]{1,0:T(8,128)(2,1)}, bf16[1536,1792]{1,0:T(8,128)(2,1)}) custom-call(bf16[1536,2560]{1,0:T(8,128)(2,1)} %copy-done.8, bf16[2560,3584]{1,0:T(8,128)(2,1)} %all-gather.9.cloned.1.call-done.gate_weight_ref.up_weight_ref.weight_ref, ...), custom_call_target="tpu_custom_call" | custom-call | flops 111000002560 | tf_op jit(solution)/shard_map/pallas_call | solution.py:320
  444.5 20.3 %shard_map.232.refs_0_ = bf16[1792,2560]{1,0:T(8,128)(2,1)} custom-call(bf16[1536,1792]{1,0:T(8,128)(2,1)} %get-tuple-element.38.refs_1_.left_ref, bf16[1536,2560]{1,0:T(8,128)(2,1)} %bitcast.205), custom_call_target="tpu_custom_call" | custom-call | flops 60000002048 | tf_op jit(solution)/shard_map/pallas_call | solution.py:588
  465.1 20.1 %shard_map.233.refs_0_ = bf16[1536,2560]{1,0:T(8,128)(2,1)} custom-call(bf16[1536,1792]{1,0:T(8,128)(2,1)} %get-tuple-element.38.refs_1_.left_ref, bf16[1792,2560]{1,0:T(8,128)(2,1)} %all-gather.11.cloned.1.call-done.right_ref.down_ref, bf16[1792,2560]{1,0:T(8,128)(2,1)} %shard_map.232.refs_0_), custom_call_target="tpu_custom_call" | custom-call | flops 60000002048 | tf_op jit(solution)/shard_map/pallas_call | solution.py:613
  491.4 25.5 %shard_map.234 = (bf16[1536,1792]{1,0:T(8,128)(2,1)}, bf16[1536,1792]{1,0:T(8,128)(2,1)}) custom-call(bf16[1536,2560]{1,0:T(8,128)(2,1)} %bitcast.206, bf16[1792,2560]{1,0:T(8,128)(2,1)} %all-gather.11.cloned.1.call-done.right_ref.down_ref, bf16[1536,1792]{1,0:T(8,128)(2,1)} %get-tuple-element.39.gate_ref, bf16[1536,1792]{1,0:T(8,128)(2,1)} %get-tuple-element.40.up_ref, ...), custom_call_target="tpu_custom_call" | custom-call | flops 77999996928 | tf_op jit(solution)/shard_map/pallas_call | solution.py:352
  516.9 20.5 %shard_map.235.refs_1_.refs_0_ = bf16[2560,1792]{1,0:T(8,128)(2,1)} custom-call(bf16[1536,2560]{1,0:T(8,128)(2,1)} %copy-done.8, bf16[1536,1792]{1,0:T(8,128)(2,1)} %get-tuple-element.41.right_ref.d_gate_ref), custom_call_target="tpu_custom_call" | custom-call | flops 60000002048 | tf_op jit(solution)/shard_map/pallas_call | solution.py:588
  559.0 43.4 %shard_map.237 = (bf16[4,1536,640]{2,1,0:T(8,128)(2,1)}, f32[1,2560]{1,0:T(1,128)}) custom-call(bf16[1536,1792]{1,0:T(8,128)(2,1)} %get-tuple-element.41.right_ref.d_gate_ref, bf16[1536,1792]{1,0:T(8,128)(2,1)} %get-tuple-element.42.d_up_ref.right_ref, bf16[2560,3584]{1,0:T(8,128)(2,1)} %all-gather.9.cloned.1.call-done.gate_weight_ref.up_weight_ref.weight_ref, ...), custom_call_target="tpu_custom_call" | custom-call | flops 131999997952 | tf_op jit(solution)/shard_map/pallas_call | solution.py:407
  641.7 19.1 %collective-permute-done.38 = bf16[768,640]{1,0:T(8,128)(2,1)S(1)} collective-permute-done((bf16[768,640]{1,0:T(8,128)(2,1)S(1)}, bf16[768,640]{1,0:T(8,128)(2,1)S(1)}, u32[]{:S(2)}, u32[]{:S(2)}) %collective-permute-start.38) | collective-permute-done | bytes 983072 | tf_op jit(solution)/shard_map/ppermute | solution.py:23
  679.6 20.4 %shard_map.239.refs_0_ = bf16[2560,1792]{1,0:T(8,128)(2,1)} custom-call(bf16[1536,2560]{1,0:T(8,128)(2,1)} %copy-done.8, bf16[1536,1792]{1,0:T(8,128)(2,1)} %get-tuple-element.42.d_up_ref.right_ref, bf16[4,1536,640]{2,1,0:T(8,128)(2,1)} %shard_map.238.refs_0_), custom_call_target="tpu_custom_call" | custom-call | flops 60000002048 | tf_op jit(solution)/shard_map/pallas_call | solution.py:588
  722.4 27.7 %all-to-all-start.2 = ((bf16[8,48,2560]{2,1,0:T(8,128)(2,1)}), bf16[8,48,2560]{2,1,0:T(8,128)(2,1)S(1)}, u32[]{:S(2)}, u32[]{:S(2)}) async-start(bf16[8,48,2560]{2,1,0:T(8,128)(2,1)} %gather_fusion.4), calls=%async_computation.2 | async-start | bytes 3932160 | tf_op jit(solution)/shard_map/all_to_all | solution.py:828
  755.9 18.3 %collective-permute-done.39 = bf16[768,640]{1,0:T(8,128)(2,1)} collective-permute-done((bf16[768,640]{1,0:T(8,128)(2,1)}, bf16[768,640]{1,0:T(8,128)(2,1)}, u32[]{:S(2)}, u32[]{:S(2)}) %collective-permute-start.39) | collective-permute-done | bytes 983072 | tf_op jit(solution)/shard_map/ppermute | solution.py:23
  774.4 21.0 %collective-permute-done.41 = bf16[768,640]{1,0:T(8,128)(2,1)S(1)} collective-permute-done((bf16[768,640]{1,0:T(8,128)(2,1)S(1)}, bf16[768,640]{1,0:T(8,128)(2,1)S(1)}, u32[]{:S(2)}, u32[]{:S(2)}) %collective-permute-start.41) | collective-permute-done | bytes 983072 | tf_op jit(solution)/shard_map/ppermute | solution.py:23
  828.9 49.9 %shard_map.244.d_qkv_ref = bf16[1536,960]{1,0:T(8,128)(2,1)} custom-call(bf16[1536,1024]{1,0:T(8,128)(2,1)} %get-tuple-element.32.q_ref, bf16[1536,256]{1,0:T(8,128)(2,1)} %copy-done.33, bf16[1536,256]{1,0:T(8,128)(2,1)} %copy-done.34, bf16[1536,640]{1,0:T(8,128)(2,1)} %pad_maximum_fusion.1.grad_ref.refs_1_, f32[8,1536]{1,0:T(8,128)} %bitcast.223, ...), custom_call_target="tpu_custom_call" | custom-call | flops 149999992832 | tf_op jit(solution)/shard_map/pallas_call | solution.py:285
  878.8 17.6 %collective-permute-done.46.refs_1_.refs_2_ = bf16[224,2560]{1,0:T(8,128)(2,1)} collective-permute-done((bf16[224,2560]{1,0:T(8,128)(2,1)}, bf16[224,2560]{1,0:T(8,128)(2,1)}, u32[]{:S(2)}, u32[]{:S(2)}) %collective-permute-start.46) | collective-permute-done | bytes 1146912 | tf_op jit(solution)/shard_map/ppermute | solution.py:23
  896.4 20.6 %shard_map.247 = (bf16[1536,2560]{1,0:T(8,128)(2,1)}, f32[1,2560]{1,0:T(1,128)}) custom-call(s32[1]{0:T(128)} %bitcast.37.place_ref, bf16[1536,960]{1,0:T(8,128)(2,1)} %shard_map.244.d_qkv_ref, bf16[2560,1024]{1,0:T(8,128)(2,1)} %all-gather.5.cloned.1.call-done.weight_ref, bf16[1536,2560]{1,0:T(8,128)(2,1)} %bitcast.17.x_ref, f32[1,2560]{1,0:T(1,128)} %copy-done.28, ...), custom_call_target="tpu_custom_call" | custom-call | flops 60000002048 | tf_op jit(solution)/shard_map/pallas_call | solution.py:448
  952.7 19.3 %collective-permute-done.50 = bf16[192,2560]{1,0:T(8,128)(2,1)S(1)} collective-permute-done((bf16[192,2560]{1,0:T(8,128)(2,1)S(1)}, bf16[192,2560]{1,0:T(8,128)(2,1)S(1)}, u32[]{:S(2)}, u32[]{:S(2)}) %collective-permute-start.50) | collective-permute-done | bytes 983072 | tf_op jit(solution)/shard_map/ppermute | solution.py:23
  973.3 18.6 %collective-permute-done.55 = bf16[192,2560]{1,0:T(8,128)(2,1)S(1)} collective-permute-done((bf16[192,2560]{1,0:T(8,128)(2,1)S(1)}, bf16[192,2560]{1,0:T(8,128)(2,1)S(1)}, u32[]{:S(2)}, u32[]{:S(2)}) %collective-permute-start.55) | collective-permute-done | bytes 983072 | tf_op jit(solution)/shard_map/ppermute | solution.py:23
  1015.7 29.9 %collective-permute-done.64.refs_3_ = bf16[320,640]{1,0:T(8,128)(2,1)} collective-permute-done((bf16[320,640]{1,0:T(8,128)(2,1)}, bf16[320,640]{1,0:T(8,128)(2,1)}, u32[]{:S(2)}, u32[]{:S(2)}) %collective-permute-start.64) | collective-permute-done | bytes 409632 | tf_op jit(solution)/shard_map/ppermute | solution.py:23
  (437 shorter events, 535.9 us)
Async XLA Ops:
  16.5 128.6 %all-gather.5.cloned.1.call-start = ((), (), s32[]{:S(2)}) async-start(), calls=%async_computation.9 | async-start | bytes 5898240 | tf_op jit(solution)/shard_map/all_gather | solution.py:844
  60.5 209.2 %all-gather.7.cloned.1.call-start = ((), (), s32[]{:S(2)}) async-start(), calls=%async_computation.10 | async-start | bytes 3686400 | tf_op jit(solution)/shard_map/all_gather | solution.py:844
  62.3 325.9 %all-gather.9.cloned.1.call-start = ((), (), s32[]{:S(2)}) async-start(), calls=%async_computation.11 | async-start | bytes 20643840 | tf_op jit(solution)/shard_map/all_gather | solution.py:844
  207.8 104.2 %all-to-all-start.1 = ((bf16[8,48,2560]{2,1,0:T(8,128)(2,1)}), bf16[8,48,2560]{2,1,0:T(8,128)(2,1)}, u32[]{:S(2)}, u32[]{:S(2)}) async-start(bf16[8,48,2560]{2,1,0:T(8,128)(2,1)} %shard_map.229), calls=%async_computation.1 | async-start | bytes 3932160 | tf_op jit(solution)/shard_map/all_to_all | solution.py:828
  217.3 247.7 %all-gather.11.cloned.1.call-start = ((), (), s32[]{:S(2)}) async-start(), calls=%async_computation.12 | async-start | bytes 10321920 | tf_op jit(solution)/shard_map/all_gather | solution.py:844
  370.9 452.7 %reduce-scatter.6.cloned.1.call-start = ((), (), s32[]{:S(2)}) async-start(), calls=%async_computation.13 | async-start | bytes 10321920 | tf_op jit(solution)/shard_map/reduce_scatter | solution.py:837
  371.2 63.2 %collective-permute-start.22 = (bf16[192,2560]{1,0:T(8,128)(2,1)}, bf16[192,2560]{1,0:T(8,128)(2,1)}, u32[]{:S(2)}, u32[]{:S(2)}) collective-permute-start(bf16[192,2560]{1,0:T(8,128)(2,1)} %get-tuple-element.85), channel_id=1, source_target_pairs={{0,8},{8,0},{16,24},{24,16},{1,9},{9,1},{17,25},{25,17},{2,10},{10... | collective-permute-start | bytes 2949128 | tf_op jit(solution)/shard_map/ppermute | solution.py:23
  372.1 64.6 %collective-permute-start.23 = (bf16[192,2560]{1,0:T(8,128)(2,1)}, bf16[192,2560]{1,0:T(8,128)(2,1)}, u32[]{:S(2)}, u32[]{:S(2)}) collective-permute-start(bf16[192,2560]{1,0:T(8,128)(2,1)} %get-tuple-element.86), channel_id=1, source_target_pairs={{0,16},{8,24},{16,0},{24,8},{1,17},{9,25},{17,1},{25,9},{2,18},{10... | collective-permute-start | bytes 2949128 | tf_op jit(solution)/shard_map/ppermute | solution.py:23
  386.7 55.5 %collective-permute-start.26 = (bf16[192,2560]{1,0:T(8,128)(2,1)S(1)}, bf16[192,2560]{1,0:T(8,128)(2,1)}, u32[]{:S(2)}, u32[]{:S(2)}) collective-permute-start(bf16[192,2560]{1,0:T(8,128)(2,1)S(1)} %collective-permute-done.24), channel_id=1, source_target_pairs={{0,8},{8,0},{16,24},{24,16},{1,9},{9,1},{17,25},{25,17},{2,10},{10... | collective-permute-start | bytes 2949128 | tf_op jit(solution)/shard_map/ppermute | solution.py:23
  464.8 358.9 %reduce-scatter.8.cloned.1.call-start = ((), (), s32[]{:S(2)}) async-start(), calls=%async_computation.14 | async-start | bytes 10321920 | tf_op jit(solution)/shard_map/reduce_scatter | solution.py:837
  488.9 54.1 %collective-permute-start.27 = (bf16[192,2560]{1,0:T(8,128)(2,1)}, bf16[192,2560]{1,0:T(8,128)(2,1)S(1)}, u32[]{:S(2)}, u32[]{:S(2)}) collective-permute-start(bf16[192,2560]{1,0:T(8,128)(2,1)} %get-tuple-element.79), channel_id=1, source_target_pairs={{0,8},{8,0},{16,24},{24,16},{1,9},{9,1},{17,25},{25,17},{2,10},{10... | collective-permute-start | bytes 2949128 | tf_op jit(solution)/shard_map/ppermute | solution.py:23
  541.5 60.9 %collective-permute-start.32 = (bf16[192,2560]{1,0:T(8,128)(2,1)S(1)}, bf16[192,2560]{1,0:T(8,128)(2,1)S(1)}, u32[]{:S(2)}, u32[]{:S(2)}) collective-permute-start(bf16[192,2560]{1,0:T(8,128)(2,1)S(1)} %get-tuple-element.82), channel_id=1, source_target_pairs={{0,16},{8,24},{16,0},{24,8},{1,17},{9,25},{17,1},{25,9},{2,18},{10... | collective-permute-start | bytes 2949128 | tf_op jit(solution)/shard_map/ppermute | solution.py:23
  542.5 468.0 %reduce-scatter.12.cloned.1.call-start = ((), (), s32[]{:S(2)}) async-start(), calls=%async_computation.16 | async-start | bytes 3686400 | tf_op jit(solution)/shard_map/reduce_scatter | solution.py:837
  722.4 105.2 %all-to-all-start.2 = ((bf16[8,48,2560]{2,1,0:T(8,128)(2,1)}), bf16[8,48,2560]{2,1,0:T(8,128)(2,1)S(1)}, u32[]{:S(2)}, u32[]{:S(2)}) async-start(bf16[8,48,2560]{2,1,0:T(8,128)(2,1)} %gather_fusion.4), calls=%async_computation.2 | async-start | bytes 3932160 | tf_op jit(solution)/shard_map/all_to_all | solution.py:828
  750.1 262.8 %reduce-scatter.14.cloned.1.call-start = ((), (), s32[]{:S(2)}) async-start(), calls=%async_computation.17 | async-start | bytes 10321920 | tf_op jit(solution)/shard_map/reduce_scatter | solution.py:837
  755.6 60.9 %collective-permute-start.44 = (bf16[768,640]{1,0:T(8,128)(2,1)}, bf16[768,640]{1,0:T(8,128)(2,1)}, u32[]{:S(2)}, u32[]{:S(2)}) collective-permute-start(bf16[768,640]{1,0:T(8,128)(2,1)} %get-tuple-element.70), channel_id=1, source_target_pairs={{0,16},{8,24},{16,0},{24,8},{1,17},{9,25},{17,1},{25,9},{2,18},{10... | collective-permute-start | bytes 2949128 | tf_op jit(solution)/shard_map/ppermute | solution.py:23
  802.4 266.9 %reduce-scatter.10.cloned.1.call-start = ((), (), s32[]{:S(2)}) async-start(), calls=%async_computation.15 | async-start | bytes 5898240 | tf_op jit(solution)/shard_map/reduce_scatter | solution.py:837
  823.6 55.2 %collective-permute-start.49 = (bf16[320,1792]{1,0:T(8,128)(2,1)}, bf16[320,1792]{1,0:T(8,128)(2,1)}, u32[]{:S(2)}, u32[]{:S(2)}) collective-permute-start(bf16[320,1792]{1,0:T(8,128)(2,1)} %shard_map.246.refs_0_), channel_id=1, source_target_pairs={{0,16},{8,24},{16,0},{24,8},{1,17},{9,25},{17,1},{25,9},{2,18},{10... | collective-permute-start | bytes 3440648 | tf_op jit(solution)/shard_map/ppermute | solution.py:23
  823.9 55.0 %collective-permute-start.48 = (bf16[320,1792]{1,0:T(8,128)(2,1)}, bf16[320,1792]{1,0:T(8,128)(2,1)}, u32[]{:S(2)}, u32[]{:S(2)}) collective-permute-start(bf16[320,1792]{1,0:T(8,128)(2,1)} %shard_map.246.refs_0_), channel_id=1, source_target_pairs={{0,8},{8,0},{16,24},{24,16},{1,9},{9,1},{17,25},{25,17},{2,10},{10... | collective-permute-start | bytes 3440648 | tf_op jit(solution)/shard_map/ppermute | solution.py:23
  824.9 53.9 %collective-permute-start.47 = (bf16[224,2560]{1,0:T(8,128)(2,1)}, bf16[224,2560]{1,0:T(8,128)(2,1)}, u32[]{:S(2)}, u32[]{:S(2)}) collective-permute-start(bf16[224,2560]{1,0:T(8,128)(2,1)} %shard_map.245.refs_2_.refs_0_), channel_id=1, source_target_pairs={{0,24},{8,16},{16,8},{24,0},{1,25},{9,17},{17,9},{25,1},{2,26},{10... | collective-permute-start | bytes 3440648 | tf_op jit(solution)/shard_map/ppermute | solution.py:23
  826.3 70.1 %collective-permute-start.46 = (bf16[224,2560]{1,0:T(8,128)(2,1)}, bf16[224,2560]{1,0:T(8,128)(2,1)}, u32[]{:S(2)}, u32[]{:S(2)}) collective-permute-start(bf16[224,2560]{1,0:T(8,128)(2,1)} %shard_map.245.refs_2_.refs_0_), channel_id=1, source_target_pairs={{0,16},{8,24},{16,0},{24,8},{1,17},{9,25},{17,1},{25,9},{2,18},{10... | collective-permute-start | bytes 3440648 | tf_op jit(solution)/shard_map/ppermute | solution.py:23
  826.5 69.9 %collective-permute-start.45 = (bf16[224,2560]{1,0:T(8,128)(2,1)}, bf16[224,2560]{1,0:T(8,128)(2,1)}, u32[]{:S(2)}, u32[]{:S(2)}) collective-permute-start(bf16[224,2560]{1,0:T(8,128)(2,1)} %shard_map.245.refs_2_.refs_0_), channel_id=1, source_target_pairs={{0,8},{8,0},{16,24},{24,16},{1,9},{9,1},{17,25},{25,17},{2,10},{10... | collective-permute-start | bytes 3440648 | tf_op jit(solution)/shard_map/ppermute | solution.py:23
  994.5 134.3 %all-to-all-start.3 = ((bf16[8,48,2560]{2,1,0:T(8,128)(2,1)}), bf16[8,48,2560]{2,1,0:T(8,128)(2,1)}, u32[]{:S(2)}, u32[]{:S(2)}) async-start(bf16[8,48,2560]{2,1,0:T(8,128)(2,1)} %gather_fusion.6), calls=%async_computation.5 | async-start | bytes 3932160 | tf_op jit(solution)/shard_map/all_to_all | solution.py:828
  1009.3 61.9 %collective-permute-start.65 = (bf16[320,1792]{1,0:T(8,128)(2,1)S(1)}, bf16[320,1792]{1,0:T(8,128)(2,1)}, u32[]{:S(2)}, u32[]{:S(2)}) collective-permute-start(bf16[320,1792]{1,0:T(8,128)(2,1)S(1)} %copy-done.13), channel_id=1, source_target_pairs={{0,24},{8,16},{16,8},{24,0},{1,25},{9,17},{17,9},{25,1},{2,26},{10... | collective-permute-start | bytes 3440648 | tf_op jit(solution)/shard_map/ppermute | solution.py:23
  (124 other events, 2575.5 us)
Sparse Core Ops, SparseCore 0:
  60.6 56.2 all-gather.4
  118.6 38.8 all-gather.6
  159.7 199.8 all-gather.8
  371.1 91.4 all-gather.10
  465.3 106.0 reduce-scatter.5
  574.2 95.2 reduce-scatter.7
  679.7 62.3 reduce-scatter.11
  802.5 98.0 reduce-scatter.13
  929.6 62.3 reduce-scatter.9

commit v6 on v5

--- a/solution.py
+++ b/solution.py
@@ -37,7 +37,8 @@
     first, second = value[:half], value[half:]
     x_first, y_second = swap(first, 1), swap(second, 2)
     x_second, y_first = swap(second, 1), swap(first, 2)
-    far_first, far_second = swap(x_first, 2), swap(y_second, 1)
+    far_first, far_second = (after(v, *hold) if hold else v for v in (x_first, y_second))
+    far_first, far_second = swap(far_first, 2), swap(far_second, 1)
     out = jnp.zeros((size,) + value.shape, value.dtype)
     if hold:
         out = after(out, *hold)
@@ -69,11 +70,12 @@
     return jnp.stack(here, axis=0)
 
 
-def scatter_sp(parts, *hold):
+def scatter_sp(parts, hook=None):
     size = lax.axis_size("sp")
     if size != 4:
         summed = lax.psum_scatter(parts, "sp", scatter_dimension=0, tiled=False)
-        return summed.astype(jnp.float32), ((summed,), (summed,))
+        given = hook((summed,)) if hook else ()
+        return summed.astype(jnp.float32), (summed,), (summed,), given
     place = lax.axis_index("sp")
     half = parts.shape[1] // 2
     parts = row_major(parts)
@@ -84,16 +86,26 @@
 
     wide = jnp.float32
     low = parts.dtype
+
+    def added(*values):
+        values = lax.optimization_barrier(values)
+        total = values[0].astype(wide)
+        for value in values[1:]:
+            total = total + value.astype(wide)
+        return total
+
     from_x, from_y = swap(block(3, True), 1), swap(block(3, False), 2)
-    if hold:
-        from_x = after(from_x, *hold)
+    given = hook((from_x, from_y)) if hook else ()
+    if given:
+        from_x, from_y = after(from_x, *given), after(from_y, *given)
     x_first, y_second = swap(block(1, True), 1), swap(block(2, False), 2)
-    y_sent = (block(2, True).astype(wide) + from_x.astype(wide)).astype(low)
-    x_sent = (block(1, False).astype(wide) + from_y.astype(wide)).astype(low)
+    y_sent = added(block(2, True), from_x).astype(low)
+    x_sent = added(block(1, False), from_y).astype(low)
     y_first, x_second = swap(y_sent, 2), swap(x_sent, 1)
-    first = block(0, True).astype(wide) + x_first.astype(wide) + y_first.astype(wide)
-    second = block(0, False).astype(wide) + x_second.astype(wide) + y_second.astype(wide)
-    return jnp.concatenate([first, second], axis=0), ((y_sent, x_sent), (x_first, y_second))
+    first = added(block(0, True), x_first, y_first)
+    second = added(block(0, False), y_second, x_second)
+    stage = (y_sent, x_sent, x_first, y_second)
+    return jnp.concatenate([first, second], axis=0), stage, (y_first, x_second), given
 
 
 def rotary_tables(positions):
@@ -173,7 +185,7 @@
         ],
         compiler_params=pltpu.CompilerParams(vmem_limit_bytes=48 * 2**20),
         cost_estimate=pl.CostEstimate(
-            flops=72 * 10**9, bytes_accessed=0, transcendentals=0
+            flops=120 * 10**9, bytes_accessed=0, transcendentals=0
         ),
     )(x, gain, weight, cosine, sine)
 
@@ -220,7 +232,7 @@
         scratch_shapes=[pltpu.VMEM((block, total), jnp.float32)],
         compiler_params=pltpu.CompilerParams(vmem_limit_bytes=56 * 2**20),
         cost_estimate=pl.CostEstimate(
-            flops=84 * 10**9, bytes_accessed=0, transcendentals=0
+            flops=140 * 10**9, bytes_accessed=0, transcendentals=0
         ),
     )(q, k, v, start, *when)
 
@@ -294,7 +306,7 @@
         ],
         compiler_params=pltpu.CompilerParams(vmem_limit_bytes=56 * 2**20),
         cost_estimate=pl.CostEstimate(
-            flops=150 * 10**9, bytes_accessed=0, transcendentals=0
+            flops=250 * 10**9, bytes_accessed=0, transcendentals=0
         ),
     )(q, k, v, grad, lse_rows, start_row, cosine, sine_back, *when)
 
@@ -329,7 +341,7 @@
         out_shape=[jax.ShapeDtypeStruct((total, units), jnp.bfloat16)] * 3,
         compiler_params=pltpu.CompilerParams(vmem_limit_bytes=56 * 2**20),
         cost_estimate=pl.CostEstimate(
-            flops=111 * 10**9, bytes_accessed=0, transcendentals=0
+            flops=185 * 10**9, bytes_accessed=0, transcendentals=0
         ),
     )(x, weights, weights)
 
@@ -363,7 +375,7 @@
         out_shape=[jax.ShapeDtypeStruct((total, units), jnp.bfloat16)] * 2,
         compiler_params=pltpu.CompilerParams(vmem_limit_bytes=56 * 2**20),
         cost_estimate=pl.CostEstimate(
-            flops=78 * 10**9, bytes_accessed=0, transcendentals=0
+            flops=130 * 10**9, bytes_accessed=0, transcendentals=0
         ),
     )(incoming, down, gate, up, *when)
 
@@ -419,7 +431,7 @@
         ],
         compiler_params=pltpu.CompilerParams(vmem_limit_bytes=60 * 2**20),
         cost_estimate=pl.CostEstimate(
-            flops=132 * 10**9, bytes_accessed=0, transcendentals=0
+            flops=220 * 10**9, bytes_accessed=0, transcendentals=0
         ),
     )(d_gate, d_up, weights, x, gain, *when)
 
@@ -464,7 +476,7 @@
         ],
         compiler_params=pltpu.CompilerParams(vmem_limit_bytes=56 * 2**20),
         cost_estimate=pl.CostEstimate(
-            flops=60 * 10**9, bytes_accessed=0, transcendentals=0
+            flops=100 * 10**9, bytes_accessed=0, transcendentals=0
         ),
     )(place, d_qkv, weights, x, gain, own, *when)
 
@@ -488,7 +500,7 @@
         out_shape=jax.ShapeDtypeStruct((parts, total, rows), jnp.bfloat16),
         compiler_params=pltpu.CompilerParams(vmem_limit_bytes=32 * 2**20),
         cost_estimate=pl.CostEstimate(
-            flops=24 * 10**9, bytes_accessed=0, transcendentals=0
+            flops=40 * 10**9, bytes_accessed=0, transcendentals=0
         ),
     )(d_branch, weights, *when)
 
@@ -521,7 +533,7 @@
         out_specs=[row, row],
         out_shape=[jax.ShapeDtypeStruct((total, parts * share), jnp.bfloat16)] * 2,
         compiler_params=pltpu.CompilerParams(vmem_limit_bytes=32 * 2**20),
-        cost_estimate=pl.CostEstimate(flops=24 * 10**9, bytes_accessed=0, transcendentals=0),
+        cost_estimate=pl.CostEstimate(flops=40 * 10**9, bytes_accessed=0, transcendentals=0),
     )(stack, gain)
 
 
@@ -551,7 +563,7 @@
         out_specs=row,
         out_shape=jax.ShapeDtypeStruct((total, columns), jnp.bfloat16),
         compiler_params=pltpu.CompilerParams(vmem_limit_bytes=40 * 2**20),
-        cost_estimate=pl.CostEstimate(flops=27 * 10**9, bytes_accessed=0, transcendentals=0),
+        cost_estimate=pl.CostEstimate(flops=45 * 10**9, bytes_accessed=0, transcendentals=0),
     )(stack, weight, x)
 
 
@@ -573,7 +585,7 @@
         out_specs=pl.BlockSpec((rows, columns), lambda i: (i, 0)),
         out_shape=jax.ShapeDtypeStruct((parts * rows, columns), jnp.bfloat16),
         compiler_params=pltpu.CompilerParams(vmem_limit_bytes=40 * 2**20),
-        cost_estimate=pl.CostEstimate(flops=45 * 10**9, bytes_accessed=0, transcendentals=0),
+        cost_estimate=pl.CostEstimate(flops=0 * 10**9, bytes_accessed=0, transcendentals=0),
     )(stack, right, *when)
 
 
@@ -596,7 +608,7 @@
         out_specs=pl.BlockSpec((rows, block), lambda j: (0, j)),
         out_shape=jax.ShapeDtypeStruct((rows, columns), jnp.bfloat16),
         compiler_params=pltpu.CompilerParams(vmem_limit_bytes=56 * 2**20),
-        cost_estimate=pl.CostEstimate(flops=60 * 10**9, bytes_accessed=0, transcendentals=0),
+        cost_estimate=pl.CostEstimate(flops=0 if when else 100 * 10**9, bytes_accessed=0, transcendentals=0),
     )(left, right, *when)
 
 
@@ -621,7 +633,7 @@
         out_specs=pl.BlockSpec((total, block), lambda j: (0, j)),
         out_shape=jax.ShapeDtypeStruct((total, columns), jnp.bfloat16),
         compiler_params=pltpu.CompilerParams(vmem_limit_bytes=56 * 2**20),
-        cost_estimate=pl.CostEstimate(flops=60 * 10**9, bytes_accessed=0, transcendentals=0),
+        cost_estimate=pl.CostEstimate(flops=100 * 10**9, bytes_accessed=0, transcendentals=0),
     )(left, right, *when)
 
 
@@ -651,11 +663,11 @@
         out_specs=pl.BlockSpec((block, columns), lambda i: (i, 0)),
         out_shape=jax.ShapeDtypeStruct((width, columns), jnp.bfloat16),
         compiler_params=pltpu.CompilerParams(vmem_limit_bytes=48 * 2**20),
-        cost_estimate=pl.CostEstimate(flops=36 * 10**9, bytes_accessed=0, transcendentals=0),
+        cost_estimate=pl.CostEstimate(flops=60 * 10**9, bytes_accessed=0, transcendentals=0),
     )(normed, d_qkv, gain_grads, *when)
 
 
-def pieces_sp(value, split):
+def pieces_sp(value, split, *hold):
     size = lax.axis_size("sp")
     columns = value.shape[1]
     if not split or size != 4 or columns % (2 * LANES):
@@ -665,7 +677,8 @@
     left, right = value[:, :half], value[:, half:]
     x_left, y_right = swap(left, 1), swap(right, 2)
     x_right, y_left = swap(right, 1), swap(left, 2)
-    far_left, far_right = swap(x_left, 2), swap(y_right, 1)
+    far_left, far_right = (after(v, *hold) if hold else v for v in (x_left, y_right))
+    far_left, far_right = swap(far_left, 2), swap(far_right, 1)
     return (
         [(left, right), (x_left, x_right), (y_left, y_right), (far_left, far_right)],
         [x_left, y_right, x_right, y_left],
@@ -718,7 +731,7 @@
             out_ref[place_ref[0] ^ turn, :, chunk * size : (chunk + 1) * size] = value
 
 
-def stack_call(place, pieces):
+def stack_call(place, pieces, *when):
     count, chunks = len(pieces), len(pieces[0])
     rows, columns = pieces[0][0].shape
     block = 32 if rows % 32 == 0 else rows
@@ -726,14 +739,15 @@
         functools.partial(stack_kernel, count, chunks),
         grid=(rows // block,),
         in_specs=[pl.BlockSpec(memory_space=pltpu.SMEM)]
-        + [pl.BlockSpec((block, columns), lambda i: (i, 0))] * (count * chunks),
+        + [pl.BlockSpec((block, columns), lambda i: (i, 0))] * (count * chunks)
+        + [pl.BlockSpec(memory_space=pl.ANY)] * len(when),
         out_specs=pl.BlockSpec((count, block, chunks * columns), lambda i: (0, i, 0)),
         out_shape=jax.ShapeDtypeStruct((count, rows, chunks * columns), jnp.float32),
         compiler_params=pltpu.CompilerParams(vmem_limit_bytes=40 * 2**20),
         cost_estimate=pl.CostEstimate(
             flops=0, bytes_accessed=6 * count * chunks * rows * columns, transcendentals=0
         ),
-    )(place, *[chunk for piece in pieces for chunk in piece]).reshape(count * rows, chunks * columns)
+    )(place, *[chunk for piece in pieces for chunk in piece], *when).reshape(count * rows, chunks * columns)
 
 
 def pass_kernel(*refs):
@@ -859,8 +873,8 @@
         [column_share(w_query), column_share(key_weight), column_share(value_weight), gains], axis=1
     )
     came_incoming = deal(after(picked(cotangent), came_tokens))
-    qkv_all = gather_fsdp(after(qkv_shard, came_tokens))
     out_all = gather_fsdp(column_share(w_out))
+    qkv_all = gather_fsdp(after(qkv_shard, came_tokens, out_all))
     gate_up_all = gather_fsdp(gate_up_shard)
     down_all = gather_fsdp(lax.dynamic_slice_in_dim(w_down, sp_place * ff_share, ff_share, axis=0))
     gain_one = qkv_all[:, qkv_cols].astype(wide)[None, :]
@@ -897,52 +911,57 @@
     result_part = product_call(active_low, down_all, grad_down)
     d_gate, d_up = unit_back_call(group_incoming, down_all, gate, upward, result_part)
     grad_gate = rows_call(normed_two, d_gate)
-    result_sum, (sums_result, _) = scatter_sp(result_part.reshape(parts, rows, width), grad_gate)
+    result_sum, sums_result, last_result, _ = scatter_sp(
+        result_part.reshape(parts, rows, width), lambda first: (grad_gate,)
+    )
     own_hidden_rows = lax.dynamic_slice_in_dim(hidden_low, sp_place * rows, rows, axis=0)
     blocks_result = blocks_back((own_hidden_rows.astype(wide) + result_sum).astype(low))
 
     back_two, grad_gain_two = mlp_back_call(
         d_gate, d_up, gate_up_all, hidden_low, gain_two, parts, grad_gate, *sums_result
     )
-    back_two = after(back_two, result_sum)
-    from_others, _ = scatter_sp(back_two)
-    grad_up = rows_call(normed_two, d_up, back_two)
+    from_others, _, _, (grad_up,) = scatter_sp(
+        after(back_two, *last_result), lambda first: (rows_call(normed_two, d_up, *first),)
+    )
     gone_result = deal(blocks_result)
     own_d_hidden = own_columns(group_incoming).astype(wide) + from_others
     d_branch = own_d_hidden.astype(low)
-    grad_up = after(grad_up, d_branch)
-    grad_out = stack_rows_call(mixed, d_branch)
-    d_mixed, _ = scatter_sp(out_back_call(d_branch, out_all, parts, grad_up), grad_out)
+    d_mixed, _, _, (grad_out,) = scatter_sp(
+        out_back_call(d_branch, out_all, parts), lambda first: (stack_rows_call(mixed, d_branch, *first),)
+    )
     d_mixed = d_mixed.astype(low)
 
     down_sum = after(scatter_fsdp(grad_down), d_mixed)
-    gate_sum = after(scatter_fsdp(grad_gate), d_mixed, down_sum)
     down_pieces, down_first, _ = pieces_sp(down_sum, False)
+    gate_sum = after(scatter_fsdp(grad_gate), *down_first)
     gate_pieces, gate_first, _ = pieces_sp(gate_sum, False)
     d_qkv = attend_back_call(
         query_low, key_low, value_low, d_mixed, logs.T, start[None, :], cosine, sine, gone_result
     )
     back_one, grad_gain_one = attend_norm_call(
-        place, d_qkv, qkv_all, group_inputs, gain_one, own_d_hidden, parts, *down_first, *gate_first[:-1]
+        place, d_qkv, qkv_all, group_inputs, gain_one, own_d_hidden, parts, *down_first
     )
     gain_grads = jnp.concatenate(
         [grad_gain_one, grad_gain_two, jnp.zeros((6, width), wide)], axis=0
     )
-    grad_qkv = qkv_grad_call(normed, d_qkv, gain_grads, qkv_all.shape[1])
-    d_inputs = scatter_sp(back_one.reshape(parts, rows, width))[0]
+    layer_out = rows_of(gone_result, target).reshape(tokens.shape)
+
+    grad_qkv = qkv_grad_call(normed, d_qkv, gain_grads, qkv_all.shape[1], *gate_first[:-1])
+    d_inputs, _, _, (down_shard, layer_out) = scatter_sp(
+        back_one.reshape(parts, rows, width),
+        lambda first: (stack_call(place, down_pieces, *first), layer_out),
+    )
     gone_grad = deal(blocks_back(d_inputs.astype(low)))
-    layer_out = rows_of(gone_result, target).reshape(tokens.shape)
     input_grad = rows_of(gone_grad, target).reshape(tokens.shape)
 
-    up_pieces = pieces_sp(scatter_fsdp(grad_up), True)[0]
-    out_pieces = pieces_sp(scatter_fsdp(grad_out), False)[0]
-    qkv_pieces = pieces_sp(scatter_fsdp(grad_qkv), True)[0]
-
-    down_shard = stack_call(place, down_pieces)
     hidden_layout = [
         (j * ff_share, ff_share, 0, j * parts * ff_share, ff_share) for j in range(groups)
     ]
     (gate_shard,) = spread_call(place, gate_pieces, hidden_layout, [w_gate.shape[1]])
+    up_pieces, up_first, _ = pieces_sp(scatter_fsdp(after(grad_up, d_branch)), True)
+    out_sum = after(scatter_fsdp(after(grad_out, d_mixed)), *up_first[:2])
+    out_pieces = pieces_sp(out_sum, False)[0]
+    qkv_pieces = pieces_sp(after(scatter_fsdp(grad_qkv), out_sum), True, gate_shard)[0]
     (up_shard,) = spread_call(place, up_pieces, hidden_layout, [w_up.shape[1]])
     (out_shard,) = spread_call(place, out_pieces, [(0, share, 0, 0, share)], [width])
     qkv_layout = [

time: 1160 us -> 1110 us (0.957)
  waiting for transfers between devices: 425 us -> 386 us
    ppermute x72, waiting for transfers between devices: 361 us -> 277 us  [swap(): return lax.ppermute(value, 'sp', [(i, i ^ bit) for i in range(size)])]
    all_to_all x4, waiting for transfers between devices: 63.8 us -> 109 us  [deal(): lax.all_to_all(blocks, 'fsdp', split_axis=0, concat_axis=0, tiled=True)]
    unnamed x126 -> x178, local copies, waits for them, and re-layouts: 39.8 us -> 40.2 us
  transfers between devices with their start and end apart: 85 -> 85, of which waited for: 33 -> 33; matrix products, arithmetic and copies ran while one was open for 14% -> 15% of each run, Pallas kernels for 33% -> 34%
where the time goes in v6:
time: 1110 us; the launch traced here: 1100 us
  waiting for transfers between devices  386 us (35%)
  Pallas kernels  384 us (35%)
  local copies, waits for them, and re-layouts  157 us (14%)
  starting transfers between devices  107 us (10%)
  other arithmetic  50.8 us (5%)
  between operations  15.5 us (1%)
    ppermute x72, waiting for transfers between devices, swap(): return lax.ppermute(value, 'sp', [(i, i ^ bit) for i in range(size)])  277 us
    all_to_all x4, waiting for transfers between devices, deal(): lax.all_to_all(blocks, 'fsdp', split_axis=0, concat_axis=0, tiled=True)  109 us
    pallas_call x3, Pallas kernels, rows_call(): pl.pallas_call(rows_kernel, grid=(columns // block,), in_specs=[pl.BlockS...  61.6 us
    ppermute x72, starting transfers between devices, swap(): return lax.ppermute(value, 'sp', [(i, i ^ bit) for i in range(size)])  54 us
    all_to_all x4, starting transfers between devices, deal(): lax.all_to_all(blocks, 'fsdp', split_axis=0, concat_axis=0, tiled=True)  51.5 us
    pallas_call x1, Pallas kernels, attend_back_call(): pl.pallas_call(functools.partial(attend_back_kernel, heads, keys, block),...  49.8 us
    pallas_call x1, Pallas kernels, mlp_back_call(): pl.pallas_call(mlp_back_kernel, grid=(total // block,), in_specs=[row(uni...  43.4 us
    unnamed x178, local copies, waits for them, and re-layouts  40.2 us
  transfers between devices with their start and end apart: 85, of which 33 were waited for; matrix products, arithmetic and copies ran while one was open for 15% of the time, Pallas kernels for 34%

profile of v6, /device:TPU:9, one launch (start us, length us, event | category | flops | bytes accessed | tf_op | source)
XLA Modules:
  0.0 1100.9 jit_solution(8579763707844490206)
XLA Ops:
  21.4 65.4 %all-to-all-done.refs_1_._ = bf16[8,48,2560]{2,1,0:T(8,128)(2,1)S(1)} async-done(((bf16[8,48,2560]{2,1,0:T(8,128)(2,1)}), bf16[8,48,2560]{2,1,0:T(8,128)(2,1)S(1)}, u32[]{:S(2)}, u32[]{:S(2)}) %all-to-all-start) | async-done | bytes 1966112 | tf_op jit(solution)/shard_map/all_to_all | solution.py:842
  130.4 16.3 %collective-permute-done.1 = bf16[192,2560]{1,0:T(8,128)(2,1)} collective-permute-done((bf16[192,2560]{1,0:T(8,128)(2,1)}, bf16[192,2560]{1,0:T(8,128)(2,1)}, u32[]{:S(2)}, u32[]{:S(2)}) %collective-permute-start.1) | collective-permute-done | bytes 983072 | tf_op jit(solution)/shard_map/ppermute | solution.py:23
  153.3 15.4 %collective-permute-done.4 = bf16[192,2560]{1,0:T(8,128)(2,1)S(1)} collective-permute-done((bf16[192,2560]{1,0:T(8,128)(2,1)}, bf16[192,2560]{1,0:T(8,128)(2,1)S(1)}, u32[]{:S(2)}, u32[]{:S(2)}) %collective-permute-start.4) | collective-permute-done | bytes 983072 | tf_op jit(solution)/shard_map/ppermute | solution.py:23
  173.8 23.5 %shard_map.222 = (bf16[1536,2560]{1,0:T(8,128)(2,1)}, bf16[1536,1024]{1,0:T(8,128)(2,1)}, bf16[1536,256]{1,0:T(8,128)(2,1)S(1)}, bf16[1536,256]{1,0:T(8,128)(2,1)S(1)}) custom-call(bf16[1536,2560]{1,0:T(8,128)(2,1)} %bitcast.17.x_ref, f32[1,2560]{1,0:T(1,128)S(1)} %reshape.298.gain_ref, bf16[2560,1024]{1,0:T(8,128)(2,1)} %all-gather.7.cloned.1.call-done.weight_ref, ...), custom_call_target="tpu_custom_call" | custom-call | flops 120000004096 | tf_op jit(solution)/shard_map/pallas_call | solution.py:175
  199.1 27.6 %shard_map.223 = (bf16[1536,640]{1,0:T(8,128)(2,1)}, f32[1536,8]{1,0:T(8,128)}) custom-call(bf16[1536,1024]{1,0:T(8,128)(2,1)} %get-tuple-element.72.q_ref, bf16[1536,256]{1,0:T(8,128)(2,1)} %copy-done.46, bf16[1536,256]{1,0:T(8,128)(2,1)} %copy-done.47, s32[1536,1]{1,0:T(8,128)} %broadcast_in_dim.224.start_ref), custom_call_target="tpu_custom_call" | custom-call | flops 140000002048 | tf_op jit(solution)/shard_map/pallas_call | solution.py:224
  253.9 19.1 %collective-permute-done.10 = bf16[768,640]{1,0:T(8,128)(2,1)S(1)} collective-permute-done((bf16[768,640]{1,0:T(8,128)(2,1)}, bf16[768,640]{1,0:T(8,128)(2,1)S(1)}, u32[]{:S(2)}, u32[]{:S(2)}) %collective-permute-start.10) | collective-permute-done | bytes 983072 | tf_op jit(solution)/shard_map/ppermute | solution.py:23
  273.5 19.6 %collective-permute-done.13 = bf16[768,640]{1,0:T(8,128)(2,1)S(1)} collective-permute-done((bf16[768,640]{1,0:T(8,128)(2,1)}, bf16[768,640]{1,0:T(8,128)(2,1)S(1)}, u32[]{:S(2)}, u32[]{:S(2)}) %collective-permute-start.13) | collective-permute-done | bytes 983072 | tf_op jit(solution)/shard_map/ppermute | solution.py:23
  313.9 24.0 %all-to-all-done.1.refs_0_ = bf16[8,48,2560]{2,1,0:T(8,128)(2,1)} async-done(((bf16[8,48,2560]{2,1,0:T(8,128)(2,1)}), bf16[8,48,2560]{2,1,0:T(8,128)(2,1)}, u32[]{:S(2)}, u32[]{:S(2)}) %all-to-all-start.1) | async-done | bytes 1966112 | tf_op jit(solution)/shard_map/all_to_all | solution.py:842
  352.8 17.6 %collective-permute-done.19 = bf16[768,640]{1,0:T(8,128)(2,1)S(1)} collective-permute-done((bf16[768,640]{1,0:T(8,128)(2,1)}, bf16[768,640]{1,0:T(8,128)(2,1)S(1)}, u32[]{:S(2)}, u32[]{:S(2)}) %collective-permute-start.19) | collective-permute-done | bytes 983072 | tf_op jit(solution)/shard_map/ppermute | solution.py:23
  393.4 36.8 %shard_map.227 = (bf16[1536,1792]{1,0:T(8,128)(2,1)}, bf16[1536,1792]{1,0:T(8,128)(2,1)}, bf16[1536,1792]{1,0:T(8,128)(2,1)}) custom-call(bf16[1536,2560]{1,0:T(8,128)(2,1)} %copy-done.5, bf16[2560,3584]{1,0:T(8,128)(2,1)} %all-gather.9.cloned.1.call-done.gate_weight_ref.up_weight_ref.weight_ref, ...), custom_call_target="tpu_custom_call" | custom-call | flops 185000001536 | tf_op jit(solution)/shard_map/pallas_call | solution.py:332
  465.7 20.3 %shard_map.234.refs_0_ = bf16[1792,2560]{1,0:T(8,128)(2,1)} custom-call(bf16[1536,1792]{1,0:T(8,128)(2,1)} %get-tuple-element.78.refs_1_.left_ref, bf16[1536,2560]{1,0:T(8,128)(2,1)} %bitcast.192), custom_call_target="tpu_custom_call" | custom-call | flops 99999997952 | tf_op jit(solution)/shard_map/pallas_call | solution.py:600
  486.3 20.0 %shard_map.235.refs_0_ = bf16[1536,2560]{1,0:T(8,128)(2,1)} custom-call(bf16[1536,1792]{1,0:T(8,128)(2,1)} %get-tuple-element.78.refs_1_.left_ref, bf16[1792,2560]{1,0:T(8,128)(2,1)} %all-gather.11.cloned.1.call-done.right_ref.down_ref, bf16[1792,2560]{1,0:T(8,128)(2,1)} %shard_map.234.refs_0_), custom_call_target="tpu_custom_call" | custom-call | flops 99999997952 | tf_op jit(solution)/shard_map/pallas_call | solution.py:625
  515.7 25.6 %shard_map.236 = (bf16[1536,1792]{1,0:T(8,128)(2,1)}, bf16[1536,1792]{1,0:T(8,128)(2,1)}) custom-call(bf16[1536,2560]{1,0:T(8,128)(2,1)} %bitcast.193, bf16[1792,2560]{1,0:T(8,128)(2,1)} %all-gather.11.cloned.1.call-done.right_ref.down_ref, bf16[1536,1792]{1,0:T(8,128)(2,1)} %get-tuple-element.79.gate_ref, bf16[1536,1792]{1,0:T(8,128)(2,1)} %get-tuple-element.80.up_ref, ...), custom_call_target="tpu_custom_call" | custom-call | flops 130000003072 | tf_op jit(solution)/shard_map/pallas_call | solution.py:364
  541.3 20.5 %shard_map.237.refs_1_.refs_0_ = bf16[2560,1792]{1,0:T(8,128)(2,1)} custom-call(bf16[1536,2560]{1,0:T(8,128)(2,1)} %copy-done.5, bf16[1536,1792]{1,0:T(8,128)(2,1)} %get-tuple-element.81.right_ref.d_gate_ref), custom_call_target="tpu_custom_call" | custom-call | flops 99999997952 | tf_op jit(solution)/shard_map/pallas_call | solution.py:600
  569.7 43.4 %shard_map.240 = (bf16[4,1536,640]{2,1,0:T(8,128)(2,1)}, f32[1,2560]{1,0:T(1,128)}) custom-call(bf16[1536,1792]{1,0:T(8,128)(2,1)} %get-tuple-element.81.right_ref.d_gate_ref, bf16[1536,1792]{1,0:T(8,128)(2,1)} %get-tuple-element.92.d_up_ref.right_ref, bf16[2560,3584]{1,0:T(8,128)(2,1)} %all-gather.9.cloned.1.call-done.gate_weight_ref.up_weight_ref.weight_ref, ...), custom_call_target="tpu_custom_call" | custom-call | flops 219999993856 | tf_op jit(solution)/shard_map/pallas_call | solution.py:419
  635.9 20.8 %shard_map.242.refs_1_.refs_0_ = bf16[2560,1792]{1,0:T(8,128)(2,1)} custom-call(bf16[1536,2560]{1,0:T(8,128)(2,1)} %copy-done.5, bf16[1536,1792]{1,0:T(8,128)(2,1)} %get-tuple-element.92.d_up_ref.right_ref, bf16[768,640]{1,0:T(8,128)(2,1)} %copy-done.51, bf16[768,640]{1,0:T(8,128)(2,1)} %copy-done.50), custom_call_target="tpu_custom_call" | custom-call | tf_op jit(solution)/shard_map/pallas_call | solution.py:600
  660.5 14.7 %collective-permute-done.38 = bf16[768,640]{1,0:T(8,128)(2,1)S(1)} collective-permute-done((bf16[768,640]{1,0:T(8,128)(2,1)S(1)}, bf16[768,640]{1,0:T(8,128)(2,1)S(1)}, u32[]{:S(2)}, u32[]{:S(2)}) %collective-permute-start.38) | collective-permute-done | bytes 983072 | tf_op jit(solution)/shard_map/ppermute | solution.py:23
  708.2 23.5 %all-to-all-start.2 = ((bf16[8,48,2560]{2,1,0:T(8,128)(2,1)}), bf16[8,48,2560]{2,1,0:T(8,128)(2,1)}, u32[]{:S(2)}, u32[]{:S(2)}) async-start(bf16[8,48,2560]{2,1,0:T(8,128)(2,1)} %gather_fusion.4), calls=%async_computation.2 | async-start | bytes 3932160 | tf_op jit(solution)/shard_map/all_to_all | solution.py:842
  754.9 21.6 %collective-permute-done.44 = bf16[768,640]{1,0:T(8,128)(2,1)} collective-permute-done((bf16[768,640]{1,0:T(8,128)(2,1)}, bf16[768,640]{1,0:T(8,128)(2,1)}, u32[]{:S(2)}, u32[]{:S(2)}) %collective-permute-start.44) | collective-permute-done | bytes 983072 | tf_op jit(solution)/shard_map/ppermute | solution.py:23
  785.6 19.8 %all-to-all-done.2.refs_0_ = bf16[8,48,2560]{2,1,0:T(8,128)(2,1)} async-done(((bf16[8,48,2560]{2,1,0:T(8,128)(2,1)}), bf16[8,48,2560]{2,1,0:T(8,128)(2,1)}, u32[]{:S(2)}, u32[]{:S(2)}) %all-to-all-start.2) | async-done | bytes 1966112 | tf_op jit(solution)/shard_map/all_to_all | solution.py:842
  805.4 49.8 %shard_map.249.d_qkv_ref = bf16[1536,960]{1,0:T(8,128)(2,1)} custom-call(bf16[1536,1024]{1,0:T(8,128)(2,1)} %get-tuple-element.72.q_ref, bf16[1536,256]{1,0:T(8,128)(2,1)} %copy-done.46, bf16[1536,256]{1,0:T(8,128)(2,1)} %copy-done.47, bf16[1536,640]{1,0:T(8,128)(2,1)} %pad_maximum_fusion.grad_ref.refs_1_, f32[8,1536]{1,0:T(8,128)} %bitcast.205, ...), custom_call_target="tpu_custom_call" | custom-call | flops 249999998976 | tf_op jit(solution)/shard_map/pallas_call | solution.py:297
  856.8 20.6 %shard_map.251 = (bf16[1536,2560]{1,0:T(8,128)(2,1)}, f32[1,2560]{1,0:T(1,128)}) custom-call(s32[1]{0:T(128)} %bitcast.37.place_ref, bf16[1536,960]{1,0:T(8,128)(2,1)} %shard_map.249.d_qkv_ref, bf16[2560,1024]{1,0:T(8,128)(2,1)} %all-gather.7.cloned.1.call-done.weight_ref, bf16[1536,2560]{1,0:T(8,128)(2,1)} %bitcast.17.x_ref, f32[1,2560]{1,0:T(1,128)} %copy-done.43, ...), custom_call_target="tpu_custom_call" | custom-call | flops 99999997952 | tf_op jit(solution)/shard_map/pallas_call | solution.py:460
  944.4 21.3 %collective-permute-done.53 = bf16[192,2560]{1,0:T(8,128)(2,1)S(1)} collective-permute-done((bf16[192,2560]{1,0:T(8,128)(2,1)S(1)}, bf16[192,2560]{1,0:T(8,128)(2,1)S(1)}, u32[]{:S(2)}, u32[]{:S(2)}) %collective-permute-start.53) | collective-permute-done | bytes 983072 | tf_op jit(solution)/shard_map/ppermute | solution.py:23
  988.7 35.2 %collective-permute-done.57.refs_2_.refs_5_ = bf16[320,896]{1,0:T(8,128)(2,1)S(1)} collective-permute-done((bf16[320,896]{1,0:T(8,128)(2,1)S(1)}, bf16[320,896]{1,0:T(8,128)(2,1)S(1)}, u32[]{:S(2)}, u32[]{:S(2)}) %collective-permute-start.57) | collective-permute-done | bytes 573472 | tf_op jit(solution)/shard_map/ppermute | solution.py:23
  (506 shorter events, 463.0 us)
Async XLA Ops:
  7.2 79.6 %all-gather.5.cloned.1.call-start = ((), (), s32[]{:S(2)}) async-start(), calls=%async_computation.9 | async-start | bytes 3686400 | tf_op jit(solution)/shard_map/all_gather | solution.py:858
  12.0 74.8 %all-to-all-start = ((bf16[8,48,2560]{2,1,0:T(8,128)(2,1)}), bf16[8,48,2560]{2,1,0:T(8,128)(2,1)S(1)}, u32[]{:S(2)}, u32[]{:S(2)}) async-start(bf16[8,48,2560]{2,1,0:T(8,128)(2,1)} %gather_fusion), calls=%async_computation | async-start | bytes 3932160 | tf_op jit(solution)/shard_map/all_to_all | solution.py:842
  17.8 153.0 %all-gather.7.cloned.1.call-start = ((), (), s32[]{:S(2)}) async-start(), calls=%async_computation.10 | async-start | bytes 5898240 | tf_op jit(solution)/shard_map/all_gather | solution.py:858
  88.1 305.3 %all-gather.9.cloned.1.call-start = ((), (), s32[]{:S(2)}) async-start(), calls=%async_computation.11 | async-start | bytes 20643840 | tf_op jit(solution)/shard_map/all_gather | solution.py:858
  233.4 104.4 %all-to-all-start.1 = ((bf16[8,48,2560]{2,1,0:T(8,128)(2,1)}), bf16[8,48,2560]{2,1,0:T(8,128)(2,1)}, u32[]{:S(2)}, u32[]{:S(2)}) async-start(bf16[8,48,2560]{2,1,0:T(8,128)(2,1)} %shard_map.229), calls=%async_computation.1 | async-start | bytes 3932160 | tf_op jit(solution)/shard_map/all_to_all | solution.py:842
  243.6 242.7 %all-gather.11.cloned.1.call-start = ((), (), s32[]{:S(2)}) async-start(), calls=%async_computation.12 | async-start | bytes 10321920 | tf_op jit(solution)/shard_map/all_gather | solution.py:858
  312.7 470.2 %reduce-scatter.6.cloned.1.call-start = ((), (), s32[]{:S(2)}) async-start(), calls=%async_computation.13 | async-start | bytes 10321920 | tf_op jit(solution)/shard_map/reduce_scatter | solution.py:851
  390.4 50.2 %collective-permute-start.22 = (bf16[192,2560]{1,0:T(8,128)(2,1)}, bf16[192,2560]{1,0:T(8,128)(2,1)}, u32[]{:S(2)}, u32[]{:S(2)}) collective-permute-start(bf16[192,2560]{1,0:T(8,128)(2,1)} %get-tuple-element.171), channel_id=1, source_target_pairs={{0,8},{8,0},{16,24},{24,16},{1,9},{9,1},{17,25},{25,17},{2,10},{10... | collective-permute-start | bytes 2949128 | tf_op jit(solution)/shard_map/ppermute | solution.py:23
  391.0 54.1 %collective-permute-start.24 = (bf16[192,2560]{1,0:T(8,128)(2,1)}, bf16[192,2560]{1,0:T(8,128)(2,1)}, u32[]{:S(2)}, u32[]{:S(2)}) collective-permute-start(bf16[192,2560]{1,0:T(8,128)(2,1)} %get-tuple-element.171), channel_id=1, source_target_pairs={{0,16},{8,24},{16,0},{24,8},{1,17},{9,25},{17,1},{25,9},{2,18},{10... | collective-permute-start | bytes 2949128 | tf_op jit(solution)/shard_map/ppermute | solution.py:23
  392.7 50.1 %collective-permute-start.23 = (bf16[192,2560]{1,0:T(8,128)(2,1)}, bf16[192,2560]{1,0:T(8,128)(2,1)}, u32[]{:S(2)}, u32[]{:S(2)}) collective-permute-start(bf16[192,2560]{1,0:T(8,128)(2,1)} %get-tuple-element.172), channel_id=1, source_target_pairs={{0,16},{8,24},{16,0},{24,8},{1,17},{9,25},{17,1},{25,9},{2,18},{10... | collective-permute-start | bytes 2949128 | tf_op jit(solution)/shard_map/ppermute | solution.py:23
  486.0 369.2 %reduce-scatter.8.cloned.1.call-start = ((), (), s32[]{:S(2)}) async-start(), calls=%async_computation.14 | async-start | bytes 10321920 | tf_op jit(solution)/shard_map/reduce_scatter | solution.py:851
  512.8 52.7 %collective-permute-start.28 = (bf16[192,2560]{1,0:T(8,128)(2,1)}, bf16[192,2560]{1,0:T(8,128)(2,1)}, u32[]{:S(2)}, u32[]{:S(2)}) collective-permute-start(bf16[192,2560]{1,0:T(8,128)(2,1)} %get-tuple-element.163), channel_id=1, source_target_pairs={{0,8},{8,0},{16,24},{24,16},{1,9},{9,1},{17,25},{25,17},{2,10},{10... | collective-permute-start | bytes 2949128 | tf_op jit(solution)/shard_map/ppermute | solution.py:23
  513.5 56.3 %collective-permute-start.30 = (bf16[192,2560]{1,0:T(8,128)(2,1)}, bf16[192,2560]{1,0:T(8,128)(2,1)}, u32[]{:S(2)}, u32[]{:S(2)}) collective-permute-start(bf16[192,2560]{1,0:T(8,128)(2,1)} %get-tuple-element.165), channel_id=1, source_target_pairs={{0,16},{8,24},{16,0},{24,8},{1,17},{9,25},{17,1},{25,9},{2,18},{10... | collective-permute-start | bytes 2949128 | tf_op jit(solution)/shard_map/ppermute | solution.py:23
  514.4 55.3 %collective-permute-start.27 = (bf16[192,2560]{1,0:T(8,128)(2,1)}, bf16[192,2560]{1,0:T(8,128)(2,1)}, u32[]{:S(2)}, u32[]{:S(2)}) collective-permute-start(bf16[192,2560]{1,0:T(8,128)(2,1)} %get-tuple-element.168), channel_id=1, source_target_pairs={{0,8},{8,0},{16,24},{24,16},{1,9},{9,1},{17,25},{25,17},{2,10},{10... | collective-permute-start | bytes 2949128 | tf_op jit(solution)/shard_map/ppermute | solution.py:23
  561.8 422.5 %reduce-scatter.14.cloned.1.call-start = ((), (), s32[]{:S(2)}) async-start(), calls=%async_computation.17 | async-start | bytes 10321920 | tf_op jit(solution)/shard_map/reduce_scatter | solution.py:851
  621.3 53.8 %collective-permute-start.33 = (bf16[768,640]{1,0:T(8,128)(2,1)}, bf16[768,640]{1,0:T(8,128)(2,1)}, u32[]{:S(2)}, u32[]{:S(2)}) collective-permute-start(bf16[768,640]{1,0:T(8,128)(2,1)} %get-tuple-element.160), channel_id=1, source_target_pairs={{0,8},{8,0},{16,24},{24,16},{1,9},{9,1},{17,25},{25,17},{2,10},{10... | collective-permute-start | bytes 2949128 | tf_op jit(solution)/shard_map/ppermute | solution.py:23
  708.2 97.3 %all-to-all-start.2 = ((bf16[8,48,2560]{2,1,0:T(8,128)(2,1)}), bf16[8,48,2560]{2,1,0:T(8,128)(2,1)}, u32[]{:S(2)}, u32[]{:S(2)}) async-start(bf16[8,48,2560]{2,1,0:T(8,128)(2,1)} %gather_fusion.4), calls=%async_computation.2 | async-start | bytes 3932160 | tf_op jit(solution)/shard_map/all_to_all | solution.py:842
  731.6 257.1 %reduce-scatter.12.cloned.1.call-start = ((), (), s32[]{:S(2)}) async-start(), calls=%async_computation.16 | async-start | bytes 3686400 | tf_op jit(solution)/shard_map/reduce_scatter | solution.py:851
  782.6 242.2 %reduce-scatter.10.cloned.1.call-start = ((), (), s32[]{:S(2)}) async-start(), calls=%async_computation.15 | async-start | bytes 5898240 | tf_op jit(solution)/shard_map/reduce_scatter | solution.py:851
  782.9 72.4 %collective-permute-start.47 = (bf16[224,2560]{1,0:T(8,128)(2,1)}, bf16[224,2560]{1,0:T(8,128)(2,1)}, u32[]{:S(2)}, u32[]{:S(2)}) collective-permute-start(bf16[224,2560]{1,0:T(8,128)(2,1)} %shard_map.250.refs_0_), channel_id=1, source_target_pairs={{0,24},{8,16},{16,8},{24,0},{1,25},{9,17},{17,9},{25,1},{2,26},{10... | collective-permute-start | bytes 3440648 | tf_op jit(solution)/shard_map/ppermute | solution.py:23
  783.8 71.5 %collective-permute-start.46 = (bf16[224,2560]{1,0:T(8,128)(2,1)}, bf16[224,2560]{1,0:T(8,128)(2,1)}, u32[]{:S(2)}, u32[]{:S(2)}) collective-permute-start(bf16[224,2560]{1,0:T(8,128)(2,1)} %shard_map.250.refs_0_), channel_id=1, source_target_pairs={{0,16},{8,24},{16,0},{24,8},{1,17},{9,25},{17,1},{25,9},{2,18},{10... | collective-permute-start | bytes 3440648 | tf_op jit(solution)/shard_map/ppermute | solution.py:23
  784.6 70.7 %collective-permute-start.45 = (bf16[224,2560]{1,0:T(8,128)(2,1)}, bf16[224,2560]{1,0:T(8,128)(2,1)}, u32[]{:S(2)}, u32[]{:S(2)}) collective-permute-start(bf16[224,2560]{1,0:T(8,128)(2,1)} %shard_map.250.refs_0_), channel_id=1, source_target_pairs={{0,8},{8,0},{16,24},{24,16},{1,9},{9,1},{17,25},{25,17},{2,10},{10... | collective-permute-start | bytes 3440648 | tf_op jit(solution)/shard_map/ppermute | solution.py:23
  908.5 57.3 %collective-permute-start.48 = (bf16[192,2560]{1,0:T(8,128)(2,1)}, bf16[192,2560]{1,0:T(8,128)(2,1)}, u32[]{:S(2)}, u32[]{:S(2)}) collective-permute-start(bf16[192,2560]{1,0:T(8,128)(2,1)} %get-tuple-element.144), channel_id=1, source_target_pairs={{0,8},{8,0},{16,24},{24,16},{1,9},{9,1},{17,25},{25,17},{2,10},{10... | collective-permute-start | bytes 2949128 | tf_op jit(solution)/shard_map/ppermute | solution.py:23
  971.2 113.2 %all-to-all-start.3 = ((bf16[8,48,2560]{2,1,0:T(8,128)(2,1)}), bf16[8,48,2560]{2,1,0:T(8,128)(2,1)}, u32[]{:S(2)}, u32[]{:S(2)}) async-start(bf16[8,48,2560]{2,1,0:T(8,128)(2,1)} %gather_fusion.6), calls=%async_computation.4 | async-start | bytes 3932160 | tf_op jit(solution)/shard_map/all_to_all | solution.py:842
  (149 other events, 2735.2 us)
Sparse Core Ops, SparseCore 0:
  10.2 68.7 all-gather.4
  88.2 56.3 all-gather.6
  146.8 200.5 all-gather.8
  349.4 89.8 all-gather.10
  486.1 102.8 reduce-scatter.5
  591.8 95.2 reduce-scatter.7
  689.5 149.2 reduce-scatter.13
  841.6 38.6 reduce-scatter.11
  895.6 61.5 reduce-scatter.9

commit v7 on v6

--- a/solution.py
+++ b/solution.py
@@ -80,7 +80,7 @@
     half = parts.shape[1] // 2
     parts = row_major(parts)
 
-    def block(turn, lower):
+    def block(parts, turn, lower):
         start = (place ^ turn, 0 if lower else half) + (0,) * (parts.ndim - 2)
         return lax.dynamic_slice(parts, start, (1, half) + parts.shape[2:])[0]
 
@@ -94,16 +94,18 @@
             total = total + value.astype(wide)
         return total
 
-    from_x, from_y = swap(block(3, True), 1), swap(block(3, False), 2)
+    far = block(parts, 3, True), block(parts, 3, False)
+    from_x, from_y = swap(far[0], 1), swap(far[1], 2)
+    parts = after(parts, *far)
     given = hook((from_x, from_y)) if hook else ()
     if given:
         from_x, from_y = after(from_x, *given), after(from_y, *given)
-    x_first, y_second = swap(block(1, True), 1), swap(block(2, False), 2)
-    y_sent = added(block(2, True), from_x).astype(low)
-    x_sent = added(block(1, False), from_y).astype(low)
+    x_first, y_second = swap(block(parts, 1, True), 1), swap(block(parts, 2, False), 2)
+    y_sent = added(block(parts, 2, True), from_x).astype(low)
+    x_sent = added(block(parts, 1, False), from_y).astype(low)
     y_first, x_second = swap(y_sent, 2), swap(x_sent, 1)
-    first = added(block(0, True), x_first, y_first)
-    second = added(block(0, False), y_second, x_second)
+    first = added(block(parts, 0, True), x_first, y_first)
+    second = added(block(parts, 0, False), y_second, x_second)
     stage = (y_sent, x_sent, x_first, y_second)
     return jnp.concatenate([first, second], axis=0), stage, (y_first, x_second), given
 
@@ -146,12 +148,12 @@
     return jnp.where(lane < half, pltpu.roll(padded, LANES - half, 1), pltpu.roll(padded, half, 1))
 
 
-def qkv_kernel(heads, keys, x_ref, gain_ref, weight_ref, cos_ref, sin_ref, normed_ref, q_ref, k_ref, v_ref):
+def qkv_kernel(heads, keys, width, x_ref, gain_ref, weight_ref, cos_ref, sin_ref, normed_ref, q_ref, k_ref, v_ref):
     x = x_ref[...].astype(jnp.float32)
     scale = lax.rsqrt(jnp.mean(x * x, axis=1, keepdims=True) + eps)
     normed = (x * scale * gain_ref[...]).astype(jnp.bfloat16)
     normed_ref[...] = normed
-    rows = jnp.dot(normed, weight_ref[...], preferred_element_type=jnp.float32)
+    rows = jnp.dot(normed, weight_ref[:, :width], preferred_element_type=jnp.float32)
     cosine, sine = cos_ref[...], sin_ref[...]
     inside = lax.broadcasted_iota(jnp.int32, cosine.shape, 1) < HEAD_SIZE
     for i in range(heads + keys):
@@ -166,14 +168,14 @@
         v_ref[:, i * LANES : (i + 1) * LANES] = jnp.where(inside, v, 0.0).astype(jnp.bfloat16)
 
 
-def qkv_call(x, gain, weight, cosine, sine, heads, keys):
+def qkv_call(x, gain, weight, cosine, sine, heads, keys, used):
     total, width = x.shape
     block = 256
     bf = jnp.bfloat16
     row = lambda n: pl.BlockSpec((block, n), lambda i: (i, 0))
     whole = lambda a: pl.BlockSpec(a.shape, lambda i: (0, 0))
     return pl.pallas_call(
-        functools.partial(qkv_kernel, heads, keys),
+        functools.partial(qkv_kernel, heads, keys, used),
         grid=(total // block,),
         in_specs=[row(width), whole(gain), whole(weight), row(LANES), row(LANES)],
         out_specs=[row(width), row(heads * LANES), row(keys * LANES), row(keys * LANES)],
@@ -185,7 +187,7 @@
         ],
         compiler_params=pltpu.CompilerParams(vmem_limit_bytes=48 * 2**20),
         cost_estimate=pl.CostEstimate(
-            flops=120 * 10**9, bytes_accessed=0, transcendentals=0
+            flops=96 * 10**9, bytes_accessed=0, transcendentals=0
         ),
     )(x, gain, weight, cosine, sine)
 
@@ -232,7 +234,7 @@
         scratch_shapes=[pltpu.VMEM((block, total), jnp.float32)],
         compiler_params=pltpu.CompilerParams(vmem_limit_bytes=56 * 2**20),
         cost_estimate=pl.CostEstimate(
-            flops=140 * 10**9, bytes_accessed=0, transcendentals=0
+            flops=112 * 10**9, bytes_accessed=0, transcendentals=0
         ),
     )(q, k, v, start, *when)
 
@@ -306,7 +308,7 @@
         ],
         compiler_params=pltpu.CompilerParams(vmem_limit_bytes=56 * 2**20),
         cost_estimate=pl.CostEstimate(
-            flops=250 * 10**9, bytes_accessed=0, transcendentals=0
+            flops=200 * 10**9, bytes_accessed=0, transcendentals=0
         ),
     )(q, k, v, grad, lse_rows, start_row, cosine, sine_back, *when)
 
@@ -341,7 +343,7 @@
         out_shape=[jax.ShapeDtypeStruct((total, units), jnp.bfloat16)] * 3,
         compiler_params=pltpu.CompilerParams(vmem_limit_bytes=56 * 2**20),
         cost_estimate=pl.CostEstimate(
-            flops=185 * 10**9, bytes_accessed=0, transcendentals=0
+            flops=148 * 10**9, bytes_accessed=0, transcendentals=0
         ),
     )(x, weights, weights)
 
@@ -375,7 +377,7 @@
         out_shape=[jax.ShapeDtypeStruct((total, units), jnp.bfloat16)] * 2,
         compiler_params=pltpu.CompilerParams(vmem_limit_bytes=56 * 2**20),
         cost_estimate=pl.CostEstimate(
-            flops=130 * 10**9, bytes_accessed=0, transcendentals=0
+            flops=104 * 10**9, bytes_accessed=0, transcendentals=0
         ),
     )(incoming, down, gate, up, *when)
 
@@ -431,7 +433,7 @@
         ],
         compiler_params=pltpu.CompilerParams(vmem_limit_bytes=60 * 2**20),
         cost_estimate=pl.CostEstimate(
-            flops=220 * 10**9, bytes_accessed=0, transcendentals=0
+            flops=176 * 10**9, bytes_accessed=0, transcendentals=0
         ),
     )(d_gate, d_up, weights, x, gain, *when)
 
@@ -476,7 +478,7 @@
         ],
         compiler_params=pltpu.CompilerParams(vmem_limit_bytes=56 * 2**20),
         cost_estimate=pl.CostEstimate(
-            flops=100 * 10**9, bytes_accessed=0, transcendentals=0
+            flops=80 * 10**9, bytes_accessed=0, transcendentals=0
         ),
     )(place, d_qkv, weights, x, gain, own, *when)
 
@@ -500,7 +502,7 @@
         out_shape=jax.ShapeDtypeStruct((parts, total, rows), jnp.bfloat16),
         compiler_params=pltpu.CompilerParams(vmem_limit_bytes=32 * 2**20),
         cost_estimate=pl.CostEstimate(
-            flops=40 * 10**9, bytes_accessed=0, transcendentals=0
+            flops=32 * 10**9, bytes_accessed=0, transcendentals=0
         ),
     )(d_branch, weights, *when)
 
@@ -533,7 +535,7 @@
         out_specs=[row, row],
         out_shape=[jax.ShapeDtypeStruct((total, parts * share), jnp.bfloat16)] * 2,
         compiler_params=pltpu.CompilerParams(vmem_limit_bytes=32 * 2**20),
-        cost_estimate=pl.CostEstimate(flops=40 * 10**9, bytes_accessed=0, transcendentals=0),
+        cost_estimate=pl.CostEstimate(flops=32 * 10**9, bytes_accessed=0, transcendentals=0),
     )(stack, gain)
 
 
@@ -563,7 +565,7 @@
         out_specs=row,
         out_shape=jax.ShapeDtypeStruct((total, columns), jnp.bfloat16),
         compiler_params=pltpu.CompilerParams(vmem_limit_bytes=40 * 2**20),
-        cost_estimate=pl.CostEstimate(flops=45 * 10**9, bytes_accessed=0, transcendentals=0),
+        cost_estimate=pl.CostEstimate(flops=36 * 10**9, bytes_accessed=0, transcendentals=0),
     )(stack, weight, x)
 
 
@@ -608,7 +610,7 @@
         out_specs=pl.BlockSpec((rows, block), lambda j: (0, j)),
         out_shape=jax.ShapeDtypeStruct((rows, columns), jnp.bfloat16),
         compiler_params=pltpu.CompilerParams(vmem_limit_bytes=56 * 2**20),
-        cost_estimate=pl.CostEstimate(flops=0 if when else 100 * 10**9, bytes_accessed=0, transcendentals=0),
+        cost_estimate=pl.CostEstimate(flops=0 if when else 80 * 10**9, bytes_accessed=0, transcendentals=0),
     )(left, right, *when)
 
 
@@ -633,7 +635,7 @@
         out_specs=pl.BlockSpec((total, block), lambda j: (0, j)),
         out_shape=jax.ShapeDtypeStruct((total, columns), jnp.bfloat16),
         compiler_params=pltpu.CompilerParams(vmem_limit_bytes=56 * 2**20),
-        cost_estimate=pl.CostEstimate(flops=100 * 10**9, bytes_accessed=0, transcendentals=0),
+        cost_estimate=pl.CostEstimate(flops=80 * 10**9, bytes_accessed=0, transcendentals=0),
     )(left, right, *when)
 
 
@@ -663,7 +665,7 @@
         out_specs=pl.BlockSpec((block, columns), lambda i: (i, 0)),
         out_shape=jax.ShapeDtypeStruct((width, columns), jnp.bfloat16),
         compiler_params=pltpu.CompilerParams(vmem_limit_bytes=48 * 2**20),
-        cost_estimate=pl.CostEstimate(flops=60 * 10**9, bytes_accessed=0, transcendentals=0),
+        cost_estimate=pl.CostEstimate(flops=48 * 10**9, bytes_accessed=0, transcendentals=0),
     )(normed, d_qkv, gain_grads, *when)
 
 
@@ -686,8 +688,8 @@
     )
 
 
-def spread_kernel(layout, count, chunks, place_ref, *refs):
-    pieces, outs = refs[: count * chunks], refs[count * chunks :]
+def spread_kernel(layout, count, chunks, outputs, place_ref, *refs):
+    pieces, outs = refs[: count * chunks], refs[-outputs:]
     size = pieces[0].shape[1]
     for place in range(count):
 
@@ -704,22 +706,23 @@
                         first, goal, width = first + some, goal + some, width - some
 
 
-def spread_call(place, pieces, layout, widths):
+def spread_call(place, pieces, layout, widths, *when):
     count, chunks = len(pieces), len(pieces[0])
     rows, columns = pieces[0][0].shape
     block = rows // 5 if rows % 80 == 0 else rows
     return pl.pallas_call(
-        functools.partial(spread_kernel, layout, count, chunks),
+        functools.partial(spread_kernel, layout, count, chunks, len(widths)),
         grid=(rows // block,),
         in_specs=[pl.BlockSpec(memory_space=pltpu.SMEM)]
-        + [pl.BlockSpec((block, columns), lambda i: (i, 0))] * (count * chunks),
+        + [pl.BlockSpec((block, columns), lambda i: (i, 0))] * (count * chunks)
+        + [pl.BlockSpec(memory_space=pl.ANY)] * len(when),
         out_specs=[pl.BlockSpec((block, w), lambda i: (i, 0)) for w in widths],
         out_shape=[jax.ShapeDtypeStruct((rows, w), jnp.float32) for w in widths],
         compiler_params=pltpu.CompilerParams(vmem_limit_bytes=40 * 2**20),
         cost_estimate=pl.CostEstimate(
             flops=0, bytes_accessed=6 * count * chunks * rows * columns, transcendentals=0
         ),
-    )(place, *[chunk for piece in pieces for chunk in piece])
+    )(place, *[chunk for piece in pieces for chunk in piece], *when)
 
 
 def stack_kernel(count, chunks, place_ref, *refs):
@@ -873,21 +876,24 @@
         [column_share(w_query), column_share(key_weight), column_share(value_weight), gains], axis=1
     )
     came_incoming = deal(after(picked(cotangent), came_tokens))
-    out_all = gather_fsdp(column_share(w_out))
-    qkv_all = gather_fsdp(after(qkv_shard, came_tokens, out_all))
+    qkv_width = qkv_shard.shape[1]
+    qkv_shard = jnp.concatenate([qkv_shard, column_share(w_out)], axis=1)
+    qkv_all = gather_fsdp(after(qkv_shard, came_tokens))
+    out_all = qkv_all[:, qkv_width:]
     gate_up_all = gather_fsdp(gate_up_shard)
     down_all = gather_fsdp(lax.dynamic_slice_in_dim(w_down, sp_place * ff_share, ff_share, axis=0))
     gain_one = qkv_all[:, qkv_cols].astype(wide)[None, :]
     gain_two = qkv_all[:, qkv_cols + 1].astype(wide)[None, :]
 
-    group_inputs = gather_sp(in_place(came_tokens))[0].reshape(-1, width)
-    group_positions = gather_small(positions.reshape(-1)).reshape(-1)
+    group_inputs, passed = gather_sp(in_place(came_tokens))
+    group_inputs = group_inputs.reshape(-1, width)
+    group_positions = gather_small(after(positions.reshape(-1), passed[0])).reshape(-1)
     total = group_inputs.shape[0]
 
     cosine, sine = rotary_tables(group_positions)
     heads, keys = query_cols // HEAD_SIZE, key_cols // HEAD_SIZE
     normed, query_low, key_low, value_low = qkv_call(
-        group_inputs, gain_one, qkv_all, cosine, sine, heads, keys
+        group_inputs, gain_one, qkv_all, cosine, sine, heads, keys, qkv_width
     )
     sizes = lengths.reshape(-1)
     ends = jnp.cumsum(sizes)
@@ -933,35 +939,38 @@
 
     down_sum = after(scatter_fsdp(grad_down), d_mixed)
     down_pieces, down_first, _ = pieces_sp(down_sum, False)
-    gate_sum = after(scatter_fsdp(grad_gate), *down_first)
+    gate_sum = after(scatter_fsdp(grad_gate), d_mixed, down_sum)
     gate_pieces, gate_first, _ = pieces_sp(gate_sum, False)
     d_qkv = attend_back_call(
-        query_low, key_low, value_low, d_mixed, logs.T, start[None, :], cosine, sine, gone_result
+        query_low, key_low, value_low, d_mixed, logs.T, start[None, :], cosine, sine
     )
     back_one, grad_gain_one = attend_norm_call(
-        place, d_qkv, qkv_all, group_inputs, gain_one, own_d_hidden, parts, *down_first
+        place, d_qkv, qkv_all, group_inputs, gain_one, own_d_hidden, parts, gone_result, *down_first, *gate_first[:2]
     )
     gain_grads = jnp.concatenate(
         [grad_gain_one, grad_gain_two, jnp.zeros((6, width), wide)], axis=0
     )
     layer_out = rows_of(gone_result, target).reshape(tokens.shape)
 
-    grad_qkv = qkv_grad_call(normed, d_qkv, gain_grads, qkv_all.shape[1], *gate_first[:-1])
-    d_inputs, _, _, (down_shard, layer_out) = scatter_sp(
-        back_one.reshape(parts, rows, width),
-        lambda first: (stack_call(place, down_pieces, *first), layer_out),
-    )
-    gone_grad = deal(blocks_back(d_inputs.astype(low)))
-    input_grad = rows_of(gone_grad, target).reshape(tokens.shape)
-
+    grad_qkv = qkv_grad_call(normed, d_qkv, gain_grads, qkv_width, *gate_first[2:])
     hidden_layout = [
         (j * ff_share, ff_share, 0, j * parts * ff_share, ff_share) for j in range(groups)
     ]
-    (gate_shard,) = spread_call(place, gate_pieces, hidden_layout, [w_gate.shape[1]])
+
+    def beside(first):
+        gate_shard = spread_call(place, gate_pieces, hidden_layout, [w_gate.shape[1]], *first)[0]
+        return stack_call(place, down_pieces, *first), gate_shard, layer_out
+
+    d_inputs, _, _, (down_shard, gate_shard, layer_out) = scatter_sp(
+        back_one.reshape(parts, rows, width), beside
+    )
+    gone_grad = deal(blocks_back(d_inputs.astype(low)))
+    input_grad = rows_of(gone_grad, target).reshape(tokens.shape)
+
     up_pieces, up_first, _ = pieces_sp(scatter_fsdp(after(grad_up, d_branch)), True)
     out_sum = after(scatter_fsdp(after(grad_out, d_mixed)), *up_first[:2])
     out_pieces = pieces_sp(out_sum, False)[0]
-    qkv_pieces = pieces_sp(after(scatter_fsdp(grad_qkv), out_sum), True, gate_shard)[0]
+    qkv_pieces = pieces_sp(after(scatter_fsdp(grad_qkv), out_sum), True)[0]
     (up_shard,) = spread_call(place, up_pieces, hidden_layout, [w_up.shape[1]])
     (out_shard,) = spread_call(place, out_pieces, [(0, share, 0, 0, share)], [width])
     qkv_layout = [

time: 1110 us -> 1090 us (0.982)
  waiting for transfers between devices: 386 us -> 325 us
  local copies, waits for them, and re-layouts: 157 us -> 180 us
  starting transfers between devices: 107 us -> 125 us
    ppermute x72, waiting for transfers between devices: 277 us -> 198 us  [swap(): return lax.ppermute(value, 'sp', [(i, i ^ bit) for i in range(size)])]
    reduce_scatter x5, waiting for transfers between devices: 0.02 us -> 56.4 us  [scatter_fsdp(): return lax.psum_scatter(matrix, 'fsdp', scatter_dimension=0, tiled=True)]
    all_to_all x4, waiting for transfers between devices: 109 us -> 69.2 us  [deal(): lax.all_to_all(blocks, 'fsdp', split_axis=0, concat_axis=0, tiled=True)]
    squeeze x4 -> x8, local copies, waits for them, and re-layouts: 22 us -> 31.2 us  [block(): return lax.dynamic_slice(parts, start, (1, half) + parts.shape[2:])[0]]
    unnamed x178 -> x164, local copies, waits for them, and re-layouts: 40.2 us -> 48.6 us
  transfers between devices with their start and end apart: 85 -> 84, of which waited for: 33 -> 30; matrix products, arithmetic and copies ran while one was open for 15% -> 16% of each run, Pallas kernels for 34% -> 35%
where the time goes in v7:
time: 1090 us; the launch traced here: 1080 us
  Pallas kernels  384 us (35%)
  waiting for transfers between devices  325 us (30%)
  local copies, waits for them, and re-layouts  180 us (17%)
  starting transfers between devices  125 us (11%)
  other arithmetic  47.9 us (4%)
  between operations  15.6 us (1%)
    ppermute x72, waiting for transfers between devices, swap(): return lax.ppermute(value, 'sp', [(i, i ^ bit) for i in range(size)])  198 us
    all_to_all x4, waiting for transfers between devices, deal(): lax.all_to_all(blocks, 'fsdp', split_axis=0, concat_axis=0, tiled=True)  69.2 us
    ppermute x72, starting transfers between devices, swap(): return lax.ppermute(value, 'sp', [(i, i ^ bit) for i in range(size)])  63.9 us
    pallas_call x3, Pallas kernels, rows_call(): pl.pallas_call(rows_kernel, grid=(columns // block,), in_specs=[pl.BlockS...  61.5 us
    all_to_all x4, starting transfers between devices, deal(): lax.all_to_all(blocks, 'fsdp', split_axis=0, concat_axis=0, tiled=True)  59.8 us
    reduce_scatter x5, waiting for transfers between devices, scatter_fsdp(): return lax.psum_scatter(matrix, 'fsdp', scatter_dimension=0, tiled=True)  56.4 us
    pallas_call x1, Pallas kernels, attend_back_call(): pl.pallas_call(functools.partial(attend_back_kernel, heads, keys, block),...  49.8 us
    unnamed x164, local copies, waits for them, and re-layouts  48.6 us
  transfers between devices with their start and end apart: 84, of which 30 were waited for; matrix products, arithmetic and copies ran while one was open for 16% of the time, Pallas kernels for 35%

profile of v7, /device:TPU:9, one launch (start us, length us, event | category | flops | bytes accessed | tf_op | source)
XLA Modules:
  0.0 1077.5 jit_solution(11282542585473200214)
XLA Ops:
  21.2 38.0 %all-to-all-done.refs_1_._ = bf16[8,48,2560]{2,1,0:T(8,128)(2,1)S(1)} async-done(((bf16[8,48,2560]{2,1,0:T(8,128)(2,1)}), bf16[8,48,2560]{2,1,0:T(8,128)(2,1)S(1)}, u32[]{:S(2)}, u32[]{:S(2)}) %all-to-all-start) | async-done | bytes 1966112 | tf_op jit(solution)/shard_map/all_to_all | solution.py:845
  97.8 15.4 %collective-permute-done.1 = bf16[192,2560]{1,0:T(8,128)(2,1)} collective-permute-done((bf16[192,2560]{1,0:T(8,128)(2,1)}, bf16[192,2560]{1,0:T(8,128)(2,1)}, u32[]{:S(2)}, u32[]{:S(2)}) %collective-permute-start.1) | collective-permute-done | bytes 983072 | tf_op jit(solution)/shard_map/ppermute | solution.py:23
  126.0 12.4 %collective-permute-done.4 = bf16[192,2560]{1,0:T(8,128)(2,1)} collective-permute-done((bf16[192,2560]{1,0:T(8,128)(2,1)S(1)}, bf16[192,2560]{1,0:T(8,128)(2,1)}, u32[]{:S(2)}, u32[]{:S(2)}) %collective-permute-start.4) | collective-permute-done | bytes 983072 | tf_op jit(solution)/shard_map/ppermute | solution.py:23
  146.0 24.3 %shard_map.223 = (bf16[1536,2560]{1,0:T(8,128)(2,1)}, bf16[1536,1024]{1,0:T(8,128)(2,1)}, bf16[1536,256]{1,0:T(8,128)(2,1)S(1)}, bf16[1536,256]{1,0:T(8,128)(2,1)S(1)}) custom-call(bf16[1536,2560]{1,0:T(8,128)(2,1)} %bitcast.17.x_ref, f32[1,2560]{1,0:T(1,128)S(1)} %reshape.298.gain_ref, bf16[2560,1664]{1,0:T(8,128)(2,1)} %all-gather.4.cloned.1.call-done.weight_ref, ...), custom_call_target="tpu_custom_call" | custom-call | flops 96000000000 | tf_op jit(solution)/shard_map/pallas_call | solution.py:177
  172.1 27.7 %shard_map.224 = (bf16[1536,640]{1,0:T(8,128)(2,1)}, f32[1536,8]{1,0:T(8,128)}) custom-call(bf16[1536,1024]{1,0:T(8,128)(2,1)} %get-tuple-element.72.q_ref, bf16[1536,256]{1,0:T(8,128)(2,1)} %copy-done.38, bf16[1536,256]{1,0:T(8,128)(2,1)} %copy-done.39, s32[1536,1]{1,0:T(8,128)} %broadcast_in_dim.224.start_ref), custom_call_target="tpu_custom_call" | custom-call | flops 112000000000 | tf_op jit(solution)/shard_map/pallas_call | solution.py:226
  229.2 17.3 %collective-permute-done.10 = bf16[768,640]{1,0:T(8,128)(2,1)S(1)} collective-permute-done((bf16[768,640]{1,0:T(8,128)(2,1)}, bf16[768,640]{1,0:T(8,128)(2,1)S(1)}, u32[]{:S(2)}, u32[]{:S(2)}) %collective-permute-start.10) | collective-permute-done | bytes 983072 | tf_op jit(solution)/shard_map/ppermute | solution.py:23
  247.1 19.3 %collective-permute-done.13 = bf16[768,640]{1,0:T(8,128)(2,1)S(1)} collective-permute-done((bf16[768,640]{1,0:T(8,128)(2,1)}, bf16[768,640]{1,0:T(8,128)(2,1)S(1)}, u32[]{:S(2)}, u32[]{:S(2)}) %collective-permute-start.13) | collective-permute-done | bytes 983072 | tf_op jit(solution)/shard_map/ppermute | solution.py:23
  288.2 22.2 %all-to-all-done.1.refs_0_ = bf16[8,48,2560]{2,1,0:T(8,128)(2,1)} async-done(((bf16[8,48,2560]{2,1,0:T(8,128)(2,1)}), bf16[8,48,2560]{2,1,0:T(8,128)(2,1)}, u32[]{:S(2)}, u32[]{:S(2)}) %all-to-all-start.1) | async-done | bytes 1966112 | tf_op jit(solution)/shard_map/all_to_all | solution.py:845
  328.3 16.3 %collective-permute-done.19 = bf16[768,640]{1,0:T(8,128)(2,1)S(1)} collective-permute-done((bf16[768,640]{1,0:T(8,128)(2,1)}, bf16[768,640]{1,0:T(8,128)(2,1)S(1)}, u32[]{:S(2)}, u32[]{:S(2)}) %collective-permute-start.19) | collective-permute-done | bytes 983072 | tf_op jit(solution)/shard_map/ppermute | solution.py:23
  369.7 36.7 %shard_map.228 = (bf16[1536,1792]{1,0:T(8,128)(2,1)}, bf16[1536,1792]{1,0:T(8,128)(2,1)}, bf16[1536,1792]{1,0:T(8,128)(2,1)}) custom-call(bf16[1536,2560]{1,0:T(8,128)(2,1)} %copy-done.5, bf16[2560,3584]{1,0:T(8,128)(2,1)} %all-gather.6.cloned.1.call-done.gate_weight_ref.up_weight_ref.weight_ref, ...), custom_call_target="tpu_custom_call" | custom-call | flops 147999997952 | tf_op jit(solution)/shard_map/pallas_call | solution.py:334
  442.8 20.3 %shard_map.235.refs_0_ = bf16[1792,2560]{1,0:T(8,128)(2,1)} custom-call(bf16[1536,1792]{1,0:T(8,128)(2,1)} %get-tuple-element.78.refs_1_.left_ref, bf16[1536,2560]{1,0:T(8,128)(2,1)} %bitcast.190), custom_call_target="tpu_custom_call" | custom-call | flops 80000000000 | tf_op jit(solution)/shard_map/pallas_call | solution.py:602
  463.4 20.0 %shard_map.236.refs_0_ = bf16[1536,2560]{1,0:T(8,128)(2,1)} custom-call(bf16[1536,1792]{1,0:T(8,128)(2,1)} %get-tuple-element.78.refs_1_.left_ref, bf16[1792,2560]{1,0:T(8,128)(2,1)} %all-gather.8.cloned.1.call-done.right_ref.down_ref, bf16[1792,2560]{1,0:T(8,128)(2,1)} %shard_map.235.refs_0_), custom_call_target="tpu_custom_call" | custom-call | flops 80000000000 | tf_op jit(solution)/shard_map/pallas_call | solution.py:627
  489.0 25.5 %shard_map.238 = (bf16[1536,1792]{1,0:T(8,128)(2,1)}, bf16[1536,1792]{1,0:T(8,128)(2,1)}) custom-call(bf16[1536,2560]{1,0:T(8,128)(2,1)} %bitcast.191, bf16[1792,2560]{1,0:T(8,128)(2,1)} %all-gather.8.cloned.1.call-done.right_ref.down_ref, bf16[1536,1792]{1,0:T(8,128)(2,1)} %get-tuple-element.79.gate_ref, bf16[1536,1792]{1,0:T(8,128)(2,1)} %get-tuple-element.80.up_ref, ...), custom_call_target="tpu_custom_call" | custom-call | flops 103999995904 | tf_op jit(solution)/shard_map/pallas_call | solution.py:366
  519.8 20.5 %shard_map.239.refs_1_.refs_0_ = bf16[2560,1792]{1,0:T(8,128)(2,1)} custom-call(bf16[1536,2560]{1,0:T(8,128)(2,1)} %copy-done.5, bf16[1536,1792]{1,0:T(8,128)(2,1)} %get-tuple-element.81.right_ref.d_gate_ref), custom_call_target="tpu_custom_call" | custom-call | flops 80000000000 | tf_op jit(solution)/shard_map/pallas_call | solution.py:602
  548.8 43.7 %shard_map.242 = (bf16[4,1536,640]{2,1,0:T(8,128)(2,1)}, f32[1,2560]{1,0:T(1,128)}) custom-call(bf16[1536,1792]{1,0:T(8,128)(2,1)} %get-tuple-element.81.right_ref.d_gate_ref, bf16[1536,1792]{1,0:T(8,128)(2,1)} %get-tuple-element.92.d_up_ref.right_ref, bf16[2560,3584]{1,0:T(8,128)(2,1)} %all-gather.6.cloned.1.call-done.gate_weight_ref.up_weight_ref.weight_ref, ...), custom_call_target="tpu_custom_call" | custom-call | flops 176000008192 | tf_op jit(solution)/shard_map/pallas_call | solution.py:421
  613.6 20.7 %shard_map.245.refs_1_.refs_0_ = bf16[2560,1792]{1,0:T(8,128)(2,1)} custom-call(bf16[1536,2560]{1,0:T(8,128)(2,1)} %copy-done.5, bf16[1536,1792]{1,0:T(8,128)(2,1)} %get-tuple-element.92.d_up_ref.right_ref, bf16[768,640]{1,0:T(8,128)(2,1)} %copy-done.43, bf16[768,640]{1,0:T(8,128)(2,1)} %copy-done.42), custom_call_target="tpu_custom_call" | custom-call | tf_op jit(solution)/shard_map/pallas_call | solution.py:602
  712.5 36.4 %all-to-all-start.2 = ((bf16[8,48,2560]{2,1,0:T(8,128)(2,1)}), bf16[8,48,2560]{2,1,0:T(8,128)(2,1)}, u32[]{:S(2)}, u32[]{:S(2)}) async-start(bf16[8,48,2560]{2,1,0:T(8,128)(2,1)} %gather_fusion.4), calls=%async_computation.2 | async-start | bytes 3932160 | tf_op jit(solution)/shard_map/all_to_all | solution.py:845
  759.1 49.8 %shard_map.253.d_qkv_ref = bf16[1536,960]{1,0:T(8,128)(2,1)} custom-call(bf16[1536,1024]{1,0:T(8,128)(2,1)} %get-tuple-element.72.q_ref, bf16[1536,256]{1,0:T(8,128)(2,1)} %copy-done.38, bf16[1536,256]{1,0:T(8,128)(2,1)} %copy-done.39, bf16[1536,640]{1,0:T(8,128)(2,1)} %pad_maximum_fusion.grad_ref.refs_1_, f32[8,1536]{1,0:T(8,128)} %bitcast.208, ...), custom_call_target="tpu_custom_call" | custom-call | flops 199999995904 | tf_op jit(solution)/shard_map/pallas_call | solution.py:299
  820.9 10.5 collective-permute-done.46.refs_2_
  831.4 19.6 %shard_map.256 = (bf16[1536,2560]{1,0:T(8,128)(2,1)}, f32[1,2560]{1,0:T(1,128)}) custom-call(s32[1]{0:T(128)} %bitcast.37.place_ref, bf16[1536,960]{1,0:T(8,128)(2,1)} %shard_map.253.d_qkv_ref, bf16[2560,1664]{1,0:T(8,128)(2,1)} %all-gather.4.cloned.1.call-done.weight_ref, bf16[1536,2560]{1,0:T(8,128)(2,1)} %bitcast.17.x_ref, f32[1,2560]{1,0:T(1,128)} %copy-done.35, ...), custom_call_target="tpu_custom_call" | custom-call | flops 80000000000 | tf_op jit(solution)/shard_map/pallas_call | solution.py:462
  856.7 12.0 %shard_map.262 = bf16[2560,1024]{1,0:T(8,128)(2,1)} custom-call(bf16[1536,2560]{1,0:T(8,128)(2,1)} %get-tuple-element.126.normed_ref, bf16[1536,960]{1,0:T(8,128)(2,1)S(1)} %copy-done.37, f32[8,2560]{1,0:T(8,128)S(1)} %maximum_maximum_fusion.2.gain_ref, bf16[320,1792]{1,0:T(8,128)(2,1)S(1)} %collective-permute-done.53.refs_3_.refs_0_), custom_call_target="tpu_custom_call" | custom-call | flops 48000000000 | tf_op jit(solution)/shard_map/pallas_call | solution.py:656
  914.9 19.4 %collective-permute-done.56 = bf16[192,2560]{1,0:T(8,128)(2,1)S(1)} collective-permute-done((bf16[192,2560]{1,0:T(8,128)(2,1)S(1)}, bf16[192,2560]{1,0:T(8,128)(2,1)S(1)}, u32[]{:S(2)}, u32[]{:S(2)}) %collective-permute-start.56) | collective-permute-done | bytes 983072 | tf_op jit(solution)/shard_map/ppermute | solution.py:23
  953.4 11.4 %collective-permute-done.58.refs_2_.refs_5_ = bf16[320,896]{1,0:T(8,128)(2,1)S(1)} collective-permute-done((bf16[320,896]{1,0:T(8,128)(2,1)S(1)}, bf16[320,896]{1,0:T(8,128)(2,1)S(1)}, u32[]{:S(2)}, u32[]{:S(2)}) %collective-permute-start.58) | collective-permute-done | bytes 573472 | tf_op jit(solution)/shard_map/ppermute | solution.py:23
  968.3 56.4 %reduce-scatter.10.cloned.1.call-done.refs_0_ = bf16[320,1024]{1,0:T(8,128)(2,1)} async-done(((bf16[2560,1024]{1,0:T(8,128)(2,1)}), bf16[320,1024]{1,0:T(8,128)(2,1)}) %reduce-scatter.10.cloned.1.call-update) | async-done | bytes 655376 | tf_op jit(solution)/shard_map/reduce_scatter | solution.py:854
  (496 shorter events, 466.0 us)
Async XLA Ops:
  16.5 126.7 %all-gather.4.cloned.1.call-start = ((), (), s32[]{:S(2)}) async-start(), calls=%async_computation.9 | async-start | bytes 9584640 | tf_op jit(solution)/shard_map/all_gather | solution.py:861
  60.5 309.2 %all-gather.6.cloned.1.call-start = ((), (), s32[]{:S(2)}) async-start(), calls=%async_computation.10 | async-start | bytes 20643840 | tf_op jit(solution)/shard_map/all_gather | solution.py:861
  207.5 102.9 %all-to-all-start.1 = ((bf16[8,48,2560]{2,1,0:T(8,128)(2,1)}), bf16[8,48,2560]{2,1,0:T(8,128)(2,1)}, u32[]{:S(2)}, u32[]{:S(2)}) async-start(bf16[8,48,2560]{2,1,0:T(8,128)(2,1)} %shard_map.230), calls=%async_computation.1 | async-start | bytes 3932160 | tf_op jit(solution)/shard_map/all_to_all | solution.py:845
  215.8 247.5 %all-gather.8.cloned.1.call-start = ((), (), s32[]{:S(2)}) async-start(), calls=%async_computation.11 | async-start | bytes 10321920 | tf_op jit(solution)/shard_map/all_gather | solution.py:861
  287.1 468.3 %reduce-scatter.6.cloned.1.call-start = ((), (), s32[]{:S(2)}) async-start(), calls=%async_computation.12 | async-start | bytes 10321920 | tf_op jit(solution)/shard_map/reduce_scatter | solution.py:854
  463.1 292.3 %reduce-scatter.8.cloned.1.call-start = ((), (), s32[]{:S(2)}) async-start(), calls=%async_computation.13 | async-start | bytes 10321920 | tf_op jit(solution)/shard_map/reduce_scatter | solution.py:854
  486.3 54.0 %collective-permute-start.31 = (bf16[192,2560]{1,0:T(8,128)(2,1)}, bf16[192,2560]{1,0:T(8,128)(2,1)}, u32[]{:S(2)}, u32[]{:S(2)}) collective-permute-start(bf16[192,2560]{1,0:T(8,128)(2,1)} %get-tuple-element.169.refs_2_), channel_id=1, source_target_pairs={{0,16},{8,24},{16,0},{24,8},{1,17},{9,25},{17,1},{25,9},{2,18},{10... | collective-permute-start | bytes 2949128 | tf_op jit(solution)/shard_map/ppermute | solution.py:23
  487.7 55.0 %collective-permute-start.28 = (bf16[192,2560]{1,0:T(8,128)(2,1)}, bf16[192,2560]{1,0:T(8,128)(2,1)}, u32[]{:S(2)}, u32[]{:S(2)}) collective-permute-start(bf16[192,2560]{1,0:T(8,128)(2,1)} %get-tuple-element.170.refs_1_), channel_id=1, source_target_pairs={{0,8},{8,0},{16,24},{24,16},{1,9},{9,1},{17,25},{25,17},{2,10},{10... | collective-permute-start | bytes 2949128 | tf_op jit(solution)/shard_map/ppermute | solution.py:23
  682.8 67.0 %collective-permute-start.43 = (bf16[768,640]{1,0:T(8,128)(2,1)}, bf16[768,640]{1,0:T(8,128)(2,1)}, u32[]{:S(2)}, u32[]{:S(2)}) collective-permute-start(bf16[768,640]{1,0:T(8,128)(2,1)} %get-tuple-element.149), channel_id=1, source_target_pairs={{0,16},{8,24},{16,0},{24,8},{1,17},{9,25},{17,1},{25,9},{2,18},{10... | collective-permute-start | bytes 2949128 | tf_op jit(solution)/shard_map/ppermute | solution.py:23
  683.8 65.9 %collective-permute-start.39 = (bf16[768,640]{1,0:T(8,128)(2,1)}, bf16[768,640]{1,0:T(8,128)(2,1)}, u32[]{:S(2)}, u32[]{:S(2)}) collective-permute-start(bf16[768,640]{1,0:T(8,128)(2,1)} %get-tuple-element.151), channel_id=1, source_target_pairs={{0,8},{8,0},{16,24},{24,16},{1,9},{9,1},{17,25},{25,17},{2,10},{10... | collective-permute-start | bytes 2949128 | tf_op jit(solution)/shard_map/ppermute | solution.py:23
  712.5 108.4 %all-to-all-start.2 = ((bf16[8,48,2560]{2,1,0:T(8,128)(2,1)}), bf16[8,48,2560]{2,1,0:T(8,128)(2,1)}, u32[]{:S(2)}, u32[]{:S(2)}) async-start(bf16[8,48,2560]{2,1,0:T(8,128)(2,1)} %gather_fusion.4), calls=%async_computation.2 | async-start | bytes 3932160 | tf_op jit(solution)/shard_map/all_to_all | solution.py:845
  748.9 200.1 %reduce-scatter.14.cloned.1.call-start = ((), (), s32[]{:S(2)}) async-start(), calls=%async_computation.16 | async-start | bytes 10321920 | tf_op jit(solution)/shard_map/reduce_scatter | solution.py:854
  749.5 203.9 %reduce-scatter.12.cloned.1.call-start = ((), (), s32[]{:S(2)}) async-start(), calls=%async_computation.15 | async-start | bytes 3686400 | tf_op jit(solution)/shard_map/reduce_scatter | solution.py:854
  755.6 65.3 %collective-permute-start.48 = (bf16[320,1792]{1,0:T(8,128)(2,1)}, bf16[320,1792]{1,0:T(8,128)(2,1)}, u32[]{:S(2)}, u32[]{:S(2)}) collective-permute-start(bf16[320,1792]{1,0:T(8,128)(2,1)} %shard_map.255.refs_0_), channel_id=1, source_target_pairs={{0,8},{8,0},{16,24},{24,16},{1,9},{9,1},{17,25},{25,17},{2,10},{10... | collective-permute-start | bytes 3440648 | tf_op jit(solution)/shard_map/ppermute | solution.py:23
  756.4 64.5 %collective-permute-start.47 = (bf16[224,2560]{1,0:T(8,128)(2,1)}, bf16[224,2560]{1,0:T(8,128)(2,1)}, u32[]{:S(2)}, u32[]{:S(2)}) collective-permute-start(bf16[224,2560]{1,0:T(8,128)(2,1)} %shard_map.254.refs_2_.refs_0_), channel_id=1, source_target_pairs={{0,24},{8,16},{16,8},{24,0},{1,25},{9,17},{17,9},{25,1},{2,26},{10... | collective-permute-start | bytes 3440648 | tf_op jit(solution)/shard_map/ppermute | solution.py:23
  758.0 73.3 %collective-permute-start.46 = (bf16[224,2560]{1,0:T(8,128)(2,1)}, bf16[224,2560]{1,0:T(8,128)(2,1)}, u32[]{:S(2)}, u32[]{:S(2)}) collective-permute-start(bf16[224,2560]{1,0:T(8,128)(2,1)} %shard_map.254.refs_2_.refs_0_), channel_id=1, source_target_pairs={{0,16},{8,24},{16,0},{24,8},{1,17},{9,25},{17,1},{25,9},{2,18},{10... | collective-permute-start | bytes 3440648 | tf_op jit(solution)/shard_map/ppermute | solution.py:23
  758.2 73.1 %collective-permute-start.45 = (bf16[224,2560]{1,0:T(8,128)(2,1)}, bf16[224,2560]{1,0:T(8,128)(2,1)}, u32[]{:S(2)}, u32[]{:S(2)}) collective-permute-start(bf16[224,2560]{1,0:T(8,128)(2,1)} %shard_map.254.refs_2_.refs_0_), channel_id=1, source_target_pairs={{0,8},{8,0},{16,24},{24,16},{1,9},{9,1},{17,25},{25,17},{2,10},{10... | collective-permute-start | bytes 3440648 | tf_op jit(solution)/shard_map/ppermute | solution.py:23
  808.9 215.8 %reduce-scatter.10.cloned.1.call-start = ((), (), s32[]{:S(2)}) async-start(), calls=%async_computation.14 | async-start | bytes 5898240 | tf_op jit(solution)/shard_map/reduce_scatter | solution.py:854
  939.8 120.5 %all-to-all-start.3 = ((bf16[8,48,2560]{2,1,0:T(8,128)(2,1)}), bf16[8,48,2560]{2,1,0:T(8,128)(2,1)}, u32[]{:S(2)}, u32[]{:S(2)}) async-start(bf16[8,48,2560]{2,1,0:T(8,128)(2,1)} %gather_fusion.6), calls=%async_computation.5 | async-start | bytes 3932160 | tf_op jit(solution)/shard_map/all_to_all | solution.py:845
  952.2 72.5 %collective-permute-start.68 = (bf16[320,896]{1,0:T(8,128)(2,1)S(1)}, bf16[320,896]{1,0:T(8,128)(2,1)S(1)}, u32[]{:S(2)}, u32[]{:S(2)}) collective-permute-start(bf16[320,896]{1,0:T(8,128)(2,1)S(1)} %get-tuple-element.179.refs_1_), channel_id=1, source_target_pairs={{0,8},{8,0},{16,24},{24,16},{1,9},{9,1},{17,25},{25,17},{2,10},{10... | collective-permute-start | bytes 1720328 | tf_op jit(solution)/shard_map/ppermute | solution.py:23
  953.2 74.6 %collective-permute-start.69 = (bf16[320,896]{1,0:T(8,128)(2,1)S(1)}, bf16[320,896]{1,0:T(8,128)(2,1)}, u32[]{:S(2)}, u32[]{:S(2)}) collective-permute-start(bf16[320,896]{1,0:T(8,128)(2,1)S(1)} %get-tuple-element.180.refs_0_), channel_id=1, source_target_pairs={{0,16},{8,24},{16,0},{24,8},{1,17},{9,25},{17,1},{25,9},{2,18},{10... | collective-permute-start | bytes 1720328 | tf_op jit(solution)/shard_map/ppermute | solution.py:23
  965.7 63.3 %collective-permute-start.67 = (bf16[320,640]{1,0:T(8,128)(2,1)}, bf16[320,640]{1,0:T(8,128)(2,1)S(1)}, u32[]{:S(2)}, u32[]{:S(2)}) collective-permute-start(bf16[320,640]{1,0:T(8,128)(2,1)} %shard_map.265.refs_1_.refs_0_), channel_id=1, source_target_pairs={{0,24},{8,16},{16,8},{24,0},{1,25},{9,17},{17,9},{25,1},{2,26},{10... | collective-permute-start | bytes 1228808 | tf_op jit(solution)/shard_map/ppermute | solution.py:23
  967.1 62.9 %collective-permute-start.66 = (bf16[320,640]{1,0:T(8,128)(2,1)}, bf16[320,640]{1,0:T(8,128)(2,1)S(1)}, u32[]{:S(2)}, u32[]{:S(2)}) collective-permute-start(bf16[320,640]{1,0:T(8,128)(2,1)} %shard_map.265.refs_1_.refs_0_), channel_id=1, source_target_pairs={{0,16},{8,24},{16,0},{24,8},{1,17},{9,25},{17,1},{25,9},{2,18},{10... | collective-permute-start | bytes 1228808 | tf_op jit(solution)/shard_map/ppermute | solution.py:23
  967.6 63.4 %collective-permute-start.65 = (bf16[320,640]{1,0:T(8,128)(2,1)}, bf16[320,640]{1,0:T(8,128)(2,1)}, u32[]{:S(2)}, u32[]{:S(2)}) collective-permute-start(bf16[320,640]{1,0:T(8,128)(2,1)} %shard_map.265.refs_1_.refs_0_), channel_id=1, source_target_pairs={{0,8},{8,0},{16,24},{24,16},{1,9},{9,1},{17,25},{25,17},{2,10},{10... | collective-permute-start | bytes 1228808 | tf_op jit(solution)/shard_map/ppermute | solution.py:23
  (142 other events, 2570.0 us)
Sparse Core Ops, SparseCore 0:
  60.6 82.5 all-gather.3
  145.4 201.1 all-gather.5
  348.2 89.9 all-gather.7
  463.2 104.1 reduce-scatter.5
  570.2 95.3 reduce-scatter.7
  751.8 129.2 reduce-scatter.13
  883.9 37.1 reduce-scatter.11
  923.5 101.1 reduce-scatter.9

commit v8 on v7

--- a/solution.py
+++ b/solution.py
@@ -308,7 +308,7 @@
         ],
         compiler_params=pltpu.CompilerParams(vmem_limit_bytes=56 * 2**20),
         cost_estimate=pl.CostEstimate(
-            flops=200 * 10**9, bytes_accessed=0, transcendentals=0
+            flops=100 * 10**9, bytes_accessed=0, transcendentals=0
         ),
     )(q, k, v, grad, lse_rows, start_row, cosine, sine_back, *when)
 
@@ -945,7 +945,7 @@
         query_low, key_low, value_low, d_mixed, logs.T, start[None, :], cosine, sine
     )
     back_one, grad_gain_one = attend_norm_call(
-        place, d_qkv, qkv_all, group_inputs, gain_one, own_d_hidden, parts, gone_result, *down_first, *gate_first[:2]
+        place, d_qkv, qkv_all, group_inputs, gain_one, own_d_hidden, parts, *down_first, *gate_first[:2]
     )
     gain_grads = jnp.concatenate(
         [grad_gain_one, grad_gain_two, jnp.zeros((6, width), wide)], axis=0

time: 1090 us -> 1060 us (0.972)
  waiting for transfers between devices: 325 us -> 298 us
    reduce_scatter x5, waiting for transfers between devices: 56.4 us -> 0.03 us  [scatter_fsdp(): return lax.psum_scatter(matrix, 'fsdp', scatter_dimension=0, tiled=True)]
    ppermute x72, waiting for transfers between devices: 198 us -> 238 us  [swap(): return lax.ppermute(value, 'sp', [(i, i ^ bit) for i in range(size)])]
    unnamed x164 -> x168, local copies, waits for them, and re-layouts: 48.6 us -> 50.7 us
  transfers between devices with their start and end apart: 84 -> 84, of which waited for: 30 -> 32; matrix products, arithmetic and copies ran while one was open for 16% -> 17% of each run, Pallas kernels for 35% -> 36%
where the time goes in v8:
time: 1060 us; the launch traced here: 1050 us
  Pallas kernels  383 us (36%)
  waiting for transfers between devices  298 us (28%)
  local copies, waits for them, and re-layouts  181 us (17%)
  starting transfers between devices  121 us (11%)
  other arithmetic  47.2 us (4%)
  between operations  15.7 us (1%)
    ppermute x72, waiting for transfers between devices, swap(): return lax.ppermute(value, 'sp', [(i, i ^ bit) for i in range(size)])  238 us
    pallas_call x3, Pallas kernels, rows_call(): pl.pallas_call(rows_kernel, grid=(columns // block,), in_specs=[pl.BlockS...  61.5 us
    ppermute x72, starting transfers between devices, swap(): return lax.ppermute(value, 'sp', [(i, i ^ bit) for i in range(size)])  60.9 us
    all_to_all x4, waiting for transfers between devices, deal(): lax.all_to_all(blocks, 'fsdp', split_axis=0, concat_axis=0, tiled=True)  60.3 us
    all_to_all x4, starting transfers between devices, deal(): lax.all_to_all(blocks, 'fsdp', split_axis=0, concat_axis=0, tiled=True)  58.7 us
    unnamed x168, local copies, waits for them, and re-layouts  50.7 us
    pallas_call x1, Pallas kernels, attend_back_call(): pl.pallas_call(functools.partial(attend_back_kernel, heads, keys, block),...  49.9 us
    pallas_call x1, Pallas kernels, mlp_back_call(): pl.pallas_call(mlp_back_kernel, grid=(total // block,), in_specs=[row(uni...  43.3 us
  transfers between devices with their start and end apart: 84, of which 32 were waited for; matrix products, arithmetic and copies ran while one was open for 17% of the time, Pallas kernels for 36%

profile of v8, /device:TPU:9, one launch (start us, length us, event | category | flops | bytes accessed | tf_op | source)
XLA Modules:
  0.0 1046.3 jit_solution(15244962459626410667)
XLA Ops:
  21.2 38.0 %all-to-all-done.refs_1_._ = bf16[8,48,2560]{2,1,0:T(8,128)(2,1)S(1)} async-done(((bf16[8,48,2560]{2,1,0:T(8,128)(2,1)}), bf16[8,48,2560]{2,1,0:T(8,128)(2,1)S(1)}, u32[]{:S(2)}, u32[]{:S(2)}) %all-to-all-start) | async-done | bytes 1966112 | tf_op jit(solution)/shard_map/all_to_all | solution.py:845
  97.8 15.4 %collective-permute-done.1 = bf16[192,2560]{1,0:T(8,128)(2,1)} collective-permute-done((bf16[192,2560]{1,0:T(8,128)(2,1)}, bf16[192,2560]{1,0:T(8,128)(2,1)}, u32[]{:S(2)}, u32[]{:S(2)}) %collective-permute-start.1) | collective-permute-done | bytes 983072 | tf_op jit(solution)/shard_map/ppermute | solution.py:23
  126.1 12.4 %collective-permute-done.4 = bf16[192,2560]{1,0:T(8,128)(2,1)} collective-permute-done((bf16[192,2560]{1,0:T(8,128)(2,1)S(1)}, bf16[192,2560]{1,0:T(8,128)(2,1)}, u32[]{:S(2)}, u32[]{:S(2)}) %collective-permute-start.4) | collective-permute-done | bytes 983072 | tf_op jit(solution)/shard_map/ppermute | solution.py:23
  146.1 24.3 %shard_map.223 = (bf16[1536,2560]{1,0:T(8,128)(2,1)}, bf16[1536,1024]{1,0:T(8,128)(2,1)}, bf16[1536,256]{1,0:T(8,128)(2,1)S(1)}, bf16[1536,256]{1,0:T(8,128)(2,1)S(1)}) custom-call(bf16[1536,2560]{1,0:T(8,128)(2,1)} %bitcast.17.x_ref, f32[1,2560]{1,0:T(1,128)S(1)} %reshape.298.gain_ref, bf16[2560,1664]{1,0:T(8,128)(2,1)} %all-gather.4.cloned.1.call-done.weight_ref, ...), custom_call_target="tpu_custom_call" | custom-call | flops 96000000000 | tf_op jit(solution)/shard_map/pallas_call | solution.py:177
  172.2 27.7 %shard_map.224 = (bf16[1536,640]{1,0:T(8,128)(2,1)}, f32[1536,8]{1,0:T(8,128)}) custom-call(bf16[1536,1024]{1,0:T(8,128)(2,1)} %get-tuple-element.72.q_ref, bf16[1536,256]{1,0:T(8,128)(2,1)} %copy-done.40, bf16[1536,256]{1,0:T(8,128)(2,1)} %copy-done.41, s32[1536,1]{1,0:T(8,128)} %broadcast_in_dim.224.start_ref), custom_call_target="tpu_custom_call" | custom-call | flops 112000000000 | tf_op jit(solution)/shard_map/pallas_call | solution.py:226
  229.4 17.3 %collective-permute-done.10 = bf16[768,640]{1,0:T(8,128)(2,1)S(1)} collective-permute-done((bf16[768,640]{1,0:T(8,128)(2,1)}, bf16[768,640]{1,0:T(8,128)(2,1)S(1)}, u32[]{:S(2)}, u32[]{:S(2)}) %collective-permute-start.10) | collective-permute-done | bytes 983072 | tf_op jit(solution)/shard_map/ppermute | solution.py:23
  247.2 19.2 %collective-permute-done.13 = bf16[768,640]{1,0:T(8,128)(2,1)S(1)} collective-permute-done((bf16[768,640]{1,0:T(8,128)(2,1)}, bf16[768,640]{1,0:T(8,128)(2,1)S(1)}, u32[]{:S(2)}, u32[]{:S(2)}) %collective-permute-start.13) | collective-permute-done | bytes 983072 | tf_op jit(solution)/shard_map/ppermute | solution.py:23
  288.3 22.3 %all-to-all-done.1.refs_0_ = bf16[8,48,2560]{2,1,0:T(8,128)(2,1)} async-done(((bf16[8,48,2560]{2,1,0:T(8,128)(2,1)}), bf16[8,48,2560]{2,1,0:T(8,128)(2,1)}, u32[]{:S(2)}, u32[]{:S(2)}) %all-to-all-start.1) | async-done | bytes 1966112 | tf_op jit(solution)/shard_map/all_to_all | solution.py:845
  328.3 16.4 %collective-permute-done.19 = bf16[768,640]{1,0:T(8,128)(2,1)S(1)} collective-permute-done((bf16[768,640]{1,0:T(8,128)(2,1)}, bf16[768,640]{1,0:T(8,128)(2,1)S(1)}, u32[]{:S(2)}, u32[]{:S(2)}) %collective-permute-start.19) | collective-permute-done | bytes 983072 | tf_op jit(solution)/shard_map/ppermute | solution.py:23
  369.6 36.7 %shard_map.228 = (bf16[1536,1792]{1,0:T(8,128)(2,1)}, bf16[1536,1792]{1,0:T(8,128)(2,1)}, bf16[1536,1792]{1,0:T(8,128)(2,1)}) custom-call(bf16[1536,2560]{1,0:T(8,128)(2,1)} %copy-done.5, bf16[2560,3584]{1,0:T(8,128)(2,1)} %all-gather.6.cloned.1.call-done.gate_weight_ref.up_weight_ref.weight_ref, ...), custom_call_target="tpu_custom_call" | custom-call | flops 147999997952 | tf_op jit(solution)/shard_map/pallas_call | solution.py:334
  442.8 20.3 %shard_map.235.refs_0_ = bf16[1792,2560]{1,0:T(8,128)(2,1)} custom-call(bf16[1536,1792]{1,0:T(8,128)(2,1)} %get-tuple-element.78.refs_1_.left_ref, bf16[1536,2560]{1,0:T(8,128)(2,1)} %bitcast.190), custom_call_target="tpu_custom_call" | custom-call | flops 80000000000 | tf_op jit(solution)/shard_map/pallas_call | solution.py:602
  463.4 19.9 %shard_map.236.refs_0_ = bf16[1536,2560]{1,0:T(8,128)(2,1)} custom-call(bf16[1536,1792]{1,0:T(8,128)(2,1)} %get-tuple-element.78.refs_1_.left_ref, bf16[1792,2560]{1,0:T(8,128)(2,1)} %all-gather.8.cloned.1.call-done.right_ref.down_ref, bf16[1792,2560]{1,0:T(8,128)(2,1)} %shard_map.235.refs_0_), custom_call_target="tpu_custom_call" | custom-call | flops 80000000000 | tf_op jit(solution)/shard_map/pallas_call | solution.py:627
  488.7 25.5 %shard_map.238 = (bf16[1536,1792]{1,0:T(8,128)(2,1)}, bf16[1536,1792]{1,0:T(8,128)(2,1)}) custom-call(bf16[1536,2560]{1,0:T(8,128)(2,1)} %bitcast.191, bf16[1792,2560]{1,0:T(8,128)(2,1)} %all-gather.8.cloned.1.call-done.right_ref.down_ref, bf16[1536,1792]{1,0:T(8,128)(2,1)} %get-tuple-element.79.gate_ref, bf16[1536,1792]{1,0:T(8,128)(2,1)} %get-tuple-element.80.up_ref, ...), custom_call_target="tpu_custom_call" | custom-call | flops 103999995904 | tf_op jit(solution)/shard_map/pallas_call | solution.py:366
  519.8 20.5 %shard_map.239.refs_1_.refs_0_ = bf16[2560,1792]{1,0:T(8,128)(2,1)} custom-call(bf16[1536,2560]{1,0:T(8,128)(2,1)} %copy-done.5, bf16[1536,1792]{1,0:T(8,128)(2,1)} %get-tuple-element.81.right_ref.d_gate_ref), custom_call_target="tpu_custom_call" | custom-call | flops 80000000000 | tf_op jit(solution)/shard_map/pallas_call | solution.py:602
  548.9 43.3 %shard_map.242 = (bf16[4,1536,640]{2,1,0:T(8,128)(2,1)}, f32[1,2560]{1,0:T(1,128)}) custom-call(bf16[1536,1792]{1,0:T(8,128)(2,1)} %get-tuple-element.81.right_ref.d_gate_ref, bf16[1536,1792]{1,0:T(8,128)(2,1)} %get-tuple-element.92.d_up_ref.right_ref, bf16[2560,3584]{1,0:T(8,128)(2,1)} %all-gather.6.cloned.1.call-done.gate_weight_ref.up_weight_ref.weight_ref, ...), custom_call_target="tpu_custom_call" | custom-call | flops 176000008192 | tf_op jit(solution)/shard_map/pallas_call | solution.py:421
  613.2 20.7 %shard_map.245.refs_1_.refs_0_ = bf16[2560,1792]{1,0:T(8,128)(2,1)} custom-call(bf16[1536,2560]{1,0:T(8,128)(2,1)} %copy-done.5, bf16[1536,1792]{1,0:T(8,128)(2,1)} %get-tuple-element.92.d_up_ref.right_ref, bf16[768,640]{1,0:T(8,128)(2,1)} %copy-done.45, bf16[768,640]{1,0:T(8,128)(2,1)} %copy-done.44), custom_call_target="tpu_custom_call" | custom-call | tf_op jit(solution)/shard_map/pallas_call | solution.py:602
  636.8 14.7 %collective-permute-done.38 = bf16[768,640]{1,0:T(8,128)(2,1)S(1)} collective-permute-done((bf16[768,640]{1,0:T(8,128)(2,1)S(1)}, bf16[768,640]{1,0:T(8,128)(2,1)S(1)}, u32[]{:S(2)}, u32[]{:S(2)}) %collective-permute-start.38) | collective-permute-done | bytes 983072 | tf_op jit(solution)/shard_map/ppermute | solution.py:23
  715.6 35.3 %all-to-all-start.2 = ((bf16[8,48,2560]{2,1,0:T(8,128)(2,1)}), bf16[8,48,2560]{2,1,0:T(8,128)(2,1)}, u32[]{:S(2)}, u32[]{:S(2)}) async-start(bf16[8,48,2560]{2,1,0:T(8,128)(2,1)} %gather_fusion.4), calls=%async_computation.2 | async-start | bytes 3932160 | tf_op jit(solution)/shard_map/all_to_all | solution.py:845
  760.7 49.9 %shard_map.253.d_qkv_ref = bf16[1536,960]{1,0:T(8,128)(2,1)} custom-call(bf16[1536,1024]{1,0:T(8,128)(2,1)} %get-tuple-element.72.q_ref, bf16[1536,256]{1,0:T(8,128)(2,1)} %copy-done.40, bf16[1536,256]{1,0:T(8,128)(2,1)} %copy-done.41, bf16[1536,640]{1,0:T(8,128)(2,1)} %pad_maximum_fusion.grad_ref.refs_1_, f32[8,1536]{1,0:T(8,128)} %bitcast.208, ...), custom_call_target="tpu_custom_call" | custom-call | flops 99999997952 | tf_op jit(solution)/shard_map/pallas_call | solution.py:299
  813.0 19.6 %collective-permute-done.46.refs_1_.refs_2_ = bf16[224,2560]{1,0:T(8,128)(2,1)} collective-permute-done((bf16[224,2560]{1,0:T(8,128)(2,1)S(1)}, bf16[224,2560]{1,0:T(8,128)(2,1)}, u32[]{:S(2)}, u32[]{:S(2)}) %collective-permute-start.46) | collective-permute-done | bytes 1146912 | tf_op jit(solution)/shard_map/ppermute | solution.py:23
  832.7 19.6 %shard_map.256 = (bf16[1536,2560]{1,0:T(8,128)(2,1)}, f32[1,2560]{1,0:T(1,128)}) custom-call(s32[1]{0:T(128)} %bitcast.37.place_ref, bf16[1536,960]{1,0:T(8,128)(2,1)} %shard_map.253.d_qkv_ref, bf16[2560,1664]{1,0:T(8,128)(2,1)} %all-gather.4.cloned.1.call-done.weight_ref, bf16[1536,2560]{1,0:T(8,128)(2,1)} %bitcast.17.x_ref, f32[1,2560]{1,0:T(1,128)} %copy-done.37, ...), custom_call_target="tpu_custom_call" | custom-call | flops 80000000000 | tf_op jit(solution)/shard_map/pallas_call | solution.py:462
  858.0 11.5 %shard_map.262 = bf16[2560,1024]{1,0:T(8,128)(2,1)} custom-call(bf16[1536,2560]{1,0:T(8,128)(2,1)} %get-tuple-element.126.normed_ref, bf16[1536,960]{1,0:T(8,128)(2,1)S(1)} %copy-done.39, f32[8,2560]{1,0:T(8,128)S(1)} %maximum_maximum_fusion.2.gain_ref, bf16[320,1792]{1,0:T(8,128)(2,1)S(1)} %collective-permute-done.53.refs_3_.refs_0_), custom_call_target="tpu_custom_call" | custom-call | flops 48000000000 | tf_op jit(solution)/shard_map/pallas_call | solution.py:656
  916.7 19.6 %collective-permute-done.56 = bf16[192,2560]{1,0:T(8,128)(2,1)S(1)} collective-permute-done((bf16[192,2560]{1,0:T(8,128)(2,1)S(1)}, bf16[192,2560]{1,0:T(8,128)(2,1)S(1)}, u32[]{:S(2)}, u32[]{:S(2)}) %collective-permute-start.56) | collective-permute-done | bytes 983072 | tf_op jit(solution)/shard_map/ppermute | solution.py:23
  955.4 11.4 %collective-permute-done.58.refs_2_.refs_5_ = bf16[320,896]{1,0:T(8,128)(2,1)S(1)} collective-permute-done((bf16[320,896]{1,0:T(8,128)(2,1)S(1)}, bf16[320,896]{1,0:T(8,128)(2,1)S(1)}, u32[]{:S(2)}, u32[]{:S(2)}) %collective-permute-start.58) | collective-permute-done | bytes 573472 | tf_op jit(solution)/shard_map/ppermute | solution.py:23
  (500 shorter events, 469.0 us)
Async XLA Ops:
  16.5 126.6 %all-gather.4.cloned.1.call-start = ((), (), s32[]{:S(2)}) async-start(), calls=%async_computation.9 | async-start | bytes 9584640 | tf_op jit(solution)/shard_map/all_gather | solution.py:861
  60.5 309.1 %all-gather.6.cloned.1.call-start = ((), (), s32[]{:S(2)}) async-start(), calls=%async_computation.10 | async-start | bytes 20643840 | tf_op jit(solution)/shard_map/all_gather | solution.py:861
  207.7 103.0 %all-to-all-start.1 = ((bf16[8,48,2560]{2,1,0:T(8,128)(2,1)}), bf16[8,48,2560]{2,1,0:T(8,128)(2,1)}, u32[]{:S(2)}, u32[]{:S(2)}) async-start(bf16[8,48,2560]{2,1,0:T(8,128)(2,1)} %shard_map.230), calls=%async_computation.1 | async-start | bytes 3932160 | tf_op jit(solution)/shard_map/all_to_all | solution.py:845
  216.0 247.4 %all-gather.8.cloned.1.call-start = ((), (), s32[]{:S(2)}) async-start(), calls=%async_computation.11 | async-start | bytes 10321920 | tf_op jit(solution)/shard_map/all_gather | solution.py:861
  287.2 469.3 %reduce-scatter.6.cloned.1.call-start = ((), (), s32[]{:S(2)}) async-start(), calls=%async_computation.12 | async-start | bytes 10321920 | tf_op jit(solution)/shard_map/reduce_scatter | solution.py:854
  366.5 50.2 %collective-permute-start.22 = (bf16[192,2560]{1,0:T(8,128)(2,1)}, bf16[192,2560]{1,0:T(8,128)(2,1)}, u32[]{:S(2)}, u32[]{:S(2)}) collective-permute-start(bf16[192,2560]{1,0:T(8,128)(2,1)} %get-tuple-element.171), channel_id=1, source_target_pairs={{0,8},{8,0},{16,24},{24,16},{1,9},{9,1},{17,25},{25,17},{2,10},{10... | collective-permute-start | bytes 2949128 | tf_op jit(solution)/shard_map/ppermute | solution.py:23
  368.1 53.0 %collective-permute-start.24 = (bf16[192,2560]{1,0:T(8,128)(2,1)}, bf16[192,2560]{1,0:T(8,128)(2,1)}, u32[]{:S(2)}, u32[]{:S(2)}) collective-permute-start(bf16[192,2560]{1,0:T(8,128)(2,1)} %get-tuple-element.171), channel_id=1, source_target_pairs={{0,16},{8,24},{16,0},{24,8},{1,17},{9,25},{17,1},{25,9},{2,18},{10... | collective-permute-start | bytes 2949128 | tf_op jit(solution)/shard_map/ppermute | solution.py:23
  369.0 50.0 %collective-permute-start.23 = (bf16[192,2560]{1,0:T(8,128)(2,1)}, bf16[192,2560]{1,0:T(8,128)(2,1)}, u32[]{:S(2)}, u32[]{:S(2)}) collective-permute-start(bf16[192,2560]{1,0:T(8,128)(2,1)} %get-tuple-element.172), channel_id=1, source_target_pairs={{0,16},{8,24},{16,0},{24,8},{1,17},{9,25},{17,1},{25,9},{2,18},{10... | collective-permute-start | bytes 2949128 | tf_op jit(solution)/shard_map/ppermute | solution.py:23
  463.1 293.4 %reduce-scatter.8.cloned.1.call-start = ((), (), s32[]{:S(2)}) async-start(), calls=%async_computation.13 | async-start | bytes 10321920 | tf_op jit(solution)/shard_map/reduce_scatter | solution.py:854
  486.3 54.5 %collective-permute-start.31 = (bf16[192,2560]{1,0:T(8,128)(2,1)}, bf16[192,2560]{1,0:T(8,128)(2,1)}, u32[]{:S(2)}, u32[]{:S(2)}) collective-permute-start(bf16[192,2560]{1,0:T(8,128)(2,1)} %get-tuple-element.169.refs_2_), channel_id=1, source_target_pairs={{0,16},{8,24},{16,0},{24,8},{1,17},{9,25},{17,1},{25,9},{2,18},{10... | collective-permute-start | bytes 2949128 | tf_op jit(solution)/shard_map/ppermute | solution.py:23
  487.4 55.8 %collective-permute-start.28 = (bf16[192,2560]{1,0:T(8,128)(2,1)}, bf16[192,2560]{1,0:T(8,128)(2,1)}, u32[]{:S(2)}, u32[]{:S(2)}) collective-permute-start(bf16[192,2560]{1,0:T(8,128)(2,1)} %get-tuple-element.170.refs_1_), channel_id=1, source_target_pairs={{0,8},{8,0},{16,24},{24,16},{1,9},{9,1},{17,25},{25,17},{2,10},{10... | collective-permute-start | bytes 2949128 | tf_op jit(solution)/shard_map/ppermute | solution.py:23
  540.3 410.7 %reduce-scatter.14.cloned.1.call-start = ((), (), s32[]{:S(2)}) async-start(), calls=%async_computation.16 | async-start | bytes 10321920 | tf_op jit(solution)/shard_map/reduce_scatter | solution.py:854
  685.9 65.2 %collective-permute-start.43 = (bf16[768,640]{1,0:T(8,128)(2,1)}, bf16[768,640]{1,0:T(8,128)(2,1)}, u32[]{:S(2)}, u32[]{:S(2)}) collective-permute-start(bf16[768,640]{1,0:T(8,128)(2,1)} %get-tuple-element.149), channel_id=1, source_target_pairs={{0,16},{8,24},{16,0},{24,8},{1,17},{9,25},{17,1},{25,9},{2,18},{10... | collective-permute-start | bytes 2949128 | tf_op jit(solution)/shard_map/ppermute | solution.py:23
  686.5 64.6 %collective-permute-start.39 = (bf16[768,640]{1,0:T(8,128)(2,1)}, bf16[768,640]{1,0:T(8,128)(2,1)}, u32[]{:S(2)}, u32[]{:S(2)}) collective-permute-start(bf16[768,640]{1,0:T(8,128)(2,1)} %get-tuple-element.151), channel_id=1, source_target_pairs={{0,8},{8,0},{16,24},{24,16},{1,9},{9,1},{17,25},{25,17},{2,10},{10... | collective-permute-start | bytes 2949128 | tf_op jit(solution)/shard_map/ppermute | solution.py:23
  715.6 159.9 %all-to-all-start.2 = ((bf16[8,48,2560]{2,1,0:T(8,128)(2,1)}), bf16[8,48,2560]{2,1,0:T(8,128)(2,1)}, u32[]{:S(2)}, u32[]{:S(2)}) async-start(bf16[8,48,2560]{2,1,0:T(8,128)(2,1)} %gather_fusion.4), calls=%async_computation.2 | async-start | bytes 3932160 | tf_op jit(solution)/shard_map/all_to_all | solution.py:845
  750.9 204.5 %reduce-scatter.12.cloned.1.call-start = ((), (), s32[]{:S(2)}) async-start(), calls=%async_computation.15 | async-start | bytes 3686400 | tf_op jit(solution)/shard_map/reduce_scatter | solution.py:854
  756.5 54.4 %collective-permute-start.49 = (bf16[320,1792]{1,0:T(8,128)(2,1)}, bf16[320,1792]{1,0:T(8,128)(2,1)}, u32[]{:S(2)}, u32[]{:S(2)}) collective-permute-start(bf16[320,1792]{1,0:T(8,128)(2,1)} %shard_map.255.refs_0_), channel_id=1, source_target_pairs={{0,16},{8,24},{16,0},{24,8},{1,17},{9,25},{17,1},{25,9},{2,18},{10... | collective-permute-start | bytes 3440648 | tf_op jit(solution)/shard_map/ppermute | solution.py:23
  757.1 56.0 %collective-permute-start.48 = (bf16[320,1792]{1,0:T(8,128)(2,1)}, bf16[320,1792]{1,0:T(8,128)(2,1)}, u32[]{:S(2)}, u32[]{:S(2)}) collective-permute-start(bf16[320,1792]{1,0:T(8,128)(2,1)} %shard_map.255.refs_0_), channel_id=1, source_target_pairs={{0,8},{8,0},{16,24},{24,16},{1,9},{9,1},{17,25},{25,17},{2,10},{10... | collective-permute-start | bytes 3440648 | tf_op jit(solution)/shard_map/ppermute | solution.py:23
  758.0 55.0 %collective-permute-start.47 = (bf16[224,2560]{1,0:T(8,128)(2,1)S(1)}, bf16[224,2560]{1,0:T(8,128)(2,1)}, u32[]{:S(2)}, u32[]{:S(2)}) collective-permute-start(bf16[224,2560]{1,0:T(8,128)(2,1)S(1)} %copy-done.14), channel_id=1, source_target_pairs={{0,24},{8,16},{16,8},{24,0},{1,25},{9,17},{17,9},{25,1},{2,26},{10... | collective-permute-start | bytes 3440648 | tf_op jit(solution)/shard_map/ppermute | solution.py:23
  759.2 73.4 %collective-permute-start.46 = (bf16[224,2560]{1,0:T(8,128)(2,1)S(1)}, bf16[224,2560]{1,0:T(8,128)(2,1)}, u32[]{:S(2)}, u32[]{:S(2)}) collective-permute-start(bf16[224,2560]{1,0:T(8,128)(2,1)S(1)} %copy-done.14), channel_id=1, source_target_pairs={{0,16},{8,24},{16,0},{24,8},{1,17},{9,25},{17,1},{25,9},{2,18},{10... | collective-permute-start | bytes 3440648 | tf_op jit(solution)/shard_map/ppermute | solution.py:23
  759.7 73.0 %collective-permute-start.45 = (bf16[224,2560]{1,0:T(8,128)(2,1)S(1)}, bf16[224,2560]{1,0:T(8,128)(2,1)}, u32[]{:S(2)}, u32[]{:S(2)}) collective-permute-start(bf16[224,2560]{1,0:T(8,128)(2,1)S(1)} %copy-done.14), channel_id=1, source_target_pairs={{0,8},{8,0},{16,24},{24,16},{1,9},{9,1},{17,25},{25,17},{2,10},{10... | collective-permute-start | bytes 3440648 | tf_op jit(solution)/shard_map/ppermute | solution.py:23
  810.6 159.6 %reduce-scatter.10.cloned.1.call-start = ((), (), s32[]{:S(2)}) async-start(), calls=%async_computation.14 | async-start | bytes 5898240 | tf_op jit(solution)/shard_map/reduce_scatter | solution.py:854
  885.3 51.0 %collective-permute-start.50 = (bf16[192,2560]{1,0:T(8,128)(2,1)}, bf16[192,2560]{1,0:T(8,128)(2,1)}, u32[]{:S(2)}, u32[]{:S(2)}) collective-permute-start(bf16[192,2560]{1,0:T(8,128)(2,1)} %get-tuple-element.143), channel_id=1, source_target_pairs={{0,8},{8,0},{16,24},{24,16},{1,9},{9,1},{17,25},{25,17},{2,10},{10... | collective-permute-start | bytes 2949128 | tf_op jit(solution)/shard_map/ppermute | solution.py:23
  941.8 87.3 %all-to-all-start.3 = ((bf16[8,48,2560]{2,1,0:T(8,128)(2,1)}), bf16[8,48,2560]{2,1,0:T(8,128)(2,1)}, u32[]{:S(2)}, u32[]{:S(2)}) async-start(bf16[8,48,2560]{2,1,0:T(8,128)(2,1)} %gather_fusion.6), calls=%async_computation.5 | async-start | bytes 3932160 | tf_op jit(solution)/shard_map/all_to_all | solution.py:845
  (144 other events, 2445.2 us)
Sparse Core Ops, SparseCore 0:
  60.6 82.4 all-gather.3
  145.3 201.1 all-gather.5
  348.2 89.8 all-gather.7
  463.2 104.1 reduce-scatter.5
  570.1 95.2 reduce-scatter.7
  667.6 144.5 reduce-scatter.13
  815.1 39.4 reduce-scatter.11
  870.7 59.2 reduce-scatter.9

commit v9 on v8

--- a/solution.py
+++ b/solution.py
@@ -70,7 +70,7 @@
     return jnp.stack(here, axis=0)
 
 
-def scatter_sp(parts, hook=None):
+def scatter_sp(parts, hook=None, apart=True):
     size = lax.axis_size("sp")
     if size != 4:
         summed = lax.psum_scatter(parts, "sp", scatter_dimension=0, tiled=False)
@@ -96,7 +96,7 @@
 
     far = block(parts, 3, True), block(parts, 3, False)
     from_x, from_y = swap(far[0], 1), swap(far[1], 2)
-    parts = after(parts, *far)
+    parts = after(parts, *far) if apart else parts
     given = hook((from_x, from_y)) if hook else ()
     if given:
         from_x, from_y = after(from_x, *given), after(from_y, *given)
@@ -610,7 +610,7 @@
         out_specs=pl.BlockSpec((rows, block), lambda j: (0, j)),
         out_shape=jax.ShapeDtypeStruct((rows, columns), jnp.bfloat16),
         compiler_params=pltpu.CompilerParams(vmem_limit_bytes=56 * 2**20),
-        cost_estimate=pl.CostEstimate(flops=0 if when else 80 * 10**9, bytes_accessed=0, transcendentals=0),
+        cost_estimate=pl.CostEstimate(flops=0 if len(when) > 1 else 80 * 10**9, bytes_accessed=0, transcendentals=0),
     )(left, right, *when)
 
 
@@ -913,12 +913,12 @@
     active_low, gate, upward = gate_up_call(normed_two, gate_up_all)
     own_incoming = after(in_place(after(came_incoming, own_hidden)), normed_two)
     group_incoming = gather_sp(own_incoming, active_low)[0].reshape(-1, width)
-    grad_down = rows_call(active_low, group_incoming)
-    result_part = product_call(active_low, down_all, grad_down)
-    d_gate, d_up = unit_back_call(group_incoming, down_all, gate, upward, result_part)
+    result_part = product_call(active_low, down_all)
+    grad_down = rows_call(active_low, group_incoming, result_part)
+    d_gate, d_up = unit_back_call(group_incoming, down_all, gate, upward, grad_down)
     grad_gate = rows_call(normed_two, d_gate)
     result_sum, sums_result, last_result, _ = scatter_sp(
-        result_part.reshape(parts, rows, width), lambda first: (grad_gate,)
+        result_part.reshape(parts, rows, width), lambda first: (grad_gate,), False
     )
     own_hidden_rows = lax.dynamic_slice_in_dim(hidden_low, sp_place * rows, rows, axis=0)
     blocks_result = blocks_back((own_hidden_rows.astype(wide) + result_sum).astype(low))

time: 1060 us -> 1060 us (level)
  starting transfers between devices: 121 us -> 106 us
  Pallas kernels: 383 us -> 395 us
    all_to_all x4, starting transfers between devices: 58.7 us -> 46.9 us  [deal(): lax.all_to_all(blocks, 'fsdp', split_axis=0, concat_axis=0, tiled=True)]
    pallas_call x1, Pallas kernels: 27.7 us -> 38.3 us  [attend_call(): pl.pallas_call(functools.partial(attend_kernel, heads, keys, block), in_s...]
    squeeze x8 -> x7, local copies, waits for them, and re-layouts: 31.1 us -> 30.1 us  [block(): return lax.dynamic_slice(parts, start, (1, half) + parts.shape[2:])[0]]
  transfers between devices with their start and end apart: 84 -> 84, of which waited for: 32 -> 30; matrix products, arithmetic and copies ran while one was open for 17% -> 17% of each run, Pallas kernels for 36% -> 35%
where the time goes in v9:
time: 1060 us; the launch traced here: 1040 us
  Pallas kernels  395 us (37%)
  waiting for transfers between devices  298 us (28%)
  local copies, waits for them, and re-layouts  181 us (17%)
  starting transfers between devices  106 us (10%)
  other arithmetic  47.3 us (4%)
  between operations  15.5 us (1%)
    ppermute x72, waiting for transfers between devices, swap(): return lax.ppermute(value, 'sp', [(i, i ^ bit) for i in range(size)])  234 us
    pallas_call x3, Pallas kernels, rows_call(): pl.pallas_call(rows_kernel, grid=(columns // block,), in_specs=[pl.BlockS...  61.8 us
    all_to_all x4, waiting for transfers between devices, deal(): lax.all_to_all(blocks, 'fsdp', split_axis=0, concat_axis=0, tiled=True)  59.9 us
    ppermute x72, starting transfers between devices, swap(): return lax.ppermute(value, 'sp', [(i, i ^ bit) for i in range(size)])  57.9 us
    unnamed x168, local copies, waits for them, and re-layouts  51.3 us
    pallas_call x1, Pallas kernels, attend_back_call(): pl.pallas_call(functools.partial(attend_back_kernel, heads, keys, block),...  49.9 us
    all_to_all x4, starting transfers between devices, deal(): lax.all_to_all(blocks, 'fsdp', split_axis=0, concat_axis=0, tiled=True)  46.9 us
    pallas_call x1, Pallas kernels, mlp_back_call(): pl.pallas_call(mlp_back_kernel, grid=(total // block,), in_specs=[row(uni...  43.4 us
  transfers between devices with their start and end apart: 84, of which 30 were waited for; matrix products, arithmetic and copies ran while one was open for 17% of the time, Pallas kernels for 35%

profile of v9, /device:TPU:9, one launch (start us, length us, event | category | flops | bytes accessed | tf_op | source)
XLA Modules:
  0.0 1042.1 jit_solution(8522268801741459033)
XLA Ops:
  21.2 38.0 %all-to-all-done.refs_1_._ = bf16[8,48,2560]{2,1,0:T(8,128)(2,1)S(1)} async-done(((bf16[8,48,2560]{2,1,0:T(8,128)(2,1)}), bf16[8,48,2560]{2,1,0:T(8,128)(2,1)S(1)}, u32[]{:S(2)}, u32[]{:S(2)}) %all-to-all-start) | async-done | bytes 1966112 | tf_op jit(solution)/shard_map/all_to_all | solution.py:845
  97.9 15.4 %collective-permute-done.1 = bf16[192,2560]{1,0:T(8,128)(2,1)} collective-permute-done((bf16[192,2560]{1,0:T(8,128)(2,1)}, bf16[192,2560]{1,0:T(8,128)(2,1)}, u32[]{:S(2)}, u32[]{:S(2)}) %collective-permute-start.1) | collective-permute-done | bytes 983072 | tf_op jit(solution)/shard_map/ppermute | solution.py:23
  126.1 12.4 %collective-permute-done.4 = bf16[192,2560]{1,0:T(8,128)(2,1)} collective-permute-done((bf16[192,2560]{1,0:T(8,128)(2,1)S(1)}, bf16[192,2560]{1,0:T(8,128)(2,1)}, u32[]{:S(2)}, u32[]{:S(2)}) %collective-permute-start.4) | collective-permute-done | bytes 983072 | tf_op jit(solution)/shard_map/ppermute | solution.py:23
  146.0 24.4 %shard_map.223 = (bf16[1536,2560]{1,0:T(8,128)(2,1)}, bf16[1536,1024]{1,0:T(8,128)(2,1)}, bf16[1536,256]{1,0:T(8,128)(2,1)S(1)}, bf16[1536,256]{1,0:T(8,128)(2,1)S(1)}) custom-call(bf16[1536,2560]{1,0:T(8,128)(2,1)} %bitcast.17.x_ref, f32[1,2560]{1,0:T(1,128)S(1)} %reshape.298.gain_ref, bf16[2560,1664]{1,0:T(8,128)(2,1)} %all-gather.4.cloned.1.call-done.weight_ref, ...), custom_call_target="tpu_custom_call" | custom-call | flops 96000000000 | tf_op jit(solution)/shard_map/pallas_call | solution.py:177
  172.1 38.3 %shard_map.224 = (bf16[1536,640]{1,0:T(8,128)(2,1)}, f32[1536,8]{1,0:T(8,128)}) custom-call(bf16[1536,1024]{1,0:T(8,128)(2,1)} %get-tuple-element.72.q_ref, bf16[1536,256]{1,0:T(8,128)(2,1)} %copy-done.40, bf16[1536,256]{1,0:T(8,128)(2,1)} %copy-done.41, s32[1536,1]{1,0:T(8,128)} %broadcast_in_dim.224.start_ref), custom_call_target="tpu_custom_call" | custom-call | flops 112000000000 | tf_op jit(solution)/shard_map/pallas_call | solution.py:226
  239.9 17.3 %collective-permute-done.10 = bf16[768,640]{1,0:T(8,128)(2,1)S(1)} collective-permute-done((bf16[768,640]{1,0:T(8,128)(2,1)}, bf16[768,640]{1,0:T(8,128)(2,1)S(1)}, u32[]{:S(2)}, u32[]{:S(2)}) %collective-permute-start.10) | collective-permute-done | bytes 983072 | tf_op jit(solution)/shard_map/ppermute | solution.py:23
  257.7 19.2 %collective-permute-done.13 = bf16[768,640]{1,0:T(8,128)(2,1)S(1)} collective-permute-done((bf16[768,640]{1,0:T(8,128)(2,1)}, bf16[768,640]{1,0:T(8,128)(2,1)S(1)}, u32[]{:S(2)}, u32[]{:S(2)}) %collective-permute-start.13) | collective-permute-done | bytes 983072 | tf_op jit(solution)/shard_map/ppermute | solution.py:23
  299.3 22.0 %all-to-all-done.1.refs_0_ = bf16[8,48,2560]{2,1,0:T(8,128)(2,1)} async-done(((bf16[8,48,2560]{2,1,0:T(8,128)(2,1)}), bf16[8,48,2560]{2,1,0:T(8,128)(2,1)}, u32[]{:S(2)}, u32[]{:S(2)}) %all-to-all-start.1) | async-done | bytes 1966112 | tf_op jit(solution)/shard_map/all_to_all | solution.py:845
  338.9 16.1 %collective-permute-done.19 = bf16[768,640]{1,0:T(8,128)(2,1)S(1)} collective-permute-done((bf16[768,640]{1,0:T(8,128)(2,1)}, bf16[768,640]{1,0:T(8,128)(2,1)S(1)}, u32[]{:S(2)}, u32[]{:S(2)}) %collective-permute-start.19) | collective-permute-done | bytes 983072 | tf_op jit(solution)/shard_map/ppermute | solution.py:23
  379.8 36.9 %shard_map.228 = (bf16[1536,1792]{1,0:T(8,128)(2,1)}, bf16[1536,1792]{1,0:T(8,128)(2,1)}, bf16[1536,1792]{1,0:T(8,128)(2,1)}) custom-call(bf16[1536,2560]{1,0:T(8,128)(2,1)} %copy-done.5, bf16[2560,3584]{1,0:T(8,128)(2,1)} %all-gather.6.cloned.1.call-done.gate_weight_ref.up_weight_ref.weight_ref, ...), custom_call_target="tpu_custom_call" | custom-call | flops 147999997952 | tf_op jit(solution)/shard_map/pallas_call | solution.py:334
  438.1 19.9 %shard_map.229.refs_0_ = bf16[1536,2560]{1,0:T(8,128)(2,1)} custom-call(bf16[1536,1792]{1,0:T(8,128)(2,1)} %get-tuple-element.78.left_ref.refs_1_, bf16[1792,2560]{1,0:T(8,128)(2,1)} %all-gather.8.cloned.1.call-done.right_ref.down_ref), custom_call_target="tpu_custom_call" | custom-call | flops 80000000000 | tf_op jit(solution)/shard_map/pallas_call | solution.py:627
  460.1 20.3 %shard_map.236.refs_0_ = bf16[1792,2560]{1,0:T(8,128)(2,1)} custom-call(bf16[1536,1792]{1,0:T(8,128)(2,1)} %get-tuple-element.78.left_ref.refs_1_, bf16[1536,2560]{1,0:T(8,128)(2,1)} %bitcast.190, bf16[1536,2560]{1,0:T(8,128)(2,1)} %shard_map.229.refs_0_), custom_call_target="tpu_custom_call" | custom-call | flops 80000000000 | tf_op jit(solution)/shard_map/pallas_call | solution.py:602
  490.2 25.5 %shard_map.237 = (bf16[1536,1792]{1,0:T(8,128)(2,1)}, bf16[1536,1792]{1,0:T(8,128)(2,1)}) custom-call(bf16[1536,2560]{1,0:T(8,128)(2,1)} %bitcast.191, bf16[1792,2560]{1,0:T(8,128)(2,1)} %all-gather.8.cloned.1.call-done.right_ref.down_ref, bf16[1536,1792]{1,0:T(8,128)(2,1)} %get-tuple-element.79.gate_ref, bf16[1536,1792]{1,0:T(8,128)(2,1)} %get-tuple-element.80.up_ref, ...), custom_call_target="tpu_custom_call" | custom-call | flops 103999995904 | tf_op jit(solution)/shard_map/pallas_call | solution.py:366
  515.7 20.5 %shard_map.238.refs_1_.refs_0_ = bf16[2560,1792]{1,0:T(8,128)(2,1)} custom-call(bf16[1536,2560]{1,0:T(8,128)(2,1)} %copy-done.5, bf16[1536,1792]{1,0:T(8,128)(2,1)} %get-tuple-element.81.right_ref.d_gate_ref), custom_call_target="tpu_custom_call" | custom-call | flops 80000000000 | tf_op jit(solution)/shard_map/pallas_call | solution.py:602
  544.8 43.4 %shard_map.241 = (bf16[4,1536,640]{2,1,0:T(8,128)(2,1)}, f32[1,2560]{1,0:T(1,128)}) custom-call(bf16[1536,1792]{1,0:T(8,128)(2,1)} %get-tuple-element.81.right_ref.d_gate_ref, bf16[1536,1792]{1,0:T(8,128)(2,1)} %get-tuple-element.92.d_up_ref.right_ref, bf16[2560,3584]{1,0:T(8,128)(2,1)} %all-gather.6.cloned.1.call-done.gate_weight_ref.up_weight_ref.weight_ref, ...), custom_call_target="tpu_custom_call" | custom-call | flops 176000008192 | tf_op jit(solution)/shard_map/pallas_call | solution.py:421
  599.4 13.4 %collective-permute-done.35.refs_1_.refs_0_ = bf16[768,640]{1,0:T(8,128)(2,1)S(1)} collective-permute-done((bf16[768,640]{1,0:T(8,128)(2,1)}, bf16[768,640]{1,0:T(8,128)(2,1)S(1)}, u32[]{:S(2)}, u32[]{:S(2)}) %collective-permute-start.35) | collective-permute-done | bytes 983072 | tf_op jit(solution)/shard_map/ppermute | solution.py:23
  614.6 21.0 %shard_map.244.refs_1_.refs_0_ = bf16[2560,1792]{1,0:T(8,128)(2,1)} custom-call(bf16[1536,2560]{1,0:T(8,128)(2,1)} %copy-done.5, bf16[1536,1792]{1,0:T(8,128)(2,1)} %get-tuple-element.92.d_up_ref.right_ref, bf16[768,640]{1,0:T(8,128)(2,1)} %copy-done.45, bf16[768,640]{1,0:T(8,128)(2,1)} %copy-done.44), custom_call_target="tpu_custom_call" | custom-call | tf_op jit(solution)/shard_map/pallas_call | solution.py:602
  638.3 16.9 %collective-permute-done.38 = bf16[768,640]{1,0:T(8,128)(2,1)S(1)} collective-permute-done((bf16[768,640]{1,0:T(8,128)(2,1)S(1)}, bf16[768,640]{1,0:T(8,128)(2,1)S(1)}, u32[]{:S(2)}, u32[]{:S(2)}) %collective-permute-start.38) | collective-permute-done | bytes 983072 | tf_op jit(solution)/shard_map/ppermute | solution.py:23
  723.6 24.0 %all-to-all-start.2 = ((bf16[8,48,2560]{2,1,0:T(8,128)(2,1)}), bf16[8,48,2560]{2,1,0:T(8,128)(2,1)}, u32[]{:S(2)}, u32[]{:S(2)}) async-start(bf16[8,48,2560]{2,1,0:T(8,128)(2,1)} %gather_fusion.4), calls=%async_computation.2 | async-start | bytes 3932160 | tf_op jit(solution)/shard_map/all_to_all | solution.py:845
  756.9 49.9 %shard_map.252.d_qkv_ref = bf16[1536,960]{1,0:T(8,128)(2,1)} custom-call(bf16[1536,1024]{1,0:T(8,128)(2,1)} %get-tuple-element.72.q_ref, bf16[1536,256]{1,0:T(8,128)(2,1)} %copy-done.40, bf16[1536,256]{1,0:T(8,128)(2,1)} %copy-done.41, bf16[1536,640]{1,0:T(8,128)(2,1)} %pad_maximum_fusion.grad_ref.refs_1_, f32[8,1536]{1,0:T(8,128)} %bitcast.207, ...), custom_call_target="tpu_custom_call" | custom-call | flops 99999997952 | tf_op jit(solution)/shard_map/pallas_call | solution.py:299
  809.6 19.4 %collective-permute-done.46.refs_1_.refs_2_ = bf16[224,2560]{1,0:T(8,128)(2,1)} collective-permute-done((bf16[224,2560]{1,0:T(8,128)(2,1)S(1)}, bf16[224,2560]{1,0:T(8,128)(2,1)}, u32[]{:S(2)}, u32[]{:S(2)}) %collective-permute-start.46) | collective-permute-done | bytes 1146912 | tf_op jit(solution)/shard_map/ppermute | solution.py:23
  829.1 19.6 %shard_map.255 = (bf16[1536,2560]{1,0:T(8,128)(2,1)}, f32[1,2560]{1,0:T(1,128)}) custom-call(s32[1]{0:T(128)} %bitcast.37.place_ref, bf16[1536,960]{1,0:T(8,128)(2,1)} %shard_map.252.d_qkv_ref, bf16[2560,1664]{1,0:T(8,128)(2,1)} %all-gather.4.cloned.1.call-done.weight_ref, bf16[1536,2560]{1,0:T(8,128)(2,1)} %bitcast.17.x_ref, f32[1,2560]{1,0:T(1,128)} %copy-done.37, ...), custom_call_target="tpu_custom_call" | custom-call | flops 80000000000 | tf_op jit(solution)/shard_map/pallas_call | solution.py:462
  854.4 11.5 %shard_map.261 = bf16[2560,1024]{1,0:T(8,128)(2,1)} custom-call(bf16[1536,2560]{1,0:T(8,128)(2,1)} %get-tuple-element.126.normed_ref, bf16[1536,960]{1,0:T(8,128)(2,1)S(1)} %copy-done.39, f32[8,2560]{1,0:T(8,128)S(1)} %maximum_maximum_fusion.2.gain_ref, bf16[320,1792]{1,0:T(8,128)(2,1)S(1)} %collective-permute-done.53.refs_3_.refs_0_), custom_call_target="tpu_custom_call" | custom-call | flops 48000000000 | tf_op jit(solution)/shard_map/pallas_call | solution.py:656
  912.9 19.8 %collective-permute-done.56 = bf16[192,2560]{1,0:T(8,128)(2,1)S(1)} collective-permute-done((bf16[192,2560]{1,0:T(8,128)(2,1)S(1)}, bf16[192,2560]{1,0:T(8,128)(2,1)S(1)}, u32[]{:S(2)}, u32[]{:S(2)}) %collective-permute-start.56) | collective-permute-done | bytes 983072 | tf_op jit(solution)/shard_map/ppermute | solution.py:23
  (498 shorter events, 461.6 us)
Async XLA Ops:
  16.5 126.6 %all-gather.4.cloned.1.call-start = ((), (), s32[]{:S(2)}) async-start(), calls=%async_computation.9 | async-start | bytes 9584640 | tf_op jit(solution)/shard_map/all_gather | solution.py:861
  60.5 319.3 %all-gather.6.cloned.1.call-start = ((), (), s32[]{:S(2)}) async-start(), calls=%async_computation.10 | async-start | bytes 20643840 | tf_op jit(solution)/shard_map/all_gather | solution.py:861
  218.3 103.0 %all-to-all-start.1 = ((bf16[8,48,2560]{2,1,0:T(8,128)(2,1)}), bf16[8,48,2560]{2,1,0:T(8,128)(2,1)}, u32[]{:S(2)}, u32[]{:S(2)}) async-start(bf16[8,48,2560]{2,1,0:T(8,128)(2,1)} %shard_map.231), calls=%async_computation.1 | async-start | bytes 3932160 | tf_op jit(solution)/shard_map/all_to_all | solution.py:845
  226.7 211.5 %all-gather.8.cloned.1.call-start = ((), (), s32[]{:S(2)}) async-start(), calls=%async_computation.11 | async-start | bytes 10321920 | tf_op jit(solution)/shard_map/all_gather | solution.py:861
  297.7 455.3 %reduce-scatter.6.cloned.1.call-start = ((), (), s32[]{:S(2)}) async-start(), calls=%async_computation.12 | async-start | bytes 10321920 | tf_op jit(solution)/shard_map/reduce_scatter | solution.py:854
  376.6 50.2 %collective-permute-start.24 = (bf16[192,2560]{1,0:T(8,128)(2,1)}, bf16[192,2560]{1,0:T(8,128)(2,1)}, u32[]{:S(2)}, u32[]{:S(2)}) collective-permute-start(bf16[192,2560]{1,0:T(8,128)(2,1)} %get-tuple-element.171), channel_id=1, source_target_pairs={{0,8},{8,0},{16,24},{24,16},{1,9},{9,1},{17,25},{25,17},{2,10},{10... | collective-permute-start | bytes 2949128 | tf_op jit(solution)/shard_map/ppermute | solution.py:23
  378.3 53.0 %collective-permute-start.26 = (bf16[192,2560]{1,0:T(8,128)(2,1)}, bf16[192,2560]{1,0:T(8,128)(2,1)}, u32[]{:S(2)}, u32[]{:S(2)}) collective-permute-start(bf16[192,2560]{1,0:T(8,128)(2,1)} %get-tuple-element.171), channel_id=1, source_target_pairs={{0,16},{8,24},{16,0},{24,8},{1,17},{9,25},{17,1},{25,9},{2,18},{10... | collective-permute-start | bytes 2949128 | tf_op jit(solution)/shard_map/ppermute | solution.py:23
  480.4 272.6 %reduce-scatter.8.cloned.1.call-start = ((), (), s32[]{:S(2)}) async-start(), calls=%async_computation.13 | async-start | bytes 10321920 | tf_op jit(solution)/shard_map/reduce_scatter | solution.py:854
  488.6 56.2 %collective-permute-start.30 = (bf16[192,2560]{1,0:T(8,128)(2,1)}, bf16[192,2560]{1,0:T(8,128)(2,1)}, u32[]{:S(2)}, u32[]{:S(2)}) collective-permute-start(bf16[192,2560]{1,0:T(8,128)(2,1)} %get-tuple-element.165), channel_id=1, source_target_pairs={{0,16},{8,24},{16,0},{24,8},{1,17},{9,25},{17,1},{25,9},{2,18},{10... | collective-permute-start | bytes 2949128 | tf_op jit(solution)/shard_map/ppermute | solution.py:23
  489.8 55.0 %collective-permute-start.21 = (bf16[192,2560]{1,0:T(8,128)(2,1)}, bf16[192,2560]{1,0:T(8,128)(2,1)}, u32[]{:S(2)}, u32[]{:S(2)}) collective-permute-start(bf16[192,2560]{1,0:T(8,128)(2,1)} %get-tuple-element.168), channel_id=1, source_target_pairs={{0,8},{8,0},{16,24},{24,16},{1,9},{9,1},{17,25},{25,17},{2,10},{10... | collective-permute-start | bytes 2949128 | tf_op jit(solution)/shard_map/ppermute | solution.py:23
  536.3 410.8 %reduce-scatter.14.cloned.1.call-start = ((), (), s32[]{:S(2)}) async-start(), calls=%async_computation.16 | async-start | bytes 10321920 | tf_op jit(solution)/shard_map/reduce_scatter | solution.py:854
  598.4 56.8 %collective-permute-start.33 = (bf16[768,640]{1,0:T(8,128)(2,1)}, bf16[768,640]{1,0:T(8,128)(2,1)}, u32[]{:S(2)}, u32[]{:S(2)}) collective-permute-start(bf16[768,640]{1,0:T(8,128)(2,1)} %get-tuple-element.159), channel_id=1, source_target_pairs={{0,8},{8,0},{16,24},{24,16},{1,9},{9,1},{17,25},{25,17},{2,10},{10... | collective-permute-start | bytes 2949128 | tf_op jit(solution)/shard_map/ppermute | solution.py:23
  690.3 57.4 %collective-permute-start.43 = (bf16[768,640]{1,0:T(8,128)(2,1)}, bf16[768,640]{1,0:T(8,128)(2,1)}, u32[]{:S(2)}, u32[]{:S(2)}) collective-permute-start(bf16[768,640]{1,0:T(8,128)(2,1)} %get-tuple-element.149), channel_id=1, source_target_pairs={{0,16},{8,24},{16,0},{24,8},{1,17},{9,25},{17,1},{25,9},{2,18},{10... | collective-permute-start | bytes 2949128 | tf_op jit(solution)/shard_map/ppermute | solution.py:23
  691.7 56.0 %collective-permute-start.39 = (bf16[768,640]{1,0:T(8,128)(2,1)}, bf16[768,640]{1,0:T(8,128)(2,1)}, u32[]{:S(2)}, u32[]{:S(2)}) collective-permute-start(bf16[768,640]{1,0:T(8,128)(2,1)} %get-tuple-element.151), channel_id=1, source_target_pairs={{0,8},{8,0},{16,24},{24,16},{1,9},{9,1},{17,25},{25,17},{2,10},{10... | collective-permute-start | bytes 2949128 | tf_op jit(solution)/shard_map/ppermute | solution.py:23
  723.6 147.4 %all-to-all-start.2 = ((bf16[8,48,2560]{2,1,0:T(8,128)(2,1)}), bf16[8,48,2560]{2,1,0:T(8,128)(2,1)}, u32[]{:S(2)}, u32[]{:S(2)}) async-start(bf16[8,48,2560]{2,1,0:T(8,128)(2,1)} %gather_fusion.4), calls=%async_computation.2 | async-start | bytes 3932160 | tf_op jit(solution)/shard_map/all_to_all | solution.py:845
  747.5 203.9 %reduce-scatter.12.cloned.1.call-start = ((), (), s32[]{:S(2)}) async-start(), calls=%async_computation.15 | async-start | bytes 3686400 | tf_op jit(solution)/shard_map/reduce_scatter | solution.py:854
  753.0 54.0 %collective-permute-start.49 = (bf16[320,1792]{1,0:T(8,128)(2,1)}, bf16[320,1792]{1,0:T(8,128)(2,1)}, u32[]{:S(2)}, u32[]{:S(2)}) collective-permute-start(bf16[320,1792]{1,0:T(8,128)(2,1)} %shard_map.254.refs_0_), channel_id=1, source_target_pairs={{0,16},{8,24},{16,0},{24,8},{1,17},{9,25},{17,1},{25,9},{2,18},{10... | collective-permute-start | bytes 3440648 | tf_op jit(solution)/shard_map/ppermute | solution.py:23
  753.5 56.1 %collective-permute-start.48 = (bf16[320,1792]{1,0:T(8,128)(2,1)}, bf16[320,1792]{1,0:T(8,128)(2,1)}, u32[]{:S(2)}, u32[]{:S(2)}) collective-permute-start(bf16[320,1792]{1,0:T(8,128)(2,1)} %shard_map.254.refs_0_), channel_id=1, source_target_pairs={{0,8},{8,0},{16,24},{24,16},{1,9},{9,1},{17,25},{25,17},{2,10},{10... | collective-permute-start | bytes 3440648 | tf_op jit(solution)/shard_map/ppermute | solution.py:23
  754.3 55.3 %collective-permute-start.47 = (bf16[224,2560]{1,0:T(8,128)(2,1)S(1)}, bf16[224,2560]{1,0:T(8,128)(2,1)}, u32[]{:S(2)}, u32[]{:S(2)}) collective-permute-start(bf16[224,2560]{1,0:T(8,128)(2,1)S(1)} %copy-done.14), channel_id=1, source_target_pairs={{0,24},{8,16},{16,8},{24,0},{1,25},{9,17},{17,9},{25,1},{2,26},{10... | collective-permute-start | bytes 3440648 | tf_op jit(solution)/shard_map/ppermute | solution.py:23
  755.7 73.2 %collective-permute-start.46 = (bf16[224,2560]{1,0:T(8,128)(2,1)S(1)}, bf16[224,2560]{1,0:T(8,128)(2,1)}, u32[]{:S(2)}, u32[]{:S(2)}) collective-permute-start(bf16[224,2560]{1,0:T(8,128)(2,1)S(1)} %copy-done.14), channel_id=1, source_target_pairs={{0,16},{8,24},{16,0},{24,8},{1,17},{9,25},{17,1},{25,9},{2,18},{10... | collective-permute-start | bytes 3440648 | tf_op jit(solution)/shard_map/ppermute | solution.py:23
  756.1 73.0 %collective-permute-start.45 = (bf16[224,2560]{1,0:T(8,128)(2,1)S(1)}, bf16[224,2560]{1,0:T(8,128)(2,1)}, u32[]{:S(2)}, u32[]{:S(2)}) collective-permute-start(bf16[224,2560]{1,0:T(8,128)(2,1)S(1)} %copy-done.14), channel_id=1, source_target_pairs={{0,8},{8,0},{16,24},{24,16},{1,9},{9,1},{17,25},{25,17},{2,10},{10... | collective-permute-start | bytes 3440648 | tf_op jit(solution)/shard_map/ppermute | solution.py:23
  806.8 159.7 %reduce-scatter.10.cloned.1.call-start = ((), (), s32[]{:S(2)}) async-start(), calls=%async_computation.14 | async-start | bytes 5898240 | tf_op jit(solution)/shard_map/reduce_scatter | solution.py:854
  881.4 51.3 %collective-permute-start.50 = (bf16[192,2560]{1,0:T(8,128)(2,1)}, bf16[192,2560]{1,0:T(8,128)(2,1)}, u32[]{:S(2)}, u32[]{:S(2)}) collective-permute-start(bf16[192,2560]{1,0:T(8,128)(2,1)} %get-tuple-element.143), channel_id=1, source_target_pairs={{0,8},{8,0},{16,24},{24,16},{1,9},{9,1},{17,25},{25,17},{2,10},{10... | collective-permute-start | bytes 2949128 | tf_op jit(solution)/shard_map/ppermute | solution.py:23
  938.2 86.8 %all-to-all-start.3 = ((bf16[8,48,2560]{2,1,0:T(8,128)(2,1)}), bf16[8,48,2560]{2,1,0:T(8,128)(2,1)}, u32[]{:S(2)}, u32[]{:S(2)}) async-start(bf16[8,48,2560]{2,1,0:T(8,128)(2,1)} %gather_fusion.6), calls=%async_computation.5 | async-start | bytes 3932160 | tf_op jit(solution)/shard_map/all_to_all | solution.py:845
  (144 other events, 2509.5 us)
Sparse Core Ops, SparseCore 0:
  60.6 82.4 all-gather.3
  145.3 201.2 all-gather.5
  348.3 89.8 all-gather.7
  480.5 97.2 reduce-scatter.5
  580.6 95.3 reduce-scatter.7
  678.2 138.0 reduce-scatter.13
  819.2 38.3 reduce-scatter.11
  867.1 58.6 reduce-scatter.9
